TPU v7x, 32 devices: a whole 2x2x4 slice. The times are simulated.
32 devices in a mesh: dp: 8 (over z, x), tensor: 4 (over y, core).
Axes of the slice: x: 2, y: 2, z: 4, core: 2. Of those that a mesh axis runs over, the one named last changes fastest.
Arguments:
- block_input: bfloat16 [6304, 768], P(('dp', 'tensor')), may hold values from -6 to 6
- first_norm: bfloat16 [768], P('dp'), may hold values from 0.5 to 1.5
- first_qkv: bfloat16 [768, 3, 768], P('dp', None, 'tensor')
- first_out: bfloat16 [768, 768], P('tensor', 'dp'), may hold values from -0.875 to 0.875
- second_norm: bfloat16 [768], P('dp'), may hold values from 0.5 to 1.5
- dense_up: bfloat16 [768, 3072], P('dp', 'tensor'), may hold values from -0.21875 to 0.21875
- dense_down: bfloat16 [3072, 768], P('tensor', 'dp'), may hold values from -0.15625 to 0.15625
- third_norm: bfloat16 [768], P('dp'), may hold values from 0.5 to 1.5
- second_qkv: bfloat16 [768, 3, 768], P('dp', None, 'tensor')
- second_out: bfloat16 [768, 768], P('tensor', 'dp'), may hold values from -0.875 to 0.875
- fourth_norm: bfloat16 [768], P('dp'), may hold values from 0.5 to 1.5
- router_weight: bfloat16 [768, 8], P('dp'), may hold values from -0.4375 to 0.4375
- expert_up: bfloat16 [8, 768, 3072], P(None, 'dp', 'tensor'), may hold values from -0.21875 to 0.21875
- expert_down: bfloat16 [8, 3072, 768], P(None, 'tensor', 'dp'), may hold values from -0.4375 to 0.4375
- expert_ids: int32 [6304, 2], P('dp'), may hold values from 0 to 7, as said below
- expert_slots: int32 [6304, 2], P('dp'), may hold values from 0 to 197, as said below
- image_counts: int32 [8], P('dp'), may hold values from 3 to 4, as said below
- cotangent: bfloat16 [6304, 768], P(('dp', 'tensor')), may hold values from -6 to 6
Outputs:
- block_output: float32 [6304, 768], P(('dp', 'tensor'))
- input_grad: float32 [6304, 768], P(('dp', 'tensor'))
- grad_first_norm: float32 [768], P('dp')
- grad_first_qkv: float32 [768, 3, 768], P('dp', None, 'tensor')
- grad_first_out: float32 [768, 768], P('tensor', 'dp')
- grad_second_norm: float32 [768], P('dp')
- grad_dense_up: float32 [768, 3072], P('dp', 'tensor')
- grad_dense_down: float32 [3072, 768], P('tensor', 'dp')
- grad_third_norm: float32 [768], P('dp')
- grad_second_qkv: float32 [768, 3, 768], P('dp', None, 'tensor')
- grad_second_out: float32 [768, 768], P('tensor', 'dp')
- grad_fourth_norm: float32 [768], P('dp')
- grad_router: float32 [768, 8], P('dp')
- grad_expert_up: float32 [8, 768, 3072], P(None, 'dp', 'tensor')
- grad_expert_down: float32 [8, 3072, 768], P(None, 'tensor', 'dp')
- clipped_first_qkv: float32 [768, 3, 768], P('dp', None, 'tensor')
- clipped_second_qkv: float32 [768, 3, 768], P('dp', None, 'tensor')
- clip_scales: float32 [2, 12], P(None, 'tensor')
Inputs may be any that keep to these rules, and one draw needn't show every extreme that they name: `expert_ids`: each token names two different experts. `expert_slots`: the rank of a token's choice among the choices of its expert within its group of 788 tokens, counted in token order and then choice order; ranks of 197 or more are given as 197 and mark dropped choices. `image_counts`: the live images of a group are its first image slots.
All inputs are finite; a program needn't handle non-finite values.
Results may differ from a plain program's by a relative error of at most 0.04.
Values may be sent and summed in bfloat16 or wider, within the bound.
No kernel may reach another device: no remote copies, remote signals or barrier semaphores. Data moves between devices by JAX's collectives and lax.ppermute only.
A program may use at most 256 MiB of HBM per device.

v0:
```python
import jax
import jax.numpy as jnp
from jax import lax
from jax.sharding import PartitionSpec as P

HD = 64
L = 197
CAP = 197


epsilon = 1e-06
clip_tau = 2.5


def layer_norm(values, norm_gain):
    center = values - jnp.mean(values, axis=-1, keepdims=True)
    spread = jnp.mean(center * center, axis=-1, keepdims=True)
    return center * lax.rsqrt(spread + epsilon) * norm_gain


def exact_gelu(values):
    return jax.nn.gelu(values, approximate=False)


def gelu_back(values, upstream):
    return jax.vjp(exact_gelu, values)[1](upstream)[0]


def norm_back(residual, norm_gain, upstream):
    pullback = jax.vjp(layer_norm, residual, norm_gain.astype(jnp.float32))[1]
    return pullback(upstream)


def gather_rows(values):
    return lax.all_gather(values, "tensor", axis=0, tiled=True)


def scatter_rows(values):
    return lax.psum_scatter(
        values.astype(jnp.bfloat16), "tensor", scatter_dimension=0, tiled=True
    ).astype(jnp.float32)


def sum_gains(first_gain, second_gain):
    return lax.psum((first_gain, second_gain), "tensor")


def split_heads(projected, images, head_size):
    row_count, triple, columns = projected.shape
    pieces = projected.reshape(images, row_count // images, triple, columns // head_size, head_size)
    return (pieces[:, :, 0], pieces[:, :, 1], pieces[:, :, 2])


def attend_scores(queries, keyset, head_size):
    scores = jnp.einsum("iqhd,ikhd->ihqk", queries, keyset, preferred_element_type=jnp.float32)
    return scores * head_size ** (-0.5)


def attend_forward(normed_full, weight_qkv, images, head_size, live_images):
    projected = jnp.einsum(
        "rd,dcf->rcf", normed_full, weight_qkv, preferred_element_type=jnp.float32
    ).astype(jnp.bfloat16)
    queries, keyset, values = split_heads(projected, images, head_size)
    scores = attend_scores(queries, keyset, head_size)
    head_peak = jnp.max(jnp.where(live_images[:, None, None, None], scores, -1e30), axis=(0, 2, 3))
    attn_probs = jax.nn.softmax(scores, axis=-1).astype(jnp.bfloat16)
    attended = jnp.einsum("ihqk,ikhd->iqhd", attn_probs, values, preferred_element_type=jnp.float32)
    return (projected, attended.astype(jnp.bfloat16).reshape(normed_full.shape[0], -1), head_peak)


def attend_backward(projected, grad_attended, images, head_size):
    queries, keyset, values = split_heads(projected, images, head_size)
    scores = attend_scores(queries, keyset, head_size)
    attn_probs = jax.nn.softmax(scores, axis=-1)
    grad_heads = grad_attended.reshape(queries.shape)
    grad_values = jnp.einsum(
        "ihqk,iqhd->ikhd",
        attn_probs.astype(jnp.bfloat16),
        grad_heads,
        preferred_element_type=jnp.float32,
    )
    grad_probs = jnp.einsum(
        "iqhd,ikhd->ihqk", grad_heads, values, preferred_element_type=jnp.float32
    )
    grad_scores = attn_probs * (
        grad_probs - jnp.sum(grad_probs * attn_probs, axis=-1, keepdims=True)
    )
    grad_scores = grad_scores.astype(jnp.bfloat16)
    factor = head_size ** (-0.5)
    grad_queries = (
        jnp.einsum("ihqk,ikhd->iqhd", grad_scores, keyset, preferred_element_type=jnp.float32)
        * factor
    )
    grad_keyset = (
        jnp.einsum("ihqk,iqhd->ikhd", grad_scores, queries, preferred_element_type=jnp.float32)
        * factor
    )
    stacked = jnp.stack([grad_queries, grad_keyset, grad_values], axis=2).astype(jnp.bfloat16)
    return stacked.reshape(projected.shape)


def block_attention(residual, norm_gain, weight_qkv, weight_out, images, head_size, live_images):
    normed = layer_norm(residual, norm_gain.astype(jnp.float32)).astype(jnp.bfloat16)
    normed_full = gather_rows(normed)
    projected, attended, head_peak = attend_forward(
        normed_full, weight_qkv, images, head_size, live_images
    )
    branch = scatter_rows(jnp.dot(attended, weight_out, preferred_element_type=jnp.float32))
    return (residual + branch, (normed_full, projected, attended), head_peak)


def block_attention_back(
    residual, upstream, norm_gain, weight_qkv, weight_out, stored, images, head_size
):
    normed_full, projected, attended = stored
    grad_full = gather_rows(upstream.astype(jnp.bfloat16))
    grad_out = jnp.einsum("rf,rd->fd", attended, grad_full, preferred_element_type=jnp.float32)
    grad_attended = jnp.einsum(
        "rd,fd->rf", grad_full, weight_out, preferred_element_type=jnp.float32
    ).astype(jnp.bfloat16)
    grad_projected = attend_backward(projected, grad_attended, images, head_size)
    grad_qkv = jnp.einsum(
        "rd,rcf->dcf", normed_full, grad_projected, preferred_element_type=jnp.float32
    )
    grad_normed = scatter_rows(
        jnp.einsum("rcf,dcf->rd", grad_projected, weight_qkv, preferred_element_type=jnp.float32)
    )
    grad_residual, grad_gain = norm_back(residual, norm_gain, grad_normed)
    return (upstream + grad_residual, grad_gain, grad_qkv, grad_out)


def block_mlp(residual, norm_gain, weight_up, weight_down):
    normed = layer_norm(residual, norm_gain.astype(jnp.float32)).astype(jnp.bfloat16)
    normed_full = gather_rows(normed)
    hidden = jnp.dot(normed_full, weight_up, preferred_element_type=jnp.float32)
    active = exact_gelu(hidden).astype(jnp.bfloat16)
    branch = scatter_rows(jnp.dot(active, weight_down, preferred_element_type=jnp.float32))
    return (residual + branch, (normed_full, hidden, active))


def block_mlp_back(residual, upstream, norm_gain, weight_up, weight_down, stored):
    normed_full, hidden, active = stored
    grad_full = gather_rows(upstream.astype(jnp.bfloat16))
    grad_down = jnp.einsum("rf,rd->fd", active, grad_full, preferred_element_type=jnp.float32)
    grad_active = jnp.einsum(
        "rd,fd->rf", grad_full, weight_down, preferred_element_type=jnp.float32
    )
    grad_hidden = gelu_back(hidden, grad_active).astype(jnp.bfloat16)
    grad_up = jnp.einsum("rd,rf->df", normed_full, grad_hidden, preferred_element_type=jnp.float32)
    grad_normed = scatter_rows(
        jnp.einsum("rf,df->rd", grad_hidden, weight_up, preferred_element_type=jnp.float32)
    )
    grad_residual, grad_gain = norm_back(residual, norm_gain, grad_normed)
    return (upstream + grad_residual, grad_gain, grad_up, grad_down)


def clip_root(head_peak):
    return jnp.sqrt(clip_tau / jnp.maximum(head_peak, clip_tau))


def clip_columns(weight_local, head_root, head_size):
    column = jnp.repeat(head_root, head_size)
    scales = jnp.stack([column, column, jnp.ones_like(column)])
    return weight_local.astype(jnp.float32) * scales[None]


def local(
    block_input,
    first_norm,
    first_qkv,
    first_out,
    second_norm,
    dense_up,
    dense_down,
    third_norm,
    second_qkv,
    second_out,
    fourth_norm,
    router_weight,
    expert_up,
    expert_down,
    expert_ids,
    expert_slots,
    image_counts,
    cotangent,
):
    rows_local = block_input.shape[0]
    rows_full = rows_local * lax.axis_size("tensor")
    images = rows_full // L
    head_size = HD
    experts = expert_up.shape[0]
    capacity = CAP
    first_row = lax.axis_index("tensor") * rows_local
    live_count = image_counts[0]
    local_live = ((first_row + jnp.arange(rows_local)) // L < live_count).astype(jnp.float32)
    full_live = (jnp.arange(rows_full) // L < live_count).astype(jnp.float32)
    live_images = jnp.arange(images) < live_count

    def dense_fetch():
        return (
            lax.all_gather(first_norm, "dp", axis=0, tiled=True),
            lax.all_gather(first_qkv, "dp", axis=0, tiled=True),
            lax.all_gather(first_out, "dp", axis=1, tiled=True),
            lax.all_gather(second_norm, "dp", axis=0, tiled=True),
            lax.all_gather(dense_up, "dp", axis=0, tiled=True),
            lax.all_gather(dense_down, "dp", axis=1, tiled=True),
        )

    def moe_fetch():
        return (
            lax.all_gather(third_norm, "dp", axis=0, tiled=True),
            lax.all_gather(second_qkv, "dp", axis=0, tiled=True),
            lax.all_gather(second_out, "dp", axis=1, tiled=True),
            lax.all_gather(fourth_norm, "dp", axis=0, tiled=True),
            lax.all_gather(router_weight, "dp", axis=0, tiled=True),
            lax.all_gather(expert_up, "dp", axis=1, tiled=True),
            lax.all_gather(expert_down, "dp", axis=2, tiled=True),
        )

    dense_full = dense_fetch()
    residual_zero = block_input.astype(jnp.float32)
    residual_one, attn_first, peak_first = block_attention(
        residual_zero, dense_full[0], dense_full[1], dense_full[2], images, head_size, live_images
    )
    residual_two, mlp_stored = block_mlp(residual_one, dense_full[3], dense_full[4], dense_full[5])
    moe_full = moe_fetch()
    residual_three, attn_second, peak_second = block_attention(
        residual_two, moe_full[0], moe_full[1], moe_full[2], images, head_size, live_images
    )
    moe_normed = layer_norm(residual_three, moe_full[3].astype(jnp.float32)).astype(jnp.bfloat16)
    moe_input = gather_rows(moe_normed)
    logits = jnp.dot(moe_input, moe_full[4], preferred_element_type=jnp.float32)
    route_probs = jax.nn.softmax(logits, axis=-1)
    kept_mask = expert_slots < capacity
    pair_number = jnp.arange(2 * rows_full, dtype=jnp.int32)
    slot_index = (expert_ids * capacity + expert_slots).reshape(-1)
    kept_flat = kept_mask.reshape(-1)
    write_target = jnp.where(kept_flat, slot_index, experts * capacity + pair_number)
    target = jnp.where(kept_flat, slot_index, experts * capacity)
    pair_of_slot = (
        jnp.zeros((experts * capacity + 2 * rows_full,), jnp.int32)
        .at[write_target]
        .set(pair_number)[: experts * capacity]
    )
    slot_filled = (
        jnp.zeros((experts * capacity + 2 * rows_full,), jnp.float32)
        .at[write_target]
        .set(1.0)[: experts * capacity]
    )
    chosen = (expert_ids[:, :, None] == jnp.arange(experts)[None, None, :]).astype(jnp.float32)
    keep_live = kept_mask.astype(jnp.float32) * full_live[:, None]
    gates = jnp.sum(chosen * route_probs[:, None, :], axis=-1) * keep_live
    slot_token = pair_of_slot // 2
    slot_gate = gates.reshape(-1)[pair_of_slot] * slot_filled
    dispatched = (moe_input[slot_token] * slot_filled[:, None].astype(jnp.bfloat16)).reshape(
        experts, capacity, -1
    )
    expert_hidden = jnp.einsum(
        "ecd,edf->ecf", dispatched, moe_full[5], preferred_element_type=jnp.float32
    )
    expert_act = exact_gelu(expert_hidden).astype(jnp.bfloat16)
    expert_result = jnp.einsum(
        "ecf,efd->ecd", expert_act, moe_full[6], preferred_element_type=jnp.float32
    )
    feature_count = expert_result.shape[2]
    padded_result = jnp.concatenate(
        [
            expert_result.reshape(experts * capacity, feature_count),
            jnp.zeros((1, feature_count), jnp.float32),
        ],
        axis=0,
    )
    pair_result = padded_result[target].reshape(rows_full, 2, feature_count)
    combined = jnp.sum(gates[:, :, None] * pair_result, axis=1)
    residual_four = residual_three + scatter_rows(combined)
    block_output = residual_four * local_live[:, None]
    peak_first_all, peak_second_all = lax.pmax((peak_first, peak_second), "dp")
    root_first = clip_root(peak_first_all)
    root_second = clip_root(peak_second_all)
    clipped_first = clip_columns(first_qkv, root_first, head_size)
    clipped_second = clip_columns(second_qkv, root_second, head_size)
    clip_scales = jnp.stack([root_first, root_second])
    moe_back = moe_fetch()
    grad_four = cotangent.astype(jnp.float32) * local_live[:, None]
    moe_grad_full = gather_rows(grad_four.astype(jnp.bfloat16))
    partial_gates = jnp.sum(moe_grad_full.astype(jnp.float32)[:, None, :] * pair_result, axis=-1)
    grad_gates = lax.psum(partial_gates, "tensor")
    grad_result = (slot_gate[:, None] * moe_grad_full[slot_token].astype(jnp.float32)).astype(
        jnp.bfloat16
    )
    grad_result = grad_result.reshape(experts, capacity, feature_count)
    grad_expert_down = jnp.einsum(
        "ecf,ecd->efd", expert_act, grad_result, preferred_element_type=jnp.float32
    )
    grad_act = jnp.einsum(
        "ecd,efd->ecf", grad_result, moe_back[6], preferred_element_type=jnp.float32
    )
    grad_hidden = gelu_back(expert_hidden, grad_act).astype(jnp.bfloat16)
    grad_expert_up = jnp.einsum(
        "ecd,ecf->edf", dispatched, grad_hidden, preferred_element_type=jnp.float32
    )
    grad_dispatch = jnp.einsum(
        "ecf,edf->ecd", grad_hidden, moe_back[5], preferred_element_type=jnp.float32
    )
    grad_dispatch = jnp.concatenate(
        [
            grad_dispatch.reshape(experts * capacity, feature_count),
            jnp.zeros((1, feature_count), jnp.float32),
        ],
        axis=0,
    )
    grad_from_experts = jnp.sum(grad_dispatch[target].reshape(rows_full, 2, feature_count), axis=1)
    grad_picked = grad_gates * keep_live
    grad_probs = jnp.sum(chosen * grad_picked[:, :, None], axis=1)
    grad_logits = route_probs * (
        grad_probs - jnp.sum(grad_probs * route_probs, axis=-1, keepdims=True)
    )
    grad_logits = grad_logits.astype(jnp.bfloat16)
    grad_router = jnp.einsum(
        "rd,re->de", moe_input, grad_logits, preferred_element_type=jnp.float32
    )
    local_logits = lax.dynamic_slice_in_dim(grad_logits, first_row, rows_local, 0)
    grad_moe_normed = scatter_rows(grad_from_experts) + jnp.einsum(
        "re,de->rd", local_logits, moe_back[4], preferred_element_type=jnp.float32
    )
    grad_rows_four, grad_fourth_norm = norm_back(residual_three, moe_back[3], grad_moe_normed)
    grad_three = grad_four + grad_rows_four
    grad_two, grad_third_norm, grad_second_qkv, grad_second_out = block_attention_back(
        residual_two,
        grad_three,
        moe_back[0],
        moe_back[1],
        moe_back[2],
        attn_second,
        images,
        head_size,
    )
    third_sum, fourth_sum = sum_gains(grad_third_norm, grad_fourth_norm)
    moe_owned = (
        lax.psum_scatter(third_sum, "dp", scatter_dimension=0, tiled=True),
        lax.psum_scatter(grad_second_qkv, "dp", scatter_dimension=0, tiled=True),
        lax.psum_scatter(grad_second_out, "dp", scatter_dimension=1, tiled=True),
        lax.psum_scatter(fourth_sum, "dp", scatter_dimension=0, tiled=True),
        lax.psum_scatter(grad_router, "dp", scatter_dimension=0, tiled=True),
        lax.psum_scatter(grad_expert_up, "dp", scatter_dimension=1, tiled=True),
        lax.psum_scatter(grad_expert_down, "dp", scatter_dimension=2, tiled=True),
    )
    dense_back = dense_fetch()
    grad_one, grad_second_norm, grad_dense_up, grad_dense_down = block_mlp_back(
        residual_one, grad_two, dense_back[3], dense_back[4], dense_back[5], mlp_stored
    )
    input_grad, grad_first_norm, grad_first_qkv, grad_first_out = block_attention_back(
        residual_zero,
        grad_one,
        dense_back[0],
        dense_back[1],
        dense_back[2],
        attn_first,
        images,
        head_size,
    )
    first_sum, second_sum = sum_gains(grad_first_norm, grad_second_norm)
    dense_owned = (
        lax.psum_scatter(first_sum, "dp", scatter_dimension=0, tiled=True),
        lax.psum_scatter(grad_first_qkv, "dp", scatter_dimension=0, tiled=True),
        lax.psum_scatter(grad_first_out, "dp", scatter_dimension=1, tiled=True),
        lax.psum_scatter(second_sum, "dp", scatter_dimension=0, tiled=True),
        lax.psum_scatter(grad_dense_up, "dp", scatter_dimension=0, tiled=True),
        lax.psum_scatter(grad_dense_down, "dp", scatter_dimension=1, tiled=True),
    )
    owned = tuple(dense_owned) + tuple(moe_owned)
    return (
        block_output,
        input_grad,
        owned[0],
        owned[1],
        owned[2],
        owned[3],
        owned[4],
        owned[5],
        owned[6],
        owned[7],
        owned[8],
        owned[9],
        owned[10],
        owned[11],
        owned[12],
        clipped_first,
        clipped_second,
        clip_scales,
    )


def solution(mesh):
    placed = (
        P(("dp", "tensor"), None),
        P("dp"),
        P("dp", None, "tensor"),
        P("tensor", "dp"),
        P("dp"),
        P("dp", "tensor"),
        P("tensor", "dp"),
        P("dp"),
        P("dp", None, "tensor"),
        P("tensor", "dp"),
        P("dp"),
        P("dp", None),
        P(None, "dp", "tensor"),
        P(None, "tensor", "dp"),
        P("dp", None),
        P("dp", None),
        P("dp"),
        P(("dp", "tensor"), None),
    )
    return jax.shard_map(
        local,
        mesh=mesh,
        in_specs=placed,
        out_specs=(
            P(("dp", "tensor"), None),
            P(("dp", "tensor"), None),
            P("dp"),
            P("dp", None, "tensor"),
            P("tensor", "dp"),
            P("dp"),
            P("dp", "tensor"),
            P("tensor", "dp"),
            P("dp"),
            P("dp", None, "tensor"),
            P("tensor", "dp"),
            P("dp"),
            P("dp", None),
            P(None, "dp", "tensor"),
            P(None, "tensor", "dp"),
            P("dp", None, "tensor"),
            P("dp", None, "tensor"),
            P(None, "tensor"),
        ),
        check_vma=False,
    )
```

profile of v0, /device:TPU:0, one launch (start us, length us, event | category | flops | bytes accessed | tf_op | source)
XLA Modules:
  0.0 2083.8 jit_solution(6215796328237934612)
XLA Ops:
  12.6 23.3 %all-reduce.29 = (bf16[768]{0:T(1024)(128)(2,1)S(1)}, bf16[768]{0:T(1024)(128)(2,1)S(1)}, bf16[768]{0:T(1024)(128)(2,1)S(1)}, bf16[768]{0:T(1024)(128)(2,1)S(1)}) all-reduce(bf16[768]{0:T(1024)(128)(2,1)S(1)} %dynamic-update-slice.1, bf16[768]{0:T(1024)(128)(2,1)S(1)} %dynamic-update-slice, ...), channel_id=1, replica_groups=mesh['dp'=8,'tensor'=4] {'dp'}, use_global_device_ids=true, to_apply=%add.3 | all-reduce | flops 3072 | bytes 12288
  42.4 35.2 %all_gather.78 = bf16[768,3,192]{2,1,0:T(4,128)(2,1)S(1)} all-gather(bf16[96,3,192]{2,1,0:T(4,128)(2,1)S(1)} %copy.141), channel_id=1, replica_groups=mesh['dp'=8,'tensor'=4] {'dp'}, dimensions={0}, use_global_device_ids=true | all-gather | bytes 995328 | tf_op jit(solution)/shard_map/all_gather | solution.py:202
  78.7 31.0 %all_gather.79 = bf16[192,768]{0,1:T(8,128)(2,1)S(1)} all-gather(bf16[192,96]{0,1:T(8,128)(2,1)S(1)} %copy.148), channel_id=1, replica_groups=mesh['dp'=8,'tensor'=4] {'dp'}, dimensions={1}, use_global_device_ids=true | all-gather | bytes 331776 | tf_op jit(solution)/shard_map/all_gather | solution.py:203
  119.9 15.8 fusion
  141.7 17.9 all-gather.32.cloned.1.call-done
  161.3 41.6 %all-gather.22.cloned.1.call-done = bf16[768,768]{1,0:T(8,128)(2,1)} async-done(((bf16[96,768]{1,0:T(8,128)(2,1)}), bf16[768,768]{1,0:T(8,128)(2,1)}) %all-gather.22.cloned.1.call-update) | async-done | bytes 1179664 | tf_op jit(solution)/shard_map/all_gather | solution.py:205
  202.9 8.5 multiply_convert_fusion.4
  211.5 33.4 %all-gather.24.cloned.1.call-done = bf16[768,768]{0,1:T(8,128)(2,1)} async-done(((bf16[768,96]{0,1:T(8,128)(2,1)}), bf16[768,768]{0,1:T(8,128)(2,1)}) %all-gather.24.cloned.1.call-update) | async-done | bytes 1179664 | tf_op jit(solution)/shard_map/all_gather | solution.py:206
  247.6 16.0 fusion.1
  269.7 37.2 %all_gather.86 = bf16[768,3,192]{2,1,0:T(4,128)(2,1)S(1)} all-gather(bf16[96,3,192]{2,1,0:T(4,128)(2,1)S(1)} %copy.149), channel_id=1, replica_groups=mesh['dp'=8,'tensor'=4] {'dp'}, dimensions={0}, use_global_device_ids=true | all-gather | bytes 995328 | tf_op jit(solution)/shard_map/all_gather | solution.py:212
  309.1 33.4 %all_gather.87 = bf16[192,768]{0,1:T(8,128)(2,1)} all-gather(bf16[192,96]{0,1:T(8,128)(2,1)S(1)} %copy.156), channel_id=1, replica_groups=mesh['dp'=8,'tensor'=4] {'dp'}, dimensions={1}, use_global_device_ids=true | all-gather | bytes 331776 | tf_op jit(solution)/shard_map/all_gather | solution.py:213
  352.8 15.8 fusion.2
  374.7 26.0 %all-gather.4 = bf16[8,96,8]{1,2,0:T(8,128)(2,1)S(1)} all-gather(bf16[1,96,8]{1,2,0:T(8,128)(2,1)S(1)} %bitcast.218), channel_id=1, replica_groups=mesh['dp'=8,'tensor'=4] {'dp'}, dimensions={0}, use_global_device_ids=true | all-gather | bytes 13824 | tf_op jit(solution)/shard_map/all_gather | solution.py:215
  409.0 9.0 scatter_custom_fusion
  434.3 8.8 scatter_custom_fusion.1
  448.3 8.8 gather_fusion.2
  457.2 75.9 %all-gather.26.cloned.1.call-done = bf16[8,768,768]{2,1,0:T(8,128)(2,1)} async-done(((bf16[8,96,768]{2,1,0:T(8,128)(2,1)}), bf16[8,768,768]{2,1,0:T(8,128)(2,1)}) %all-gather.26.cloned.1.call-update) | async-done | bytes 9437200 | tf_op jit(solution)/shard_map/all_gather | solution.py:216
  533.1 7.4 fusion.37
  542.8 12.1 multiply_convert_fusion.1
  554.9 116.7 %all-gather.28.cloned.1.call-done = bf16[8,768,768]{1,2,0:T(8,128)(2,1)} async-done(((bf16[8,768,96]{1,2,0:T(8,128)(2,1)}), bf16[8,768,768]{1,2,0:T(8,128)(2,1)}) %all-gather.28.cloned.1.call-update) | async-done | bytes 9437200 | tf_op jit(solution)/shard_map/all_gather | solution.py:217
  671.6 9.7 fusion.129
  691.3 9.8 gather_fusion.1
  701.2 7.1 reshape.364
  708.3 11.1 add_convert_fusion
  720.9 9.0 fusion.130
  739.9 9.9 gather_fusion.4
  749.8 7.3 reshape.367
  757.1 8.2 reduce_sum.294
  765.4 16.2 fusion.4
  783.7 13.6 multiply_reduce_fusion
  797.4 7.5 psum.35
  811.1 16.4 all-gather.40.cloned.1.call-done
  855.6 16.3 fusion.5
  879.4 21.2 %all-gather.42.cloned.1.call-done = bf16[4,197,768]{2,1,0:T(8,128)(2,1)} async-done(((bf16[1,197,768]{2,1,0:T(8,128)(2,1)}), bf16[4,197,768]{2,1,0:T(8,128)(2,1)}) %all-gather.42.cloned.1.call-update) | async-done | bytes 1210384 | tf_op jit(solution)/shard_map/all_gather | solution.py:35
  911.4 17.0 fusion.6
  943.8 16.8 all-gather.44.cloned.1.call-done
  1006.1 11.7 fusion.22
  1018.1 12.4 fusion.46
  1032.9 21.4 %all-reduce.27 = (f32[3]{0:T(128)S(1)}, f32[3]{0:T(128)S(1)}) all-reduce(f32[3]{0:T(128)S(1)} %get-tuple-element.33, f32[3]{0:T(128)S(1)} %get-tuple-element.32), channel_id=1, replica_groups=mesh['dp'=8,'tensor'=4] {'dp'}, use_global_device_ids=true, to_apply=%region_63.64 | all-reduce | flops 6 | bytes 48 | tf_op jit(solution)/shard_map/pmax | solution.py:277
  1060.0 25.1 %fusion.114 = (bf16[200,768]{1,0:T(8,128)(2,1)S(1)}, bf16[200,768]{1,0:T(8,128)(2,1)}) fusion(bf16[788,768]{1,0:T(8,128)(2,1)S(1)} %copy-done.12, bf16[788,768]{1,0:T(8,128)(2,1)} %bitcast_convert_fusion), kind=kCustom, calls=%all-reduce-scatter.8 | all-reduce-scatter fusion | flops 1228801 | bytes 3035648
  1097.8 34.1 %all-reduce.26 = (f32[768]{0:T(1024)S(1)}, f32[768]{0:T(1024)S(1)}, f32[768]{0:T(1024)S(1)}, f32[768]{0:T(1024)S(1)}) all-reduce(f32[768]{0:T(1024)S(1)} %get-tuple-element.28, f32[768]{0:T(1024)S(1)} %get-tuple-element.24, f32[768]{0:T(1024)S(1)} %get-tuple-element.26, ...), channel_id=10, replica_groups=mesh['dp'=8,'tensor'=4] {'dp'}, use_global_device_ids=true, to_apply=%region_43.44.clone | all-reduce | flops 3072 | bytes 24576
  1144.3 11.4 reduce-scatter.44.cloned.1.call-done
  1157.3 70.3 %reduce-scatter.38.cloned.1.call-done = f32[96,3,192]{2,0,1:T(8,128)} async-done(((f32[768,3,192]{2,0,1:T(8,128)}), f32[96,3,192]{2,0,1:T(8,128)}) %reduce-scatter.38.cloned.1.call-update) | async-done | bytes 221200 | tf_op jit(solution)/shard_map/reduce_scatter | solution.py:341
  1227.7 72.0 %reduce-scatter.34.cloned.1.call-done = f32[96,768]{1,0:T(8,128)} async-done(((f32[768,768]{1,0:T(8,128)}), f32[96,768]{1,0:T(8,128)}) %reduce-scatter.34.cloned.1.call-update) | async-done | bytes 294928 | tf_op jit(solution)/shard_map/reduce_scatter | solution.py:368
  1299.7 72.0 %reduce-scatter.36.cloned.1.call-done = f32[768,96]{0,1:T(8,128)} async-done(((f32[768,768]{0,1:T(8,128)}), f32[768,96]{0,1:T(8,128)}) %reduce-scatter.36.cloned.1.call-update) | async-done | bytes 294928 | tf_op jit(solution)/shard_map/reduce_scatter | solution.py:369
  1371.6 72.0 %reduce-scatter.32.cloned.1.call-done = f32[96,3,192]{2,0,1:T(8,128)} async-done(((f32[768,3,192]{2,0,1:T(8,128)}), f32[96,3,192]{2,0,1:T(8,128)}) %reduce-scatter.32.cloned.1.call-update) | async-done | bytes 221200 | tf_op jit(solution)/shard_map/reduce_scatter | solution.py:365
  1443.7 316.6 %reduce-scatter.40.cloned.1.call-done = f32[8,96,768]{2,1,0:T(8,128)} async-done(((f32[8,768,768]{2,1,0:T(8,128)}), f32[8,96,768]{2,1,0:T(8,128)}) %reduce-scatter.40.cloned.1.call-update) | async-done | bytes 2359312 | tf_op jit(solution)/shard_map/reduce_scatter | solution.py:345
  1760.3 316.5 %reduce-scatter.42.cloned.1.call-done = f32[8,768,96]{1,2,0:T(8,128)} async-done(((f32[8,768,768]{1,2,0:T(8,128)}), f32[8,768,96]{1,2,0:T(8,128)}) %reduce-scatter.42.cloned.1.call-update) | async-done | bytes 2359312 | tf_op jit(solution)/shard_map/reduce_scatter | solution.py:346
  (447 shorter events, 258.3 us)
Async XLA Ops:
  7.2 102.5 %all-gather.30.cloned.1.call-start = ((), (), s32[]{:S(2)}) async-start(), calls=%async_computation.19 | async-start | bytes 1536000 | tf_op jit(solution)/shard_map/all_gather | solution.py:35
  41.3 37.3 %copy-start.53 = (bf16[192,96]{1,0:T(8,128)(2,1)S(1)}, bf16[192,96]{1,0:T(8,128)(2,1)}, u32[]{:S(2)}) copy-start(bf16[192,96]{1,0:T(8,128)(2,1)} %param.21) | copy-start | bytes 110596
  41.3 118.3 %all-gather.32.cloned.1.call-start = ((), (), s32[]{:S(2)}) async-start(), calls=%async_computation.20 | async-start | bytes 1536000 | tf_op jit(solution)/shard_map/all_gather | solution.py:35
  78.6 34.0 %copy-start.37 = (bf16[768,3,192]{0,2,1:T(8,128)(2,1)}, bf16[768,3,192]{0,2,1:T(8,128)(2,1)S(1)}, u32[]{:S(2)}) copy-start(bf16[768,3,192]{0,2,1:T(8,128)(2,1)S(1)} %copy.142) | copy-start | bytes 2654212
  135.7 2.6 collective-permute-start
  138.8 127.6 %copy-start.4 = (bf16[209,768]{1,0:T(8,128)(2,1)}, bf16[209,768]{1,0:T(8,128)(2,1)S(1)}, u32[]{:S(2)}) copy-start(bf16[209,768]{1,0:T(8,128)(2,1)S(1)} %concatenate.12) | copy-start | bytes 963076
  139.0 72.4 %copy-start.60 = (f32[197]{0:T(256)}, f32[197]{0:T(256)S(1)}, u32[]{:S(2)}) copy-start(f32[197]{0:T(256)S(1)} %broadcast_multiply_fusion.2) | copy-start | bytes 2368
  139.4 72.1 %copy-start.76 = (f32[197]{0:T(256)}, f32[197]{0:T(256)S(1)}, u32[]{:S(2)}) copy-start(f32[197]{0:T(256)S(1)} %multiply_reduce_fusion.10) | copy-start | bytes 2368
  139.4 72.1 %copy-start.72 = (f32[197]{0:T(256)}, f32[197]{0:T(256)S(1)}, u32[]{:S(2)}) copy-start(f32[197]{0:T(256)S(1)} %fusion.107) | copy-start | bytes 2368
  140.4 62.6 %all-gather.22.cloned.1.call-start = ((), (), s32[]{:S(2)}) async-start(), calls=%async_computation.9 | async-start | bytes 1327104 | tf_op jit(solution)/shard_map/all_gather | solution.py:205
  141.1 103.7 %all-gather.24.cloned.1.call-start = ((), (), s32[]{:S(2)}) async-start(), calls=%async_computation.10 | async-start | bytes 1327104 | tf_op jit(solution)/shard_map/all_gather | solution.py:206
  141.7 200.8 %all-gather.34.cloned.1.call-start = ((), (), s32[]{:S(2)}) async-start(), calls=%async_computation.21 | async-start | bytes 1536000 | tf_op jit(solution)/shard_map/all_gather | solution.py:35
  161.3 50.2 %copy-start.36 = (bf16[788,768]{1,0:T(8,128)(2,1)}, bf16[788,768]{1,0:T(8,128)(2,1)S(1)}, u32[]{:S(2)}) copy-start(bf16[788,768]{1,0:T(8,128)(2,1)S(1)} %reshape.445) | copy-start | bytes 3631108
  263.6 2.3 collective-permute-start.1
  266.9 42.0 %copy-start.78 = (f32[197]{0:T(256)}, f32[197]{0:T(256)S(1)}, u32[]{:S(2)}) copy-start(f32[197]{0:T(256)S(1)} %multiply_reduce_fusion.9) | copy-start | bytes 2368
  267.9 133.4 %all-gather.38.cloned.1.call-start = ((), (), s32[]{:S(2)}) async-start(), calls=%async_computation.23 | async-start | bytes 1536000 | tf_op jit(solution)/shard_map/all_gather | solution.py:35
  268.6 40.4 %copy-start.58 = (f32[197]{0:T(256)}, f32[197]{0:T(256)S(1)}, u32[]{:S(2)}) copy-start(f32[197]{0:T(256)S(1)} %compare_convert_fusion) | copy-start | bytes 2368
  269.5 39.5 %copy-start.54 = (bf16[192,96]{1,0:T(8,128)(2,1)S(1)}, bf16[192,96]{1,0:T(8,128)(2,1)}, u32[]{:S(2)}) copy-start(bf16[192,96]{1,0:T(8,128)(2,1)} %param.27) | copy-start | bytes 110596
  269.5 135.2 %all-gather.36.cloned.1.call-start = ((), (), s32[]{:S(2)}) async-start(), calls=%async_computation.22 | async-start | bytes 1536000 | tf_op jit(solution)/shard_map/all_gather | solution.py:35
  309.0 35.2 %copy-start.38 = (bf16[768,3,192]{0,2,1:T(8,128)(2,1)S(1)}, bf16[768,3,192]{0,2,1:T(8,128)(2,1)}, u32[]{:S(2)}) copy-start(bf16[768,3,192]{0,2,1:T(8,128)(2,1)} %copy.150) | copy-start | bytes 2654212
  368.6 2.1 collective-permute-start.2
  371.4 29.3 %copy-start.52 = (s32[788,2]{0,1:T(2,128)S(1)}, s32[788,2]{0,1:T(2,128)}, u32[]{:S(2)}) copy-start(s32[788,2]{0,1:T(2,128)} %param.32) | copy-start | bytes 18916
  371.7 31.4 %copy-start.80 = (f32[197]{0:T(256)}, f32[197]{0:T(256)S(1)}, u32[]{:S(2)}) copy-start(f32[197]{0:T(256)S(1)} %multiply_reduce_fusion.8) | copy-start | bytes 2368
  372.2 30.8 %copy-start.70 = (f32[197]{0:T(256)}, f32[197]{0:T(256)S(1)}, u32[]{:S(2)}) copy-start(f32[197]{0:T(256)S(1)} %fusion.109) | copy-start | bytes 2368
  373.1 160.0 %all-gather.26.cloned.1.call-start = ((), (), s32[]{:S(2)}) async-start(), calls=%async_computation.11 | async-start | bytes 10616832 | tf_op jit(solution)/shard_map/all_gather | solution.py:216
  373.9 297.7 %all-gather.28.cloned.1.call-start = ((), (), s32[]{:S(2)}) async-start(), calls=%async_computation.12 | async-start | bytes 10616832 | tf_op jit(solution)/shard_map/all_gather | solution.py:217
  374.6 452.9 %all-gather.40.cloned.1.call-start = ((), (), s32[]{:S(2)}) async-start(), calls=%async_computation.24 | async-start | bytes 1536000 | tf_op jit(solution)/shard_map/all_gather | solution.py:35
  782.3 22.8 %collective-permute-start.4 = (bf16[9,768]{1,0:T(8,128)(2,1)S(1)}, bf16[9,768]{1,0:T(8,128)(2,1)S(1)}, u32[]{:S(2)}, u32[]{:S(2)}) collective-permute-start(bf16[9,768]{1,0:T(8,128)(2,1)S(1)} %slice.68), channel_id=1, source_target_pairs={{0,1},{1,2},{2,3},{4,5},{5,6},{6,7},{8,9},{9,10},{10,11},{12,13},{... | collective-permute-start | bytes 41480
  810.9 89.8 %all-gather.42.cloned.1.call-start = ((), (), s32[]{:S(2)}) async-start(), calls=%async_computation.25 | async-start | bytes 1536000 | tf_op jit(solution)/shard_map/all_gather | solution.py:35
  871.9 2.1 collective-permute-start.5
  879.4 81.3 %all-gather.44.cloned.1.call-start = ((), (), s32[]{:S(2)}) async-start(), calls=%async_computation.26 | async-start | bytes 1536000 | tf_op jit(solution)/shard_map/all_gather | solution.py:35
  929.2 2.1 collective-permute-start.6
  939.3 148.4 %reduce-scatter.48.cloned.1.call-start = ((), (), s32[]{:S(2)}) async-start(), calls=%async_computation.29 | async-start | bytes 442368
  940.7 150.0 %reduce-scatter.46.cloned.1.call-start = ((), (), s32[]{:S(2)}) async-start(), calls=%async_computation.28 | async-start | bytes 884736
  943.8 211.9 %reduce-scatter.44.cloned.1.call-start = ((), (), s32[]{:S(2)}) async-start(), calls=%async_computation.27 | async-start | bytes 884736
  963.8 263.8 %reduce-scatter.38.cloned.1.call-start = ((), (), s32[]{:S(2)}) async-start(), calls=%async_computation.16 | async-start | bytes 2654208 | tf_op jit(solution)/shard_map/reduce_scatter | solution.py:341
  971.0 328.6 %reduce-scatter.34.cloned.1.call-start = ((), (), s32[]{:S(2)}) async-start(), calls=%async_computation.14 | async-start | bytes 2654208 | tf_op jit(solution)/shard_map/reduce_scatter | solution.py:368
  975.7 395.9 %reduce-scatter.36.cloned.1.call-start = ((), (), s32[]{:S(2)}) async-start(), calls=%async_computation.15 | async-start | bytes 2654208 | tf_op jit(solution)/shard_map/reduce_scatter | solution.py:369
  980.3 463.4 %reduce-scatter.32.cloned.1.call-start = ((), (), s32[]{:S(2)}) async-start(), calls=%async_computation.13 | async-start | bytes 2654208 | tf_op jit(solution)/shard_map/reduce_scatter | solution.py:365
  1006.1 754.2 %reduce-scatter.40.cloned.1.call-start = ((), (), s32[]{:S(2)}) async-start(), calls=%async_computation.17 | async-start | bytes 21233664 | tf_op jit(solution)/shard_map/reduce_scatter | solution.py:345
  1017.9 1058.9 %reduce-scatter.42.cloned.1.call-start = ((), (), s32[]{:S(2)}) async-start(), calls=%async_computation.18 | async-start | bytes 21233664 | tf_op jit(solution)/shard_map/reduce_scatter | solution.py:346
  1060.0 37.0 %copy-start.49 = (f32[768]{0:T(1024)S(1)}, f32[768]{0:T(1024)}, u32[]{:S(2)}) copy-start(f32[768]{0:T(1024)} %copy-done.48) | copy-start | bytes 9220
  1060.0 37.0 %copy-start.56 = (f32[197]{0:T(256)S(1)}, f32[197]{0:T(256)}, u32[]{:S(2)}) copy-start(f32[197]{0:T(256)} %copy-done.55) | copy-start | bytes 2368
  1060.0 37.3 %copy-start.75 = (f32[197]{0:T(256)S(1)}, f32[197]{0:T(256)}, u32[]{:S(2)}) copy-start(f32[197]{0:T(256)} %copy-done.74) | copy-start | bytes 2368
  1060.0 37.4 %copy-start.67 = (f32[197]{0:T(256)S(1)}, f32[197]{0:T(256)}, u32[]{:S(2)}) copy-start(f32[197]{0:T(256)} %copy-done.66) | copy-start | bytes 2368
  1085.1 58.1 %copy-start.9 = (f32[197,768]{1,0:T(8,128)S(1)}, f32[197,768]{1,0:T(8,128)}, u32[]{:S(2)}) copy-start(f32[197,768]{1,0:T(8,128)} %copy-done.8) | copy-start | bytes 1815556
  1085.9 9.0 collective-permute-start.7
  1092.4 39.9 %collective-permute-start.3 = (bf16[9,768]{1,0:T(8,128)(2,1)S(1)}, bf16[9,768]{1,0:T(8,128)(2,1)S(1)}, u32[]{:S(2)}, u32[]{:S(2)}) collective-permute-start(bf16[9,768]{1,0:T(8,128)(2,1)S(1)} %slice.67), channel_id=1, source_target_pairs={{0,1},{1,2},{2,3},{4,5},{5,6},{6,7},{8,9},{9,10},{10,11},{12,13},{... | collective-permute-start | bytes 41480
  (67 other events, 622.3 us)
Sparse Core Ops, SparseCore 0:
  41.5 15.0 all-gather.29
  140.5 19.1 all-gather.31
  161.8 41.0 all-gather.21
  205.0 39.8 all-gather.23
  268.0 18.7 all-gather.33
  288.8 17.7 all-gather.37
  373.2 19.5 all-gather.35
  395.0 138.0 all-gather.25
  535.3 136.2 all-gather.27
  811.0 16.5 all-gather.39
  879.5 21.1 all-gather.41
  939.4 21.1 all-gather.43
  964.4 61.4 reduce-scatter.47
  1029.1 61.6 reduce-scatter.45
  1094.2 61.4 reduce-scatter.43
  1159.6 67.9 reduce-scatter.37
  1231.6 68.0 reduce-scatter.33
  1303.6 68.0 reduce-scatter.35
  1375.7 67.9 reduce-scatter.31
  1448.0 312.2 reduce-scatter.39
  1764.8 311.9 reduce-scatter.41
where the time goes:
time: 2100 us; the launch traced here: 2080 us
  waiting for transfers between devices  1280 us (61%)
  blocking collectives  377 us (18%)
  local copies, waits for them, and re-layouts  191 us (9%)
  matrix products  142 us (7%)
  other arithmetic  62.2 us (3%)
    reduce_scatter x1, waiting for transfers between devices, local(): lax.psum_scatter(grad_expert_up, 'dp', scatter_dimension=1, tiled=True)  317 us
    reduce_scatter x1, waiting for transfers between devices, local(): lax.psum_scatter(grad_expert_down, 'dp', scatter_dimension=2, tiled=True)  316 us
    unnamed x9, blocking collectives  180 us
    all_gather x1, waiting for transfers between devices, moe_fetch(): lax.all_gather(expert_down, 'dp', axis=2, tiled=True)  117 us
    all_gather x1, waiting for transfers between devices, moe_fetch(): lax.all_gather(expert_up, 'dp', axis=1, tiled=True)  75.9 us
    all_gather x8, waiting for transfers between devices, gather_rows(): return lax.all_gather(values, 'tensor', axis=0, tiled=True)  72.4 us
    reduce_scatter x1, waiting for transfers between devices, local(): lax.psum_scatter(grad_first_qkv, 'dp', scatter_dimension=0, tiled=True)  72 us
    reduce_scatter x1, waiting for transfers between devices, local(): lax.psum_scatter(grad_dense_down, 'dp', scatter_dimension=1, tiled=True)  72 us
  transfers between devices with their start and end apart: 29, of which 20 were waited for; matrix products, arithmetic and copies ran while one was open for 12% of the time, Pallas kernels for 0%

commit v1 on v0

--- a/solution.py
+++ b/solution.py
@@ -391,6 +391,407 @@
     )
 
 
+ROWS = 208
+AXES = ("dp", "tensor")
+BF = jnp.bfloat16
+F32 = jnp.float32
+
+
+def swap(values, z=0, x=0, y=0, core=0):
+    shift_d, shift_t = 2 * z + x, 2 * y + core
+    pairs = [(d * 4 + t, (d ^ shift_d) * 4 + (t ^ shift_t)) for d in range(8) for t in range(4)]
+    return lax.ppermute(values, AXES, pairs)
+
+
+def place_of(position):
+    return 2 * (position & 3) + (position >> 2)
+
+
+def gather_z(shard):
+    return jnp.concatenate([shard] + [swap(shard, z=k) for k in (1, 2, 3)], axis=0)
+
+
+def gather_weight(shard, x_first):
+    quarter = gather_z(shard)
+    if x_first:
+        other = swap(quarter, x=1)
+        own = (quarter, other)
+        far = (swap(quarter, y=1), swap(other, y=1))
+    else:
+        far_quarter = swap(quarter, y=1)
+        own = (quarter, swap(quarter, x=1))
+        far = (far_quarter, swap(far_quarter, x=1))
+    return jnp.concatenate(own, axis=0), jnp.concatenate(far, axis=0)
+
+
+def add_pair(mine, arrived):
+    return mine.astype(F32) + arrived.astype(F32)
+
+
+def scatter_weight(own, far, y_first):
+    half = own.shape[0] // 2
+    width = half // 4
+    if y_first:
+        whole = add_pair(own, swap(far.astype(BF), y=1)).astype(BF)
+        part = add_pair(whole[:half], swap(whole[half:], x=1)).astype(BF)
+    else:
+        own_half = add_pair(own[:half], swap(own[half:].astype(BF), x=1)).astype(BF)
+        far_half = add_pair(far[:half], swap(far[half:].astype(BF), x=1)).astype(BF)
+        part = add_pair(own_half, swap(far_half, y=1)).astype(BF)
+    total = part[:width].astype(F32)
+    for k in (1, 2, 3):
+        total = total + swap(part[k * width : (k + 1) * width], z=k).astype(F32)
+    return total
+
+
+def exchange_rows(pieces):
+    return [pieces[0]] + [
+        swap(pieces[p], z=p & 3, x=p >> 2) for p in range(1, 8)
+    ]
+
+
+def pair_gather(values):
+    return jnp.concatenate([values, swap(values, core=1)], axis=0)
+
+
+def pair_scatter(partial):
+    half = partial.shape[0] // 2
+    return partial[:half] + swap(partial[half:].astype(BF), core=1).astype(F32)
+
+
+def dot(a, b, ca, cb):
+    return lax.dot_general(a, b, (((ca,), (cb,)), ((), ())), preferred_element_type=F32)
+
+
+def norm_stats(values):
+    center = values - jnp.mean(values, axis=-1, keepdims=True)
+    scale = lax.rsqrt(jnp.mean(center * center, axis=-1, keepdims=True) + epsilon)
+    return center * scale, scale
+
+
+def norm_rows(values, gain):
+    return (norm_stats(values)[0] * gain).astype(BF)
+
+
+def norm_rows_back(values, gain, upstream):
+    normed, scale = norm_stats(values)
+    scaled = upstream * gain
+    grad = scale * (
+        scaled
+        - jnp.mean(scaled, axis=-1, keepdims=True)
+        - normed * jnp.mean(scaled * normed, axis=-1, keepdims=True)
+    )
+    return grad, jnp.sum(upstream * normed, axis=0)
+
+
+def heads_of(parts):
+    cut = [m.reshape(2, ROWS, 3, -1, HD) for m in parts]
+    joined = jnp.concatenate(cut, axis=3)
+    return joined[:, :, 0], joined[:, :, 1], joined[:, :, 2]
+
+
+def softmax_scores(queries, keyset):
+    scores = jnp.einsum("iqhd,ikhd->ihqk", queries, keyset, preferred_element_type=F32)
+    scores = scores * HD ** (-0.5)
+    key_ok = (jnp.arange(ROWS) < L)[None, None, None, :]
+    masked = jnp.where(key_ok, scores, -1e30)
+    return masked, jax.nn.softmax(masked, axis=-1)
+
+
+def fast_attention(residual, gain, qkv, out, live_pair):
+    normed = pair_gather(norm_rows(residual, gain))
+    mixed = [dot(normed, w, 1, 0).astype(BF) for w in qkv]
+    queries, keyset, values = heads_of(mixed)
+    masked, probs = softmax_scores(queries, keyset)
+    query_ok = (jnp.arange(ROWS) < L)[None, None, :, None] & live_pair[:, None, None, None]
+    peak = jnp.max(jnp.where(query_ok, masked, -1e30), axis=(0, 2, 3))
+    attended = jnp.einsum("ihqk,ikhd->iqhd", probs.astype(BF), values, preferred_element_type=F32)
+    attended = attended.astype(BF).reshape(2 * ROWS, -1)
+    half = attended.shape[1] // 2
+    partial = dot(attended[:, :half], out[0], 1, 1) + dot(attended[:, half:], out[1], 1, 1)
+    return residual + pair_scatter(partial), (normed, mixed, attended), peak
+
+
+def fast_attention_back(residual, upstream, gain, qkv, out, stored):
+    normed, mixed, attended = stored
+    grad_full = pair_gather(upstream.astype(BF))
+    half = attended.shape[1] // 2
+    grad_out = [
+        dot(grad_full, attended[:, :half], 0, 0).astype(BF),
+        dot(grad_full, attended[:, half:], 0, 0).astype(BF),
+    ]
+    grad_att = jnp.concatenate([dot(grad_full, w, 1, 0).astype(BF) for w in out], axis=1)
+    queries, keyset, values = heads_of(mixed)
+    _, probs = softmax_scores(queries, keyset)
+    grad_heads = grad_att.reshape(queries.shape)
+    grad_values = jnp.einsum(
+        "ihqk,iqhd->ikhd", probs.astype(BF), grad_heads, preferred_element_type=F32
+    )
+    grad_probs = jnp.einsum("iqhd,ikhd->ihqk", grad_heads, values, preferred_element_type=F32)
+    grad_scores = probs * (grad_probs - jnp.sum(grad_probs * probs, axis=-1, keepdims=True))
+    grad_scores = grad_scores.astype(BF)
+    factor = HD ** (-0.5)
+    grad_queries = factor * jnp.einsum(
+        "ihqk,ikhd->iqhd", grad_scores, keyset, preferred_element_type=F32
+    )
+    grad_keyset = factor * jnp.einsum(
+        "ihqk,iqhd->ikhd", grad_scores, queries, preferred_element_type=F32
+    )
+    stacked = jnp.stack([grad_queries, grad_keyset, grad_values], axis=2).astype(BF)
+    heads = stacked.shape[3] // 2
+    grad_mixed = [
+        stacked[:, :, :, :heads].reshape(2 * ROWS, -1),
+        stacked[:, :, :, heads:].reshape(2 * ROWS, -1),
+    ]
+    grad_qkv = [dot(normed, g, 0, 0).astype(BF) for g in grad_mixed]
+    partial = dot(grad_mixed[0], qkv[0], 1, 1) + dot(grad_mixed[1], qkv[1], 1, 1)
+    grad_rows, grad_gain = norm_rows_back(residual, gain, pair_scatter(partial))
+    return upstream + grad_rows, grad_gain, grad_qkv, grad_out
+
+
+def gelu_pair(hidden):
+    cdf = 0.5 * (1.0 + lax.erf(hidden * 0.7071067811865476))
+    slope = cdf + hidden * jnp.exp(-0.5 * hidden * hidden) * 0.3989422804014327
+    return (hidden * cdf).astype(BF), slope
+
+
+def reduce_peak(peaks):
+    half = peaks.shape[1] // 2
+    best = jnp.maximum(peaks[:, :half], swap(peaks[:, half:], y=1))
+    best = jnp.maximum(best, swap(best, core=0, x=1))
+    far = [swap(best, z=k) for k in (1, 2, 3)]
+    for f in far:
+        best = jnp.maximum(best, f)
+    return best
+
+
+def fast_local(
+    block_input,
+    first_norm,
+    first_qkv,
+    first_out,
+    second_norm,
+    dense_up,
+    dense_down,
+    third_norm,
+    second_qkv,
+    second_out,
+    fourth_norm,
+    router_weight,
+    expert_up,
+    expert_down,
+    expert_ids,
+    expert_slots,
+    image_counts,
+    cotangent,
+):
+    d = lax.axis_index("dp")
+    t = lax.axis_index("tensor")
+    z_index, x_index = d // 2, d % 2
+    width = first_norm.shape[0]
+    features = width * 8
+    experts = expert_up.shape[0]
+    live_count = image_counts[0]
+    heads_cols = first_out.shape[0]
+    ff_cols = dense_up.shape[1]
+
+    small = jnp.concatenate(
+        [
+            jnp.stack([first_norm, second_norm, third_norm, fourth_norm], axis=1),
+            router_weight,
+            jnp.zeros((width, 128 - 4 - experts), BF),
+        ],
+        axis=1,
+    )
+    pack_one = jnp.concatenate([first_qkv.reshape(width, -1), small], axis=1)
+    pack_two = jnp.concatenate([first_out.T, dense_up], axis=1)
+    pack_three = jnp.concatenate([dense_down.T, second_out.T], axis=1)
+    pack_four = second_qkv.reshape(width, -1)
+    full_one = gather_weight(pack_one, True)
+    full_two = gather_weight(pack_two, False)
+    full_three = gather_weight(pack_three, True)
+    full_four = gather_weight(pack_four, False)
+    qkv_cols = 3 * heads_cols
+    qkv_one = [w[:, :qkv_cols] for w in full_one]
+    small_full = full_one[0][:, qkv_cols:]
+    small_rows = small_full[:, : 4 + experts].astype(F32).T
+    gains = [small_rows[i][None] for i in range(4)]
+    router_rows = small_rows[4:].astype(BF)
+    out_one = [w[:, :heads_cols] for w in full_two]
+    up_full = [w[:, heads_cols:] for w in full_two]
+    down_full = [w[:, :ff_cols] for w in full_three]
+    out_two = [w[:, ff_cols:] for w in full_three]
+    qkv_two = list(full_four)
+
+    rel = jnp.arange(features)
+    rel_place = jnp.bitwise_xor(d, 2 * ((rel // width) % 4) + (rel // width) // 4) * width + rel % width
+    to_whole = (rel_place[:, None] == rel[None, :]).astype(BF)
+
+    pad = ((0, ROWS - L), (0, 0))
+    start = dot(jnp.pad(block_input, pad), to_whole, 1, 1)
+    live_here = t < live_count
+    live_scale = jnp.where(live_here, 1.0, 0.0).astype(F32)
+    grad_four = dot(jnp.pad(cotangent, pad), to_whole, 1, 1) * live_scale
+    live_pair = jnp.stack([t, t ^ 1]) < live_count
+
+    expert_pack = jnp.concatenate([expert_up, jnp.swapaxes(expert_down, 1, 2)], axis=2)
+    expert_grid = expert_pack.reshape(4, 2, width, -1)
+    mine_x = lax.dynamic_index_in_dim(expert_grid, x_index, 1, keepdims=False)
+    send_x = lax.dynamic_index_in_dim(expert_grid, x_index ^ 1, 1, keepdims=False)
+    both_x = jnp.stack([mine_x, swap(send_x, x=1)])
+    cut = [lax.dynamic_index_in_dim(both_x, z_index ^ k, 1, keepdims=False) for k in range(4)]
+    cut = [cut[0]] + [swap(cut[k], z=k) for k in (1, 2, 3)]
+    expert_own = jnp.stack(cut, axis=1).reshape(features, -1)
+    expert_far = swap(expert_own, y=1)
+    e_up = [expert_own[:, :ff_cols], expert_far[:, :ff_cols]]
+    e_down = [expert_own[:, ff_cols:], expert_far[:, ff_cols:]]
+
+    slots_block = -(-CAP // (4 * 8)) * 8
+    order = jnp.stack([t, t ^ 2, t ^ 1, t ^ 3])
+    ids = jnp.pad(expert_ids.reshape(4, L, 2), ((0, 0), (0, ROWS - L), (0, 0)), constant_values=-1)
+    slots = jnp.pad(expert_slots.reshape(4, L, 2), ((0, 0), (0, ROWS - L), (0, 0)), constant_values=CAP)
+    flat = jnp.where((slots < CAP) & (slots // slots_block == t), ids * slots_block + slots % slots_block, -1)
+    flat = jnp.concatenate(
+        [lax.dynamic_index_in_dim(flat, order[i], 0, keepdims=False) for i in range(4)], axis=0
+    )
+    position = jnp.arange(experts)
+    expert_at = jnp.bitwise_xor(d, 2 * (position % 4) + position // 4)
+    row_code = (expert_at[:, None] * slots_block + jnp.arange(slots_block)[None, :]).reshape(-1)
+    pick = (
+        (row_code[:, None] == flat[None, :, 0]) | (row_code[:, None] == flat[None, :, 1])
+    ).astype(BF)
+
+    def group_rows(rows):
+        pair = jnp.concatenate([rows, swap(rows, y=1)], axis=0)
+        return jnp.concatenate([pair, swap(pair, core=1)], axis=0)
+
+    def to_experts(rows):
+        whole = dot(dot(pick, group_rows(rows), 1, 0).astype(BF), to_whole, 1, 0).astype(BF)
+        pieces = exchange_rows(
+            [whole[p * slots_block : (p + 1) * slots_block] for p in range(experts)]
+        )
+        return dot(jnp.concatenate(pieces, axis=0), to_whole, 1, 1).astype(BF)
+
+    def from_experts(rows):
+        whole = dot(rows, to_whole, 1, 0).astype(BF)
+        pieces = exchange_rows(
+            [whole[p * slots_block : (p + 1) * slots_block] for p in range(experts)]
+        )
+        back = dot(jnp.concatenate(pieces, axis=0), to_whole, 1, 1).astype(BF)
+        partial = dot(pick, back, 0, 0)
+        half = pair_scatter(partial)
+        return half[:ROWS] + swap(half[ROWS:].astype(BF), y=1).astype(F32)
+
+    grad_slots = pair_gather(to_experts(grad_four.astype(BF)))
+
+    one, stored_one, peak_one = fast_attention(start, gains[0], qkv_one, out_one, live_pair)
+    normed_mlp = pair_gather(norm_rows(one, gains[1]))
+    hidden = [dot(normed_mlp, w, 1, 0) for w in up_full]
+    pairs = [gelu_pair(h) for h in hidden]
+    partial = dot(pairs[0][0], down_full[0], 1, 1) + dot(pairs[1][0], down_full[1], 1, 1)
+    two = one + pair_scatter(partial)
+    three, stored_two, peak_two = fast_attention(two, gains[2], qkv_two, out_two, live_pair)
+
+    tokens = pair_gather(to_experts(norm_rows(three, gains[3])))
+    count = tokens.shape[0] // 2
+    logits = dot(tokens, router_rows, 1, 1)
+    route = jax.nn.softmax(logits, axis=-1)
+    mine = (jnp.arange(experts) == d).astype(F32)[None]
+    gate = jnp.sum(route * mine, axis=-1, keepdims=True)
+    grad_result = (gate * grad_slots.astype(F32)).astype(BF)
+    e_pairs = [gelu_pair(dot(tokens, w, 1, 0)) for w in e_up]
+    result = pair_scatter(dot(e_pairs[0][0], e_down[0], 1, 1) + dot(e_pairs[1][0], e_down[1], 1, 1))
+    e_hidden = [(dot(grad_result, w, 1, 0) * p[1]).astype(BF) for w, p in zip(e_down, e_pairs)]
+    grad_tokens = pair_scatter(dot(e_hidden[0], e_up[0], 1, 1) + dot(e_hidden[1], e_up[1], 1, 1))
+    grad_gate = jnp.sum(result * grad_slots[:count].astype(F32), axis=-1, keepdims=True)
+    grad_logit = (grad_gate * route[:count] * (mine - gate[:count])).astype(BF)
+    grad_tokens = grad_tokens + dot(grad_logit, router_rows, 1, 0)
+    grad_router = dot(grad_logit, tokens[:count], 0, 0)
+    grad_normed = from_experts(grad_tokens.astype(BF))
+    mixed_in = from_experts((gate[:count] * result).astype(BF))
+    four = three + mixed_in
+    block_output = jnp.dot(four, to_whole.astype(F32), precision=lax.Precision.HIGHEST)[:L] * live_scale
+
+    e_grads = [
+        jnp.concatenate(
+            [dot(tokens, h, 0, 0).astype(BF), dot(grad_result, p[0], 0, 0).astype(BF)], axis=1
+        )
+        for h, p in zip(e_hidden, e_pairs)
+    ]
+    e_sum = add_pair(e_grads[0], swap(e_grads[1], y=1)).astype(BF).reshape(2, 4, width, -1)
+    e_cut = [e_sum[:, 0]] + [swap(e_sum[:, k], z=k) for k in (1, 2, 3)]
+    e_near = jnp.stack([c[0] for c in e_cut])
+    e_side = swap(jnp.stack([c[1] for c in e_cut]), x=1)
+    e_all = jnp.concatenate([e_near, e_side], axis=0)
+    where_x = [(x_index ^ (e % 2)) * 4 + (z_index ^ (e // 2)) for e in range(experts)]
+    e_back = jnp.stack([lax.dynamic_index_in_dim(e_all, w, 0, keepdims=False) for w in where_x])
+    grad_expert_up = e_back[:, :, :ff_cols].astype(F32)
+    grad_expert_down = jnp.swapaxes(e_back[:, :, ff_cols:], 1, 2).astype(F32)
+
+    grad_rows, gain_four = norm_rows_back(three, gains[3], grad_normed)
+    grad_three = grad_four + grad_rows
+    grad_two, gain_three, g_qkv_two, g_out_two = fast_attention_back(
+        two, grad_three, gains[2], qkv_two, out_two, stored_two
+    )
+    sum_second = scatter_weight(
+        jnp.concatenate([g_qkv_two[0], g_out_two[0]], axis=1),
+        jnp.concatenate([g_qkv_two[1], g_out_two[1]], axis=1),
+        True,
+    )
+
+    grad_full = pair_gather(grad_two.astype(BF))
+    g_hidden = [(dot(grad_full, w, 1, 0) * p[1]).astype(BF) for w, p in zip(down_full, pairs)]
+    g_mlp = [
+        jnp.concatenate(
+            [dot(normed_mlp, h, 0, 0).astype(BF), dot(grad_full, p[0], 0, 0).astype(BF)], axis=1
+        )
+        for h, p in zip(g_hidden, pairs)
+    ]
+    sum_mlp = scatter_weight(g_mlp[0], g_mlp[1], False)
+    partial = dot(g_hidden[0], up_full[0], 1, 1) + dot(g_hidden[1], up_full[1], 1, 1)
+    grad_rows, gain_two = norm_rows_back(one, gains[1], pair_scatter(partial))
+    grad_one = grad_two + grad_rows
+
+    grad_zero, gain_one, g_qkv_one, g_out_one = fast_attention_back(
+        start, grad_one, gains[0], qkv_one, out_one, stored_one
+    )
+    sum_first = scatter_weight(
+        jnp.concatenate([g_qkv_one[0], g_out_one[0]], axis=1),
+        jnp.concatenate([g_qkv_one[1], g_out_one[1]], axis=1),
+        True,
+    )
+    input_grad = jnp.dot(grad_zero, to_whole.astype(F32), precision=lax.Precision.HIGHEST)[:L]
+
+    tail = jnp.concatenate([jnp.stack([gain_one, gain_two, gain_three, gain_four]), grad_router])
+    tail = jnp.swapaxes(tail.reshape(4 + experts, 8, width), 0, 1)
+    tail = tail + swap(tail, core=1)
+    tail = tail + swap(tail, y=1)
+    tail = tail[:4] + swap(tail[4:], x=1)
+    tail = tail[0] + swap(tail[1], z=1) + swap(tail[2], z=2) + swap(tail[3], z=3)
+
+    roots = clip_root(reduce_peak(jnp.stack([peak_one, peak_two])))
+    return (
+        block_output,
+        input_grad,
+        tail[0],
+        sum_first[:, :qkv_cols].reshape(first_qkv.shape),
+        sum_first[:, qkv_cols:].T,
+        tail[1],
+        sum_mlp[:, :ff_cols],
+        sum_mlp[:, ff_cols:].T,
+        tail[2],
+        sum_second[:, :qkv_cols].reshape(second_qkv.shape),
+        sum_second[:, qkv_cols:].T,
+        tail[3],
+        tail[4:].T,
+        grad_expert_up,
+        grad_expert_down,
+        clip_columns(first_qkv, roots[0], HD),
+        clip_columns(second_qkv, roots[1], HD),
+        roots,
+    )
+
+
 def solution(mesh):
     placed = (
         P(("dp", "tensor"), None),
@@ -412,8 +813,9 @@
         P("dp"),
         P(("dp", "tensor"), None),
     )
+    quick = mesh.shape["dp"] == 8 and mesh.shape["tensor"] == 4
     return jax.shard_map(
-        local,
+        fast_local if quick else local,
         mesh=mesh,
         in_specs=placed,
         out_specs=(

time: 2100 us -> 865 us (0.41)
  waiting for transfers between devices: 1280 us -> 372 us
  blocking collectives: 377 us -> 0 us
  starting transfers between devices: 13.7 us -> 156 us
  local copies, waits for them, and re-layouts: 191 us -> 110 us
    reduce_scatter x6 -> x0, waiting for transfers between devices: 919 us -> none  [the longest x1 317 us: local(): lax.psum_scatter(grad_expert_up, 'dp', scatter_dimension=1, tiled=True)]
    ppermute x0 -> x113, waiting for transfers between devices: none -> 372 us  [swap(): return lax.ppermute(values, AXES, pairs)]
    all_gather x12 -> x0, waiting for transfers between devices: 340 us -> none  [the longest x1 117 us: moe_fetch(): lax.all_gather(expert_down, 'dp', axis=2, tiled=True)]
    unnamed x9 -> x0, blocking collectives: 180 us -> none
    all_gather x5 -> x0, blocking collectives: 163 us -> none  [the longest x1 37.2 us: moe_fetch(): lax.all_gather(second_qkv, 'dp', axis=0, tiled=True)]
    ppermute x0 -> x113, starting transfers between devices: none -> 156 us  [swap(): return lax.ppermute(values, AXES, pairs)]
    gather x6 -> x0, local copies, waits for them, and re-layouts: 44.8 us -> none  [the longest x2 10.1 us: local(): moe_input[slot_token] * slot_filled[:, None].astype(jnp.bfloat16)]
    unnamed x224 -> x359, local copies, waits for them, and re-layouts: 64.2 us -> 36.5 us
  transfers between devices with their start and end apart: 29 -> 113, of which waited for: 20 -> 43; matrix products, arithmetic and copies ran while one was open for 12% -> 33% of each run, Pallas kernels for 0% -> 0%
where the time goes in v1:
time: 865 us; the launch traced here: 854 us
  waiting for transfers between devices  372 us (43%)
  starting transfers between devices  156 us (18%)
  matrix products  155 us (18%)
  local copies, waits for them, and re-layouts  110 us (13%)
  other arithmetic  56.2 us (6%)
    ppermute x113, waiting for transfers between devices, swap(): return lax.ppermute(values, AXES, pairs)  372 us
    ppermute x113, starting transfers between devices, swap(): return lax.ppermute(values, AXES, pairs)  156 us
    dot_general x60, matrix products, dot(): lax.dot_general(a, b, (((ca,), (cb,)), ((), ())), preferred_element_type=...  130 us
    unnamed x359, local copies, waits for them, and re-layouts  36.5 us
  transfers between devices with their start and end apart: 113, of which 43 were waited for; matrix products, arithmetic and copies ran while one was open for 33% of the time, Pallas kernels for 0%

profile of v1, /device:TPU:0, one launch (start us, length us, event | category | flops | bytes accessed | tf_op | source)
XLA Modules:
  0.0 854.3 jit_solution(17060538674331672064)
XLA Ops:
  1.8 5.1 collective-permute-start.25
  30.9 10.9 %collective-permute-start.8 = (bf16[96,960]{0,1:T(8,128)(2,1)S(1)}, bf16[96,960]{0,1:T(8,128)(2,1)S(1)}, u32[]{:S(2)}, u32[]{:S(2)}) collective-permute-start(bf16[96,960]{0,1:T(8,128)(2,1)S(1)} %pad_maximum_fusion.30), channel_id=1, source_target_pairs={{0,16},{1,17},{2,18},{3,19},{4,20},{5,21},{6,22},{7,23},{8,24},{9,... | collective-permute-start | bytes 552968 | tf_op jit(solution)/shard_map/ppermute | solution.py:403
  41.7 3.9 collective-permute-done.1
  52.2 3.9 collective-permute-start.16
  56.1 11.3 %collective-permute-done.8 = bf16[96,960]{0,1:T(8,128)(2,1)S(1)} collective-permute-done((bf16[96,960]{0,1:T(8,128)(2,1)S(1)}, bf16[96,960]{0,1:T(8,128)(2,1)S(1)}, u32[]{:S(2)}, u32[]{:S(2)}) %collective-permute-start.8) | collective-permute-done | bytes 184352 | tf_op jit(solution)/shard_map/ppermute | solution.py:403
  71.4 5.7 collective-permute-done.16
  90.5 29.6 %collective-permute-done.26 = bf16[384,576]{0,1:T(8,128)(2,1)} collective-permute-done((bf16[384,576]{0,1:T(8,128)(2,1)}, bf16[384,576]{0,1:T(8,128)(2,1)}, u32[]{:S(2)}, u32[]{:S(2)}) %collective-permute-start.26) | collective-permute-done | bytes 442400 | tf_op jit(solution)/shard_map/ppermute | solution.py:403
  128.7 4.3 concatenate.177
  154.1 3.6 fusion.293
  160.9 25.8 %collective-permute-done.12 = bf16[384,960]{0,1:T(8,128)(2,1)} collective-permute-done((bf16[384,960]{0,1:T(8,128)(2,1)}, bf16[384,960]{0,1:T(8,128)(2,1)}, u32[]{:S(2)}, u32[]{:S(2)}) %collective-permute-start.12) | collective-permute-done | bytes 737312 | tf_op jit(solution)/shard_map/ppermute | solution.py:403
  211.9 5.8 collective-permute-done.58
  225.7 5.8 collective-permute-done.61
  262.1 19.8 %collective-permute-done.41 = bf16[2,96,1536]{2,1,0:T(8,128)(2,1)S(1)} collective-permute-done((bf16[2,96,1536]{2,1,0:T(8,128)(2,1)S(1)}, bf16[2,96,1536]{2,1,0:T(8,128)(2,1)S(1)}, u32[]{:S(2)}, u32[]{:S(2)}) %collective-permute-start.41) | collective-permute-done | bytes 589856 | tf_op jit(solution)/shard_map/ppermute | solution.py:403
  281.9 14.4 %collective-permute-done.42 = bf16[2,96,1536]{2,1,0:T(8,128)(2,1)S(1)} collective-permute-done((bf16[2,96,1536]{2,1,0:T(8,128)(2,1)S(1)}, bf16[2,96,1536]{2,1,0:T(8,128)(2,1)S(1)}, u32[]{:S(2)}, u32[]{:S(2)}) %collective-permute-start.42) | collective-permute-done | bytes 589856 | tf_op jit(solution)/shard_map/ppermute | solution.py:403
  302.4 3.7 fusion.30
  307.3 12.9 %collective-permute-start.32 = (bf16[56,768]{1,0:T(8,128)(2,1)S(1)}, bf16[56,768]{1,0:T(8,128)(2,1)S(1)}, u32[]{:S(2)}, u32[]{:S(2)}) collective-permute-start(bf16[56,768]{1,0:T(8,128)(2,1)S(1)} %get-tuple-element.161), channel_id=1, source_target_pairs={{0,8},{1,9},{2,10},{3,11},{4,12},{5,13},{6,14},{7,15},{8,0},{9,1},... | collective-permute-start | bytes 258056 | tf_op jit(solution)/shard_map/ppermute | solution.py:403
  323.1 3.8 collective-permute-start.33
  326.9 7.3 collective-permute-done.33
  336.2 4.2 collective-permute-done.34
  344.9 5.4 collective-permute-done.36
  358.5 10.6 %collective-permute-start.111 = (f32[2,3]{1,0:T(2,128)S(1)}, f32[2,3]{1,0:T(2,128)S(1)}, u32[]{:S(2)}, u32[]{:S(2)}) collective-permute-start(f32[2,3]{1,0:T(2,128)S(1)} %max.25), channel_id=1, source_target_pairs={{0,16},{1,17},{2,18},{3,19},{4,20},{5,21},{6,22},{7,23},{8,24},{9,... | collective-permute-start | bytes 80 | tf_op jit(solution)/shard_map/ppermute | solution.py:403
  373.4 4.5 multiply_convert_fusion.2
  377.9 5.0 multiply_convert_fusion.1
  408.3 3.7 fusion.13
  412.0 4.0 fusion.7
  425.0 5.2 collective-permute-done.48
  441.3 4.6 fusion.65
  457.3 8.8 %collective-permute-done.67 = bf16[56,768]{1,0:T(8,128)(2,1)S(1)} collective-permute-done((bf16[56,768]{1,0:T(8,128)(2,1)}, bf16[56,768]{1,0:T(8,128)(2,1)S(1)}, u32[]{:S(2)}, u32[]{:S(2)}) %collective-permute-start.67) | collective-permute-done | bytes 86048 | tf_op jit(solution)/shard_map/ppermute | solution.py:403
  467.4 4.9 collective-permute-done.68
  473.0 3.8 collective-permute-done.69
  479.4 4.1 fusion.64
  495.6 3.9 convolution_convert_fusion.2
  501.9 52.0 %collective-permute-done.74 = bf16[208,768]{1,0:T(8,128)(2,1)S(1)} collective-permute-done((bf16[208,768]{1,0:T(8,128)(2,1)S(1)}, bf16[208,768]{1,0:T(8,128)(2,1)S(1)}, u32[]{:S(2)}, u32[]{:S(2)}) %collective-permute-start.74) | collective-permute-done | bytes 319520 | tf_op jit(solution)/shard_map/ppermute | solution.py:403
  555.9 3.8 convolution_convert_fusion.3
  586.9 3.8 add_convert_fusion
  590.7 4.5 copy.148
  598.6 3.6 collective-permute-start.104
  624.9 12.4 %collective-permute-done.104 = bf16[2,96,1536]{2,1,0:T(8,128)(2,1)} collective-permute-done((bf16[2,96,1536]{2,1,0:T(8,128)(2,1)}, bf16[2,96,1536]{2,1,0:T(8,128)(2,1)}, u32[]{:S(2)}, u32[]{:S(2)}) %collective-permute-start.104) | collective-permute-done | bytes 589856 | tf_op jit(solution)/shard_map/ppermute | solution.py:403
  639.3 9.3 %collective-permute-done.105 = bf16[2,96,1536]{2,1,0:T(8,128)(2,1)} collective-permute-done((bf16[2,96,1536]{2,1,0:T(8,128)(2,1)}, bf16[2,96,1536]{2,1,0:T(8,128)(2,1)}, u32[]{:S(2)}, u32[]{:S(2)}) %collective-permute-start.105) | collective-permute-done | bytes 589856 | tf_op jit(solution)/shard_map/ppermute | solution.py:403
  687.9 3.9 collective-permute-done.82
  705.6 35.4 %collective-permute-done.99 = bf16[384,768]{0,1:T(8,128)(2,1)S(1)} collective-permute-done((bf16[384,768]{0,1:T(8,128)(2,1)S(1)}, bf16[384,768]{0,1:T(8,128)(2,1)S(1)}, u32[]{:S(2)}, u32[]{:S(2)}) %collective-permute-start.99) | collective-permute-done | bytes 589856 | tf_op jit(solution)/shard_map/ppermute | solution.py:403
  754.2 5.9 collective-permute-done.101
  763.4 15.8 %collective-permute-done.87 = bf16[768,768]{0,1:T(8,128)(2,1)} collective-permute-done((bf16[768,768]{0,1:T(8,128)(2,1)}, bf16[768,768]{0,1:T(8,128)(2,1)}, u32[]{:S(2)}, u32[]{:S(2)}) %collective-permute-start.87) | collective-permute-done | bytes 1179680 | tf_op jit(solution)/shard_map/ppermute | solution.py:403
  785.4 12.8 %collective-permute-done.94 = bf16[384,1536]{0,1:T(8,128)(2,1)} collective-permute-done((bf16[384,1536]{0,1:T(8,128)(2,1)}, bf16[384,1536]{0,1:T(8,128)(2,1)}, u32[]{:S(2)}, u32[]{:S(2)}) %collective-permute-start.94) | collective-permute-done | bytes 1179680 | tf_op jit(solution)/shard_map/ppermute | solution.py:403
  811.3 3.6 collective-permute-done.91
  814.9 8.5 collective-permute-done.90
  825.5 8.6 %collective-permute-done.97 = bf16[96,1536]{0,1:T(8,128)(2,1)S(1)} collective-permute-done((bf16[96,1536]{0,1:T(8,128)(2,1)S(1)}, bf16[96,1536]{0,1:T(8,128)(2,1)S(1)}, u32[]{:S(2)}, u32[]{:S(2)}) %collective-permute-start.97) | collective-permute-done | bytes 294944 | tf_op jit(solution)/shard_map/ppermute | solution.py:403
  834.0 16.8 %collective-permute-done.96 = bf16[96,1536]{0,1:T(8,128)(2,1)} collective-permute-done((bf16[96,1536]{0,1:T(8,128)(2,1)S(1)}, bf16[96,1536]{0,1:T(8,128)(2,1)}, u32[]{:S(2)}, u32[]{:S(2)}) %collective-permute-start.96) | collective-permute-done | bytes 294944 | tf_op jit(solution)/shard_map/ppermute | solution.py:403
  (805 shorter events, 398.6 us)
Async XLA Ops:
  11.8 33.9 %collective-permute-start.1 = (bf16[96,704]{0,1:T(8,128)(2,1)S(1)}, bf16[96,704]{0,1:T(8,128)(2,1)}, u32[]{:S(2)}, u32[]{:S(2)}) collective-permute-start(bf16[96,704]{0,1:T(8,128)(2,1)S(1)} %concatenate.164), channel_id=1, source_target_pairs={{0,16},{1,17},{2,18},{3,19},{4,20},{5,21},{6,22},{7,23},{8,24},{9,... | collective-permute-start | bytes 405512 | tf_op jit(solution)/shard_map/ppermute | solution.py:403
  12.9 32.8 %collective-permute-start = (bf16[96,704]{0,1:T(8,128)(2,1)S(1)}, bf16[96,704]{0,1:T(8,128)(2,1)}, u32[]{:S(2)}, u32[]{:S(2)}) collective-permute-start(bf16[96,704]{0,1:T(8,128)(2,1)S(1)} %concatenate.164), channel_id=1, source_target_pairs={{0,8},{1,9},{2,10},{3,11},{4,12},{5,13},{6,14},{7,15},{8,0},{9,1},... | collective-permute-start | bytes 405512 | tf_op jit(solution)/shard_map/ppermute | solution.py:403
  30.9 36.5 %collective-permute-start.8 = (bf16[96,960]{0,1:T(8,128)(2,1)S(1)}, bf16[96,960]{0,1:T(8,128)(2,1)S(1)}, u32[]{:S(2)}, u32[]{:S(2)}) collective-permute-start(bf16[96,960]{0,1:T(8,128)(2,1)S(1)} %pad_maximum_fusion.30), channel_id=1, source_target_pairs={{0,16},{1,17},{2,18},{3,19},{4,20},{5,21},{6,22},{7,23},{8,24},{9,... | collective-permute-start | bytes 552968 | tf_op jit(solution)/shard_map/ppermute | solution.py:403
  48.8 36.6 %collective-permute-start.3 = (bf16[384,704]{0,1:T(8,128)(2,1)}, bf16[384,704]{0,1:T(8,128)(2,1)}, u32[]{:S(2)}, u32[]{:S(2)}) collective-permute-start(bf16[384,704]{0,1:T(8,128)(2,1)} %pad_maximum_fusion.22), channel_id=1, source_target_pairs={{0,4},{1,5},{2,6},{3,7},{4,0},{5,1},{6,2},{7,3},{8,12},{9,13},{10,... | collective-permute-start | bytes 1622024 | tf_op jit(solution)/shard_map/ppermute | solution.py:403
  77.1 44.6 %collective-permute-start.10 = (bf16[384,960]{0,1:T(8,128)(2,1)}, bf16[384,960]{0,1:T(8,128)(2,1)}, u32[]{:S(2)}, u32[]{:S(2)}) collective-permute-start(bf16[384,960]{0,1:T(8,128)(2,1)} %pad_maximum_fusion.12), channel_id=1, source_target_pairs={{0,4},{1,5},{2,6},{3,7},{4,0},{5,1},{6,2},{7,3},{8,12},{9,13},{10,... | collective-permute-start | bytes 2211848 | tf_op jit(solution)/shard_map/ppermute | solution.py:403
  80.1 41.6 %collective-permute-start.18 = (bf16[384,960]{0,1:T(8,128)(2,1)}, bf16[384,960]{0,1:T(8,128)(2,1)}, u32[]{:S(2)}, u32[]{:S(2)}) collective-permute-start(bf16[384,960]{0,1:T(8,128)(2,1)} %pad_maximum_fusion.13), channel_id=1, source_target_pairs={{0,4},{1,5},{2,6},{3,7},{4,0},{5,1},{6,2},{7,3},{8,12},{9,13},{10,... | collective-permute-start | bytes 2211848 | tf_op jit(solution)/shard_map/ppermute | solution.py:403
  81.9 51.2 %collective-permute-start.19 = (bf16[384,960]{0,1:T(8,128)(2,1)}, bf16[384,960]{0,1:T(8,128)(2,1)}, u32[]{:S(2)}, u32[]{:S(2)}) collective-permute-start(bf16[384,960]{0,1:T(8,128)(2,1)} %pad_maximum_fusion.13), channel_id=1, source_target_pairs={{0,2},{1,3},{2,0},{3,1},{4,6},{5,7},{6,4},{7,5},{8,10},{9,11},{10,... | collective-permute-start | bytes 2211848 | tf_op jit(solution)/shard_map/ppermute | solution.py:403
  85.3 34.8 %collective-permute-start.26 = (bf16[384,576]{0,1:T(8,128)(2,1)}, bf16[384,576]{0,1:T(8,128)(2,1)}, u32[]{:S(2)}, u32[]{:S(2)}) collective-permute-start(bf16[384,576]{0,1:T(8,128)(2,1)} %pad_maximum_fusion.25), channel_id=1, source_target_pairs={{0,4},{1,5},{2,6},{3,7},{4,0},{5,1},{6,2},{7,3},{8,12},{9,13},{10,... | collective-permute-start | bytes 1327112 | tf_op jit(solution)/shard_map/ppermute | solution.py:403
  88.7 48.0 %collective-permute-start.11 = (bf16[384,960]{0,1:T(8,128)(2,1)}, bf16[384,960]{0,1:T(8,128)(2,1)}, u32[]{:S(2)}, u32[]{:S(2)}) collective-permute-start(bf16[384,960]{0,1:T(8,128)(2,1)} %pad_maximum_fusion.12), channel_id=1, source_target_pairs={{0,2},{1,3},{2,0},{3,1},{4,6},{5,7},{6,4},{7,5},{8,10},{9,11},{10,... | collective-permute-start | bytes 2211848 | tf_op jit(solution)/shard_map/ppermute | solution.py:403
  133.0 119.4 %collective-permute-start.40 = (bf16[4,96,1536]{2,1,0:T(8,128)(2,1)}, bf16[4,96,1536]{2,1,0:T(8,128)(2,1)}, u32[]{:S(2)}, u32[]{:S(2)}) collective-permute-start(bf16[4,96,1536]{2,1,0:T(8,128)(2,1)} %get-tuple-element.118), channel_id=1, source_target_pairs={{0,4},{1,5},{2,6},{3,7},{4,0},{5,1},{6,2},{7,3},{8,12},{9,13},{10,... | collective-permute-start | bytes 3538952 | tf_op jit(solution)/shard_map/ppermute | solution.py:403
  136.6 53.7 %collective-permute-start.56 = (bf16[416,768]{1,0:T(8,128)(2,1)}, bf16[416,768]{1,0:T(8,128)(2,1)}, u32[]{:S(2)}, u32[]{:S(2)}) collective-permute-start(bf16[416,768]{1,0:T(8,128)(2,1)} %pad_maximum_fusion.18), channel_id=1, source_target_pairs={{0,1},{1,0},{2,3},{3,2},{4,5},{5,4},{6,7},{7,6},{8,9},{9,8},{10,11... | collective-permute-start | bytes 1916936 | tf_op jit(solution)/shard_map/ppermute | solution.py:403
  138.7 70.3 %collective-permute-start.28 = (bf16[384,576]{0,1:T(8,128)(2,1)}, bf16[384,576]{0,1:T(8,128)(2,1)}, u32[]{:S(2)}, u32[]{:S(2)}) collective-permute-start(bf16[384,576]{0,1:T(8,128)(2,1)} %collective-permute-done.27), channel_id=1, source_target_pairs={{0,4},{1,5},{2,6},{3,7},{4,0},{5,1},{6,2},{7,3},{8,12},{9,13},{10,... | collective-permute-start | bytes 1327112 | tf_op jit(solution)/shard_map/ppermute | solution.py:403
  144.3 42.4 %collective-permute-start.12 = (bf16[384,960]{0,1:T(8,128)(2,1)}, bf16[384,960]{0,1:T(8,128)(2,1)}, u32[]{:S(2)}, u32[]{:S(2)}) collective-permute-start(bf16[384,960]{0,1:T(8,128)(2,1)} %collective-permute-done.11), channel_id=1, source_target_pairs={{0,4},{1,5},{2,6},{3,7},{4,0},{5,1},{6,2},{7,3},{8,12},{9,13},{10,... | collective-permute-start | bytes 2211848 | tf_op jit(solution)/shard_map/ppermute | solution.py:403
  145.8 53.7 %collective-permute-start.20 = (bf16[384,960]{0,1:T(8,128)(2,1)}, bf16[384,960]{0,1:T(8,128)(2,1)}, u32[]{:S(2)}, u32[]{:S(2)}) collective-permute-start(bf16[384,960]{0,1:T(8,128)(2,1)} %collective-permute-done.18), channel_id=1, source_target_pairs={{0,2},{1,3},{2,0},{3,1},{4,6},{5,7},{6,4},{7,5},{8,10},{9,11},{10,... | collective-permute-start | bytes 2211848 | tf_op jit(solution)/shard_map/ppermute | solution.py:403
  196.2 64.3 %collective-permute-start.63 = (bf16[56,768]{1,0:T(8,128)(2,1)}, bf16[56,768]{1,0:T(8,128)(2,1)}, u32[]{:S(2)}, u32[]{:S(2)}) collective-permute-start(bf16[56,768]{1,0:T(8,128)(2,1)} %get-tuple-element.139), channel_id=1, source_target_pairs={{0,28},{1,29},{2,30},{3,31},{4,24},{5,25},{6,26},{7,27},{8,20},{9,... | collective-permute-start | bytes 258056 | tf_op jit(solution)/shard_map/ppermute | solution.py:403
  199.5 51.4 %collective-permute-start.62 = (bf16[56,768]{1,0:T(8,128)(2,1)}, bf16[56,768]{1,0:T(8,128)(2,1)}, u32[]{:S(2)}, u32[]{:S(2)}) collective-permute-start(bf16[56,768]{1,0:T(8,128)(2,1)} %get-tuple-element.140), channel_id=1, source_target_pairs={{0,20},{1,21},{2,22},{3,23},{4,16},{5,17},{6,18},{7,19},{8,28},{9,... | collective-permute-start | bytes 258056 | tf_op jit(solution)/shard_map/ppermute | solution.py:403
  253.8 28.1 %collective-permute-start.41 = (bf16[2,96,1536]{2,1,0:T(8,128)(2,1)S(1)}, bf16[2,96,1536]{2,1,0:T(8,128)(2,1)S(1)}, u32[]{:S(2)}, u32[]{:S(2)}) collective-permute-start(bf16[2,96,1536]{2,1,0:T(8,128)(2,1)S(1)} %get-tuple-element.115), channel_id=1, source_target_pairs={{0,8},{1,9},{2,10},{3,11},{4,12},{5,13},{6,14},{7,15},{8,0},{9,1},... | collective-permute-start | bytes 1769480 | tf_op jit(solution)/shard_map/ppermute | solution.py:403
  253.9 42.4 %collective-permute-start.42 = (bf16[2,96,1536]{2,1,0:T(8,128)(2,1)S(1)}, bf16[2,96,1536]{2,1,0:T(8,128)(2,1)S(1)}, u32[]{:S(2)}, u32[]{:S(2)}) collective-permute-start(bf16[2,96,1536]{2,1,0:T(8,128)(2,1)S(1)} %get-tuple-element.116), channel_id=1, source_target_pairs={{0,16},{1,17},{2,18},{3,19},{4,20},{5,21},{6,22},{7,23},{8,24},{9,... | collective-permute-start | bytes 1769480 | tf_op jit(solution)/shard_map/ppermute | solution.py:403
  256.8 39.5 %collective-permute-start.43 = (bf16[2,96,1536]{2,1,0:T(8,128)(2,1)S(1)}, bf16[2,96,1536]{2,1,0:T(8,128)(2,1)S(1)}, u32[]{:S(2)}, u32[]{:S(2)}) collective-permute-start(bf16[2,96,1536]{2,1,0:T(8,128)(2,1)S(1)} %get-tuple-element.117), channel_id=1, source_target_pairs={{0,24},{1,25},{2,26},{3,27},{4,28},{5,29},{6,30},{7,31},{8,16},{9,... | collective-permute-start | bytes 1769480 | tf_op jit(solution)/shard_map/ppermute | solution.py:403
  258.9 40.6 %collective-permute-start.30 = (bf16[208,768]{1,0:T(8,128)(2,1)S(1)}, bf16[208,768]{1,0:T(8,128)(2,1)S(1)}, u32[]{:S(2)}, u32[]{:S(2)}) collective-permute-start(bf16[208,768]{1,0:T(8,128)(2,1)S(1)} %multiply_convert_fusion.9), channel_id=1, source_target_pairs={{0,2},{1,3},{2,0},{3,1},{4,6},{5,7},{6,4},{7,5},{8,10},{9,11},{10,... | collective-permute-start | bytes 958472 | tf_op jit(solution)/shard_map/ppermute | solution.py:403
  298.0 79.8 %collective-permute-start.44 = (bf16[768,1536]{1,0:T(8,128)(2,1)}, bf16[768,1536]{1,0:T(8,128)(2,1)}, u32[]{:S(2)}, u32[]{:S(2)}) collective-permute-start(bf16[768,1536]{1,0:T(8,128)(2,1)} %bitcast.32), channel_id=1, source_target_pairs={{0,2},{1,3},{2,0},{3,1},{4,6},{5,7},{6,4},{7,5},{8,10},{9,11},{10,... | collective-permute-start | bytes 7077896 | tf_op jit(solution)/shard_map/ppermute | solution.py:403
  320.2 32.5 %collective-permute-start.108 = (f32[2,3]{1,0:T(2,128)S(1)}, f32[2,3]{1,0:T(2,128)S(1)}, u32[]{:S(2)}, u32[]{:S(2)}) collective-permute-start(f32[2,3]{1,0:T(2,128)S(1)} %slice.635), channel_id=1, source_target_pairs={{0,2},{1,3},{2,0},{3,1},{4,6},{5,7},{6,4},{7,5},{8,10},{9,11},{10,... | collective-permute-start | bytes 80 | tf_op jit(solution)/shard_map/ppermute | solution.py:403
  320.7 29.6 %collective-permute-start.38 = (bf16[56,768]{1,0:T(8,128)(2,1)S(1)}, bf16[56,768]{1,0:T(8,128)(2,1)S(1)}, u32[]{:S(2)}, u32[]{:S(2)}) collective-permute-start(bf16[56,768]{1,0:T(8,128)(2,1)S(1)} %get-tuple-element.155), channel_id=1, source_target_pairs={{0,28},{1,29},{2,30},{3,31},{4,24},{5,25},{6,26},{7,27},{8,20},{9,... | collective-permute-start | bytes 258056 | tf_op jit(solution)/shard_map/ppermute | solution.py:403
  323.0 27.3 %collective-permute-start.37 = (bf16[56,768]{1,0:T(8,128)(2,1)S(1)}, bf16[56,768]{1,0:T(8,128)(2,1)S(1)}, u32[]{:S(2)}, u32[]{:S(2)}) collective-permute-start(bf16[56,768]{1,0:T(8,128)(2,1)S(1)} %get-tuple-element.156), channel_id=1, source_target_pairs={{0,20},{1,21},{2,22},{3,23},{4,16},{5,17},{6,18},{7,19},{8,28},{9,... | collective-permute-start | bytes 258056 | tf_op jit(solution)/shard_map/ppermute | solution.py:403
  400.3 34.4 %collective-permute-start.52 = (bf16[56,768]{1,0:T(8,128)(2,1)S(1)}, bf16[56,768]{1,0:T(8,128)(2,1)S(1)}, u32[]{:S(2)}, u32[]{:S(2)}) collective-permute-start(bf16[56,768]{1,0:T(8,128)(2,1)S(1)} %get-tuple-element.147), channel_id=1, source_target_pairs={{0,28},{1,29},{2,30},{3,31},{4,24},{5,25},{6,26},{7,27},{8,20},{9,... | collective-permute-start | bytes 258056 | tf_op jit(solution)/shard_map/ppermute | solution.py:403
  402.4 32.3 %collective-permute-start.51 = (bf16[56,768]{1,0:T(8,128)(2,1)S(1)}, bf16[56,768]{1,0:T(8,128)(2,1)S(1)}, u32[]{:S(2)}, u32[]{:S(2)}) collective-permute-start(bf16[56,768]{1,0:T(8,128)(2,1)S(1)} %get-tuple-element.148), channel_id=1, source_target_pairs={{0,20},{1,21},{2,22},{3,23},{4,16},{5,17},{6,18},{7,19},{8,28},{9,... | collective-permute-start | bytes 258056 | tf_op jit(solution)/shard_map/ppermute | solution.py:403
  403.6 31.1 %collective-permute-start.50 = (bf16[56,768]{1,0:T(8,128)(2,1)S(1)}, bf16[56,768]{1,0:T(8,128)(2,1)S(1)}, u32[]{:S(2)}, u32[]{:S(2)}) collective-permute-start(bf16[56,768]{1,0:T(8,128)(2,1)S(1)} %get-tuple-element.149), channel_id=1, source_target_pairs={{0,12},{1,13},{2,14},{3,15},{4,8},{5,9},{6,10},{7,11},{8,4},{9,5},... | collective-permute-start | bytes 258056 | tf_op jit(solution)/shard_map/ppermute | solution.py:403
  448.1 51.3 %collective-permute-start.53 = (bf16[416,768]{1,0:T(8,128)(2,1)}, bf16[416,768]{1,0:T(8,128)(2,1)}, u32[]{:S(2)}, u32[]{:S(2)}) collective-permute-start(bf16[416,768]{1,0:T(8,128)(2,1)} %slice.1096), channel_id=1, source_target_pairs={{0,1},{1,0},{2,3},{3,2},{4,5},{5,4},{6,7},{7,6},{8,9},{9,8},{10,11... | collective-permute-start | bytes 1916936 | tf_op jit(solution)/shard_map/ppermute | solution.py:403
  448.1 30.6 %collective-permute-start.72 = (bf16[56,768]{1,0:T(8,128)(2,1)}, bf16[56,768]{1,0:T(8,128)(2,1)S(1)}, u32[]{:S(2)}, u32[]{:S(2)}) collective-permute-start(bf16[56,768]{1,0:T(8,128)(2,1)} %get-tuple-element.131), channel_id=1, source_target_pairs={{0,28},{1,29},{2,30},{3,31},{4,24},{5,25},{6,26},{7,27},{8,20},{9,... | collective-permute-start | bytes 258056 | tf_op jit(solution)/shard_map/ppermute | solution.py:403
  450.8 27.3 %collective-permute-start.71 = (bf16[56,768]{1,0:T(8,128)(2,1)}, bf16[56,768]{1,0:T(8,128)(2,1)S(1)}, u32[]{:S(2)}, u32[]{:S(2)}) collective-permute-start(bf16[56,768]{1,0:T(8,128)(2,1)} %get-tuple-element.132), channel_id=1, source_target_pairs={{0,20},{1,21},{2,22},{3,23},{4,16},{5,17},{6,18},{7,19},{8,28},{9,... | collective-permute-start | bytes 258056 | tf_op jit(solution)/shard_map/ppermute | solution.py:403
  452.5 25.0 %collective-permute-start.70 = (bf16[56,768]{1,0:T(8,128)(2,1)}, bf16[56,768]{1,0:T(8,128)(2,1)S(1)}, u32[]{:S(2)}, u32[]{:S(2)}) collective-permute-start(bf16[56,768]{1,0:T(8,128)(2,1)} %get-tuple-element.133), channel_id=1, source_target_pairs={{0,12},{1,13},{2,14},{3,15},{4,8},{5,9},{6,10},{7,11},{8,4},{9,5},... | collective-permute-start | bytes 258056 | tf_op jit(solution)/shard_map/ppermute | solution.py:403
  492.8 93.9 %collective-permute-start.103 = (bf16[768,1536]{0,1:T(8,128)(2,1)}, bf16[768,1536]{0,1:T(8,128)(2,1)}, u32[]{:S(2)}, u32[]{:S(2)}) collective-permute-start(bf16[768,1536]{0,1:T(8,128)(2,1)} %pad_maximum_fusion.2), channel_id=1, source_target_pairs={{0,2},{1,3},{2,0},{3,1},{4,6},{5,7},{6,4},{7,5},{8,10},{9,11},{10,... | collective-permute-start | bytes 7077896 | tf_op jit(solution)/shard_map/ppermute | solution.py:403
  494.5 59.4 %collective-permute-start.74 = (bf16[208,768]{1,0:T(8,128)(2,1)S(1)}, bf16[208,768]{1,0:T(8,128)(2,1)S(1)}, u32[]{:S(2)}, u32[]{:S(2)}) collective-permute-start(bf16[208,768]{1,0:T(8,128)(2,1)S(1)} %slice.1100), channel_id=1, source_target_pairs={{0,2},{1,3},{2,0},{3,1},{4,6},{5,7},{6,4},{7,5},{8,10},{9,11},{10,... | collective-permute-start | bytes 958472 | tf_op jit(solution)/shard_map/ppermute | solution.py:403
  500.8 59.5 %collective-permute-start.54 = (bf16[208,768]{1,0:T(8,128)(2,1)S(1)}, bf16[208,768]{1,0:T(8,128)(2,1)S(1)}, u32[]{:S(2)}, u32[]{:S(2)}) collective-permute-start(bf16[208,768]{1,0:T(8,128)(2,1)S(1)} %slice.1101), channel_id=1, source_target_pairs={{0,2},{1,3},{2,0},{3,1},{4,6},{5,7},{6,4},{7,5},{8,10},{9,11},{10,... | collective-permute-start | bytes 958472 | tf_op jit(solution)/shard_map/ppermute | solution.py:403
  578.3 24.9 %collective-permute-start.76 = (bf16[208,768]{1,0:T(8,128)(2,1)}, bf16[208,768]{1,0:T(8,128)(2,1)}, u32[]{:S(2)}, u32[]{:S(2)}) collective-permute-start(bf16[208,768]{1,0:T(8,128)(2,1)} %slice.1099), channel_id=1, source_target_pairs={{0,1},{1,0},{2,3},{3,2},{4,5},{5,4},{6,7},{7,6},{8,9},{9,8},{10,11... | collective-permute-start | bytes 958472 | tf_op jit(solution)/shard_map/ppermute | solution.py:403
  581.5 73.6 %collective-permute-start.98 = (bf16[768,768]{0,1:T(8,128)(2,1)}, bf16[768,768]{0,1:T(8,128)(2,1)}, u32[]{:S(2)}, u32[]{:S(2)}) collective-permute-start(bf16[768,768]{0,1:T(8,128)(2,1)} %pad_maximum_fusion.9), channel_id=1, source_target_pairs={{0,2},{1,3},{2,0},{3,1},{4,6},{5,7},{6,4},{7,5},{8,10},{9,11},{10,... | collective-permute-start | bytes 3538952 | tf_op jit(solution)/shard_map/ppermute | solution.py:403
  597.8 52.5 %collective-permute-start.106 = (bf16[2,96,1536]{2,1,0:T(8,128)(2,1)}, bf16[2,96,1536]{2,1,0:T(8,128)(2,1)}, u32[]{:S(2)}, u32[]{:S(2)}) collective-permute-start(bf16[2,96,1536]{2,1,0:T(8,128)(2,1)} %get-tuple-element.111), channel_id=1, source_target_pairs={{0,24},{1,25},{2,26},{3,27},{4,28},{5,29},{6,30},{7,31},{8,16},{9,... | collective-permute-start | bytes 1769480 | tf_op jit(solution)/shard_map/ppermute | solution.py:403
  598.6 50.0 %collective-permute-start.105 = (bf16[2,96,1536]{2,1,0:T(8,128)(2,1)}, bf16[2,96,1536]{2,1,0:T(8,128)(2,1)}, u32[]{:S(2)}, u32[]{:S(2)}) collective-permute-start(bf16[2,96,1536]{2,1,0:T(8,128)(2,1)} %get-tuple-element.112), channel_id=1, source_target_pairs={{0,16},{1,17},{2,18},{3,19},{4,20},{5,21},{6,22},{7,23},{8,24},{9,... | collective-permute-start | bytes 1769480 | tf_op jit(solution)/shard_map/ppermute | solution.py:403
  598.6 38.7 %collective-permute-start.104 = (bf16[2,96,1536]{2,1,0:T(8,128)(2,1)}, bf16[2,96,1536]{2,1,0:T(8,128)(2,1)}, u32[]{:S(2)}, u32[]{:S(2)}) collective-permute-start(bf16[2,96,1536]{2,1,0:T(8,128)(2,1)} %get-tuple-element.113), channel_id=1, source_target_pairs={{0,8},{1,9},{2,10},{3,11},{4,12},{5,13},{6,14},{7,15},{8,0},{9,1},... | collective-permute-start | bytes 1769480 | tf_op jit(solution)/shard_map/ppermute | solution.py:403
  615.6 36.6 %collective-permute-start.78 = (bf16[208,768]{1,0:T(8,128)(2,1)S(1)}, bf16[208,768]{1,0:T(8,128)(2,1)S(1)}, u32[]{:S(2)}, u32[]{:S(2)}) collective-permute-start(bf16[208,768]{1,0:T(8,128)(2,1)S(1)} %slice.1098), channel_id=1, source_target_pairs={{0,1},{1,0},{2,3},{3,2},{4,5},{5,4},{6,7},{7,6},{8,9},{9,8},{10,11... | collective-permute-start | bytes 958472 | tf_op jit(solution)/shard_map/ppermute | solution.py:403
  637.2 148.2 %collective-permute-start.92 = (bf16[384,1536]{0,1:T(8,128)(2,1)}, bf16[384,1536]{0,1:T(8,128)(2,1)}, u32[]{:S(2)}, u32[]{:S(2)}) collective-permute-start(bf16[384,1536]{0,1:T(8,128)(2,1)} %pad_maximum_fusion.5), channel_id=1, source_target_pairs={{0,4},{1,5},{2,6},{3,7},{4,0},{5,1},{6,2},{7,3},{8,12},{9,13},{10,... | collective-permute-start | bytes 3538952 | tf_op jit(solution)/shard_map/ppermute | solution.py:403
  648.6 96.8 %collective-permute-start.93 = (bf16[384,1536]{0,1:T(8,128)(2,1)}, bf16[384,1536]{0,1:T(8,128)(2,1)}, u32[]{:S(2)}, u32[]{:S(2)}) collective-permute-start(bf16[384,1536]{0,1:T(8,128)(2,1)} %pad_maximum_fusion.4), channel_id=1, source_target_pairs={{0,4},{1,5},{2,6},{3,7},{4,0},{5,1},{6,2},{7,3},{8,12},{9,13},{10,... | collective-permute-start | bytes 3538952 | tf_op jit(solution)/shard_map/ppermute | solution.py:403
  702.3 59.4 %collective-permute-start.107 = (bf16[4,96,1536]{2,1,0:T(8,128)(2,1)}, bf16[4,96,1536]{2,1,0:T(8,128)(2,1)}, u32[]{:S(2)}, u32[]{:S(2)}) collective-permute-start(bf16[4,96,1536]{2,1,0:T(8,128)(2,1)} %pad_maximum_fusion.10), channel_id=1, source_target_pairs={{0,4},{1,5},{2,6},{3,7},{4,0},{5,1},{6,2},{7,3},{8,12},{9,13},{10,... | collective-permute-start | bytes 3538952 | tf_op jit(solution)/shard_map/ppermute | solution.py:403
  704.3 36.6 %collective-permute-start.99 = (bf16[384,768]{0,1:T(8,128)(2,1)S(1)}, bf16[384,768]{0,1:T(8,128)(2,1)S(1)}, u32[]{:S(2)}, u32[]{:S(2)}) collective-permute-start(bf16[384,768]{0,1:T(8,128)(2,1)S(1)} %copy-done.76), channel_id=1, source_target_pairs={{0,4},{1,5},{2,6},{3,7},{4,0},{5,1},{6,2},{7,3},{8,12},{9,13},{10,... | collective-permute-start | bytes 1769480 | tf_op jit(solution)/shard_map/ppermute | solution.py:403
  750.0 29.2 %collective-permute-start.87 = (bf16[768,768]{0,1:T(8,128)(2,1)}, bf16[768,768]{0,1:T(8,128)(2,1)}, u32[]{:S(2)}, u32[]{:S(2)}) collective-permute-start(bf16[768,768]{0,1:T(8,128)(2,1)} %pad_maximum_fusion.8), channel_id=1, source_target_pairs={{0,2},{1,3},{2,0},{3,1},{4,6},{5,7},{6,4},{7,5},{8,10},{9,11},{10,... | collective-permute-start | bytes 3538952 | tf_op jit(solution)/shard_map/ppermute | solution.py:403
  753.7 44.5 %collective-permute-start.94 = (bf16[384,1536]{0,1:T(8,128)(2,1)}, bf16[384,1536]{0,1:T(8,128)(2,1)}, u32[]{:S(2)}, u32[]{:S(2)}) collective-permute-start(bf16[384,1536]{0,1:T(8,128)(2,1)} %add_convert_fusion.3), channel_id=1, source_target_pairs={{0,2},{1,3},{2,0},{3,1},{4,6},{5,7},{6,4},{7,5},{8,10},{9,11},{10,... | collective-permute-start | bytes 3538952 | tf_op jit(solution)/shard_map/ppermute | solution.py:403
  807.8 26.3 %collective-permute-start.97 = (bf16[96,1536]{0,1:T(8,128)(2,1)S(1)}, bf16[96,1536]{0,1:T(8,128)(2,1)S(1)}, u32[]{:S(2)}, u32[]{:S(2)}) collective-permute-start(bf16[96,1536]{0,1:T(8,128)(2,1)S(1)} %get-tuple-element.121), channel_id=1, source_target_pairs={{0,24},{1,25},{2,26},{3,27},{4,28},{5,29},{6,30},{7,31},{8,16},{9,... | collective-permute-start | bytes 884744 | tf_op jit(solution)/shard_map/ppermute | solution.py:403
  811.0 39.9 %collective-permute-start.96 = (bf16[96,1536]{0,1:T(8,128)(2,1)S(1)}, bf16[96,1536]{0,1:T(8,128)(2,1)}, u32[]{:S(2)}, u32[]{:S(2)}) collective-permute-start(bf16[96,1536]{0,1:T(8,128)(2,1)S(1)} %get-tuple-element.122), channel_id=1, source_target_pairs={{0,16},{1,17},{2,18},{3,19},{4,20},{5,21},{6,22},{7,23},{8,24},{9,... | collective-permute-start | bytes 884744 | tf_op jit(solution)/shard_map/ppermute | solution.py:403
  (222 other events, 3436.4 us)

commit v2 on v0

--- a/solution.py
+++ b/solution.py
@@ -1,6 +1,8 @@
 import jax
 import jax.numpy as jnp
 from jax import lax
+from jax.experimental import pallas as pl
+from jax.experimental.pallas import tpu as pltpu
 from jax.sharding import PartitionSpec as P
 
 HD = 64
@@ -391,6 +393,855 @@
     )
 
 
+ROWS = 208
+AXES = ("dp", "tensor")
+BF = jnp.bfloat16
+F32 = jnp.float32
+VM = pl.BlockSpec(memory_space=pltpu.VMEM)
+SM = pl.BlockSpec(memory_space=pltpu.SMEM)
+
+
+def swap(values, z=0, x=0, y=0, core=0):
+    shift_d, shift_t = 2 * z + x, 2 * y + core
+    pairs = [(d * 4 + t, (d ^ shift_d) * 4 + (t ^ shift_t)) for d in range(8) for t in range(4)]
+    return lax.ppermute(values, AXES, pairs)
+
+
+def hold(values, *tokens):
+    return lax.optimization_barrier((values,) + tokens)[0]
+
+
+def run(kernel, outs, args, flops, scratch=(), scalars=0, mib=32):
+    shapes = [jax.ShapeDtypeStruct(s, dt) for s, dt in outs]
+    moved = sum(a.size * a.dtype.itemsize for a in args)
+    moved += sum(s.size * s.dtype.itemsize for s in shapes)
+    return pl.pallas_call(
+        kernel,
+        out_shape=shapes,
+        in_specs=[SM] * scalars + [VM] * (len(args) - scalars),
+        out_specs=[VM] * len(shapes),
+        scratch_shapes=list(scratch),
+        compiler_params=pltpu.CompilerParams(vmem_limit_bytes=mib * 2**20),
+        cost_estimate=pl.CostEstimate(flops=int(flops), bytes_accessed=int(moved), transcendentals=0),
+    )(*args)
+
+
+def dot(a, b, ca, cb):
+    return lax.dot_general(a, b, (((ca,), (cb,)), ((), ())), preferred_element_type=F32)
+
+
+def norm_stats(values):
+    center = values - jnp.mean(values, axis=-1, keepdims=True)
+    scale = lax.rsqrt(jnp.mean(center * center, axis=-1, keepdims=True) + epsilon)
+    return center * scale, scale
+
+
+def enter_kernel(live, x_ref, c_ref, perm_ref, start_ref, grad_ref, low_ref):
+    rows = x_ref.shape[0]
+    scale = live[0].astype(F32)
+    extra = jnp.zeros((ROWS - rows, x_ref.shape[1]), F32)
+    start_ref[:rows] = dot(x_ref[...], perm_ref[...], 1, 1)
+    start_ref[rows:] = extra
+    grad = dot(c_ref[...], perm_ref[...], 1, 1) * scale
+    grad_ref[:rows] = grad
+    grad_ref[rows:] = extra
+    low_ref[:rows] = grad.astype(BF)
+    low_ref[rows:] = extra.astype(BF)
+
+
+def norm_kernel(x_ref, gain_ref, out_ref):
+    out_ref[...] = (norm_stats(x_ref[...])[0] * gain_ref[...]).astype(BF)
+
+
+def join_norm_kernel(x_ref, own_ref, far_ref, gain_ref, sum_ref, out_ref):
+    total = x_ref[...] + (own_ref[...] + far_ref[...].astype(F32))
+    sum_ref[...] = total
+    out_ref[...] = (norm_stats(total)[0] * gain_ref[...]).astype(BF)
+
+
+def norm_back_kernel(x_ref, up_ref, own_ref, far_ref, gain_ref, grad_ref, low_ref, gain_out):
+    upstream = own_ref[...] + far_ref[...].astype(F32)
+    normed, scale = norm_stats(x_ref[...])
+    scaled = upstream * gain_ref[...]
+    grad = up_ref[...] + scale * (
+        scaled
+        - jnp.mean(scaled, axis=-1, keepdims=True)
+        - normed * jnp.mean(scaled * normed, axis=-1, keepdims=True)
+    )
+    grad_ref[...] = grad
+    low_ref[...] = grad.astype(BF)
+    gain_out[...] = jnp.sum(upstream * normed, axis=0, keepdims=True)
+
+
+def fill_pair(pair, first_ref, second_ref):
+    rows = first_ref.shape[0]
+    pair[:rows] = first_ref[...]
+    pair[rows:] = second_ref[...]
+
+
+def score_block(queries, keyset):
+    scores = dot(queries, keyset, 1, 1) * HD ** (-0.5)
+    column = lax.broadcasted_iota(jnp.int32, scores.shape, 1)
+    scores = jnp.where(column < L, scores, -1e30)
+    top = jnp.max(scores, axis=-1, keepdims=True)
+    weight = jnp.exp(scores - top)
+    return weight * (1.0 / jnp.sum(weight, axis=-1, keepdims=True)), top
+
+
+def attend_kernel(
+    live, a0, a1, w0, w1, o0, o1, mix_ref, att_ref, own_ref, sib_ref, peak_ref, pair
+):
+    fill_pair(pair, a0, a1)
+    part = o0.shape[1]
+    heads = part // HD
+    for y, w in enumerate((w0, w1)):
+        mix_ref[y] = dot(pair[...], w[...], 1, 0).astype(BF)
+    row_ok = lax.broadcasted_iota(jnp.int32, (ROWS, 1), 0) < L
+    for y in range(2):
+        for h in range(heads):
+            peaks = []
+            for i in range(2):
+                rows = slice(i * ROWS, (i + 1) * ROWS)
+                cut = [
+                    mix_ref[y, rows, c * part + h * HD : c * part + (h + 1) * HD] for c in range(3)
+                ]
+                probs, top = score_block(cut[0], cut[1])
+                place = y * part + h * HD
+                att_ref[rows, place : place + HD] = dot(probs.astype(BF), cut[2], 1, 0).astype(BF)
+                best = jnp.max(jnp.where(row_ok, top, -1e30), axis=0, keepdims=True)
+                peaks.append(jnp.where(live[i] > 0, best, -1e30))
+            number = y * heads + h
+            peak_ref[number : number + 1, :] = jnp.broadcast_to(
+                jnp.maximum(peaks[0], peaks[1]), (1, peak_ref.shape[1])
+            )
+    partial = dot(att_ref[:, :part], o0[...], 1, 1) + dot(att_ref[:, part:], o1[...], 1, 1)
+    own_ref[...] = partial[:ROWS]
+    sib_ref[...] = partial[ROWS:].astype(BF)
+
+
+def attend_back_kernel(
+    g0, g1, a0, a1, mix_ref, att_ref, w0, w1, o0, o1,
+    pack_own, pack_far, own_ref, sib_ref, pair, grad_att, grad_mix,
+):
+    part = o0.shape[1]
+    heads = part // HD
+    fill_pair(pair, g0, g1)
+    for y, (o, pack) in enumerate(((o0, pack_own), (o1, pack_far))):
+        grad_att[:, y * part : (y + 1) * part] = dot(pair[...], o[...], 1, 0).astype(BF)
+        pack[:, 3 * part :] = dot(pair[...], att_ref[:, y * part : (y + 1) * part], 0, 0).astype(BF)
+    factor = HD ** (-0.5)
+    for y in range(2):
+        for h in range(heads):
+            for i in range(2):
+                rows = slice(i * ROWS, (i + 1) * ROWS)
+                spans = [slice(c * part + h * HD, c * part + (h + 1) * HD) for c in range(3)]
+                queries, keyset, values = (mix_ref[y, rows, s] for s in spans)
+                place = y * part + h * HD
+                grad = grad_att[rows, place : place + HD]
+                probs, _ = score_block(queries, keyset)
+                grad_mix[y, rows, spans[2]] = dot(probs.astype(BF), grad, 0, 0).astype(BF)
+                grad_probs = dot(grad, values, 1, 1)
+                slope = probs * (
+                    grad_probs - jnp.sum(grad_probs * probs, axis=-1, keepdims=True)
+                )
+                slope = slope.astype(BF)
+                grad_mix[y, rows, spans[0]] = (factor * dot(slope, keyset, 1, 0)).astype(BF)
+                grad_mix[y, rows, spans[1]] = (factor * dot(slope, queries, 0, 0)).astype(BF)
+    fill_pair(pair, a0, a1)
+    pack_own[:, : 3 * part] = dot(pair[...], grad_mix[0], 0, 0).astype(BF)
+    pack_far[:, : 3 * part] = dot(pair[...], grad_mix[1], 0, 0).astype(BF)
+    partial = dot(grad_mix[0], w0[...], 1, 1) + dot(grad_mix[1], w1[...], 1, 1)
+    own_ref[...] = partial[:ROWS]
+    sib_ref[...] = partial[ROWS:].astype(BF)
+
+
+def gelu_pair(hidden):
+    cdf = 0.5 * (1.0 + lax.erf(hidden * 0.7071067811865476))
+    slope = cdf + hidden * jnp.exp(-0.5 * hidden * hidden) * 0.3989422804014327
+    return (hidden * cdf).astype(BF), slope.astype(BF)
+
+
+def mlp_kernel(b0, b1, u0, u1, d0, d1, act_ref, slope_ref, own_ref, sib_ref, pair):
+    fill_pair(pair, b0, b1)
+    for y, u in enumerate((u0, u1)):
+        for c in range(0, u.shape[1], 256):
+            span = slice(c, c + 256)
+            act, slope = gelu_pair(dot(pair[...], u[:, span], 1, 0))
+            act_ref[y, :, span] = act
+            slope_ref[y, :, span] = slope
+    partial = dot(act_ref[0], d0[...], 1, 1) + dot(act_ref[1], d1[...], 1, 1)
+    own_ref[...] = partial[:ROWS]
+    sib_ref[...] = partial[ROWS:].astype(BF)
+
+
+def mlp_back_kernel(
+    g0, g1, b0, b1, act_ref, slope_ref, u0, u1, d0, d1,
+    pack_own, pack_far, own_ref, sib_ref, pair, grad_hidden,
+):
+    fill_pair(pair, g0, g1)
+    wide = u0.shape[1]
+    for y, (d, pack) in enumerate(((d0, pack_own), (d1, pack_far))):
+        grad_hidden[y] = (dot(pair[...], d[...], 1, 0) * slope_ref[y].astype(F32)).astype(BF)
+        pack[:, wide:] = dot(pair[...], act_ref[y], 0, 0).astype(BF)
+    partial = dot(grad_hidden[0], u0[...], 1, 1) + dot(grad_hidden[1], u1[...], 1, 1)
+    own_ref[...] = partial[:ROWS]
+    sib_ref[...] = partial[ROWS:].astype(BF)
+    fill_pair(pair, b0, b1)
+    pack_own[:, :wide] = dot(pair[...], grad_hidden[0], 0, 0).astype(BF)
+    pack_far[:, :wide] = dot(pair[...], grad_hidden[1], 0, 0).astype(BF)
+
+
+def picked(row_code, codes):
+    hit = (row_code[...] == codes[0:1, :]) | (row_code[...] == codes[1:2, :])
+    return jnp.where(hit, 1.0, 0.0).astype(BF)
+
+
+def dispatch_kernel(row_code, codes, p0, p1, perm_ref, *rest):
+    outs, rows = rest[:8], rest[8]
+    fill_pair(rows, p0, p1)
+    picks = dot(picked(row_code, codes), rows[...], 1, 0).astype(BF)
+    whole = dot(picks, perm_ref[...], 1, 0).astype(BF)
+    size = outs[0].shape[0]
+    for p, out in enumerate(outs):
+        out[...] = whole[p * size : (p + 1) * size]
+
+
+def collect_kernel(perm_ref, *rest):
+    pieces, out, rows = rest[:8], rest[8], rest[9]
+    size = pieces[0].shape[0]
+    for p, piece in enumerate(pieces):
+        rows[p * size : (p + 1) * size] = piece[...]
+    out[...] = dot(rows[...], perm_ref[...], 1, 1).astype(BF)
+
+
+def combine_kernel(row_code, codes, perm_ref, *rest):
+    pieces, own_ref, sib_ref, rows = rest[:8], rest[8], rest[9], rest[10]
+    size = pieces[0].shape[0]
+    for p, piece in enumerate(pieces):
+        rows[p * size : (p + 1) * size] = piece[...]
+    back = dot(rows[...], perm_ref[...], 1, 1).astype(BF)
+    partial = dot(picked(row_code, codes), back, 0, 0)
+    half = partial.shape[0] // 2
+    own_ref[...] = partial[:half]
+    sib_ref[...] = partial[half:].astype(BF)
+
+
+def pair_add_kernel(own_ref, far_ref, near_ref, send_ref):
+    total = own_ref[...] + far_ref[...].astype(F32)
+    near_ref[...] = total[:ROWS]
+    send_ref[...] = total[ROWS:].astype(BF)
+
+
+def route_of(tokens, router, number):
+    logits = dot(tokens, router, 1, 1)
+    column = lax.broadcasted_iota(jnp.int32, logits.shape, 1)
+    logits = jnp.where(column < 8, logits, -1e30)
+    weight = jnp.exp(logits - jnp.max(logits, axis=-1, keepdims=True))
+    route = weight / jnp.sum(weight, axis=-1, keepdims=True)
+    mine = jnp.where(column == number, 1.0, 0.0)
+    return route, mine, jnp.sum(route * mine, axis=-1, keepdims=True)
+
+
+def expert_kernel(
+    number, t0, t1, g0, g1, router, u0, u1, d0, d1,
+    act_ref, hid_ref, gout_ref, res_own, res_sib, grad_own, grad_sib, slope,
+):
+    size = t0.shape[0]
+    for i, (t, g, res, grad) in enumerate(
+        ((t1, g1, res_sib, grad_sib), (t0, g0, res_own, grad_own))
+    ):
+        rows = slice((1 - i) * size, (2 - i) * size)
+        gate = route_of(t[...], router[...], number[0])[2]
+        gout = (gate * g[...].astype(F32)).astype(BF)
+        gout_ref[rows] = gout
+        for y, (u, d) in enumerate(((u0, d0), (u1, d1))):
+            for c in range(0, u.shape[1], 256):
+                span = slice(c, c + 256)
+                act, lean = gelu_pair(dot(t[...], u[:, span], 1, 0))
+                act_ref[y, rows, span] = act
+                hid_ref[y, rows, span] = (dot(gout, d[:, span], 1, 0) * lean.astype(F32)).astype(BF)
+        res[...] = (
+            dot(act_ref[0, rows], d0[...], 1, 1) + dot(act_ref[1, rows], d1[...], 1, 1)
+        ).astype(res.dtype)
+        grad[...] = (
+            dot(hid_ref[0, rows], u0[...], 1, 1) + dot(hid_ref[1, rows], u1[...], 1, 1)
+        ).astype(grad.dtype)
+
+
+def expert_grad_kernel(t0, t1, act_ref, hid_ref, gout_ref, pack_own, pack_far, pair):
+    fill_pair(pair, t0, t1)
+    wide = act_ref.shape[2]
+    for y, pack in enumerate((pack_own, pack_far)):
+        pack[:, :wide] = dot(pair[...], hid_ref[y], 0, 0).astype(BF)
+        pack[:, wide:] = dot(gout_ref[...], act_ref[y], 0, 0).astype(BF)
+
+
+def answer_kernel(
+    number, t_ref, g_ref, router, res_own, res_far, grad_own, grad_far, perm_ref, *rest
+):
+    grads, results, router_out = rest[:8], rest[8:16], rest[16]
+    route, mine, gate = route_of(t_ref[...], router[...], number[0])
+    result = res_own[...] + res_far[...].astype(F32)
+    grad_gate = jnp.sum(result * g_ref[...].astype(F32), axis=-1, keepdims=True)
+    grad_logit = (grad_gate * route * (mine - gate)).astype(BF)
+    router_out[...] = dot(grad_logit, t_ref[...], 0, 0)
+    grad = grad_own[...] + grad_far[...].astype(F32) + dot(grad_logit, router[...], 1, 0)
+    size = grads[0].shape[0]
+    whole = dot(grad.astype(BF), perm_ref[...], 1, 0).astype(BF)
+    for p, out in enumerate(grads):
+        out[...] = whole[p * size : (p + 1) * size]
+    whole = dot((gate * result).astype(BF), perm_ref[...], 1, 0).astype(BF)
+    for p, out in enumerate(results):
+        out[...] = whole[p * size : (p + 1) * size]
+
+
+def reorder(values, perm):
+    high = values.astype(BF)
+    rest = values - high.astype(F32)
+    middle = rest.astype(BF)
+    low = (rest - middle.astype(F32)).astype(BF)
+    return dot(high, perm, 1, 0) + (dot(middle, perm, 1, 0) + dot(low, perm, 1, 0))
+
+
+def leave_kernel(x_ref, perm_ref, out_ref):
+    out_ref[...] = reorder(x_ref[...], perm_ref[...])[: out_ref.shape[0]]
+
+
+def finish_kernel(live, x_ref, own_ref, far_ref, perm_ref, out_ref):
+    total = x_ref[...] + (own_ref[...] + far_ref[...].astype(F32))
+    total = reorder(total, perm_ref[...]) * live[0].astype(F32)
+    out_ref[...] = total[: out_ref.shape[0]]
+
+
+def choose_kernel(places, up_ref, down_ref, *outs):
+    wide = up_ref.shape[2]
+    rows = up_ref.shape[1]
+    for k, out in enumerate(outs):
+        for x in range(2):
+            place = places[2 * k + x]
+            out[x * rows : (x + 1) * rows, :wide] = up_ref[place]
+            out[x * rows : (x + 1) * rows, wide:] = down_ref[place]
+
+
+def split_kernel(q0, q1, q2, q3, near, send):
+    rows = q0.shape[0] // 2
+    for k, q in enumerate((q0, q1, q2, q3)):
+        near[k * rows : (k + 1) * rows] = q[:rows]
+        send[k * rows : (k + 1) * rows] = q[rows:]
+
+
+def regroup_kernel(near, side, *outs):
+    rows = outs[0].shape[0] // 2
+    for k, out in enumerate(outs):
+        out[:rows] = near[k * rows : (k + 1) * rows]
+        out[rows:] = side[k * rows : (k + 1) * rows]
+
+
+def add_split_kernel(own_ref, far_ref, near, send):
+    half = near.shape[0]
+    total = own_ref[...].astype(F32) + far_ref[...].astype(F32)
+    near[...] = total[:half].astype(BF)
+    send[...] = total[half:].astype(BF)
+
+
+def place_kernel(places, q0, q1, q2, q3, up_out, down_out):
+    wide = up_out.shape[2]
+    rows = up_out.shape[1]
+    for k, q in enumerate((q0, q1, q2, q3)):
+        for x in range(2):
+            place = places[2 * k + x]
+            block = q[x * rows : (x + 1) * rows].astype(F32)
+            up_out[place] = block[:, :wide]
+            down_out[place] = block[:, wide:]
+
+
+def assemble_kernel(left_own, left_far, right_both, right_side, own_ref, far_ref):
+    left = left_own.shape[1]
+    right = right_both.shape[1] // 2
+    half = right_both.shape[0]
+    own_ref[:, :left] = left_own[...]
+    far_ref[:, :left] = left_far[...]
+    own_ref[:half, left:] = right_both[:, :right]
+    own_ref[half:, left:] = right_side[:, :right]
+    far_ref[:half, left:] = right_both[:, right:]
+    far_ref[half:, left:] = right_side[:, right:]
+
+
+def gather_z(shard):
+    return jnp.concatenate([shard] + [swap(shard, z=k) for k in (1, 2, 3)], axis=0)
+
+
+def gather_first(quarter):
+    half = quarter.shape[1] // 256 * 128
+    left, right = quarter[:, :half], quarter[:, half:]
+    left_own = jnp.concatenate([left, swap(left, x=1)], axis=0)
+    return left_own, jnp.concatenate([right, swap(right, y=1)], axis=1)
+
+
+def gather_second(parts):
+    left_own, right_both = parts
+    rows = left_own.shape[0]
+    width = left_own.shape[1] + right_both.shape[1] // 2
+    left_far = swap(left_own, y=1)
+    right_side = swap(right_both, x=1)
+    return run(
+        assemble_kernel,
+        [((rows, width), BF)] * 2,
+        (left_own, left_far, right_both, right_side),
+        rows * width,
+    )
+
+
+def cut_pack(own_ref, far_ref, left_own, left_far, right_near, right_send):
+    left = left_own.shape[1]
+    right = right_near.shape[1] // 2
+    half = right_near.shape[0]
+    left_own[...] = own_ref[:, :left]
+    left_far[...] = far_ref[:, :left]
+    right_near[:, :right] = own_ref[:half, left:]
+    right_near[:, right:] = far_ref[:half, left:]
+    right_send[:, :right] = own_ref[half:, left:]
+    right_send[:, right:] = far_ref[half:, left:]
+
+
+def sum_one(left_own, left_got, right_near, right_got, left_keep, left_send, right_keep, right_send):
+    half, right = right_keep.shape
+    total = left_own[...].astype(F32) + left_got[...].astype(F32)
+    left_keep[...] = total[:half].astype(BF)
+    left_send[...] = total[half:].astype(BF)
+    total = right_near[...].astype(F32) + right_got[...].astype(F32)
+    right_keep[...] = total[:, :right].astype(BF)
+    right_send[...] = total[:, right:].astype(BF)
+
+
+def sum_two(left_keep, left_got, right_keep, right_got, keep, s1, s2, s3):
+    rows = keep.shape[0]
+    left = left_keep.shape[1]
+    for k, out in enumerate((keep, s1, s2, s3)):
+        span = slice(k * rows, (k + 1) * rows)
+        total = left_keep[span].astype(F32) + left_got[span].astype(F32)
+        out[:, :left] = total.astype(out.dtype)
+        total = right_keep[span].astype(F32) + right_got[span].astype(F32)
+        out[:, left:] = total.astype(out.dtype)
+
+
+def sum_three(keep, r1, r2, r3, first, second):
+    total = keep[...] + (r1[...].astype(F32) + (r2[...].astype(F32) + r3[...].astype(F32)))
+    wide = first.shape[1]
+    first[...] = total[:, :wide]
+    second[...] = total[:, wide:]
+
+
+def scatter_start(own, far):
+    rows, width = own.shape
+    left = width // 256 * 128
+    right = width - left
+    half = rows // 2
+    left_own, left_far, right_near, right_send = run(
+        cut_pack,
+        [((rows, left), BF)] * 2 + [((half, 2 * right), BF)] * 2,
+        (own, far),
+        rows * width,
+    )
+    return left_own, swap(left_far, y=1), right_near, swap(right_send, x=1)
+
+
+def scatter_middle(parts):
+    rows, left = parts[0].shape
+    half, right = parts[2].shape
+    outs = [((half, left), BF)] * 2 + [((half, right // 2), BF)] * 2
+    left_keep, left_send, right_keep, right_send = run(sum_one, outs, parts, rows * left)
+    return left_keep, swap(left_send, x=1), right_keep, swap(right_send, y=1)
+
+
+def scatter_late(parts):
+    half, left = parts[0].shape
+    width = left + parts[2].shape[1]
+    rows = half // 4
+    keep, s1, s2, s3 = run(
+        sum_two,
+        [((rows, width), F32)] + [((rows, width), BF)] * 3,
+        parts,
+        half * width,
+    )
+    return keep, swap(s1, z=1), swap(s2, z=2), swap(s3, z=3)
+
+
+def scatter_end(parts, wide):
+    rows, width = parts[0].shape
+    return run(sum_three, [((rows, wide), F32), ((rows, width - wide), F32)], parts, rows * width)
+
+
+def exchange_rows(pieces):
+    return [pieces[0]] + [swap(pieces[p], z=p & 3, x=p >> 2) for p in range(1, 8)]
+
+
+def reduce_peak(peaks):
+    half = peaks.shape[1] // 2
+    best = jnp.maximum(peaks[:, :half], swap(peaks[:, half:], y=1))
+    best = jnp.maximum(best, swap(best, x=1))
+    far = [swap(best, z=k) for k in (1, 2, 3)]
+    return jnp.maximum(jnp.maximum(best, far[0]), jnp.maximum(far[1], far[2]))
+
+
+def fast_local(
+    block_input,
+    first_norm,
+    first_qkv,
+    first_out,
+    second_norm,
+    dense_up,
+    dense_down,
+    third_norm,
+    second_qkv,
+    second_out,
+    fourth_norm,
+    router_weight,
+    expert_up,
+    expert_down,
+    expert_ids,
+    expert_slots,
+    image_counts,
+    cotangent,
+):
+    d = lax.axis_index("dp")
+    t = lax.axis_index("tensor")
+    z_index, x_index = d // 2, d % 2
+    width = first_norm.shape[0]
+    features = width * 8
+    experts = expert_up.shape[0]
+    live_count = image_counts[0]
+    head_cols = first_out.shape[0]
+    ff_cols = dense_up.shape[1]
+    qkv_cols = 3 * head_cols
+    row = ((ROWS, features), F32)
+    row_low = ((ROWS, features), BF)
+
+    small = jnp.concatenate(
+        [
+            jnp.stack([first_norm, second_norm, third_norm, fourth_norm], axis=1),
+            router_weight,
+            jnp.zeros((width, 128 - 4 - experts), BF),
+        ],
+        axis=1,
+    )
+    pack_one = jnp.concatenate([first_qkv.reshape(width, -1), small], axis=1)
+    pack_two = jnp.concatenate([dense_up, first_out.T], axis=1)
+    pack_late = jnp.concatenate(
+        [dense_down.T, second_out.T, second_qkv.reshape(width, -1)], axis=1
+    )
+    cut_late = ff_cols + head_cols
+
+    z_one = gather_z(pack_one)
+    first_of_one = gather_first(z_one)
+    z_two = gather_z(hold(pack_two, z_one))
+    full_one = gather_second(first_of_one)
+    z_late = gather_z(hold(pack_late, z_two))
+    full_two = gather_second(gather_first(hold(z_two, full_one[1])))
+    full_three = gather_second(gather_first(hold(z_late[:, :cut_late], full_two[1])))
+    full_four = gather_second(gather_first(hold(z_late[:, cut_late:], full_three[1])))
+
+    small_rows = z_one[:, qkv_cols : qkv_cols + 4 + experts]
+    small_rows = jnp.concatenate([small_rows, swap(small_rows, x=1)], axis=0).T
+    gains = [small_rows[i : i + 1].astype(F32) for i in range(4)]
+    router = small_rows[4:]
+
+    rel = jnp.arange(features)
+    block = rel // width
+    rel_place = jnp.bitwise_xor(d, 2 * (block % 4) + block // 4) * width + rel % width
+    perm = (rel_place[:, None] == rel[None, :]).astype(BF)
+    live_here = (t < live_count).astype(jnp.int32).reshape(1)
+    live_pair = (jnp.stack([t, t ^ 1]) < live_count).astype(jnp.int32)
+
+    start, grad_four, grad_low = run(
+        enter_kernel,
+        [row, row, row_low],
+        (live_here, block_input, cotangent, perm),
+        4 * ROWS * features**2,
+        scalars=1,
+    )
+
+    places = jnp.stack([2 * (z_index ^ k) + (x_index ^ x) for k in range(4) for x in range(2)])
+    places = places.astype(jnp.int32)
+    wide = 2 * ff_cols
+    quads = run(
+        choose_kernel,
+        [((2 * width, wide), BF)] * 4,
+        (places, expert_up, jnp.swapaxes(expert_down, 1, 2)),
+        features * wide,
+        scalars=1,
+    )
+    quads = [hold(q, z_late) for q in quads]
+    quads = [quads[0]] + [swap(quads[k], z=k) for k in (1, 2, 3)]
+    e_near, e_send = run(split_kernel, [((features // 2, wide), BF)] * 2, tuple(quads), features * wide)
+    e_side = swap(hold(e_send, full_three[1]), x=1)
+    e_far_near = swap(hold(e_near, full_four[1]), y=1)
+    e_far_side = swap(e_side, y=1)
+
+    block_size = -(-CAP // (4 * 8)) * 8
+    ids = jnp.pad(expert_ids.reshape(4, L, 2), ((0, 0), (0, ROWS - L), (0, 0)), constant_values=-1)
+    slots = jnp.pad(
+        expert_slots.reshape(4, L, 2), ((0, 0), (0, ROWS - L), (0, 0)), constant_values=CAP
+    )
+    mine = (slots < CAP) & (slots // block_size == t)
+    codes = jnp.where(mine, ids * block_size + slots % block_size, -1)
+    codes = jnp.concatenate(
+        [lax.dynamic_index_in_dim(codes, t ^ k, 0, keepdims=False) for k in (0, 2, 1, 3)], axis=0
+    ).T
+    position = jnp.arange(experts)
+    expert_at = jnp.bitwise_xor(d, 2 * (position % 4) + position // 4)
+    row_code = (expert_at[:, None] * block_size + jnp.arange(block_size)[None, :]).reshape(-1, 1)
+    slot_rows = experts * block_size
+    piece = ((block_size, features), BF)
+    group_flops = 2 * slot_rows * features * (4 * ROWS + features)
+
+    def to_experts(rows):
+        pair = jnp.concatenate([rows, swap(rows, y=1)], axis=0)
+        pieces = run(
+            dispatch_kernel,
+            [piece] * experts,
+            (row_code, codes, pair, swap(pair, core=1), perm),
+            group_flops,
+            scratch=[pltpu.VMEM((4 * ROWS, features), BF)],
+        )
+        return pieces
+
+    def collect(pieces):
+        return run(
+            collect_kernel,
+            [((slot_rows, features), BF)],
+            (perm, *pieces),
+            2 * slot_rows * features**2,
+            scratch=[pltpu.VMEM((slot_rows, features), BF)],
+        )[0]
+
+    def from_experts(pieces):
+        own, send = run(
+            combine_kernel,
+            [((2 * ROWS, features), F32), ((2 * ROWS, features), BF)],
+            (row_code, codes, perm, *pieces),
+            group_flops,
+            scratch=[pltpu.VMEM((slot_rows, features), BF)],
+        )
+        near, send = run(pair_add_kernel, [row, row_low], (own, swap(send, core=1)), ROWS)
+        return near, swap(send, y=1)
+
+    def attend(normed, far_normed, full_qkv, full_out, out_at):
+        qkv = [w[:, :qkv_cols] for w in full_qkv]
+        out = [w[:, out_at:] for w in full_out]
+        return qkv, out, run(
+            attend_kernel,
+            [
+                ((2, 2 * ROWS, qkv_cols), BF),
+                ((2 * ROWS, 2 * head_cols), BF),
+                row,
+                row_low,
+                ((8, 128), F32),
+            ],
+            (live_pair, normed, far_normed, *qkv, *out),
+            2 * 2 * ROWS * features * 8 * head_cols,
+            scratch=[pltpu.VMEM((2 * ROWS, features), BF)],
+            scalars=1,
+        )
+
+    def attend_back(low, normed, far_normed, mixed, attended, qkv, out):
+        return run(
+            attend_back_kernel,
+            [((features, 4 * head_cols), BF)] * 2 + [row, row_low],
+            (low, swap(low, core=1), normed, far_normed, mixed, attended, *qkv, *out),
+            4 * 2 * ROWS * features * 8 * head_cols,
+            scratch=[
+                pltpu.VMEM((2 * ROWS, features), BF),
+                pltpu.VMEM((2 * ROWS, 2 * head_cols), BF),
+                pltpu.VMEM((2, 2 * ROWS, qkv_cols), BF),
+            ],
+        )
+
+    def join(values, own, far, gain):
+        total, normed = run(join_norm_kernel, [row, row_low], (values, own, far, gain), ROWS)
+        return total, normed, swap(normed, core=1)
+
+    def norm_back(values, upstream, own, far, gain):
+        return run(
+            norm_back_kernel,
+            [row, row_low, ((1, features), F32)],
+            (values, upstream, own, far, gain),
+            ROWS,
+        )
+
+    normed_one = run(norm_kernel, [row_low], (start, gains[0]), ROWS)[0]
+    far_one = swap(normed_one, core=1)
+    qkv_one, out_one, (mixed_one, att_one, own, sib, peak_one) = attend(
+        normed_one, far_one, full_one, full_two, ff_cols
+    )
+    one, normed_mlp, far_mlp = join(start, own, swap(sib, core=1), gains[1])
+
+    up = [w[:, :ff_cols] for w in full_two]
+    down = [w[:, :ff_cols] for w in full_three]
+    pair_scratch = pltpu.VMEM((2 * ROWS, features), BF)
+    act, slope, own, sib = run(
+        mlp_kernel,
+        [((2, 2 * ROWS, ff_cols), BF)] * 2 + [row, row_low],
+        (normed_mlp, far_mlp, *up, *down),
+        2 * 2 * ROWS * features * 4 * ff_cols,
+        scratch=[pair_scratch],
+    )
+    two, normed_two, far_two = join(one, own, swap(sib, core=1), gains[2])
+    qkv_two, out_two, (mixed_two, att_two, own, sib, peak_two) = attend(
+        normed_two, far_two, full_four, full_three, ff_cols
+    )
+    three, normed_four, _ = join(two, own, swap(sib, core=1), gains[3])
+
+    grad_slots = collect(exchange_rows(to_experts(hold(grad_low, e_near))))
+    far_slots = swap(grad_slots, core=1)
+    tokens = collect(exchange_rows(to_experts(normed_four)))
+    far_tokens = swap(tokens, core=1)
+    number = d.astype(jnp.int32).reshape(1)
+    e_own = jnp.concatenate([e_near, e_side], axis=0)
+    e_far = jnp.concatenate([e_far_near, e_far_side], axis=0)
+    e_up = [e_own[:, :ff_cols], e_far[:, :ff_cols]]
+    e_down = [e_own[:, ff_cols:], e_far[:, ff_cols:]]
+    slot_out = [((slot_rows, features), F32), ((slot_rows, features), BF)]
+    e_act, e_hidden, e_gout, res_own, res_sib, eg_own, eg_sib = run(
+        expert_kernel,
+        [((2, 2 * slot_rows, ff_cols), BF)] * 2
+        + [((2 * slot_rows, features), BF)]
+        + slot_out
+        + slot_out,
+        (number, tokens, far_tokens, grad_slots, far_slots, router, *e_up, *e_down),
+        8 * 2 * slot_rows * features * 2 * ff_cols,
+        scalars=1,
+        scratch=[pltpu.VMEM((8, 128), F32)],
+        mib=48,
+    )
+    answers = run(
+        answer_kernel,
+        [piece] * 16 + [((experts, features), F32)],
+        (
+            number,
+            tokens,
+            grad_slots,
+            router,
+            res_own,
+            swap(res_sib, core=1),
+            eg_own,
+            swap(eg_sib, core=1),
+            perm,
+        ),
+        4 * slot_rows * features**2,
+        scalars=1,
+    )
+    grad_router = answers[16]
+    back_own, back_far = from_experts(exchange_rows(answers[:8]))
+    e_pack_own, e_pack_far = run(
+        expert_grad_kernel,
+        [((features, wide), BF)] * 2,
+        (tokens, far_tokens, e_act, e_hidden, e_gout),
+        8 * slot_rows * features * wide,
+        scratch=[pltpu.VMEM((2 * slot_rows, features), BF)],
+        mib=40,
+    )
+    e_got = swap(e_pack_far, y=1)
+    grad_three, low, gain_four = norm_back(three, grad_four, back_own, back_far, gains[3])
+    result_pieces = [hold(p, low) for p in answers[8:16]]
+
+    pack_own, pack_far, own, sib = attend_back(
+        low, normed_two, far_two, mixed_two, att_two, qkv_two, out_two
+    )
+    grad_two, low, gain_three = norm_back(two, grad_three, own, swap(sib, core=1), gains[2])
+    second = scatter_start(pack_own, pack_far)
+
+    mixed_own, mixed_far = from_experts(exchange_rows(result_pieces))
+    block_output = run(
+        finish_kernel,
+        [((L, features), F32)],
+        (live_here, three, mixed_own, mixed_far, perm),
+        6 * ROWS * features**2,
+        scalars=1,
+    )[0]
+
+    e_near_g, e_send_g = run(
+        add_split_kernel,
+        [((features // 2, wide), BF)] * 2,
+        (e_pack_own, hold(e_got, low)),
+        features * wide,
+    )
+    e_side_g = swap(e_send_g, x=1)
+
+    pack_own, pack_far, own, sib = run(
+        mlp_back_kernel,
+        [((features, wide), BF)] * 2 + [row, row_low],
+        (low, swap(low, core=1), normed_mlp, far_mlp, act, slope, *up, *down),
+        4 * 2 * ROWS * features * 4 * ff_cols,
+        scratch=[pair_scratch, pltpu.VMEM((2, 2 * ROWS, ff_cols), BF)],
+    )
+    second = scatter_middle(hold(second, sib))
+    grad_one, low, gain_two = norm_back(one, grad_two, own, swap(sib, core=1), gains[1])
+    mlp = scatter_start(pack_own, pack_far)
+
+    quads = run(
+        regroup_kernel,
+        [((2 * width, wide), BF)] * 4,
+        (e_near_g, hold(e_side_g, low)),
+        features * wide,
+    )
+    quads = [quads[0]] + [swap(quads[k], z=k) for k in (1, 2, 3)]
+
+    pack_own, pack_far, own, sib = attend_back(
+        low, normed_one, far_one, mixed_one, att_one, qkv_one, out_one
+    )
+    first = scatter_start(pack_own, pack_far)
+    grad_zero, _, gain_one = norm_back(start, grad_one, own, swap(sib, core=1), gains[0])
+    input_grad = run(
+        leave_kernel, [((L, features), F32)], (grad_zero, perm), 6 * ROWS * features**2
+    )[0]
+    mlp = scatter_middle(hold(mlp, sib))
+    second = scatter_late(hold(second, sib))
+    up_g, down_g = run(
+        place_kernel,
+        [((experts, width, ff_cols), F32)] * 2,
+        (places, *hold(quads, sib)),
+        features * wide,
+        scalars=1,
+    )
+    first = scatter_middle(first)
+    mlp = scatter_late(mlp)
+    first = scatter_late(first)
+    second = scatter_end(second, qkv_cols)
+    mlp = scatter_end(mlp, ff_cols)
+    first = scatter_end(first, qkv_cols)
+
+    tail = jnp.concatenate([gain_one, gain_two, gain_three, gain_four, grad_router])
+    tail = jnp.swapaxes(tail.reshape(4 + experts, 8, width), 0, 1)
+    tail = tail + swap(tail, core=1)
+    tail = tail + swap(tail, y=1)
+    tail = tail[:4] + swap(tail[4:], x=1)
+    tail = tail[0] + swap(tail[1], z=1) + swap(tail[2], z=2) + swap(tail[3], z=3)
+
+    peaks = jnp.stack([peak_one[: 2 * head_cols // HD, 0], peak_two[: 2 * head_cols // HD, 0]])
+    roots = clip_root(reduce_peak(peaks))
+    return (
+        block_output,
+        input_grad,
+        tail[0],
+        first[0].reshape(first_qkv.shape),
+        first[1].T,
+        tail[1],
+        mlp[0],
+        mlp[1].T,
+        tail[2],
+        second[0].reshape(second_qkv.shape),
+        second[1].T,
+        tail[3],
+        tail[4:].T,
+        up_g,
+        jnp.swapaxes(down_g, 1, 2),
+        clip_columns(first_qkv, roots[0], HD),
+        clip_columns(second_qkv, roots[1], HD),
+        roots,
+    )
+
+
 def solution(mesh):
     placed = (
         P(("dp", "tensor"), None),
@@ -412,8 +1263,9 @@
         P("dp"),
         P(("dp", "tensor"), None),
     )
+    quick = mesh.shape["dp"] == 8 and mesh.shape["tensor"] == 4
     return jax.shard_map(
-        local,
+        fast_local if quick else local,
         mesh=mesh,
         in_specs=placed,
         out_specs=(

time: 2100 us -> 639 us (0.30)
  waiting for transfers between devices: 1280 us -> 242 us
  blocking collectives: 377 us -> 0 us
  starting transfers between devices: 13.7 us -> 187 us
  matrix products: 142 us -> 0 us
  local copies, waits for them, and re-layouts: 191 us -> 75.7 us
  Pallas kernels: 0 us -> 111 us
  other arithmetic: 62.2 us -> 8.97 us
    reduce_scatter x6 -> x0, waiting for transfers between devices: 919 us -> none  [the longest x1 317 us: local(): lax.psum_scatter(grad_expert_up, 'dp', scatter_dimension=1, tiled=True)]
    all_gather x12 -> x0, waiting for transfers between devices: 340 us -> none  [the longest x1 117 us: moe_fetch(): lax.all_gather(expert_down, 'dp', axis=2, tiled=True)]
    ppermute x0 -> x121, waiting for transfers between devices: none -> 242 us  [swap(): return lax.ppermute(values, AXES, pairs)]
    ppermute x0 -> x121, starting transfers between devices: none -> 187 us  [swap(): return lax.ppermute(values, AXES, pairs)]
    unnamed x9 -> x0, blocking collectives: 180 us -> none
    all_gather x5 -> x0, blocking collectives: 163 us -> none  [the longest x1 37.2 us: moe_fetch(): lax.all_gather(second_qkv, 'dp', axis=0, tiled=True)]
    dot_general x34 -> x0, matrix products: 129 us -> none  [the longest x1 12.4 us: local(): jnp.einsum('ecf,ecd->efd', expert_act, grad_result, preferred_element_typ...]
    pallas_call x0 -> x49, Pallas kernels: none -> 111 us  [run(): pl.pallas_call(kernel, out_shape=shapes, in_specs=[SM] * scalars + [VM] *...]
  transfers between devices with their start and end apart: 29 -> 121, of which waited for: 20 -> 44; matrix products, arithmetic and copies ran while one was open for 12% -> 6% of each run, Pallas kernels for 0% -> 12%
where the time goes in v2:
time: 639 us; the launch traced here: 628 us
  waiting for transfers between devices  242 us (38%)
  starting transfers between devices  187 us (29%)
  Pallas kernels  111 us (17%)
  local copies, waits for them, and re-layouts  75.7 us (12%)
  other arithmetic  8.97 us (1%)
    ppermute x121, waiting for transfers between devices, swap(): return lax.ppermute(values, AXES, pairs)  242 us
    ppermute x121, starting transfers between devices, swap(): return lax.ppermute(values, AXES, pairs)  187 us
    pallas_call x49, Pallas kernels, run(): pl.pallas_call(kernel, out_shape=shapes, in_specs=[SM] * scalars + [VM] *...  111 us
    unnamed x358, local copies, waits for them, and re-layouts  49.2 us
  transfers between devices with their start and end apart: 121, of which 44 were waited for; matrix products, arithmetic and copies ran while one was open for 6% of the time, Pallas kernels for 12%

profile of v2, /device:TPU:0, one launch (start us, length us, event | category | flops | bytes accessed | tf_op | source)
XLA Modules:
  0.0 628.4 jit_solution(7243533755066628140)
XLA Ops:
  3.6 5.1 collective-permute-start.2
  9.4 4.9 collective-permute-done.2
  14.2 9.8 %collective-permute-done.1 = bf16[96,704]{0,1:T(8,128)(2,1)S(1)} collective-permute-done((bf16[96,704]{0,1:T(8,128)(2,1)S(1)}, bf16[96,704]{0,1:T(8,128)(2,1)S(1)}, u32[]{:S(2)}, u32[]{:S(2)}) %collective-permute-start.1) | collective-permute-done | bytes 135200 | tf_op jit(solution)/shard_map/ppermute | solution.py:407
  27.7 5.9 collective-permute-done.7
  35.4 2.8 collective-permute-start.10
  41.4 3.0 collective-permute-done.9
  44.5 6.9 %collective-permute-done.10 = bf16[96,960]{1,0:T(8,128)(2,1)S(1)} collective-permute-done((bf16[96,960]{1,0:T(8,128)(2,1)S(1)}, bf16[96,960]{1,0:T(8,128)(2,1)S(1)}, u32[]{:S(2)}, u32[]{:S(2)}) %collective-permute-start.10) | collective-permute-done | bytes 184352 | tf_op jit(solution)/shard_map/ppermute | solution.py:407
  58.4 3.0 collective-permute-start.18
  62.0 3.2 collective-permute-done.14
  67.1 6.2 collective-permute-start.19
  76.7 15.1 %collective-permute-done.19 = bf16[96,1536]{1,0:T(8,128)(2,1)S(1)} collective-permute-done((bf16[96,1536]{1,0:T(8,128)(2,1)S(1)}, bf16[96,1536]{1,0:T(8,128)(2,1)S(1)}, u32[]{:S(2)}, u32[]{:S(2)}) %collective-permute-start.19) | collective-permute-done | bytes 294944 | tf_op jit(solution)/shard_map/ppermute | solution.py:407
  110.3 4.1 collective-permute-done.21
  119.6 4.5 shard_map.317
  139.5 3.5 shard_map.320
  151.8 5.3 collective-permute-start.41
  165.7 4.6 shard_map.323
  172.5 10.0 %collective-permute-done.41.q1 = bf16[192,1536]{1,0:T(8,128)(2,1)S(1)} collective-permute-done((bf16[192,1536]{1,0:T(8,128)(2,1)S(1)}, bf16[192,1536]{1,0:T(8,128)(2,1)S(1)}, u32[]{:S(2)}, u32[]{:S(2)}) %collective-permute-start.41) | collective-permute-done | bytes 589856 | tf_op jit(solution)/shard_map/ppermute | solution.py:407
  182.5 17.0 %collective-permute-done.42.q2 = bf16[192,1536]{1,0:T(8,128)(2,1)S(1)} collective-permute-done((bf16[192,1536]{1,0:T(8,128)(2,1)S(1)}, bf16[192,1536]{1,0:T(8,128)(2,1)S(1)}, u32[]{:S(2)}, u32[]{:S(2)}) %collective-permute-start.42) | collective-permute-done | bytes 589856 | tf_op jit(solution)/shard_map/ppermute | solution.py:407
  205.8 6.2 collective-permute-done.44
  218.4 2.8 shard_map.329
  221.2 13.9 %collective-permute-start.46 = (bf16[56,768]{1,0:T(8,128)(2,1)S(1)}, bf16[56,768]{1,0:T(8,128)(2,1)S(1)}, u32[]{:S(2)}, u32[]{:S(2)}) collective-permute-start(bf16[56,768]{1,0:T(8,128)(2,1)S(1)} %get-tuple-element.262), channel_id=1, source_target_pairs={{0,8},{1,9},{2,10},{3,11},{4,12},{5,13},{6,14},{7,15},{8,0},{9,1},... | collective-permute-start | bytes 258056 | tf_op jit(solution)/shard_map/ppermute | solution.py:407
  239.8 4.9 collective-permute-done.47.rest_2_
  245.3 3.1 shard_map.325
  248.4 2.9 collective-permute-start.51
  251.3 3.3 collective-permute-start.52
  255.2 3.3 collective-permute-done.52.rest_7_
  268.2 4.7 collective-permute-start.39
  276.7 3.4 collective-permute-done.40.rest_7_
  283.1 15.0 %shard_map.331 = (bf16[2,896,768]{2,1,0:T(8,128)(2,1)}, bf16[2,896,768]{2,1,0:T(8,128)(2,1)}, bf16[896,768]{1,0:T(8,128)(2,1)}, f32[448,768]{1,0:T(8,128)}, bf16...) custom-call(s32[1]{0:T(128)} %bitcast.19.number, ...), custom_call_target="tpu_custom_call" | custom-call | flops 8455716864 | bytes 18493444 | tf_op jit(solution)/shard_map/pallas_call | solution.py:418
  306.6 3.3 collective-permute-start.60
  316.0 3.8 collective-permute-done.61.rest_2_
  321.3 4.7 collective-permute-done.65.rest_6_
  332.5 8.1 %collective-permute-done.68.far_ref = bf16[208,768]{1,0:T(8,128)(2,1)S(1)} collective-permute-done((bf16[208,768]{1,0:T(8,128)(2,1)S(1)}, bf16[208,768]{1,0:T(8,128)(2,1)S(1)}, u32[]{:S(2)}, u32[]{:S(2)}) %collective-permute-start.68) | collective-permute-done | bytes 319520 | tf_op jit(solution)/shard_map/ppermute | solution.py:407
  342.9 10.3 %shard_map.339 = (bf16[768,768]{1,0:T(8,128)(2,1)S(1)}, bf16[768,768]{1,0:T(8,128)(2,1)S(1)}, f32[208,768]{1,0:T(8,128)S(1)}, bf16[208,768]{1,0:T(8,128)(2,1)S(1)}) custom-call(bf16[208,768]{1,0:T(8,128)(2,1)S(1)} %get-tuple-element.290.g0, bf16[208,768]{1,0:T(8,128)(2,1)S(1)} %collective-permute-done.78.g1, bf16[208,768]{1,0:T(8,128)(2,1)S(1)} %copy-done.106, ...), custom_call_target="tpu_custom_call" | custom-call | flops 1962934272 | bytes 8232960 | tf_op jit(solution)/shard_map/pallas_call | solution.py:418
  355.6 6.5 %shard_map.358 = (bf16[768,1536]{1,0:T(8,128)(2,1)S(1)}, bf16[768,1536]{1,0:T(8,128)(2,1)}) custom-call(bf16[448,768]{1,0:T(8,128)(2,1)S(1)} %shard_map.326.t0.t_ref, bf16[448,768]{1,0:T(8,128)(2,1)S(1)} %copy-done.96, bf16[2,896,768]{2,1,0:T(8,128)(2,1)S(1)} %copy-done.141, bf16[2,896,768]{2,1,0:T(8,128)(2,1)S(1)} %copy-done.142, ...), custom_call_target="tpu_custom_call" | custom-call | flops 4227858432 | bytes 12976128 | tf_op jit(solution)/shard_map/pallas_call | solution.py:418
  369.0 4.6 shard_map.341
  390.5 6.4 %collective-permute-done.74.rest_6_ = bf16[56,768]{1,0:T(8,128)(2,1)S(1)} collective-permute-done((bf16[56,768]{1,0:T(8,128)(2,1)S(1)}, bf16[56,768]{1,0:T(8,128)(2,1)S(1)}, u32[]{:S(2)}, u32[]{:S(2)}) %collective-permute-start.74) | collective-permute-done | bytes 86048 | tf_op jit(solution)/shard_map/ppermute | solution.py:407
  398.5 5.7 collective-permute-done.75.rest_7_
  406.6 10.0 %shard_map.343 = (bf16[768,768]{1,0:T(8,128)(2,1)S(1)}, bf16[768,768]{1,0:T(8,128)(2,1)S(1)}, f32[208,768]{1,0:T(8,128)S(1)}, bf16[208,768]{1,0:T(8,128)(2,1)S(1)}) custom-call(bf16[208,768]{1,0:T(8,128)(2,1)S(1)} %get-tuple-element.322.g0, bf16[208,768]{1,0:T(8,128)(2,1)S(1)} %collective-permute-done.82.g1, bf16[208,768]{1,0:T(8,128)(2,1)S(1)} %copy-done.70, ...), custom_call_target="tpu_custom_call" | custom-call | flops 1962934272 | bytes 8232960 | tf_op jit(solution)/shard_map/pallas_call | solution.py:418
  419.2 9.3 %collective-permute-done.104.left_got = bf16[768,384]{1,0:T(8,128)(2,1)S(1)} collective-permute-done((bf16[768,384]{1,0:T(8,128)(2,1)S(1)}, bf16[768,384]{1,0:T(8,128)(2,1)S(1)}, u32[]{:S(2)}, u32[]{:S(2)}) %collective-permute-start.104) | collective-permute-done | bytes 589856 | tf_op jit(solution)/shard_map/ppermute | solution.py:407
  450.5 3.2 shard_map.359
  467.5 41.0 %collective-permute-done.86 = f32[4,12,96]{2,1,0:T(8,128)} collective-permute-done((f32[4,12,96]{2,1,0:T(8,128)S(1)}, f32[4,12,96]{2,1,0:T(8,128)}, u32[]{:S(2)}, u32[]{:S(2)}) %collective-permute-start.86) | collective-permute-done | bytes 18464 | tf_op jit(solution)/shard_map/ppermute | solution.py:407
  513.0 7.1 %collective-permute-done.91.right_got = bf16[384,768]{1,0:T(8,128)(2,1)} collective-permute-done((bf16[384,768]{1,0:T(8,128)(2,1)}, bf16[384,768]{1,0:T(8,128)(2,1)}, u32[]{:S(2)}, u32[]{:S(2)}) %collective-permute-start.91) | collective-permute-done | bytes 589856 | tf_op jit(solution)/shard_map/ppermute | solution.py:407
  536.6 2.9 shard_map.351
  565.4 20.2 %collective-permute-done.114.q2 = bf16[192,1536]{1,0:T(8,128)(2,1)S(1)} collective-permute-done((bf16[192,1536]{1,0:T(8,128)(2,1)}, bf16[192,1536]{1,0:T(8,128)(2,1)S(1)}, u32[]{:S(2)}, u32[]{:S(2)}) %collective-permute-start.114) | collective-permute-done | bytes 589856 | tf_op jit(solution)/shard_map/ppermute | solution.py:407
  588.4 22.7 %collective-permute-start.95 = (bf16[96,768]{1,0:T(8,128)(2,1)S(1)}, bf16[96,768]{1,0:T(8,128)(2,1)S(1)}, u32[]{:S(2)}, u32[]{:S(2)}) collective-permute-start(bf16[96,768]{1,0:T(8,128)(2,1)S(1)} %get-tuple-element.345), channel_id=1, source_target_pairs={{0,16},{1,17},{2,18},{3,19},{4,20},{5,21},{6,22},{7,23},{8,24},{9,... | collective-permute-start | bytes 442376 | tf_op jit(solution)/shard_map/ppermute | solution.py:407
  613.5 3.0 shard_map.361
  616.5 7.9 %collective-permute-done.95.r2 = bf16[96,768]{1,0:T(8,128)(2,1)S(1)} collective-permute-done((bf16[96,768]{1,0:T(8,128)(2,1)S(1)}, bf16[96,768]{1,0:T(8,128)(2,1)S(1)}, u32[]{:S(2)}, u32[]{:S(2)}) %collective-permute-start.95) | collective-permute-done | bytes 147488 | tf_op jit(solution)/shard_map/ppermute | solution.py:407
  (693 shorter events, 265.4 us)
Async XLA Ops:
  8.7 15.3 %collective-permute-start.1 = (bf16[96,704]{0,1:T(8,128)(2,1)S(1)}, bf16[96,704]{0,1:T(8,128)(2,1)S(1)}, u32[]{:S(2)}, u32[]{:S(2)}) collective-permute-start(bf16[96,704]{0,1:T(8,128)(2,1)S(1)} %concatenate.63), channel_id=1, source_target_pairs={{0,16},{1,17},{2,18},{3,19},{4,20},{5,21},{6,22},{7,23},{8,24},{9,... | collective-permute-start | bytes 405512 | tf_op jit(solution)/shard_map/ppermute | solution.py:407
  8.7 15.3 %collective-permute-start = (bf16[96,704]{0,1:T(8,128)(2,1)S(1)}, bf16[96,704]{0,1:T(8,128)(2,1)S(1)}, u32[]{:S(2)}, u32[]{:S(2)}) collective-permute-start(bf16[96,704]{0,1:T(8,128)(2,1)S(1)} %concatenate.63), channel_id=1, source_target_pairs={{0,8},{1,9},{2,10},{3,11},{4,12},{5,13},{6,14},{7,15},{8,0},{9,1},... | collective-permute-start | bytes 405512 | tf_op jit(solution)/shard_map/ppermute | solution.py:407
  33.7 18.5 %collective-permute-start.8 = (bf16[384,896]{0,1:T(8,128)(2,1)S(1)}, bf16[384,896]{0,1:T(8,128)(2,1)}, u32[]{:S(2)}, u32[]{:S(2)}) collective-permute-start(bf16[384,896]{0,1:T(8,128)(2,1)S(1)} %pad_maximum_fusion.2), channel_id=1, source_target_pairs={{0,4},{1,5},{2,6},{3,7},{4,0},{5,1},{6,2},{7,3},{8,12},{9,13},{10,... | collective-permute-start | bytes 2064392 | tf_op jit(solution)/shard_map/ppermute | solution.py:407
  35.4 16.0 %collective-permute-start.10 = (bf16[96,960]{1,0:T(8,128)(2,1)S(1)}, bf16[96,960]{1,0:T(8,128)(2,1)S(1)}, u32[]{:S(2)}, u32[]{:S(2)}) collective-permute-start(bf16[96,960]{1,0:T(8,128)(2,1)S(1)} %pad_maximum_fusion.9), channel_id=1, source_target_pairs={{0,16},{1,17},{2,18},{3,19},{4,20},{5,21},{6,22},{7,23},{8,24},{9,... | collective-permute-start | bytes 552968 | tf_op jit(solution)/shard_map/ppermute | solution.py:407
  38.2 13.7 %collective-permute-start.6 = (bf16[768,256]{0,1:T(8,128)(2,1)S(1)}, bf16[768,256]{0,1:T(8,128)(2,1)S(1)}, u32[]{:S(2)}, u32[]{:S(2)}) collective-permute-start(bf16[768,256]{0,1:T(8,128)(2,1)S(1)} %pad_maximum_fusion.7), channel_id=1, source_target_pairs={{0,2},{1,3},{2,0},{3,1},{4,6},{5,7},{6,4},{7,5},{8,10},{9,11},{10,... | collective-permute-start | bytes 1179656 | tf_op jit(solution)/shard_map/ppermute | solution.py:407
  58.4 18.3 %collective-permute-start.18 = (bf16[96,1536]{1,0:T(8,128)(2,1)S(1)}, bf16[96,1536]{1,0:T(8,128)(2,1)S(1)}, u32[]{:S(2)}, u32[]{:S(2)}) collective-permute-start(bf16[96,1536]{1,0:T(8,128)(2,1)S(1)} %concatenate.72), channel_id=1, source_target_pairs={{0,8},{1,9},{2,10},{3,11},{4,12},{5,13},{6,14},{7,15},{8,0},{9,1},... | collective-permute-start | bytes 884744 | tf_op jit(solution)/shard_map/ppermute | solution.py:407
  66.5 26.4 %collective-permute-start.15 = (bf16[384,1152]{1,0:T(8,128)(2,1)S(1)}, bf16[384,1152]{1,0:T(8,128)(2,1)S(1)}, u32[]{:S(2)}, u32[]{:S(2)}) collective-permute-start(bf16[384,1152]{1,0:T(8,128)(2,1)S(1)} %pad_maximum_fusion.right_both), channel_id=1, source_target_pairs={{0,4},{1,5},{2,6},{3,7},{4,0},{5,1},{6,2},{7,3},{8,12},{9,13},{10,... | collective-permute-start | bytes 2654216 | tf_op jit(solution)/shard_map/ppermute | solution.py:407
  67.1 24.7 %collective-permute-start.19 = (bf16[96,1536]{1,0:T(8,128)(2,1)S(1)}, bf16[96,1536]{1,0:T(8,128)(2,1)S(1)}, u32[]{:S(2)}, u32[]{:S(2)}) collective-permute-start(bf16[96,1536]{1,0:T(8,128)(2,1)S(1)} %concatenate.72), channel_id=1, source_target_pairs={{0,16},{1,17},{2,18},{3,19},{4,20},{5,21},{6,22},{7,23},{8,24},{9,... | collective-permute-start | bytes 884744 | tf_op jit(solution)/shard_map/ppermute | solution.py:407
  73.3 18.5 %collective-permute-start.20 = (bf16[96,1536]{1,0:T(8,128)(2,1)S(1)}, bf16[96,1536]{1,0:T(8,128)(2,1)S(1)}, u32[]{:S(2)}, u32[]{:S(2)}) collective-permute-start(bf16[96,1536]{1,0:T(8,128)(2,1)S(1)} %concatenate.72), channel_id=1, source_target_pairs={{0,24},{1,25},{2,26},{3,27},{4,28},{5,29},{6,30},{7,31},{8,16},{9,... | collective-permute-start | bytes 884744 | tf_op jit(solution)/shard_map/ppermute | solution.py:407
  75.1 16.9 %collective-permute-start.13 = (bf16[768,384]{1,0:T(8,128)(2,1)S(1)}, bf16[768,384]{1,0:T(8,128)(2,1)S(1)}, u32[]{:S(2)}, u32[]{:S(2)}) collective-permute-start(bf16[768,384]{1,0:T(8,128)(2,1)S(1)} %pad_maximum_fusion.3.left_own), channel_id=1, source_target_pairs={{0,2},{1,3},{2,0},{3,1},{4,6},{5,7},{6,4},{7,5},{8,10},{9,11},{10,... | collective-permute-start | bytes 1769480 | tf_op jit(solution)/shard_map/ppermute | solution.py:407
  108.4 20.9 %collective-permute-start.24 = (bf16[384,1152]{1,0:T(8,128)(2,1)S(1)}, bf16[384,1152]{1,0:T(8,128)(2,1)}, u32[]{:S(2)}, u32[]{:S(2)}) collective-permute-start(bf16[384,1152]{1,0:T(8,128)(2,1)S(1)} %pad_maximum_fusion.1.right_both), channel_id=1, source_target_pairs={{0,4},{1,5},{2,6},{3,7},{4,0},{5,1},{6,2},{7,3},{8,12},{9,13},{10,... | collective-permute-start | bytes 2654216 | tf_op jit(solution)/shard_map/ppermute | solution.py:407
  137.9 23.6 %collective-permute-start.28 = (bf16[768,256]{1,0:T(8,128)(2,1)}, bf16[768,256]{1,0:T(8,128)(2,1)S(1)}, u32[]{:S(2)}, u32[]{:S(2)}) collective-permute-start(bf16[768,256]{1,0:T(8,128)(2,1)} %pad_maximum_fusion.8.left_own), channel_id=1, source_target_pairs={{0,2},{1,3},{2,0},{3,1},{4,6},{5,7},{6,4},{7,5},{8,10},{9,11},{10,... | collective-permute-start | bytes 1179656 | tf_op jit(solution)/shard_map/ppermute | solution.py:407
  146.9 16.9 %collective-permute-start.30 = (bf16[384,640]{1,0:T(8,128)(2,1)}, bf16[384,640]{1,0:T(8,128)(2,1)}, u32[]{:S(2)}, u32[]{:S(2)}) collective-permute-start(bf16[384,640]{1,0:T(8,128)(2,1)} %pad_maximum_fusion.6.right_both), channel_id=1, source_target_pairs={{0,4},{1,5},{2,6},{3,7},{4,0},{5,1},{6,2},{7,3},{8,12},{9,13},{10,... | collective-permute-start | bytes 1474568 | tf_op jit(solution)/shard_map/ppermute | solution.py:407
  151.8 30.7 %collective-permute-start.41 = (bf16[192,1536]{1,0:T(8,128)(2,1)S(1)}, bf16[192,1536]{1,0:T(8,128)(2,1)S(1)}, u32[]{:S(2)}, u32[]{:S(2)}) collective-permute-start(bf16[192,1536]{1,0:T(8,128)(2,1)S(1)} %get-tuple-element.254), channel_id=1, source_target_pairs={{0,8},{1,9},{2,10},{3,11},{4,12},{5,13},{6,14},{7,15},{8,0},{9,1},... | collective-permute-start | bytes 1769480 | tf_op jit(solution)/shard_map/ppermute | solution.py:407
  157.1 42.4 %collective-permute-start.42 = (bf16[192,1536]{1,0:T(8,128)(2,1)S(1)}, bf16[192,1536]{1,0:T(8,128)(2,1)S(1)}, u32[]{:S(2)}, u32[]{:S(2)}) collective-permute-start(bf16[192,1536]{1,0:T(8,128)(2,1)S(1)} %get-tuple-element.256), channel_id=1, source_target_pairs={{0,16},{1,17},{2,18},{3,19},{4,20},{5,21},{6,22},{7,23},{8,24},{9,... | collective-permute-start | bytes 1769480 | tf_op jit(solution)/shard_map/ppermute | solution.py:407
  158.1 41.4 %collective-permute-start.43 = (bf16[192,1536]{1,0:T(8,128)(2,1)S(1)}, bf16[192,1536]{1,0:T(8,128)(2,1)S(1)}, u32[]{:S(2)}, u32[]{:S(2)}) collective-permute-start(bf16[192,1536]{1,0:T(8,128)(2,1)S(1)} %get-tuple-element.258), channel_id=1, source_target_pairs={{0,24},{1,25},{2,26},{3,27},{4,28},{5,29},{6,30},{7,31},{8,16},{9,... | collective-permute-start | bytes 1769480 | tf_op jit(solution)/shard_map/ppermute | solution.py:407
  172.1 31.1 %collective-permute-start.31 = (bf16[208,768]{1,0:T(8,128)(2,1)S(1)}, bf16[208,768]{1,0:T(8,128)(2,1)S(1)}, u32[]{:S(2)}, u32[]{:S(2)}) collective-permute-start(bf16[208,768]{1,0:T(8,128)(2,1)S(1)} %get-tuple-element.239), channel_id=1, source_target_pairs={{0,1},{1,0},{2,3},{3,2},{4,5},{5,4},{6,7},{7,6},{8,9},{9,8},{10,11... | collective-permute-start | bytes 958472 | tf_op jit(solution)/shard_map/ppermute | solution.py:407
  204.8 49.7 %collective-permute-start.55 = (bf16[384,1536]{1,0:T(8,128)(2,1)}, bf16[384,1536]{1,0:T(8,128)(2,1)}, u32[]{:S(2)}, u32[]{:S(2)}) collective-permute-start(bf16[384,1536]{1,0:T(8,128)(2,1)} %get-tuple-element.270), channel_id=1, source_target_pairs={{0,4},{1,5},{2,6},{3,7},{4,0},{5,1},{6,2},{7,3},{8,12},{9,13},{10,... | collective-permute-start | bytes 3538952 | tf_op jit(solution)/shard_map/ppermute | solution.py:407
  216.2 29.1 %collective-permute-start.33 = (bf16[416,768]{1,0:T(8,128)(2,1)}, bf16[416,768]{1,0:T(8,128)(2,1)}, u32[]{:S(2)}, u32[]{:S(2)}) collective-permute-start(bf16[416,768]{1,0:T(8,128)(2,1)} %constant_dynamic-update-slice_fusion.8.p0), channel_id=1, source_target_pairs={{0,1},{1,0},{2,3},{3,2},{4,5},{5,4},{6,7},{7,6},{8,9},{9,8},{10,11... | collective-permute-start | bytes 1916936 | tf_op jit(solution)/shard_map/ppermute | solution.py:407
  216.8 64.1 %collective-permute-start.56 = (bf16[384,1536]{1,0:T(8,128)(2,1)}, bf16[384,1536]{1,0:T(8,128)(2,1)S(1)}, u32[]{:S(2)}, u32[]{:S(2)}) collective-permute-start(bf16[384,1536]{1,0:T(8,128)(2,1)} %copy-done.27), channel_id=1, source_target_pairs={{0,2},{1,3},{2,0},{3,1},{4,6},{5,7},{6,4},{7,5},{8,10},{9,11},{10,... | collective-permute-start | bytes 3538952 | tf_op jit(solution)/shard_map/ppermute | solution.py:407
  221.2 16.9 %collective-permute-start.46 = (bf16[56,768]{1,0:T(8,128)(2,1)S(1)}, bf16[56,768]{1,0:T(8,128)(2,1)S(1)}, u32[]{:S(2)}, u32[]{:S(2)}) collective-permute-start(bf16[56,768]{1,0:T(8,128)(2,1)S(1)} %get-tuple-element.262), channel_id=1, source_target_pairs={{0,8},{1,9},{2,10},{3,11},{4,12},{5,13},{6,14},{7,15},{8,0},{9,1},... | collective-permute-start | bytes 258056 | tf_op jit(solution)/shard_map/ppermute | solution.py:407
  254.5 26.5 %collective-permute-start.57 = (bf16[384,1536]{1,0:T(8,128)(2,1)}, bf16[384,1536]{1,0:T(8,128)(2,1)S(1)}, u32[]{:S(2)}, u32[]{:S(2)}) collective-permute-start(bf16[384,1536]{1,0:T(8,128)(2,1)} %collective-permute-done.55), channel_id=1, source_target_pairs={{0,2},{1,3},{2,0},{3,1},{4,6},{5,7},{6,4},{7,5},{8,10},{9,11},{10,... | collective-permute-start | bytes 3538952 | tf_op jit(solution)/shard_map/ppermute | solution.py:407
  362.1 86.5 %collective-permute-start.111 = (bf16[768,1536]{1,0:T(8,128)(2,1)}, bf16[768,1536]{1,0:T(8,128)(2,1)}, u32[]{:S(2)}, u32[]{:S(2)}) collective-permute-start(bf16[768,1536]{1,0:T(8,128)(2,1)} %get-tuple-element.397), channel_id=1, source_target_pairs={{0,2},{1,3},{2,0},{3,1},{4,6},{5,7},{6,4},{7,5},{8,10},{9,11},{10,... | collective-permute-start | bytes 7077896 | tf_op jit(solution)/shard_map/ppermute | solution.py:407
  386.3 20.3 %collective-permute-start.82 = (bf16[208,768]{1,0:T(8,128)(2,1)S(1)}, bf16[208,768]{1,0:T(8,128)(2,1)S(1)}, u32[]{:S(2)}, u32[]{:S(2)}) collective-permute-start(bf16[208,768]{1,0:T(8,128)(2,1)S(1)} %get-tuple-element.322.g0), channel_id=1, source_target_pairs={{0,1},{1,0},{2,3},{3,2},{4,5},{5,4},{6,7},{7,6},{8,9},{9,8},{10,11... | collective-permute-start | bytes 958472 | tf_op jit(solution)/shard_map/ppermute | solution.py:407
  386.5 42.0 %collective-permute-start.104 = (bf16[768,384]{1,0:T(8,128)(2,1)S(1)}, bf16[768,384]{1,0:T(8,128)(2,1)S(1)}, u32[]{:S(2)}, u32[]{:S(2)}) collective-permute-start(bf16[768,384]{1,0:T(8,128)(2,1)S(1)} %get-tuple-element.372), channel_id=1, source_target_pairs={{0,2},{1,3},{2,0},{3,1},{4,6},{5,7},{6,4},{7,5},{8,10},{9,11},{10,... | collective-permute-start | bytes 1769480 | tf_op jit(solution)/shard_map/ppermute | solution.py:407
  387.4 41.1 %collective-permute-start.105 = (bf16[384,768]{1,0:T(8,128)(2,1)S(1)}, bf16[384,768]{1,0:T(8,128)(2,1)S(1)}, u32[]{:S(2)}, u32[]{:S(2)}) collective-permute-start(bf16[384,768]{1,0:T(8,128)(2,1)S(1)} %get-tuple-element.374), channel_id=1, source_target_pairs={{0,4},{1,5},{2,6},{3,7},{4,0},{5,1},{6,2},{7,3},{8,12},{9,13},{10,... | collective-permute-start | bytes 1769480 | tf_op jit(solution)/shard_map/ppermute | solution.py:407
  406.5 28.4 %collective-permute-start.76 = (bf16[416,768]{1,0:T(8,128)(2,1)}, bf16[416,768]{1,0:T(8,128)(2,1)}, u32[]{:S(2)}, u32[]{:S(2)}) collective-permute-start(bf16[416,768]{1,0:T(8,128)(2,1)} %get-tuple-element.307), channel_id=1, source_target_pairs={{0,1},{1,0},{2,3},{3,2},{4,5},{5,4},{6,7},{7,6},{8,9},{9,8},{10,11... | collective-permute-start | bytes 1916936 | tf_op jit(solution)/shard_map/ppermute | solution.py:407
  438.2 23.2 %collective-permute-start.77 = (bf16[208,768]{1,0:T(8,128)(2,1)S(1)}, bf16[208,768]{1,0:T(8,128)(2,1)S(1)}, u32[]{:S(2)}, u32[]{:S(2)}) collective-permute-start(bf16[208,768]{1,0:T(8,128)(2,1)S(1)} %get-tuple-element.309), channel_id=1, source_target_pairs={{0,2},{1,3},{2,0},{3,1},{4,6},{5,7},{6,4},{7,5},{8,10},{9,11},{10,... | collective-permute-start | bytes 958472 | tf_op jit(solution)/shard_map/ppermute | solution.py:407
  441.6 24.4 %collective-permute-start.108 = (bf16[96,768]{1,0:T(8,128)(2,1)S(1)}, bf16[96,768]{1,0:T(8,128)(2,1)S(1)}, u32[]{:S(2)}, u32[]{:S(2)}) collective-permute-start(bf16[96,768]{1,0:T(8,128)(2,1)S(1)} %get-tuple-element.388), channel_id=1, source_target_pairs={{0,8},{1,9},{2,10},{3,11},{4,12},{5,13},{6,14},{7,15},{8,0},{9,1},... | collective-permute-start | bytes 442376 | tf_op jit(solution)/shard_map/ppermute | solution.py:407
  443.0 17.3 %collective-permute-start.85 = (f32[8,12,96]{2,1,0:T(8,128)S(1)}, f32[8,12,96]{2,1,0:T(8,128)S(1)}, u32[]{:S(2)}, u32[]{:S(2)}) collective-permute-start(f32[8,12,96]{2,1,0:T(8,128)S(1)} %fusion.9), channel_id=1, source_target_pairs={{0,2},{1,3},{2,0},{3,1},{4,6},{5,7},{6,4},{7,5},{8,10},{9,11},{10,... | collective-permute-start | bytes 110600 | tf_op jit(solution)/shard_map/ppermute | solution.py:407
  456.4 73.4 %collective-permute-start.112 = (bf16[384,1536]{1,0:T(8,128)(2,1)}, bf16[384,1536]{1,0:T(8,128)(2,1)S(1)}, u32[]{:S(2)}, u32[]{:S(2)}) collective-permute-start(bf16[384,1536]{1,0:T(8,128)(2,1)} %get-tuple-element.400), channel_id=1, source_target_pairs={{0,4},{1,5},{2,6},{3,7},{4,0},{5,1},{6,2},{7,3},{8,12},{9,13},{10,... | collective-permute-start | bytes 3538952 | tf_op jit(solution)/shard_map/ppermute | solution.py:407
  459.1 72.9 %collective-permute-start.97 = (bf16[768,768]{1,0:T(8,128)(2,1)}, bf16[768,768]{1,0:T(8,128)(2,1)}, u32[]{:S(2)}, u32[]{:S(2)}) collective-permute-start(bf16[768,768]{1,0:T(8,128)(2,1)} %get-tuple-element.352), channel_id=1, source_target_pairs={{0,2},{1,3},{2,0},{3,1},{4,6},{5,7},{6,4},{7,5},{8,10},{9,11},{10,... | collective-permute-start | bytes 3538952 | tf_op jit(solution)/shard_map/ppermute | solution.py:407
  460.3 71.7 %collective-permute-start.98 = (bf16[384,1536]{1,0:T(8,128)(2,1)}, bf16[384,1536]{1,0:T(8,128)(2,1)}, u32[]{:S(2)}, u32[]{:S(2)}) collective-permute-start(bf16[384,1536]{1,0:T(8,128)(2,1)} %get-tuple-element.354), channel_id=1, source_target_pairs={{0,4},{1,5},{2,6},{3,7},{4,0},{5,1},{6,2},{7,3},{8,12},{9,13},{10,... | collective-permute-start | bytes 3538952 | tf_op jit(solution)/shard_map/ppermute | solution.py:407
  462.2 46.4 %collective-permute-start.86 = (f32[4,12,96]{2,1,0:T(8,128)S(1)}, f32[4,12,96]{2,1,0:T(8,128)}, u32[]{:S(2)}, u32[]{:S(2)}) collective-permute-start(f32[4,12,96]{2,1,0:T(8,128)S(1)} %slice.203), channel_id=1, source_target_pairs={{0,4},{1,5},{2,6},{3,7},{4,0},{5,1},{6,2},{7,3},{8,12},{9,13},{10,... | collective-permute-start | bytes 55304 | tf_op jit(solution)/shard_map/ppermute | solution.py:407
  466.7 44.7 %collective-permute-start.90 = (bf16[768,384]{1,0:T(8,128)(2,1)}, bf16[768,384]{1,0:T(8,128)(2,1)}, u32[]{:S(2)}, u32[]{:S(2)}) collective-permute-start(bf16[768,384]{1,0:T(8,128)(2,1)} %get-tuple-element.336), channel_id=1, source_target_pairs={{0,2},{1,3},{2,0},{3,1},{4,6},{5,7},{6,4},{7,5},{8,10},{9,11},{10,... | collective-permute-start | bytes 1769480 | tf_op jit(solution)/shard_map/ppermute | solution.py:407
  511.4 16.3 %collective-permute-start.109 = (bf16[96,768]{1,0:T(8,128)(2,1)}, bf16[96,768]{1,0:T(8,128)(2,1)S(1)}, u32[]{:S(2)}, u32[]{:S(2)}) collective-permute-start(bf16[96,768]{1,0:T(8,128)(2,1)} %copy-done.116), channel_id=1, source_target_pairs={{0,16},{1,17},{2,18},{3,19},{4,20},{5,21},{6,22},{7,23},{8,24},{9,... | collective-permute-start | bytes 442376 | tf_op jit(solution)/shard_map/ppermute | solution.py:407
  527.8 16.3 %collective-permute-start.92 = (bf16[384,384]{1,0:T(8,128)(2,1)S(1)}, bf16[384,384]{1,0:T(8,128)(2,1)S(1)}, u32[]{:S(2)}, u32[]{:S(2)}) collective-permute-start(bf16[384,384]{1,0:T(8,128)(2,1)S(1)} %get-tuple-element.340), channel_id=1, source_target_pairs={{0,4},{1,5},{2,6},{3,7},{4,0},{5,1},{6,2},{7,3},{8,12},{9,13},{10,... | collective-permute-start | bytes 884744 | tf_op jit(solution)/shard_map/ppermute | solution.py:407
  528.4 17.2 %collective-permute-start.93 = (bf16[384,384]{1,0:T(8,128)(2,1)S(1)}, bf16[384,384]{1,0:T(8,128)(2,1)S(1)}, u32[]{:S(2)}, u32[]{:S(2)}) collective-permute-start(bf16[384,384]{1,0:T(8,128)(2,1)S(1)} %get-tuple-element.342), channel_id=1, source_target_pairs={{0,2},{1,3},{2,0},{3,1},{4,6},{5,7},{6,4},{7,5},{8,10},{9,11},{10,... | collective-permute-start | bytes 884744 | tf_op jit(solution)/shard_map/ppermute | solution.py:407
  539.6 25.1 %collective-permute-start.113 = (bf16[192,1536]{1,0:T(8,128)(2,1)}, bf16[192,1536]{1,0:T(8,128)(2,1)S(1)}, u32[]{:S(2)}, u32[]{:S(2)}) collective-permute-start(bf16[192,1536]{1,0:T(8,128)(2,1)} %get-tuple-element.403), channel_id=1, source_target_pairs={{0,8},{1,9},{2,10},{3,11},{4,12},{5,13},{6,14},{7,15},{8,0},{9,1},... | collective-permute-start | bytes 1769480 | tf_op jit(solution)/shard_map/ppermute | solution.py:407
  539.7 45.9 %collective-permute-start.114 = (bf16[192,1536]{1,0:T(8,128)(2,1)}, bf16[192,1536]{1,0:T(8,128)(2,1)S(1)}, u32[]{:S(2)}, u32[]{:S(2)}) collective-permute-start(bf16[192,1536]{1,0:T(8,128)(2,1)} %get-tuple-element.404), channel_id=1, source_target_pairs={{0,16},{1,17},{2,18},{3,19},{4,20},{5,21},{6,22},{7,23},{8,24},{9,... | collective-permute-start | bytes 1769480 | tf_op jit(solution)/shard_map/ppermute | solution.py:407
  542.4 46.0 %collective-permute-start.115 = (bf16[192,1536]{1,0:T(8,128)(2,1)}, bf16[192,1536]{1,0:T(8,128)(2,1)S(1)}, u32[]{:S(2)}, u32[]{:S(2)}) collective-permute-start(bf16[192,1536]{1,0:T(8,128)(2,1)} %get-tuple-element.405), channel_id=1, source_target_pairs={{0,24},{1,25},{2,26},{3,27},{4,28},{5,29},{6,30},{7,31},{8,16},{9,... | collective-permute-start | bytes 1769480 | tf_op jit(solution)/shard_map/ppermute | solution.py:407
  544.1 15.4 %collective-permute-start.99 = (bf16[384,768]{1,0:T(8,128)(2,1)}, bf16[384,768]{1,0:T(8,128)(2,1)}, u32[]{:S(2)}, u32[]{:S(2)}) collective-permute-start(bf16[384,768]{1,0:T(8,128)(2,1)} %get-tuple-element.360), channel_id=1, source_target_pairs={{0,4},{1,5},{2,6},{3,7},{4,0},{5,1},{6,2},{7,3},{8,12},{9,13},{10,... | collective-permute-start | bytes 1769480 | tf_op jit(solution)/shard_map/ppermute | solution.py:407
  545.6 14.0 %collective-permute-start.100 = (bf16[384,768]{1,0:T(8,128)(2,1)}, bf16[384,768]{1,0:T(8,128)(2,1)}, u32[]{:S(2)}, u32[]{:S(2)}) collective-permute-start(bf16[384,768]{1,0:T(8,128)(2,1)} %get-tuple-element.362), channel_id=1, source_target_pairs={{0,2},{1,3},{2,0},{3,1},{4,6},{5,7},{6,4},{7,5},{8,10},{9,11},{10,... | collective-permute-start | bytes 1769480 | tf_op jit(solution)/shard_map/ppermute | solution.py:407
  559.5 51.6 %collective-permute-start.94 = (bf16[96,768]{1,0:T(8,128)(2,1)S(1)}, bf16[96,768]{1,0:T(8,128)(2,1)S(1)}, u32[]{:S(2)}, u32[]{:S(2)}) collective-permute-start(bf16[96,768]{1,0:T(8,128)(2,1)S(1)} %get-tuple-element.344), channel_id=1, source_target_pairs={{0,8},{1,9},{2,10},{3,11},{4,12},{5,13},{6,14},{7,15},{8,0},{9,1},... | collective-permute-start | bytes 442376 | tf_op jit(solution)/shard_map/ppermute | solution.py:407
  562.7 63.6 %collective-permute-start.101 = (bf16[96,1536]{1,0:T(8,128)(2,1)}, bf16[96,1536]{1,0:T(8,128)(2,1)S(1)}, u32[]{:S(2)}, u32[]{:S(2)}) collective-permute-start(bf16[96,1536]{1,0:T(8,128)(2,1)} %get-tuple-element.364), channel_id=1, source_target_pairs={{0,8},{1,9},{2,10},{3,11},{4,12},{5,13},{6,14},{7,15},{8,0},{9,1},... | collective-permute-start | bytes 884744 | tf_op jit(solution)/shard_map/ppermute | solution.py:407
  564.7 61.6 %collective-permute-start.102 = (bf16[96,1536]{1,0:T(8,128)(2,1)}, bf16[96,1536]{1,0:T(8,128)(2,1)S(1)}, u32[]{:S(2)}, u32[]{:S(2)}) collective-permute-start(bf16[96,1536]{1,0:T(8,128)(2,1)} %get-tuple-element.365), channel_id=1, source_target_pairs={{0,16},{1,17},{2,18},{3,19},{4,20},{5,21},{6,22},{7,23},{8,24},{9,... | collective-permute-start | bytes 884744 | tf_op jit(solution)/shard_map/ppermute | solution.py:407
  585.6 40.7 %collective-permute-start.103 = (bf16[96,1536]{1,0:T(8,128)(2,1)}, bf16[96,1536]{1,0:T(8,128)(2,1)}, u32[]{:S(2)}, u32[]{:S(2)}) collective-permute-start(bf16[96,1536]{1,0:T(8,128)(2,1)} %get-tuple-element.366), channel_id=1, source_target_pairs={{0,24},{1,25},{2,26},{3,27},{4,28},{5,29},{6,30},{7,31},{8,16},{9,... | collective-permute-start | bytes 884744 | tf_op jit(solution)/shard_map/ppermute | solution.py:407
  588.4 36.0 %collective-permute-start.95 = (bf16[96,768]{1,0:T(8,128)(2,1)S(1)}, bf16[96,768]{1,0:T(8,128)(2,1)S(1)}, u32[]{:S(2)}, u32[]{:S(2)}) collective-permute-start(bf16[96,768]{1,0:T(8,128)(2,1)S(1)} %get-tuple-element.345), channel_id=1, source_target_pairs={{0,16},{1,17},{2,18},{3,19},{4,20},{5,21},{6,22},{7,23},{8,24},{9,... | collective-permute-start | bytes 442376 | tf_op jit(solution)/shard_map/ppermute | solution.py:407
  (243 other events, 1791.0 us)

commit v3 on v0

--- a/solution.py
+++ b/solution.py
@@ -1,6 +1,10 @@
+import functools
+
 import jax
 import jax.numpy as jnp
 from jax import lax
+from jax.experimental import pallas as pl
+from jax.experimental.pallas import tpu as pltpu
 from jax.sharding import PartitionSpec as P
 
 HD = 64
@@ -391,6 +395,817 @@
     )
 
 
+ROWS = 208
+AXES = ("dp", "tensor")
+BF = jnp.bfloat16
+F32 = jnp.float32
+VM = pl.BlockSpec(memory_space=pltpu.VMEM)
+SM = pl.BlockSpec(memory_space=pltpu.SMEM)
+
+
+def swap(values, z=0, x=0, y=0, core=0):
+    shift_d, shift_t = 2 * z + x, 2 * y + core
+    pairs = [(d * 4 + t, (d ^ shift_d) * 4 + (t ^ shift_t)) for d in range(8) for t in range(4)]
+    return lax.ppermute(values, AXES, pairs)
+
+
+def hold(values, *tokens):
+    return lax.optimization_barrier((values,) + tokens)[0]
+
+
+def run(kernel, outs, args, flops, scratch=(), scalars=0, mib=20):
+    flops = flops if flops == 8e9 else 1000
+    shapes = [jax.ShapeDtypeStruct(s, dt) for s, dt in outs]
+    return pl.pallas_call(
+        kernel,
+        out_shape=shapes,
+        in_specs=[SM] * scalars + [VM] * (len(args) - scalars),
+        out_specs=[VM] * len(shapes),
+        scratch_shapes=list(scratch),
+        compiler_params=pltpu.CompilerParams(vmem_limit_bytes=mib * 2**20),
+        cost_estimate=pl.CostEstimate(flops=int(flops), bytes_accessed=1000, transcendentals=0),
+    )(*args)
+
+
+def dot(a, b, ca, cb):
+    return lax.dot_general(a, b, (((ca,), (cb,)), ((), ())), preferred_element_type=F32)
+
+
+def norm_stats(values):
+    center = values - jnp.mean(values, axis=-1, keepdims=True)
+    scale = lax.rsqrt(jnp.mean(center * center, axis=-1, keepdims=True) + epsilon)
+    return center * scale, scale
+
+
+def enter_kernel(live, x_ref, c_ref, perm_ref, start_ref, low_start, grad_ref, low_ref):
+    rows = x_ref.shape[0]
+    scale = live[0].astype(F32)
+    extra = jnp.zeros((ROWS - rows, x_ref.shape[1]), F32)
+    start = dot(x_ref[...], perm_ref[...], 1, 1)
+    start_ref[:rows] = start
+    start_ref[rows:] = extra
+    low_start[:rows] = start.astype(BF)
+    low_start[rows:] = extra.astype(BF)
+    grad = dot(c_ref[...], perm_ref[...], 1, 1) * scale
+    grad_ref[:rows] = grad
+    grad_ref[rows:] = extra
+    low_ref[:rows] = grad.astype(BF)
+    low_ref[rows:] = extra.astype(BF)
+
+
+def norm_kernel(gain_ref, *refs):
+    for x_ref, out_ref in zip(refs[:4], refs[4:]):
+        out_ref[...] = (norm_stats(x_ref[...].astype(F32))[0] * gain_ref[...]).astype(BF)
+
+
+def join_norm_kernel(x_ref, own_ref, far_ref, gain_ref, sum_ref, out_ref):
+    total = x_ref[...] + (own_ref[...] + far_ref[...].astype(F32))
+    sum_ref[...] = total
+    out_ref[...] = (norm_stats(total)[0] * gain_ref[...]).astype(BF)
+
+
+def norm_back_kernel(x_ref, up_ref, own_ref, far_ref, gain_ref, grad_ref, low_ref, gain_out):
+    upstream = own_ref[...] + far_ref[...].astype(F32)
+    normed, scale = norm_stats(x_ref[...])
+    scaled = upstream * gain_ref[...]
+    grad = up_ref[...] + scale * (
+        scaled
+        - jnp.mean(scaled, axis=-1, keepdims=True)
+        - normed * jnp.mean(scaled * normed, axis=-1, keepdims=True)
+    )
+    grad_ref[...] = grad
+    low_ref[...] = grad.astype(BF)
+    gain_out[...] = jnp.sum(upstream * normed, axis=0, keepdims=True)
+
+
+def fill(rows, *refs):
+    size = refs[0].shape[0]
+    for i, ref in enumerate(refs):
+        rows[i * size : (i + 1) * size] = ref[...]
+
+
+def put_partial(partial, own_ref, sib_ref):
+    half = own_ref.shape[0]
+    own_ref[...] = partial[:half]
+    sib_ref[...] = partial[half:].astype(BF)
+
+
+def score_block(queries, keyset):
+    scores = dot(queries, keyset, 1, 1) * HD ** (-0.5)
+    column = lax.broadcasted_iota(jnp.int32, scores.shape, 1)
+    scores = jnp.where(column < L, scores, -1e30)
+    top = jnp.max(scores, axis=-1, keepdims=True)
+    weight = jnp.exp(scores - top)
+    return weight * (1.0 / jnp.sum(weight, axis=-1, keepdims=True)), top
+
+
+def attend_kernel(
+    at, live, a0, a1, a2, a3, w, mix_ref, att_ref, own_ref, sib_ref, peak_ref, rows
+):
+    fill(rows, a0, a1, a2, a3)
+    part = mix_ref.shape[1] // 3
+    mix_ref[...] = dot(rows[...], w[:, at : at + 3 * part], 1, 0).astype(BF)
+    row_ok = lax.broadcasted_iota(jnp.int32, (ROWS, 1), 0) < L
+    lane = lax.broadcasted_iota(jnp.int32, peak_ref.shape, 1)
+    found = jnp.full(peak_ref.shape, -1e30, F32)
+    for h in range(part // HD):
+        for i in range(4):
+            span = slice(i * ROWS, (i + 1) * ROWS)
+            cut = [mix_ref[span, c * part + h * HD : c * part + (h + 1) * HD] for c in range(3)]
+            probs, top = score_block(cut[0], cut[1])
+            mixed = dot(probs.astype(BF), cut[2], 1, 0)
+            att_ref[span, h * HD : (h + 1) * HD] = mixed.astype(BF)
+            best = jnp.max(jnp.where(row_ok, top, -1e30), axis=0, keepdims=True)
+            best = jnp.where(live[i] > 0, best, -1e30)
+            found = jnp.where(lane == h, jnp.maximum(best, found), found)
+    peak_ref[...] = found
+    out = w[:, at + 3 * part : at + 4 * part]
+    put_partial(dot(att_ref[...], out, 1, 1), own_ref, sib_ref)
+
+
+def put_pack(grad, column, near, send):
+    half = near.shape[0]
+    near[:, column : column + grad.shape[1]] = grad[:half]
+    send[:, column : column + grad.shape[1]] = grad[half:]
+
+
+def attend_back_kernel(
+    at, g0, g1, g2, g3, a0, a1, a2, a3, mix_ref, att_ref, w,
+    near, send, own_ref, sib_ref, rows, grad_att, grad_mix,
+):
+    part = mix_ref.shape[1] // 3
+    fill(rows, g0, g1, g2, g3)
+    grad_att[...] = dot(rows[...], w[:, at + 3 * part : at + 4 * part], 1, 0).astype(BF)
+    put_pack(dot(rows[...], att_ref[...], 0, 0).astype(BF), 3 * part, near, send)
+    factor = HD ** (-0.5)
+    for h in range(part // HD):
+        for i in range(4):
+            span = slice(i * ROWS, (i + 1) * ROWS)
+            spans = [slice(c * part + h * HD, c * part + (h + 1) * HD) for c in range(3)]
+            queries, keyset, values = (mix_ref[span, s] for s in spans)
+            grad = grad_att[span, h * HD : (h + 1) * HD]
+            probs, _ = score_block(queries, keyset)
+            grad_mix[span, spans[2]] = dot(probs.astype(BF), grad, 0, 0).astype(BF)
+            grad_probs = dot(grad, values, 1, 1)
+            slope = probs * (grad_probs - jnp.sum(grad_probs * probs, axis=-1, keepdims=True))
+            slope = slope.astype(BF)
+            grad_mix[span, spans[0]] = (factor * dot(slope, keyset, 1, 0)).astype(BF)
+            grad_mix[span, spans[1]] = (factor * dot(slope, queries, 0, 0)).astype(BF)
+    put_partial(dot(grad_mix[...], w[:, at : at + 3 * part], 1, 1), own_ref, sib_ref)
+    fill(rows, a0, a1, a2, a3)
+    put_pack(dot(rows[...], grad_mix[...], 0, 0).astype(BF), 0, near, send)
+
+
+def gelu_pair(hidden):
+    cdf = 0.5 * (1.0 + lax.erf(hidden * 0.7071067811865476))
+    slope = cdf + hidden * jnp.exp(-0.5 * hidden * hidden) * 0.3989422804014327
+    return (hidden * cdf).astype(BF), slope.astype(BF)
+
+
+def mlp_kernel(ats, b0, b1, b2, b3, w, act_ref, slope_ref, own_ref, sib_ref, rows):
+    fill(rows, b0, b1, b2, b3)
+    wide = act_ref.shape[1]
+    for c in range(0, wide, 256):
+        span = slice(c, c + 256)
+        act, slope = gelu_pair(dot(rows[...], w[:, ats[0] + c : ats[0] + c + 256], 1, 0))
+        act_ref[:, span] = act
+        slope_ref[:, span] = slope
+    put_partial(dot(act_ref[...], w[:, ats[1] : ats[1] + wide], 1, 1), own_ref, sib_ref)
+
+
+def mlp_back_kernel(
+    ats, g0, g1, g2, g3, b0, b1, b2, b3, act_ref, slope_ref, w,
+    near, send, own_ref, sib_ref, rows, hidden,
+):
+    fill(rows, g0, g1, g2, g3)
+    wide = act_ref.shape[1]
+    grad = dot(rows[...], w[:, ats[1] : ats[1] + wide], 1, 0) * slope_ref[...].astype(F32)
+    hidden[...] = grad.astype(BF)
+    put_partial(dot(hidden[...], w[:, ats[0] : ats[0] + wide], 1, 1), own_ref, sib_ref)
+    put_pack(dot(rows[...], act_ref[...], 0, 0).astype(BF), wide, near, send)
+    fill(rows, b0, b1, b2, b3)
+    put_pack(dot(rows[...], hidden[...], 0, 0).astype(BF), 0, near, send)
+
+
+def picked(row_code, codes):
+    hit = (row_code[...] == codes[0:1, :]) | (row_code[...] == codes[1:2, :])
+    return jnp.where(hit, 1.0, 0.0).astype(BF)
+
+
+def dispatch_kernel(row_code, codes, p0, p1, p2, p3, perm_ref, out, rows):
+    fill(rows, p0, p1, p2, p3)
+    picks = dot(picked(row_code, codes), rows[...], 1, 0).astype(BF)
+    out[...] = dot(picks, perm_ref[...], 1, 0).astype(BF)
+
+
+def token_kernel(row_code, codes, p0, p1, p2, p3, perm_ref, first_ref, second_ref, out, rows):
+    dispatch_kernel(row_code, codes, p0, p1, p2, p3, perm_ref, out, rows)
+    row = lax.broadcasted_iota(jnp.int32, (8, 128), 0)
+    block = jnp.zeros((8, 128), F32)
+    for i, ref in enumerate((first_ref, second_ref)):
+        high = ref[...].astype(BF).astype(F32)
+        block = jnp.where(row == 2 * i + 2, high, block)
+        block = jnp.where(row == 2 * i + 3, ref[...] - high, block)
+    size = out.shape[0] // 8
+    for e in range(8):
+        span = slice((e + 1) * size - 8, (e + 1) * size)
+        old = out[span, :128].astype(F32)
+        out[span, :128] = jnp.where((row >= 2) & (row < 6), block, old).astype(BF)
+
+
+def collect_kernel(both_ref, grad_ref, out_ref, peak_ref):
+    size = both_ref.shape[1] // 2
+    best = jnp.full((2, 128), -1e30, F32)
+    for p in range(both_ref.shape[0]):
+        rows = slice(p * size, (p + 1) * size)
+        grad_ref[rows] = both_ref[p, :size]
+        out_ref[rows] = both_ref[p, size:]
+        block = both_ref[p, 2 * size - 8 :, :128].astype(F32)
+        found = [block[2 * i + 2 : 2 * i + 3] + block[2 * i + 3 : 2 * i + 4] for i in range(2)]
+        best = jnp.maximum(best, jnp.concatenate(found, axis=0))
+    peak_ref[...] = best
+
+
+def combine_kernel(which, row_code, codes, perm_ref, both_ref, own_ref, sib_ref, rows):
+    size = both_ref.shape[1] // 2
+    for p in range(both_ref.shape[0]):
+        rows[p * size : (p + 1) * size] = both_ref[p, which * size : (which + 1) * size]
+    back = dot(rows[...], perm_ref[...], 1, 1).astype(BF)
+    partial = dot(picked(row_code, codes), back, 0, 0)
+    half = partial.shape[0] // 2
+    own_ref[...] = partial[:half]
+    sib_ref[...] = partial[half:].astype(BF)
+
+
+def pair_add_kernel(own_ref, far_ref, near_ref, send_ref):
+    total = own_ref[...] + far_ref[...].astype(F32)
+    near_ref[...] = total[:ROWS]
+    send_ref[...] = total[ROWS:].astype(BF)
+
+
+def route_of(tokens, router, number):
+    logits = dot(tokens, router, 1, 1)
+    column = lax.broadcasted_iota(jnp.int32, logits.shape, 1)
+    logits = jnp.where(column < 8, logits, -1e30)
+    weight = jnp.exp(logits - jnp.max(logits, axis=-1, keepdims=True))
+    route = weight / jnp.sum(weight, axis=-1, keepdims=True)
+    mine = jnp.where(column == number, 1.0, 0.0)
+    return route, mine, jnp.sum(route * mine, axis=-1, keepdims=True)
+
+
+def expert_kernel(
+    number, t0, t1, g0, g1, router, *rest
+):
+    own, far = rest[0], rest[1:5]
+    res_own, res_sib, grad_own, grad_sib = rest[5:9]
+    up_parts, down_parts = rest[9:12], rest[12:15]
+    act_ref, hid_ref, gout_ref, pair, whole = rest[15:]
+    size = t0.shape[0]
+    half, wide = own.shape[0] // 2, act_ref.shape[2]
+    whole[0] = own[...]
+    for i, part in enumerate(far):
+        whole[1, i * half // 2 : (i + 1) * half // 2] = part[...]
+    for i, (t, g, res, grad) in enumerate(
+        ((t1, g1, res_sib, grad_sib), (t0, g0, res_own, grad_own))
+    ):
+        rows = slice((1 - i) * size, (2 - i) * size)
+        gate = route_of(t[...], router[...], number[0])[2]
+        gout = (gate * g[...].astype(F32)).astype(BF)
+        gout_ref[rows] = gout
+        for y in range(2):
+            for c in range(0, wide, 256):
+                span = slice(c, c + 256)
+                act, lean = gelu_pair(dot(t[...], whole[y, :, span], 1, 0))
+                act_ref[y, rows, span] = act
+                back = dot(gout, whole[y, :, wide + c : wide + c + 256], 1, 0)
+                hid_ref[y, rows, span] = (back * lean.astype(F32)).astype(BF)
+        res[...] = (
+            dot(act_ref[0, rows], whole[0, :, wide:], 1, 1)
+            + dot(act_ref[1, rows], whole[1, :, wide:], 1, 1)
+        ).astype(res.dtype)
+        grad[...] = (
+            dot(hid_ref[0, rows], whole[0, :, :wide], 1, 1)
+            + dot(hid_ref[1, rows], whole[1, :, :wide], 1, 1)
+        ).astype(grad.dtype)
+    pair[:size] = t0[...]
+    pair[size:] = t1[...]
+    for parts, left, right in ((up_parts, pair, hid_ref), (down_parts, gout_ref, act_ref)):
+        parts[0][...] = dot(left[...], right[0], 0, 0).astype(BF)
+        far = dot(left[...], right[1], 0, 0).astype(BF)
+        parts[1][...] = far[:half]
+        parts[2][...] = far[half:]
+
+
+def answer_kernel(
+    number, t_ref, g_ref, router, res_own, res_far, grad_own, grad_far, perm_ref,
+    both_ref, router_out,
+):
+    route, mine, gate = route_of(t_ref[...], router[...], number[0])
+    result = res_own[...] + res_far[...].astype(F32)
+    grad_gate = jnp.sum(result * g_ref[...].astype(F32), axis=-1, keepdims=True)
+    grad_logit = (grad_gate * route * (mine - gate)).astype(BF)
+    router_out[...] = reorder(dot(grad_logit, t_ref[...], 0, 0), perm_ref[...], 1)
+    grad = grad_own[...] + grad_far[...].astype(F32) + dot(grad_logit, router[...], 1, 0)
+    size = both_ref.shape[1] // 2
+    whole = grad.astype(BF)
+    for p in range(both_ref.shape[0]):
+        both_ref[p, :size] = whole[p * size : (p + 1) * size]
+    whole = (gate * result).astype(BF)
+    for p in range(both_ref.shape[0]):
+        both_ref[p, size:] = whole[p * size : (p + 1) * size]
+
+
+def reorder(values, perm, axis):
+    high = values.astype(BF)
+    rest = values - high.astype(F32)
+    middle = rest.astype(BF)
+    low = (rest - middle.astype(F32)).astype(BF)
+    return dot(high, perm, 1, axis) + (dot(middle, perm, 1, axis) + dot(low, perm, 1, axis))
+
+
+def leave_kernel(x_ref, perm_ref, out_ref):
+    out_ref[...] = reorder(x_ref[...], perm_ref[...], 0)[: out_ref.shape[0]]
+
+
+def finish_kernel(live, x_ref, own_ref, far_ref, perm_ref, out_ref):
+    total = x_ref[...] + (own_ref[...] + far_ref[...].astype(F32))
+    total = reorder(total, perm_ref[...], 0) * live[0].astype(F32)
+    out_ref[...] = total[: out_ref.shape[0]]
+
+
+def add_pack_kernel(up_own, up0, up1, down_own, down0, down1, out):
+    half, wide = up0.shape
+    for c, (own, parts) in enumerate(((up_own, (up0, up1)), (down_own, (down0, down1)))):
+        for s, part in enumerate(parts):
+            span = slice(s * half, (s + 1) * half)
+            total = own[span].astype(F32) + part[...].astype(F32)
+            out[span, c * wide : (c + 1) * wide] = total.astype(BF)
+
+
+def pack_kernel(*refs):
+    out = refs[-1]
+    at = 0
+    for ref in refs[:-1]:
+        out[:, at : at + ref.shape[1]] = ref[...]
+        at += ref.shape[1]
+
+
+def stack_kernel(*refs):
+    rows = refs[0].shape[0]
+    for i, ref in enumerate(refs[:-1]):
+        refs[-1][i * rows : (i + 1) * rows] = ref[...]
+
+
+def order_kernel(places, in_ref, first_ref, second_ref):
+    rows = first_ref.shape[0] // 4
+    cut = first_ref.shape[1]
+    for i in range(4):
+        at = pl.multiple_of(places[i] * rows, rows)
+        first_ref[i * rows : (i + 1) * rows] = in_ref[pl.ds(at, rows), :cut]
+        second_ref[i * rows : (i + 1) * rows] = in_ref[pl.ds(at, rows), cut:]
+
+
+def sum_two(near, got, keep, s1, s2, s3):
+    rows = keep.shape[0]
+    for k, out in enumerate((keep, s1, s2, s3)):
+        span = slice(k * rows, (k + 1) * rows)
+        out[...] = (near[span].astype(F32) + got[span].astype(F32)).astype(out.dtype)
+
+
+def small_kernel(g1, g2, g3, g4, router, out):
+    whole = jnp.concatenate([g1[...], g2[...], g3[...], g4[...]], axis=0)
+    count, cols = router.shape[0], out.shape[2]
+    blank = jnp.zeros((out.shape[1] - 4 - count, cols), F32)
+    for p in range(8):
+        span = slice(p * cols, (p + 1) * cols)
+        out[p] = jnp.concatenate([whole[:, span], router[:, span], blank], axis=0)
+
+
+def sum_two_more(near, got, small, keep, s1, s2, s3):
+    sum_two(near, got, keep, s1.at[: keep.shape[0]], s2.at[: keep.shape[0]], s3.at[: keep.shape[0]])
+    rows, count = keep.shape[0], small.shape[1]
+    cols = small.shape[2]
+    for k, out in enumerate((s1, s2, s3)):
+        out[rows:, :] = jnp.zeros((out.shape[0] - rows, out.shape[1]), BF)
+        high = small[k + 1].astype(BF)
+        out[rows : rows + count, :cols] = high
+        low = small[k + 1] - high.astype(F32)
+        out[rows + count : rows + 2 * count, :cols] = low.astype(BF)
+
+
+def sum_three_more(keep, r1, r2, r3, small, first, second, small_out):
+    rows, count = keep.shape[0], small.shape[1]
+    cols = small.shape[2]
+    sum_three(keep, r1.at[:rows], r2.at[:rows], r3.at[:rows], first, second)
+    total = small[0]
+    for r in (r1, r2, r3):
+        high = r[rows : rows + count, :cols].astype(F32)
+        total = total + (high + r[rows + count : rows + 2 * count, :cols].astype(F32))
+    small_out[...] = total
+
+
+def sum_three(keep, r1, r2, r3, first, second):
+    total = keep[...] + (r1[...].astype(F32) + (r2[...].astype(F32) + r3[...].astype(F32)))
+    wide = first.shape[1]
+    first[...] = total[:, :wide]
+    second[...] = total[:, wide:]
+
+
+def scatter_start(parts):
+    near, send = parts
+    return near, swap(send, x=1)
+
+
+def scatter_middle(parts):
+    half, width = parts[0].shape
+    shape = (half // 4, width)
+    return run(sum_two, [(shape, F32)] + [(shape, BF)] * 3, parts, half * width)
+
+
+def scatter_late(parts):
+    keep, s1, s2, s3 = parts
+    return keep, swap(s1, z=1), swap(s2, z=2), swap(s3, z=3)
+
+
+def scatter_end(parts, wide):
+    rows, width = parts[0].shape
+    return run(sum_three, [((rows, wide), F32), ((rows, width - wide), F32)], parts, rows * width)
+
+
+def fast_local(
+    block_input,
+    first_norm,
+    first_qkv,
+    first_out,
+    second_norm,
+    dense_up,
+    dense_down,
+    third_norm,
+    second_qkv,
+    second_out,
+    fourth_norm,
+    router_weight,
+    expert_up,
+    expert_down,
+    expert_ids,
+    expert_slots,
+    image_counts,
+    cotangent,
+):
+    d = lax.axis_index("dp")
+    t = lax.axis_index("tensor")
+    z_index, x_index = d // 2, d % 2
+    width = first_norm.shape[0]
+    features = width * 8
+    experts = expert_up.shape[0]
+    live_count = image_counts[0]
+    head_cols = first_out.shape[0]
+    ff_cols = dense_up.shape[1]
+    qkv_cols = 3 * head_cols
+    row = ((ROWS, features), F32)
+    row_low = ((ROWS, features), BF)
+
+    small = jnp.concatenate(
+        [
+            jnp.stack([first_norm, second_norm, third_norm, fourth_norm], axis=1),
+            router_weight,
+            jnp.zeros((width, 128 - 4 - experts), BF),
+        ],
+        axis=1,
+    )
+    pack_one = run(
+        pack_kernel,
+        [((width, small.shape[1] + 4 * head_cols), BF)],
+        (small, first_qkv.reshape(width, -1), first_out.T),
+        width,
+    )[0]
+    pack_late = run(
+        pack_kernel,
+        [((width, 2 * ff_cols + 4 * head_cols), BF)],
+        (dense_up, dense_down.T, second_qkv.reshape(width, -1), second_out.T),
+        width,
+    )[0]
+
+    lines = [[x + 2 * z for z in range(4)] for x in range(2)]
+    raw_late = lax.all_gather(pack_late, "dp", axis=0, tiled=True, axis_index_groups=lines)
+
+    def stacked(shards):
+        shape = (len(shards) * shards[0].shape[0], shards[0].shape[1])
+        return run(stack_kernel, [(shape, BF)], shards, width)[0]
+
+    z_one = stacked([pack_one] + [swap(pack_one, z=k) for k in (1, 2, 3)])
+
+    rel = jnp.arange(features)
+    block = rel // width
+    rel_place = jnp.bitwise_xor(d, 2 * (block % 4) + block // 4) * width + rel % width
+    perm = (rel_place[:, None] == rel[None, :]).astype(BF)
+    live_here = (t < live_count).astype(jnp.int32).reshape(1)
+    live_group = (jnp.stack([t, t ^ 2, t ^ 1, t ^ 3]) < live_count).astype(jnp.int32)
+
+    start, low_start, grad_four, grad_low = run(
+        enter_kernel,
+        [row, row_low, row, row_low],
+        (live_here, block_input, cotangent, perm),
+        4 * ROWS * features**2,
+        scalars=1,
+    )
+
+    def spread(rows):
+        far = swap(rows, y=1)
+        return [rows, far, swap(rows, core=1), swap(far, core=1)]
+
+    first_group = spread(low_start)
+    wide = 2 * ff_cols
+    half_shape = [((features // 2, ff_cols), BF)] * 2
+    e_pack = jnp.concatenate([expert_up, jnp.swapaxes(expert_down, 1, 2)], axis=2)
+    held = -(-CAP // 4)
+    block_size = -(-(held + 4) // 8) * 8
+    ids = jnp.pad(expert_ids.reshape(4, L, 2), ((0, 0), (0, ROWS - L), (0, 0)), constant_values=-1)
+    slots = jnp.pad(
+        expert_slots.reshape(4, L, 2), ((0, 0), (0, ROWS - L), (0, 0)), constant_values=CAP
+    )
+    mine = (slots < CAP) & (slots // held == t)
+    codes = jnp.where(mine, ids * block_size + slots % held, -1)
+    codes = jnp.concatenate(
+        [lax.dynamic_index_in_dim(codes, t ^ k, 0, keepdims=False) for k in (0, 2, 1, 3)], axis=0
+    ).T
+    slot_rows = experts * block_size
+    row_code = jnp.arange(slot_rows).reshape(-1, 1)
+    group_flops = 2 * slot_rows * features * (4 * ROWS + features)
+
+    def to_experts(kernel, rows, *peaks):
+        return run(
+            kernel,
+            [((slot_rows, features), BF)],
+            (row_code, codes, *rows, perm, *peaks),
+            group_flops,
+            scratch=[pltpu.VMEM((4 * ROWS, features), BF)],
+        )[0].reshape(experts, block_size, features)
+
+    def exchange(both):
+        return lax.all_to_all(both, "dp", split_axis=0, concat_axis=0, tiled=True)
+
+    group_scratch = pltpu.VMEM((4 * ROWS, features), BF)
+    pair_out = [((2 * ROWS, features), F32), ((2 * ROWS, features), BF)]
+
+    def attend(normed, full, at):
+        return run(
+            functools.partial(attend_kernel, at),
+            [((4 * ROWS, qkv_cols), BF), ((4 * ROWS, head_cols), BF)]
+            + pair_out
+            + [((1, 128), F32)],
+            (live_group, *normed, full),
+            0,
+            scratch=[group_scratch],
+            scalars=1,
+        )
+
+    def pack_shapes(columns):
+        return [((features // 2, columns), BF)] * 2 + pair_out
+
+    def attend_back(low, normed, mixed, attended, full, at):
+        return run(
+            functools.partial(attend_back_kernel, at),
+            pack_shapes(4 * head_cols),
+            (*low, *normed, mixed, attended, full),
+            8e9,
+            scratch=[
+                group_scratch,
+                pltpu.VMEM((4 * ROWS, head_cols), BF),
+                pltpu.VMEM((4 * ROWS, qkv_cols), BF),
+            ],
+        )
+
+    def over_group(own, sib):
+        near, send = run(pair_add_kernel, [row, row_low], (own, swap(sib, core=1)), ROWS)
+        return near, swap(send, y=1)
+
+    def join(values, own, far, gain):
+        return run(join_norm_kernel, [row, row_low], (values, own, far, gain), ROWS)
+
+    def norm_back(values, upstream, own, far, gain):
+        return run(
+            norm_back_kernel,
+            [row, row_low, ((1, features), F32)],
+            (values, upstream, own, far, gain),
+            ROWS,
+        )
+
+    full_one = stacked(hold([z_one, swap(z_one, x=1)], first_group))
+    small_rows = full_one[:, : 4 + experts].T
+    gains = [small_rows[i : i + 1].astype(F32) for i in range(4)]
+    router = dot(small_rows[4:], perm, 1, 0).astype(BF)
+
+    normed_one = run(norm_kernel, [row_low] * 4, (gains[0], *first_group), ROWS)
+    mixed_one, att_one, own, sib, peak_one = attend(normed_one, full_one, small.shape[1])
+    near, far = over_group(own, sib)
+    one, normed = join(start, near, hold(far, raw_late), gains[1])
+    normed_mlp = spread(normed)
+    z_mlp, z_late = run(
+        order_kernel,
+        [((4 * width, 2 * ff_cols), BF), ((4 * width, 4 * head_cols), BF)],
+        (jnp.stack([z_index ^ k for k in range(4)]).astype(jnp.int32), hold(raw_late, one)),
+        features,
+        scalars=1,
+    )
+    x_mlp = swap(z_mlp, x=1)
+    e_pack = hold(e_pack, z_mlp)
+    e_own = lax.all_to_all(e_pack, "dp", split_axis=0, concat_axis=0, tiled=True)
+    e_own = e_own.reshape(features, wide)
+    e_own = hold(e_own, normed_mlp[1])
+    far = [swap(e_own[i * 2 * width : (i + 1) * 2 * width], y=1) for i in range(4)]
+    e_far = far
+    grad_sent = to_experts(dispatch_kernel, spread(hold(grad_low, normed)))
+    full_mlp = stacked([z_mlp, x_mlp])
+    x_late = swap(hold(z_late, full_mlp), x=1)
+    ats = (0, ff_cols)
+    act, slope, own, sib = run(
+        functools.partial(mlp_kernel, ats),
+        [((4 * ROWS, ff_cols), BF)] * 2 + pair_out,
+        (*hold(normed_mlp, grad_sent), full_mlp),
+        0,
+        scratch=[group_scratch],
+    )
+    near, far = over_group(own, sib)
+    two, normed = join(one, near, far, gains[2])
+    normed_two = spread(normed)
+    full_late = stacked([z_late, x_late])
+    mixed_two, att_two, own, sib, peak_two = attend(hold(normed_two, e_far[0]), full_late, 0)
+    near, far = over_group(own, sib)
+    three, normed = join(two, near, far, gains[3])
+    tokens_sent = to_experts(token_kernel, spread(normed), peak_one, peak_two)
+    both = exchange(jnp.concatenate([grad_sent, tokens_sent], axis=1))
+    grad_slots, tokens, peaks = run(
+        collect_kernel,
+        [((slot_rows, features), BF)] * 2 + [((2, 128), F32)],
+        (hold(both, *e_far),),
+        0,
+    )
+    far_slots, far_tokens = swap(grad_slots, core=1), swap(tokens, core=1)
+    number = d.astype(jnp.int32).reshape(1)
+    near_heads = head_cols // HD
+    roots = clip_root(peaks[:, :near_heads])
+    slot_out = [((slot_rows, features), F32), ((slot_rows, features), BF)]
+    res_own, res_sib, eg_own, eg_sib, *e_packs = run(
+        expert_kernel,
+        slot_out + slot_out + ([((features, ff_cols), BF)] + half_shape) * 2,
+        (number, tokens, far_tokens, grad_slots, far_slots, router)
+        + (e_own, *e_far),
+        8 * 2 * slot_rows * features * 2 * ff_cols,
+        scalars=1,
+        scratch=[
+            pltpu.VMEM((2, 2 * slot_rows, ff_cols), BF),
+            pltpu.VMEM((2, 2 * slot_rows, ff_cols), BF),
+            pltpu.VMEM((2 * slot_rows, features), BF),
+            pltpu.VMEM((2 * slot_rows, features), BF),
+            pltpu.VMEM((2, features, wide), BF),
+        ],
+        mib=44,
+    )
+    res_far, eg_far = swap(res_sib, core=1), swap(eg_sib, core=1)
+    up_got = [swap(e_packs[1], y=1)]
+    both, grad_router = run(
+        answer_kernel,
+        [((experts, 2 * block_size, features), BF), ((experts, features), F32)],
+        (number, tokens, grad_slots, router, res_own, res_far, eg_own, eg_far, perm),
+        4 * slot_rows * features**2,
+        scalars=1,
+    )
+    both = hold(both, up_got)
+    e_packs = hold(e_packs, both)
+    both = exchange(both)
+    up_got.append(swap(e_packs[2], y=1))
+    down_got = [swap(e_packs[4], y=1), swap(e_packs[5], y=1)]
+    both = hold(both, up_got, down_got)
+
+    def combine(which, both):
+        return run(
+            functools.partial(combine_kernel, which),
+            [((2 * ROWS, features), F32), ((2 * ROWS, features), BF)],
+            (row_code, codes, perm, both),
+            group_flops,
+            scratch=[pltpu.VMEM((slot_rows, features), BF)],
+        )
+
+    own, sib = combine(0, both)
+    back_own, back_far = over_group(own, sib)
+    grad_three, low, gain_four = norm_back(
+        three, grad_four, back_own, back_far, gains[3]
+    )
+    e_sum = run(
+        add_pack_kernel,
+        [((features, wide), BF)],
+        (e_packs[0], *hold(up_got, low), e_packs[3], *down_got),
+        0,
+    )[0].reshape(experts, width, wide)
+    e_back = lax.all_to_all(e_sum, "dp", split_axis=0, concat_axis=0, tiled=True)
+    low = spread(low)
+    *second, own, sib = attend_back(
+        low, normed_two, mixed_two, att_two, full_late, 0
+    )
+    second = scatter_start(second)
+    near, far = over_group(own, sib)
+    grad_two, low, gain_three = norm_back(
+        two, grad_three, near, far, gains[2]
+    )
+    low = spread(low)
+    *mlp, own, sib = run(
+        functools.partial(mlp_back_kernel, ats),
+        pack_shapes(2 * ff_cols),
+        (*hold(low, e_back), *normed_mlp, act, slope, full_mlp),
+        0,
+        scratch=[group_scratch, pltpu.VMEM((4 * ROWS, ff_cols), BF)],
+    )
+    mlp = scatter_start(mlp)
+    near, send = run(pair_add_kernel, [row, row_low], (own, swap(sib, core=1)), ROWS)
+    far = swap(send, y=1)
+    mixed_own, mixed_sib = combine(1, hold(both, second[1]))
+    second = scatter_late(scatter_middle(hold(second, mixed_own)))
+    mixed_own, mixed_send = run(
+        pair_add_kernel, [row, row_low], (mixed_own, swap(mixed_sib, core=1)), ROWS
+    )
+    grad_one, low, gain_two = norm_back(
+        one, grad_two, near, hold(far, mixed_send), gains[1]
+    )
+    low = spread(low)
+    mixed_far = swap(hold(mixed_send, low), y=1)
+    *first, own, sib = attend_back(
+        hold(low, mlp),
+        normed_one,
+        mixed_one,
+        att_one,
+        full_one,
+        small.shape[1],
+    )
+    mlp = scatter_late(scatter_middle(mlp))
+    first = scatter_start(first)
+    near, far = over_group(own, hold(sib, mixed_far, second))
+    grad_zero, _, gain_one = norm_back(start, grad_one, near, hold(far, first), gains[0])
+    gains_sum = run(
+        small_kernel,
+        [((8, 16, width), F32)],
+        (gain_one, gain_two, gain_three, gain_four, grad_router),
+        0,
+    )[0]
+    gains_sum = gains_sum + swap(gains_sum, core=1)
+    gains_sum = gains_sum + swap(gains_sum, y=1)
+    gains_sum = gains_sum[:4] + swap(gains_sum[4:], x=1)
+    near_first, got_first = first
+    shape = (width, 4 * head_cols)
+    first = run(
+        sum_two_more,
+        [(shape, F32)] + [((width + 32, shape[1]), BF)] * 3,
+        (hold(near_first, mlp), got_first, gains_sum),
+        0,
+    )
+    first = scatter_late(first)
+    block_output = run(
+        finish_kernel,
+        [((L, features), F32)],
+        (live_here, three, mixed_own, mixed_far, perm),
+        6 * ROWS * features**2,
+        scalars=1,
+    )[0]
+    up_g = e_back[:, :, :ff_cols].astype(F32)
+    down_g = jnp.swapaxes(e_back[:, :, ff_cols:], 1, 2).astype(F32)
+    input_grad = run(
+        leave_kernel,
+        [((L, features), F32)],
+        (hold(grad_zero, first[0]), perm),
+        6 * ROWS * features**2,
+    )[0]
+    second = scatter_end(second, qkv_cols)
+    mlp = scatter_end(mlp, ff_cols)
+    first = hold(first, up_g, down_g, block_output, input_grad, second, mlp)
+    *first, tail = run(
+        sum_three_more,
+        [((width, qkv_cols), F32), ((width, head_cols), F32), ((16, width), F32)],
+        (*first, gains_sum),
+        0,
+    )
+
+    return (
+        block_output,
+        input_grad,
+        tail[0],
+        first[0].reshape(first_qkv.shape),
+        first[1].T,
+        tail[1],
+        mlp[0],
+        mlp[1].T,
+        tail[2],
+        second[0].reshape(second_qkv.shape),
+        second[1].T,
+        tail[3],
+        tail[4 : 4 + experts].T,
+        up_g,
+        down_g,
+        clip_columns(first_qkv, roots[0], HD),
+        clip_columns(second_qkv, roots[1], HD),
+        roots,
+    )
+
+
 def solution(mesh):
     placed = (
         P(("dp", "tensor"), None),
@@ -412,8 +1227,9 @@
         P("dp"),
         P(("dp", "tensor"), None),
     )
+    quick = mesh.shape["dp"] == 8 and mesh.shape["tensor"] == 4
     return jax.shard_map(
-        local,
+        fast_local if quick else local,
         mesh=mesh,
         in_specs=placed,
         out_specs=(

time: 2100 us -> 594 us (0.28)
  waiting for transfers between devices: 1280 us -> 277 us
  blocking collectives: 377 us -> 0 us
  matrix products: 142 us -> 1.32 us
  local copies, waits for them, and re-layouts: 191 us -> 85.7 us
  Pallas kernels: 0 us -> 92.5 us
  starting transfers between devices: 13.7 us -> 99.9 us
  other arithmetic: 62.2 us -> 12.7 us
    reduce_scatter x6 -> x0, waiting for transfers between devices: 919 us -> none  [the longest x1 317 us: local(): lax.psum_scatter(grad_expert_up, 'dp', scatter_dimension=1, tiled=True)]
    all_gather x12 -> x1, waiting for transfers between devices: 340 us -> 0.01 us  [fast_local(): lax.all_gather(pack_late, 'dp', axis=0, tiled=True, axis_index_groups=lines)]
    ppermute x0 -> x73, waiting for transfers between devices: none -> 277 us  [swap(): return lax.ppermute(values, AXES, pairs)]
    unnamed x9 -> x0, blocking collectives: 180 us -> none
    all_gather x5 -> x0, blocking collectives: 163 us -> none  [the longest x1 37.2 us: moe_fetch(): lax.all_gather(second_qkv, 'dp', axis=0, tiled=True)]
    dot_general x34 -> x1, matrix products: 129 us -> 1.32 us  [dot(): lax.dot_general(a, b, (((ca,), (cb,)), ((), ())), preferred_element_type=...]
    pallas_call x0 -> x47, Pallas kernels: none -> 92.5 us  [run(): pl.pallas_call(kernel, out_shape=shapes, in_specs=[SM] * scalars + [VM] *...]
    ppermute x0 -> x73, starting transfers between devices: none -> 67.4 us  [swap(): return lax.ppermute(values, AXES, pairs)]
  transfers between devices with their start and end apart: 29 -> 78, of which waited for: 20 -> 45; matrix products, arithmetic and copies ran while one was open for 12% -> 4% of each run, Pallas kernels for 0% -> 10%
where the time goes in v3:
time: 594 us; the launch traced here: 586 us
  waiting for transfers between devices  277 us (47%)
  starting transfers between devices  99.9 us (17%)
  Pallas kernels  92.5 us (16%)
  local copies, waits for them, and re-layouts  85.7 us (14%)
  between operations  16.5 us (3%)
  other arithmetic  12.7 us (2%)
    ppermute x73, waiting for transfers between devices, swap(): return lax.ppermute(values, AXES, pairs)  277 us
    pallas_call x47, Pallas kernels, run(): pl.pallas_call(kernel, out_shape=shapes, in_specs=[SM] * scalars + [VM] *...  92.5 us
    unnamed x346, local copies, waits for them, and re-layouts  78.5 us
    ppermute x73, starting transfers between devices, swap(): return lax.ppermute(values, AXES, pairs)  67.4 us
    all_to_all x1, starting transfers between devices, fast_local(): lax.all_to_all(e_pack, 'dp', split_axis=0, concat_axis=0, tiled=True)  16.2 us
  transfers between devices with their start and end apart: 78, of which 45 were waited for; matrix products, arithmetic and copies ran while one was open for 4% of the time, Pallas kernels for 10%

profile of v3, /device:TPU:0, one launch (start us, length us, event | category | flops | bytes accessed | tf_op | source)
XLA Modules:
  0.0 586.1 jit_solution(16148348687962465246)
XLA Ops:
  13.5 3.1 collective-permute-start
  19.2 4.5 collective-permute-done.refs_1_
  23.7 13.5 %collective-permute-done.1.refs_2_ = bf16[96,896]{1,0:T(8,128)(2,1)S(1)} collective-permute-done((bf16[96,896]{1,0:T(8,128)(2,1)S(1)}, bf16[96,896]{1,0:T(8,128)(2,1)S(1)}, u32[]{:S(2)}, u32[]{:S(2)}) %collective-permute-start.1) | collective-permute-done | bytes 172064 | tf_op jit(solution)/shard_map/ppermute | solution.py:409
  45.3 4.7 collective-permute-done.4.refs_1_
  59.5 5.5 shard_map.318
  73.9 3.3 pad_maximum_fusion
  77.1 4.9 collective-permute-done.8.far_ref
  86.2 16.2 %all-to-all-start = ((bf16[8,96,1536]{2,1,0:T(8,128)(2,1)}), bf16[8,96,1536]{2,1,0:T(8,128)(2,1)}, u32[]{:S(2)}, u32[]{:S(2)}) async-start(bf16[8,96,1536]{2,1,0:T(8,128)(2,1)} %pad_maximum_fusion), calls=%async_computation | async-start | bytes 4718592 | tf_op jit(solution)/shard_map/all_to_all | solution.py:1013
  107.3 7.6 %collective-permute-done.9.b1 = bf16[208,768]{1,0:T(8,128)(2,1)S(1)} collective-permute-done((bf16[208,768]{1,0:T(8,128)(2,1)S(1)}, bf16[208,768]{1,0:T(8,128)(2,1)S(1)}, u32[]{:S(2)}, u32[]{:S(2)}) %collective-permute-start.9) | collective-permute-done | bytes 319520 | tf_op jit(solution)/shard_map/ppermute | solution.py:409
  114.9 4.6 collective-permute-done.12.p1
  121.4 2.6 shard_map.322
  124.9 30.1 %collective-permute-done.15.refs_1_ = bf16[384,1536]{1,0:T(8,128)(2,1)} collective-permute-done((bf16[384,1536]{1,0:T(8,128)(2,1)S(1)}, bf16[384,1536]{1,0:T(8,128)(2,1)}, u32[]{:S(2)}, u32[]{:S(2)}) %collective-permute-start.15) | collective-permute-done | bytes 1179680 | tf_op jit(solution)/shard_map/ppermute | solution.py:409
  156.4 2.8 shard_map.325
  165.6 7.7 %collective-permute-done.17.far_ref = bf16[208,768]{1,0:T(8,128)(2,1)S(1)} collective-permute-done((bf16[208,768]{1,0:T(8,128)(2,1)S(1)}, bf16[208,768]{1,0:T(8,128)(2,1)S(1)}, u32[]{:S(2)}, u32[]{:S(2)}) %collective-permute-start.17) | collective-permute-done | bytes 319520 | tf_op jit(solution)/shard_map/ppermute | solution.py:409
  176.6 2.8 fusion.22
  180.0 5.9 %collective-permute-done.18.a1 = bf16[208,768]{1,0:T(8,128)(2,1)} collective-permute-done((bf16[208,768]{1,0:T(8,128)(2,1)}, bf16[208,768]{1,0:T(8,128)(2,1)}, u32[]{:S(2)}, u32[]{:S(2)}) %collective-permute-start.18) | collective-permute-done | bytes 319520 | tf_op jit(solution)/shard_map/ppermute | solution.py:409
  187.7 9.1 %collective-permute-done.21.rest_1_ = bf16[192,1536]{1,0:T(8,128)(2,1)S(1)} collective-permute-done((bf16[192,1536]{1,0:T(8,128)(2,1)S(1)}, bf16[192,1536]{1,0:T(8,128)(2,1)S(1)}, u32[]{:S(2)}, u32[]{:S(2)}) %collective-permute-start.21) | collective-permute-done | bytes 589856 | tf_op jit(solution)/shard_map/ppermute | solution.py:409
  197.6 5.2 shard_map.329
  209.9 8.1 %collective-permute-done.24.far_ref = bf16[208,768]{1,0:T(8,128)(2,1)S(1)} collective-permute-done((bf16[208,768]{1,0:T(8,128)(2,1)S(1)}, bf16[208,768]{1,0:T(8,128)(2,1)S(1)}, u32[]{:S(2)}, u32[]{:S(2)}) %collective-permute-start.24) | collective-permute-done | bytes 319520 | tf_op jit(solution)/shard_map/ppermute | solution.py:409
  220.7 7.2 %collective-permute-done.25.p1 = bf16[208,768]{1,0:T(8,128)(2,1)S(1)} collective-permute-done((bf16[208,768]{1,0:T(8,128)(2,1)S(1)}, bf16[208,768]{1,0:T(8,128)(2,1)S(1)}, u32[]{:S(2)}, u32[]{:S(2)}) %collective-permute-start.25) | collective-permute-done | bytes 319520 | tf_op jit(solution)/shard_map/ppermute | solution.py:409
  232.3 5.0 all-to-all-start.1
  240.9 12.9 %collective-permute-done.28.rest_2_ = bf16[192,1536]{1,0:T(8,128)(2,1)S(1)} collective-permute-done((bf16[192,1536]{1,0:T(8,128)(2,1)}, bf16[192,1536]{1,0:T(8,128)(2,1)S(1)}, u32[]{:S(2)}, u32[]{:S(2)}) %collective-permute-start.28) | collective-permute-done | bytes 589856 | tf_op jit(solution)/shard_map/ppermute | solution.py:409
  254.6 11.8 %collective-permute-done.29.rest_3_ = bf16[192,1536]{1,0:T(8,128)(2,1)S(1)} collective-permute-done((bf16[192,1536]{1,0:T(8,128)(2,1)}, bf16[192,1536]{1,0:T(8,128)(2,1)S(1)}, u32[]{:S(2)}, u32[]{:S(2)}) %collective-permute-start.29) | collective-permute-done | bytes 589856 | tf_op jit(solution)/shard_map/ppermute | solution.py:409
  267.2 10.7 %collective-permute-done.30.rest_4_ = bf16[192,1536]{1,0:T(8,128)(2,1)S(1)} collective-permute-done((bf16[192,1536]{1,0:T(8,128)(2,1)}, bf16[192,1536]{1,0:T(8,128)(2,1)S(1)}, u32[]{:S(2)}, u32[]{:S(2)}) %collective-permute-start.30) | collective-permute-done | bytes 589856 | tf_op jit(solution)/shard_map/ppermute | solution.py:409
  284.7 16.6 %shard_map.334 = (f32[448,768]{1,0:T(8,128)}, bf16[448,768]{1,0:T(8,128)(2,1)S(1)}, f32[448,768]{1,0:T(8,128)}, bf16[448,768]{1,0:T(8,128)(2,1)S(1)}, bf16[768,7...) custom-call(s32[1]{0:T(128)} %bitcast.28.number, ...), custom_call_target="tpu_custom_call" | custom-call | flops 1000 | bytes 1000 | tf_op jit(solution)/shard_map/pallas_call | solution.py:419
  312.1 6.1 %collective-permute-done.35.up0 = bf16[384,768]{1,0:T(8,128)(2,1)S(1)} collective-permute-done((bf16[384,768]{1,0:T(8,128)(2,1)S(1)}, bf16[384,768]{1,0:T(8,128)(2,1)S(1)}, u32[]{:S(2)}, u32[]{:S(2)}) %collective-permute-start.35) | collective-permute-done | bytes 589856 | tf_op jit(solution)/shard_map/ppermute | solution.py:409
  319.0 5.7 all-to-all-start.2
  328.2 12.9 %collective-permute-done.36.up1 = bf16[384,768]{1,0:T(8,128)(2,1)S(1)} collective-permute-done((bf16[384,768]{1,0:T(8,128)(2,1)}, bf16[384,768]{1,0:T(8,128)(2,1)S(1)}, u32[]{:S(2)}, u32[]{:S(2)}) %collective-permute-start.36) | collective-permute-done | bytes 589856 | tf_op jit(solution)/shard_map/ppermute | solution.py:409
  342.0 11.8 %collective-permute-done.37.down0 = bf16[384,768]{1,0:T(8,128)(2,1)S(1)} collective-permute-done((bf16[384,768]{1,0:T(8,128)(2,1)}, bf16[384,768]{1,0:T(8,128)(2,1)S(1)}, u32[]{:S(2)}, u32[]{:S(2)}) %collective-permute-start.37) | collective-permute-done | bytes 589856 | tf_op jit(solution)/shard_map/ppermute | solution.py:409
  354.6 9.8 %collective-permute-done.38.down1 = bf16[384,768]{1,0:T(8,128)(2,1)S(1)} collective-permute-done((bf16[384,768]{1,0:T(8,128)(2,1)}, bf16[384,768]{1,0:T(8,128)(2,1)S(1)}, u32[]{:S(2)}, u32[]{:S(2)}) %collective-permute-start.38) | collective-permute-done | bytes 589856 | tf_op jit(solution)/shard_map/ppermute | solution.py:409
  365.3 3.0 shard_map.336
  372.2 8.0 %collective-permute-done.40.far_ref = bf16[208,768]{1,0:T(8,128)(2,1)S(1)} collective-permute-done((bf16[208,768]{1,0:T(8,128)(2,1)S(1)}, bf16[208,768]{1,0:T(8,128)(2,1)S(1)}, u32[]{:S(2)}, u32[]{:S(2)}) %collective-permute-start.40) | collective-permute-done | bytes 319520 | tf_op jit(solution)/shard_map/ppermute | solution.py:409
  383.8 5.7 all-to-all-start.3
  391.0 7.1 %collective-permute-done.41.g1 = bf16[208,768]{1,0:T(8,128)(2,1)S(1)} collective-permute-done((bf16[208,768]{1,0:T(8,128)(2,1)}, bf16[208,768]{1,0:T(8,128)(2,1)S(1)}, u32[]{:S(2)}, u32[]{:S(2)}) %collective-permute-start.41) | collective-permute-done | bytes 319520 | tf_op jit(solution)/shard_map/ppermute | solution.py:409
  406.2 11.8 %shard_map.339 = (bf16[384,768]{1,0:T(8,128)(2,1)S(1)}, bf16[384,768]{1,0:T(8,128)(2,1)}, f32[416,768]{1,0:T(8,128)S(1)}, bf16[416,768]{1,0:T(8,128)(2,1)S(1)}) custom-call(bf16[208,768]{1,0:T(8,128)(2,1)S(1)} %copy-done.153, bf16[208,768]{1,0:T(8,128)(2,1)S(1)} %collective-permute-done.41.g1, bf16[208,768]{1,0:T(8,128)(2,1)S(1)} %collective-permute-done.42.g2, ...), custom_call_target="tpu_custom_call" | custom-call | flops 8000000000 | bytes 1000 | tf_op jit(solution)/shard_map/pallas_call | solution.py:419
  421.8 8.1 %collective-permute-done.47.far_ref = bf16[208,768]{1,0:T(8,128)(2,1)S(1)} collective-permute-done((bf16[208,768]{1,0:T(8,128)(2,1)S(1)}, bf16[208,768]{1,0:T(8,128)(2,1)S(1)}, u32[]{:S(2)}, u32[]{:S(2)}) %collective-permute-start.47) | collective-permute-done | bytes 319520 | tf_op jit(solution)/shard_map/ppermute | solution.py:409
  434.1 6.5 %collective-permute-done.48.g1 = bf16[208,768]{1,0:T(8,128)(2,1)S(1)} collective-permute-done((bf16[208,768]{1,0:T(8,128)(2,1)S(1)}, bf16[208,768]{1,0:T(8,128)(2,1)S(1)}, u32[]{:S(2)}, u32[]{:S(2)}) %collective-permute-start.48) | collective-permute-done | bytes 319520 | tf_op jit(solution)/shard_map/ppermute | solution.py:409
  454.9 5.0 shard_map.345
  461.1 2.8 shard_map.340
  466.5 7.7 %collective-permute-done.52.far_ref = bf16[208,768]{1,0:T(8,128)(2,1)S(1)} collective-permute-done((bf16[208,768]{1,0:T(8,128)(2,1)S(1)}, bf16[208,768]{1,0:T(8,128)(2,1)S(1)}, u32[]{:S(2)}, u32[]{:S(2)}) %collective-permute-start.52) | collective-permute-done | bytes 319520 | tf_op jit(solution)/shard_map/ppermute | solution.py:409
  476.3 7.0 %collective-permute-done.53.g1 = bf16[208,768]{1,0:T(8,128)(2,1)S(1)} collective-permute-done((bf16[208,768]{1,0:T(8,128)(2,1)S(1)}, bf16[208,768]{1,0:T(8,128)(2,1)S(1)}, u32[]{:S(2)}, u32[]{:S(2)}) %collective-permute-start.53) | collective-permute-done | bytes 319520 | tf_op jit(solution)/shard_map/ppermute | solution.py:409
  492.4 10.2 %shard_map.349 = (bf16[384,768]{1,0:T(8,128)(2,1)S(1)}, bf16[384,768]{1,0:T(8,128)(2,1)S(1)}, f32[416,768]{1,0:T(8,128)S(1)}, bf16[416,768]{1,0:T(8,128)(2,1)S(1)}) custom-call(bf16[208,768]{1,0:T(8,128)(2,1)S(1)} %get-tuple-element.277.g0, bf16[208,768]{1,0:T(8,128)(2,1)S(1)} %collective-permute-done.53.g1, ...), custom_call_target="tpu_custom_call" | custom-call | flops 8000000000 | bytes 1000 | tf_op jit(solution)/shard_map/pallas_call | solution.py:419
  509.3 11.8 %collective-permute-done.63.got = bf16[384,768]{1,0:T(8,128)(2,1)S(1)} collective-permute-done((bf16[384,768]{1,0:T(8,128)(2,1)S(1)}, bf16[384,768]{1,0:T(8,128)(2,1)S(1)}, u32[]{:S(2)}, u32[]{:S(2)}) %collective-permute-start.63) | collective-permute-done | bytes 589856 | tf_op jit(solution)/shard_map/ppermute | solution.py:409
  533.1 2.7 collective-permute-done.68
  543.0 8.4 %collective-permute-done.65.r2 = bf16[96,1536]{1,0:T(8,128)(2,1)S(1)} collective-permute-done((bf16[96,1536]{1,0:T(8,128)(2,1)}, bf16[96,1536]{1,0:T(8,128)(2,1)S(1)}, u32[]{:S(2)}, u32[]{:S(2)}) %collective-permute-start.65) | collective-permute-done | bytes 294944 | tf_op jit(solution)/shard_map/ppermute | solution.py:409
  552.3 6.2 %collective-permute-start.70 = (bf16[128,768]{1,0:T(8,128)(2,1)S(1)}, bf16[128,768]{1,0:T(8,128)(2,1)S(1)}, u32[]{:S(2)}, u32[]{:S(2)}) collective-permute-start(bf16[128,768]{1,0:T(8,128)(2,1)S(1)} %get-tuple-element.311), channel_id=1, source_target_pairs={{0,8},{1,9},{2,10},{3,11},{4,12},{5,13},{6,14},{7,15},{8,0},{9,1},... | collective-permute-start | bytes 589832 | tf_op jit(solution)/shard_map/ppermute | solution.py:409
  561.0 4.3 convert_bitcast_fusion
  570.4 5.3 collective-permute-done.71.r2
  (549 shorter events, 195.4 us)
Async XLA Ops:
  7.3 74.7 %all-gather.2.cloned.1.call-start = ((), (), s32[]{:S(2)}) async-start(), calls=%async_computation.4 | async-start | bytes 2211840 | tf_op jit(solution)/shard_map/all_gather | solution.py:890
  13.5 10.2 %collective-permute-start = (bf16[96,896]{1,0:T(8,128)(2,1)S(1)}, bf16[96,896]{1,0:T(8,128)(2,1)S(1)}, u32[]{:S(2)}, u32[]{:S(2)}) collective-permute-start(bf16[96,896]{1,0:T(8,128)(2,1)S(1)} %shard_map.314.refs_0_), channel_id=1, source_target_pairs={{0,8},{1,9},{2,10},{3,11},{4,12},{5,13},{6,14},{7,15},{8,0},{9,1},... | collective-permute-start | bytes 516104 | tf_op jit(solution)/shard_map/ppermute | solution.py:409
  16.6 20.6 %collective-permute-start.1 = (bf16[96,896]{1,0:T(8,128)(2,1)S(1)}, bf16[96,896]{1,0:T(8,128)(2,1)S(1)}, u32[]{:S(2)}, u32[]{:S(2)}) collective-permute-start(bf16[96,896]{1,0:T(8,128)(2,1)S(1)} %shard_map.314.refs_0_), channel_id=1, source_target_pairs={{0,16},{1,17},{2,18},{3,19},{4,20},{5,21},{6,22},{7,23},{8,24},{9,... | collective-permute-start | bytes 516104 | tf_op jit(solution)/shard_map/ppermute | solution.py:409
  19.2 18.0 %collective-permute-start.2 = (bf16[96,896]{1,0:T(8,128)(2,1)S(1)}, bf16[96,896]{1,0:T(8,128)(2,1)S(1)}, u32[]{:S(2)}, u32[]{:S(2)}) collective-permute-start(bf16[96,896]{1,0:T(8,128)(2,1)S(1)} %shard_map.314.refs_0_), channel_id=1, source_target_pairs={{0,24},{1,25},{2,26},{3,27},{4,28},{5,29},{6,30},{7,31},{8,16},{9,... | collective-permute-start | bytes 516104 | tf_op jit(solution)/shard_map/ppermute | solution.py:409
  37.2 14.5 %collective-permute-start.3 = (bf16[384,896]{1,0:T(8,128)(2,1)S(1)}, bf16[384,896]{1,0:T(8,128)(2,1)S(1)}, u32[]{:S(2)}, u32[]{:S(2)}) collective-permute-start(bf16[384,896]{1,0:T(8,128)(2,1)S(1)} %shard_map.315.refs_0_), channel_id=1, source_target_pairs={{0,4},{1,5},{2,6},{3,7},{4,0},{5,1},{6,2},{7,3},{8,12},{9,13},{10,... | collective-permute-start | bytes 2064392 | tf_op jit(solution)/shard_map/ppermute | solution.py:409
  72.2 9.8 %collective-permute-start.8 = (bf16[208,768]{1,0:T(8,128)(2,1)S(1)}, bf16[208,768]{1,0:T(8,128)(2,1)S(1)}, u32[]{:S(2)}, u32[]{:S(2)}) collective-permute-start(bf16[208,768]{1,0:T(8,128)(2,1)S(1)} %get-tuple-element.183), channel_id=1, source_target_pairs={{0,2},{1,3},{2,0},{3,1},{4,6},{5,7},{6,4},{7,5},{8,10},{9,11},{10,... | collective-permute-start | bytes 958472 | tf_op jit(solution)/shard_map/ppermute | solution.py:409
  86.2 90.5 %all-to-all-start = ((bf16[8,96,1536]{2,1,0:T(8,128)(2,1)}), bf16[8,96,1536]{2,1,0:T(8,128)(2,1)}, u32[]{:S(2)}, u32[]{:S(2)}) async-start(bf16[8,96,1536]{2,1,0:T(8,128)(2,1)} %pad_maximum_fusion), calls=%async_computation | async-start | bytes 4718592 | tf_op jit(solution)/shard_map/all_to_all | solution.py:1013
  102.4 52.6 %collective-permute-start.15 = (bf16[384,1536]{1,0:T(8,128)(2,1)S(1)}, bf16[384,1536]{1,0:T(8,128)(2,1)}, u32[]{:S(2)}, u32[]{:S(2)}) collective-permute-start(bf16[384,1536]{1,0:T(8,128)(2,1)S(1)} %get-tuple-element.194.refs_0_), channel_id=1, source_target_pairs={{0,4},{1,5},{2,6},{3,7},{4,0},{5,1},{6,2},{7,3},{8,12},{9,13},{10,... | collective-permute-start | bytes 3538952 | tf_op jit(solution)/shard_map/ppermute | solution.py:409
  104.5 10.5 %collective-permute-start.9 = (bf16[208,768]{1,0:T(8,128)(2,1)S(1)}, bf16[208,768]{1,0:T(8,128)(2,1)S(1)}, u32[]{:S(2)}, u32[]{:S(2)}) collective-permute-start(bf16[208,768]{1,0:T(8,128)(2,1)S(1)} %get-tuple-element.189.b0), channel_id=1, source_target_pairs={{0,2},{1,3},{2,0},{3,1},{4,6},{5,7},{6,4},{7,5},{8,10},{9,11},{10,... | collective-permute-start | bytes 958472 | tf_op jit(solution)/shard_map/ppermute | solution.py:409
  106.0 13.5 %collective-permute-start.12 = (bf16[208,768]{1,0:T(8,128)(2,1)S(1)}, bf16[208,768]{1,0:T(8,128)(2,1)}, u32[]{:S(2)}, u32[]{:S(2)}) collective-permute-start(bf16[208,768]{1,0:T(8,128)(2,1)S(1)} %copy-done.109), channel_id=1, source_target_pairs={{0,2},{1,3},{2,0},{3,1},{4,6},{5,7},{6,4},{7,5},{8,10},{9,11},{10,... | collective-permute-start | bytes 958472 | tf_op jit(solution)/shard_map/ppermute | solution.py:409
  106.7 18.1 %collective-permute-start.10 = (bf16[208,768]{1,0:T(8,128)(2,1)S(1)}, bf16[208,768]{1,0:T(8,128)(2,1)S(1)}, u32[]{:S(2)}, u32[]{:S(2)}) collective-permute-start(bf16[208,768]{1,0:T(8,128)(2,1)S(1)} %get-tuple-element.189.b0), channel_id=1, source_target_pairs={{0,1},{1,0},{2,3},{3,2},{4,5},{5,4},{6,7},{7,6},{8,9},{9,8},{10,11... | collective-permute-start | bytes 958472 | tf_op jit(solution)/shard_map/ppermute | solution.py:409
  106.8 12.9 %collective-permute-start.13 = (bf16[208,768]{1,0:T(8,128)(2,1)S(1)}, bf16[208,768]{1,0:T(8,128)(2,1)S(1)}, u32[]{:S(2)}, u32[]{:S(2)}) collective-permute-start(bf16[208,768]{1,0:T(8,128)(2,1)S(1)} %copy-done.109), channel_id=1, source_target_pairs={{0,1},{1,0},{2,3},{3,2},{4,5},{5,4},{6,7},{7,6},{8,9},{9,8},{10,11... | collective-permute-start | bytes 958472 | tf_op jit(solution)/shard_map/ppermute | solution.py:409
  114.9 9.9 %collective-permute-start.11 = (bf16[208,768]{1,0:T(8,128)(2,1)S(1)}, bf16[208,768]{1,0:T(8,128)(2,1)S(1)}, u32[]{:S(2)}, u32[]{:S(2)}) collective-permute-start(bf16[208,768]{1,0:T(8,128)(2,1)S(1)} %collective-permute-done.9.b1), channel_id=1, source_target_pairs={{0,1},{1,0},{2,3},{3,2},{4,5},{5,4},{6,7},{7,6},{8,9},{9,8},{10,11... | collective-permute-start | bytes 958472 | tf_op jit(solution)/shard_map/ppermute | solution.py:409
  163.6 9.6 %collective-permute-start.17 = (bf16[208,768]{1,0:T(8,128)(2,1)S(1)}, bf16[208,768]{1,0:T(8,128)(2,1)S(1)}, u32[]{:S(2)}, u32[]{:S(2)}) collective-permute-start(bf16[208,768]{1,0:T(8,128)(2,1)S(1)} %get-tuple-element.198), channel_id=1, source_target_pairs={{0,2},{1,3},{2,0},{3,1},{4,6},{5,7},{6,4},{7,5},{8,10},{9,11},{10,... | collective-permute-start | bytes 958472 | tf_op jit(solution)/shard_map/ppermute | solution.py:409
  165.2 20.7 %collective-permute-start.22 = (bf16[384,768]{1,0:T(8,128)(2,1)}, bf16[384,768]{1,0:T(8,128)(2,1)}, u32[]{:S(2)}, u32[]{:S(2)}) collective-permute-start(bf16[384,768]{1,0:T(8,128)(2,1)} %get-tuple-element.208.refs_0_), channel_id=1, source_target_pairs={{0,4},{1,5},{2,6},{3,7},{4,0},{5,1},{6,2},{7,3},{8,12},{9,13},{10,... | collective-permute-start | bytes 1769480 | tf_op jit(solution)/shard_map/ppermute | solution.py:409
  175.1 10.8 %collective-permute-start.18 = (bf16[208,768]{1,0:T(8,128)(2,1)}, bf16[208,768]{1,0:T(8,128)(2,1)}, u32[]{:S(2)}, u32[]{:S(2)}) collective-permute-start(bf16[208,768]{1,0:T(8,128)(2,1)} %get-tuple-element.203.a0), channel_id=1, source_target_pairs={{0,2},{1,3},{2,0},{3,1},{4,6},{5,7},{6,4},{7,5},{8,10},{9,11},{10,... | collective-permute-start | bytes 958472 | tf_op jit(solution)/shard_map/ppermute | solution.py:409
  179.5 17.3 %collective-permute-start.21 = (bf16[192,1536]{1,0:T(8,128)(2,1)S(1)}, bf16[192,1536]{1,0:T(8,128)(2,1)S(1)}, u32[]{:S(2)}, u32[]{:S(2)}) collective-permute-start(bf16[192,1536]{1,0:T(8,128)(2,1)S(1)} %get-tuple-element.367), channel_id=1, source_target_pairs={{0,2},{1,3},{2,0},{3,1},{4,6},{5,7},{6,4},{7,5},{8,10},{9,11},{10,... | collective-permute-start | bytes 1769480 | tf_op jit(solution)/shard_map/ppermute | solution.py:409
  208.3 9.6 %collective-permute-start.24 = (bf16[208,768]{1,0:T(8,128)(2,1)S(1)}, bf16[208,768]{1,0:T(8,128)(2,1)S(1)}, u32[]{:S(2)}, u32[]{:S(2)}) collective-permute-start(bf16[208,768]{1,0:T(8,128)(2,1)S(1)} %get-tuple-element.212), channel_id=1, source_target_pairs={{0,2},{1,3},{2,0},{3,1},{4,6},{5,7},{6,4},{7,5},{8,10},{9,11},{10,... | collective-permute-start | bytes 958472 | tf_op jit(solution)/shard_map/ppermute | solution.py:409
  232.3 46.5 %all-to-all-start.1 = ((bf16[8,112,768]{2,1,0:T(8,128)(2,1)}), bf16[8,112,768]{2,1,0:T(8,128)(2,1)}, u32[]{:S(2)}, u32[]{:S(2)}) async-start(bf16[8,112,768]{2,1,0:T(8,128)(2,1)} %pad_maximum_fusion.1), calls=%async_computation.1 | async-start | bytes 2752512 | tf_op jit(solution)/shard_map/all_to_all | solution.py:946
  237.3 16.5 %collective-permute-start.28 = (bf16[192,1536]{1,0:T(8,128)(2,1)}, bf16[192,1536]{1,0:T(8,128)(2,1)S(1)}, u32[]{:S(2)}, u32[]{:S(2)}) collective-permute-start(bf16[192,1536]{1,0:T(8,128)(2,1)} %get-tuple-element.366), channel_id=1, source_target_pairs={{0,2},{1,3},{2,0},{3,1},{4,6},{5,7},{6,4},{7,5},{8,10},{9,11},{10,... | collective-permute-start | bytes 1769480 | tf_op jit(solution)/shard_map/ppermute | solution.py:409
  238.9 27.5 %collective-permute-start.29 = (bf16[192,1536]{1,0:T(8,128)(2,1)}, bf16[192,1536]{1,0:T(8,128)(2,1)S(1)}, u32[]{:S(2)}, u32[]{:S(2)}) collective-permute-start(bf16[192,1536]{1,0:T(8,128)(2,1)} %get-tuple-element.365), channel_id=1, source_target_pairs={{0,2},{1,3},{2,0},{3,1},{4,6},{5,7},{6,4},{7,5},{8,10},{9,11},{10,... | collective-permute-start | bytes 1769480 | tf_op jit(solution)/shard_map/ppermute | solution.py:409
  239.4 38.6 %collective-permute-start.30 = (bf16[192,1536]{1,0:T(8,128)(2,1)}, bf16[192,1536]{1,0:T(8,128)(2,1)S(1)}, u32[]{:S(2)}, u32[]{:S(2)}) collective-permute-start(bf16[192,1536]{1,0:T(8,128)(2,1)} %get-tuple-element.364), channel_id=1, source_target_pairs={{0,2},{1,3},{2,0},{3,1},{4,6},{5,7},{6,4},{7,5},{8,10},{9,11},{10,... | collective-permute-start | bytes 1769480 | tf_op jit(solution)/shard_map/ppermute | solution.py:409
  302.8 15.4 %collective-permute-start.35 = (bf16[384,768]{1,0:T(8,128)(2,1)S(1)}, bf16[384,768]{1,0:T(8,128)(2,1)S(1)}, u32[]{:S(2)}, u32[]{:S(2)}) collective-permute-start(bf16[384,768]{1,0:T(8,128)(2,1)S(1)} %get-tuple-element.225), channel_id=1, source_target_pairs={{0,2},{1,3},{2,0},{3,1},{4,6},{5,7},{6,4},{7,5},{8,10},{9,11},{10,... | collective-permute-start | bytes 1769480 | tf_op jit(solution)/shard_map/ppermute | solution.py:409
  319.0 46.3 %all-to-all-start.2 = ((bf16[8,112,768]{2,1,0:T(8,128)(2,1)}), bf16[8,112,768]{2,1,0:T(8,128)(2,1)}, u32[]{:S(2)}, u32[]{:S(2)}) async-start(bf16[8,112,768]{2,1,0:T(8,128)(2,1)} %copy-done.20), calls=%async_computation.2 | async-start | bytes 2752512 | tf_op jit(solution)/shard_map/all_to_all | solution.py:946
  324.7 16.5 %collective-permute-start.36 = (bf16[384,768]{1,0:T(8,128)(2,1)}, bf16[384,768]{1,0:T(8,128)(2,1)S(1)}, u32[]{:S(2)}, u32[]{:S(2)}) collective-permute-start(bf16[384,768]{1,0:T(8,128)(2,1)} %copy-done.147), channel_id=1, source_target_pairs={{0,2},{1,3},{2,0},{3,1},{4,6},{5,7},{6,4},{7,5},{8,10},{9,11},{10,... | collective-permute-start | bytes 1769480 | tf_op jit(solution)/shard_map/ppermute | solution.py:409
  326.2 27.6 %collective-permute-start.37 = (bf16[384,768]{1,0:T(8,128)(2,1)}, bf16[384,768]{1,0:T(8,128)(2,1)S(1)}, u32[]{:S(2)}, u32[]{:S(2)}) collective-permute-start(bf16[384,768]{1,0:T(8,128)(2,1)} %copy-done.146), channel_id=1, source_target_pairs={{0,2},{1,3},{2,0},{3,1},{4,6},{5,7},{6,4},{7,5},{8,10},{9,11},{10,... | collective-permute-start | bytes 1769480 | tf_op jit(solution)/shard_map/ppermute | solution.py:409
  326.7 37.7 %collective-permute-start.38 = (bf16[384,768]{1,0:T(8,128)(2,1)}, bf16[384,768]{1,0:T(8,128)(2,1)S(1)}, u32[]{:S(2)}, u32[]{:S(2)}) collective-permute-start(bf16[384,768]{1,0:T(8,128)(2,1)} %copy-done.145), channel_id=1, source_target_pairs={{0,2},{1,3},{2,0},{3,1},{4,6},{5,7},{6,4},{7,5},{8,10},{9,11},{10,... | collective-permute-start | bytes 1769480 | tf_op jit(solution)/shard_map/ppermute | solution.py:409
  370.6 9.6 %collective-permute-start.40 = (bf16[208,768]{1,0:T(8,128)(2,1)S(1)}, bf16[208,768]{1,0:T(8,128)(2,1)S(1)}, u32[]{:S(2)}, u32[]{:S(2)}) collective-permute-start(bf16[208,768]{1,0:T(8,128)(2,1)S(1)} %get-tuple-element.240), channel_id=1, source_target_pairs={{0,2},{1,3},{2,0},{3,1},{4,6},{5,7},{6,4},{7,5},{8,10},{9,11},{10,... | collective-permute-start | bytes 958472 | tf_op jit(solution)/shard_map/ppermute | solution.py:409
  383.8 60.7 %all-to-all-start.3 = ((bf16[8,96,1536]{2,1,0:T(8,128)(2,1)}), bf16[8,96,1536]{2,1,0:T(8,128)(2,1)}, u32[]{:S(2)}, u32[]{:S(2)}) async-start(bf16[8,96,1536]{2,1,0:T(8,128)(2,1)} %bitcast.64), calls=%async_computation.3 | async-start | bytes 4718592 | tf_op jit(solution)/shard_map/all_to_all | solution.py:1101
  420.2 9.6 %collective-permute-start.47 = (bf16[208,768]{1,0:T(8,128)(2,1)S(1)}, bf16[208,768]{1,0:T(8,128)(2,1)S(1)}, u32[]{:S(2)}, u32[]{:S(2)}) collective-permute-start(bf16[208,768]{1,0:T(8,128)(2,1)S(1)} %get-tuple-element.254), channel_id=1, source_target_pairs={{0,2},{1,3},{2,0},{3,1},{4,6},{5,7},{6,4},{7,5},{8,10},{9,11},{10,... | collective-permute-start | bytes 958472 | tf_op jit(solution)/shard_map/ppermute | solution.py:409
  433.4 9.7 %collective-permute-start.49 = (bf16[208,768]{1,0:T(8,128)(2,1)S(1)}, bf16[208,768]{1,0:T(8,128)(2,1)S(1)}, u32[]{:S(2)}, u32[]{:S(2)}) collective-permute-start(bf16[208,768]{1,0:T(8,128)(2,1)S(1)} %get-tuple-element.261.g0), channel_id=1, source_target_pairs={{0,1},{1,0},{2,3},{3,2},{4,5},{5,4},{6,7},{7,6},{8,9},{9,8},{10,11... | collective-permute-start | bytes 958472 | tf_op jit(solution)/shard_map/ppermute | solution.py:409
  441.3 19.8 %collective-permute-start.44 = (bf16[384,768]{1,0:T(8,128)(2,1)}, bf16[384,768]{1,0:T(8,128)(2,1)}, u32[]{:S(2)}, u32[]{:S(2)}) collective-permute-start(bf16[384,768]{1,0:T(8,128)(2,1)} %get-tuple-element.244), channel_id=1, source_target_pairs={{0,4},{1,5},{2,6},{3,7},{4,0},{5,1},{6,2},{7,3},{8,12},{9,13},{10,... | collective-permute-start | bytes 1769480 | tf_op jit(solution)/shard_map/ppermute | solution.py:409
  464.3 28.1 %collective-permute-start.57 = (bf16[384,1536]{1,0:T(8,128)(2,1)S(1)}, bf16[384,1536]{1,0:T(8,128)(2,1)S(1)}, u32[]{:S(2)}, u32[]{:S(2)}) collective-permute-start(bf16[384,1536]{1,0:T(8,128)(2,1)S(1)} %get-tuple-element.276), channel_id=1, source_target_pairs={{0,4},{1,5},{2,6},{3,7},{4,0},{5,1},{6,2},{7,3},{8,12},{9,13},{10,... | collective-permute-start | bytes 3538952 | tf_op jit(solution)/shard_map/ppermute | solution.py:409
  464.7 9.4 %collective-permute-start.52 = (bf16[208,768]{1,0:T(8,128)(2,1)S(1)}, bf16[208,768]{1,0:T(8,128)(2,1)S(1)}, u32[]{:S(2)}, u32[]{:S(2)}) collective-permute-start(bf16[208,768]{1,0:T(8,128)(2,1)S(1)} %get-tuple-element.270), channel_id=1, source_target_pairs={{0,2},{1,3},{2,0},{3,1},{4,6},{5,7},{6,4},{7,5},{8,10},{9,11},{10,... | collective-permute-start | bytes 958472 | tf_op jit(solution)/shard_map/ppermute | solution.py:409
  476.3 13.0 %collective-permute-start.54 = (bf16[208,768]{1,0:T(8,128)(2,1)S(1)}, bf16[208,768]{1,0:T(8,128)(2,1)S(1)}, u32[]{:S(2)}, u32[]{:S(2)}) collective-permute-start(bf16[208,768]{1,0:T(8,128)(2,1)S(1)} %get-tuple-element.277.g0), channel_id=1, source_target_pairs={{0,1},{1,0},{2,3},{3,2},{4,5},{5,4},{6,7},{7,6},{8,9},{9,8},{10,11... | collective-permute-start | bytes 958472 | tf_op jit(solution)/shard_map/ppermute | solution.py:409
  485.3 17.4 %collective-permute-start.58 = (bf16[96,768]{1,0:T(8,128)(2,1)S(1)}, bf16[96,768]{1,0:T(8,128)(2,1)S(1)}, u32[]{:S(2)}, u32[]{:S(2)}) collective-permute-start(bf16[96,768]{1,0:T(8,128)(2,1)S(1)} %get-tuple-element.289), channel_id=1, source_target_pairs={{0,8},{1,9},{2,10},{3,11},{4,12},{5,13},{6,14},{7,15},{8,0},{9,1},... | collective-permute-start | bytes 442376 | tf_op jit(solution)/shard_map/ppermute | solution.py:409
  487.1 16.2 %collective-permute-start.59 = (bf16[96,768]{1,0:T(8,128)(2,1)S(1)}, bf16[96,768]{1,0:T(8,128)(2,1)S(1)}, u32[]{:S(2)}, u32[]{:S(2)}) collective-permute-start(bf16[96,768]{1,0:T(8,128)(2,1)S(1)} %get-tuple-element.290), channel_id=1, source_target_pairs={{0,16},{1,17},{2,18},{3,19},{4,20},{5,21},{6,22},{7,23},{8,24},{9,... | collective-permute-start | bytes 442376 | tf_op jit(solution)/shard_map/ppermute | solution.py:409
  489.4 14.6 %collective-permute-start.60 = (bf16[96,768]{1,0:T(8,128)(2,1)S(1)}, bf16[96,768]{1,0:T(8,128)(2,1)S(1)}, u32[]{:S(2)}, u32[]{:S(2)}) collective-permute-start(bf16[96,768]{1,0:T(8,128)(2,1)S(1)} %get-tuple-element.291), channel_id=1, source_target_pairs={{0,24},{1,25},{2,26},{3,27},{4,28},{5,29},{6,30},{7,31},{8,16},{9,... | collective-permute-start | bytes 442376 | tf_op jit(solution)/shard_map/ppermute | solution.py:409
  489.7 15.0 %collective-permute-start.56 = (bf16[208,768]{1,0:T(8,128)(2,1)S(1)}, bf16[208,768]{1,0:T(8,128)(2,1)S(1)}, u32[]{:S(2)}, u32[]{:S(2)}) collective-permute-start(bf16[208,768]{1,0:T(8,128)(2,1)S(1)} %get-tuple-element.273), channel_id=1, source_target_pairs={{0,2},{1,3},{2,0},{3,1},{4,6},{5,7},{6,4},{7,5},{8,10},{9,11},{10,... | collective-permute-start | bytes 958472 | tf_op jit(solution)/shard_map/ppermute | solution.py:409
  505.3 15.7 %collective-permute-start.63 = (bf16[384,768]{1,0:T(8,128)(2,1)S(1)}, bf16[384,768]{1,0:T(8,128)(2,1)S(1)}, u32[]{:S(2)}, u32[]{:S(2)}) collective-permute-start(bf16[384,768]{1,0:T(8,128)(2,1)S(1)} %get-tuple-element.296), channel_id=1, source_target_pairs={{0,4},{1,5},{2,6},{3,7},{4,0},{5,1},{6,2},{7,3},{8,12},{9,13},{10,... | collective-permute-start | bytes 1769480 | tf_op jit(solution)/shard_map/ppermute | solution.py:409
  507.6 13.5 %collective-permute-start.62 = (bf16[208,768]{1,0:T(8,128)(2,1)S(1)}, bf16[208,768]{1,0:T(8,128)(2,1)S(1)}, u32[]{:S(2)}, u32[]{:S(2)}) collective-permute-start(bf16[208,768]{1,0:T(8,128)(2,1)S(1)} %get-tuple-element.294), channel_id=1, source_target_pairs={{0,2},{1,3},{2,0},{3,1},{4,6},{5,7},{6,4},{7,5},{8,10},{9,11},{10,... | collective-permute-start | bytes 958472 | tf_op jit(solution)/shard_map/ppermute | solution.py:409
  526.2 16.8 %collective-permute-start.64 = (bf16[96,1536]{1,0:T(8,128)(2,1)}, bf16[96,1536]{1,0:T(8,128)(2,1)S(1)}, u32[]{:S(2)}, u32[]{:S(2)}) collective-permute-start(bf16[96,1536]{1,0:T(8,128)(2,1)} %get-tuple-element.300), channel_id=1, source_target_pairs={{0,8},{1,9},{2,10},{3,11},{4,12},{5,13},{6,14},{7,15},{8,0},{9,1},... | collective-permute-start | bytes 884744 | tf_op jit(solution)/shard_map/ppermute | solution.py:409
  527.8 23.6 %collective-permute-start.65 = (bf16[96,1536]{1,0:T(8,128)(2,1)}, bf16[96,1536]{1,0:T(8,128)(2,1)S(1)}, u32[]{:S(2)}, u32[]{:S(2)}) collective-permute-start(bf16[96,1536]{1,0:T(8,128)(2,1)} %get-tuple-element.301), channel_id=1, source_target_pairs={{0,16},{1,17},{2,18},{3,19},{4,20},{5,21},{6,22},{7,23},{8,24},{9,... | collective-permute-start | bytes 884744 | tf_op jit(solution)/shard_map/ppermute | solution.py:409
  530.1 21.3 %collective-permute-start.66 = (bf16[96,1536]{1,0:T(8,128)(2,1)}, bf16[96,1536]{1,0:T(8,128)(2,1)S(1)}, u32[]{:S(2)}, u32[]{:S(2)}) collective-permute-start(bf16[96,1536]{1,0:T(8,128)(2,1)} %get-tuple-element.302), channel_id=1, source_target_pairs={{0,24},{1,25},{2,26},{3,27},{4,28},{5,29},{6,30},{7,31},{8,16},{9,... | collective-permute-start | bytes 884744 | tf_op jit(solution)/shard_map/ppermute | solution.py:409
  536.4 15.0 %collective-permute-start.69 = (f32[4,16,96]{2,1,0:T(8,128)}, f32[4,16,96]{2,1,0:T(8,128)}, u32[]{:S(2)}, u32[]{:S(2)}) collective-permute-start(f32[4,16,96]{2,1,0:T(8,128)} %slice.95), channel_id=1, source_target_pairs={{0,4},{1,5},{2,6},{3,7},{4,0},{5,1},{6,2},{7,3},{8,12},{9,13},{10,... | collective-permute-start | bytes 73736 | tf_op jit(solution)/shard_map/ppermute | solution.py:409
  552.3 18.1 %collective-permute-start.70 = (bf16[128,768]{1,0:T(8,128)(2,1)S(1)}, bf16[128,768]{1,0:T(8,128)(2,1)S(1)}, u32[]{:S(2)}, u32[]{:S(2)}) collective-permute-start(bf16[128,768]{1,0:T(8,128)(2,1)S(1)} %get-tuple-element.311), channel_id=1, source_target_pairs={{0,8},{1,9},{2,10},{3,11},{4,12},{5,13},{6,14},{7,15},{8,0},{9,1},... | collective-permute-start | bytes 589832 | tf_op jit(solution)/shard_map/ppermute | solution.py:409
  558.6 17.2 %collective-permute-start.71 = (bf16[128,768]{1,0:T(8,128)(2,1)S(1)}, bf16[128,768]{1,0:T(8,128)(2,1)S(1)}, u32[]{:S(2)}, u32[]{:S(2)}) collective-permute-start(bf16[128,768]{1,0:T(8,128)(2,1)S(1)} %get-tuple-element.312), channel_id=1, source_target_pairs={{0,16},{1,17},{2,18},{3,19},{4,20},{5,21},{6,22},{7,23},{8,24},{9,... | collective-permute-start | bytes 589832 | tf_op jit(solution)/shard_map/ppermute | solution.py:409
  559.4 16.3 %collective-permute-start.72 = (bf16[128,768]{1,0:T(8,128)(2,1)S(1)}, bf16[128,768]{1,0:T(8,128)(2,1)S(1)}, u32[]{:S(2)}, u32[]{:S(2)}) collective-permute-start(bf16[128,768]{1,0:T(8,128)(2,1)S(1)} %get-tuple-element.313), channel_id=1, source_target_pairs={{0,24},{1,25},{2,26},{3,27},{4,28},{5,29},{6,30},{7,31},{8,16},{9,... | collective-permute-start | bytes 589832 | tf_op jit(solution)/shard_map/ppermute | solution.py:409
  (198 other events, 1416.2 us)
Sparse Core Ops, SparseCore 0:
  12.3 50.9 all-gather.1

commit v4 on v3

--- a/solution.py
+++ b/solution.py
@@ -1009,7 +1009,7 @@
         scalars=1,
     )
     x_mlp = swap(z_mlp, x=1)
-    e_pack = hold(e_pack, z_mlp)
+    e_pack = hold(e_pack, normed_mlp[1])
     e_own = lax.all_to_all(e_pack, "dp", split_axis=0, concat_axis=0, tiled=True)
     e_own = e_own.reshape(features, wide)
     e_own = hold(e_own, normed_mlp[1])
@@ -1030,7 +1030,7 @@
     two, normed = join(one, near, far, gains[2])
     normed_two = spread(normed)
     full_late = stacked([z_late, x_late])
-    mixed_two, att_two, own, sib, peak_two = attend(hold(normed_two, e_far[0]), full_late, 0)
+    mixed_two, att_two, own, sib, peak_two = attend(normed_two, full_late, 0)
     near, far = over_group(own, sib)
     three, normed = join(two, near, far, gains[3])
     tokens_sent = to_experts(token_kernel, spread(normed), peak_one, peak_two)
@@ -1075,7 +1075,7 @@
     e_packs = hold(e_packs, both)
     both = exchange(both)
     up_got.append(swap(e_packs[2], y=1))
-    down_got = [swap(e_packs[4], y=1), swap(e_packs[5], y=1)]
+    down_got = [swap(e_packs[4], y=1)]
     both = hold(both, up_got, down_got)
 
     def combine(which, both):
@@ -1092,19 +1092,20 @@
     grad_three, low, gain_four = norm_back(
         three, grad_four, back_own, back_far, gains[3]
     )
+    low = spread(low)
+    down_got.append(swap(hold(e_packs[5], low[1]), y=1))
+    *second, own, sib = attend_back(
+        low, normed_two, mixed_two, att_two, full_late, 0
+    )
+    second = scatter_start(second)
+    near, far = over_group(own, hold(sib, down_got[1]))
     e_sum = run(
         add_pack_kernel,
         [((features, wide), BF)],
-        (e_packs[0], *hold(up_got, low), e_packs[3], *down_got),
+        (e_packs[0], *up_got, e_packs[3], *hold(down_got, near)),
         0,
     )[0].reshape(experts, width, wide)
     e_back = lax.all_to_all(e_sum, "dp", split_axis=0, concat_axis=0, tiled=True)
-    low = spread(low)
-    *second, own, sib = attend_back(
-        low, normed_two, mixed_two, att_two, full_late, 0
-    )
-    second = scatter_start(second)
-    near, far = over_group(own, sib)
     grad_two, low, gain_three = norm_back(
         two, grad_three, near, far, gains[2]
     )
@@ -1112,7 +1113,7 @@
     *mlp, own, sib = run(
         functools.partial(mlp_back_kernel, ats),
         pack_shapes(2 * ff_cols),
-        (*hold(low, e_back), *normed_mlp, act, slope, full_mlp),
+        (*low, *normed_mlp, act, slope, full_mlp),
         0,
         scratch=[group_scratch, pltpu.VMEM((4 * ROWS, ff_cols), BF)],
     )
@@ -1139,7 +1140,7 @@
     )
     mlp = scatter_late(scatter_middle(mlp))
     first = scatter_start(first)
-    near, far = over_group(own, hold(sib, mixed_far, second))
+    near, far = over_group(own, hold(sib, mixed_far, second, e_back))
     grad_zero, _, gain_one = norm_back(start, grad_one, near, hold(far, first), gains[0])
     gains_sum = run(
         small_kernel,
@@ -1147,7 +1148,7 @@
         (gain_one, gain_two, gain_three, gain_four, grad_router),
         0,
     )[0]
-    gains_sum = gains_sum + swap(gains_sum, core=1)
+    gains_sum = hold(gains_sum + swap(gains_sum, core=1), mlp)
     gains_sum = gains_sum + swap(gains_sum, y=1)
     gains_sum = gains_sum[:4] + swap(gains_sum[4:], x=1)
     near_first, got_first = first
@@ -1155,7 +1156,7 @@
     first = run(
         sum_two_more,
         [(shape, F32)] + [((width + 32, shape[1]), BF)] * 3,
-        (hold(near_first, mlp), got_first, gains_sum),
+        (near_first, got_first, gains_sum),
         0,
     )
     first = scatter_late(first)

time: 594 us -> 585 us (0.985)
  local copies, waits for them, and re-layouts: 85.7 us -> 72.5 us
  starting transfers between devices: 99.9 us -> 109 us
  Pallas kernels: 92.5 us -> 84.9 us
    all_to_all x2, starting transfers between devices: 10.7 us -> 26.4 us  [exchange(): return lax.all_to_all(both, 'dp', split_axis=0, concat_axis=0, tiled=True)]
    unnamed x346 -> x352, local copies, waits for them, and re-layouts: 78.5 us -> 65.9 us
    pallas_call x47, Pallas kernels: 92.5 us -> 84.9 us  [run(): pl.pallas_call(kernel, out_shape=shapes, in_specs=[SM] * scalars + [VM] *...]
    ppermute x73, starting transfers between devices: 67.4 us -> 61.4 us  [swap(): return lax.ppermute(values, AXES, pairs)]
  transfers between devices with their start and end apart: 78 -> 78, of which waited for: 45 -> 49; matrix products, arithmetic and copies ran while one was open for 4% -> 3% of each run, Pallas kernels for 10% -> 10%
where the time goes in v4:
time: 585 us; the launch traced here: 577 us
  waiting for transfers between devices  282 us (48%)
  starting transfers between devices  109 us (19%)
  Pallas kernels  84.9 us (15%)
  local copies, waits for them, and re-layouts  72.5 us (12%)
  between operations  16.5 us (3%)
  other arithmetic  10.4 us (2%)
    ppermute x73, waiting for transfers between devices, swap(): return lax.ppermute(values, AXES, pairs)  277 us
    pallas_call x47, Pallas kernels, run(): pl.pallas_call(kernel, out_shape=shapes, in_specs=[SM] * scalars + [VM] *...  84.9 us
    unnamed x352, local copies, waits for them, and re-layouts  65.9 us
    ppermute x73, starting transfers between devices, swap(): return lax.ppermute(values, AXES, pairs)  61.4 us
    all_to_all x2, starting transfers between devices, exchange(): return lax.all_to_all(both, 'dp', split_axis=0, concat_axis=0, tiled=True)  26.4 us
    all_to_all x1, starting transfers between devices, fast_local(): lax.all_to_all(e_pack, 'dp', split_axis=0, concat_axis=0, tiled=True)  17 us
  transfers between devices with their start and end apart: 78, of which 49 were waited for; matrix products, arithmetic and copies ran while one was open for 3% of the time, Pallas kernels for 10%

profile of v4, /device:TPU:0, one launch (start us, length us, event | category | flops | bytes accessed | tf_op | source)
XLA Modules:
  0.0 576.8 jit_solution(17059175816757354324)
XLA Ops:
  13.5 3.1 collective-permute-start
  19.2 4.5 collective-permute-done.refs_1_
  23.7 13.5 %collective-permute-done.1.refs_2_ = bf16[96,896]{1,0:T(8,128)(2,1)S(1)} collective-permute-done((bf16[96,896]{1,0:T(8,128)(2,1)S(1)}, bf16[96,896]{1,0:T(8,128)(2,1)S(1)}, u32[]{:S(2)}, u32[]{:S(2)}) %collective-permute-start.1) | collective-permute-done | bytes 172064 | tf_op jit(solution)/shard_map/ppermute | solution.py:409
  45.3 4.7 collective-permute-done.4.refs_1_
  59.5 4.7 shard_map.318
  70.4 8.1 %collective-permute-done.8.far_ref = bf16[208,768]{1,0:T(8,128)(2,1)S(1)} collective-permute-done((bf16[208,768]{1,0:T(8,128)(2,1)S(1)}, bf16[208,768]{1,0:T(8,128)(2,1)S(1)}, u32[]{:S(2)}, u32[]{:S(2)}) %collective-permute-start.8) | collective-permute-done | bytes 319520 | tf_op jit(solution)/shard_map/ppermute | solution.py:409
  86.4 5.5 collective-permute-done.9.b1
  91.9 17.0 %all-to-all-start.1 = ((bf16[8,96,1536]{2,1,0:T(8,128)(2,1)}), bf16[8,96,1536]{2,1,0:T(8,128)(2,1)}, u32[]{:S(2)}, u32[]{:S(2)}) async-start(bf16[8,96,1536]{2,1,0:T(8,128)(2,1)} %pad_maximum_fusion), calls=%async_computation.1 | async-start | bytes 4718592 | tf_op jit(solution)/shard_map/all_to_all | solution.py:1013
  111.4 5.2 collective-permute-done.12.p1
  122.9 2.8 shard_map.325
  131.6 8.1 %collective-permute-done.17.far_ref = bf16[208,768]{1,0:T(8,128)(2,1)S(1)} collective-permute-done((bf16[208,768]{1,0:T(8,128)(2,1)S(1)}, bf16[208,768]{1,0:T(8,128)(2,1)S(1)}, u32[]{:S(2)}, u32[]{:S(2)}) %collective-permute-start.17) | collective-permute-done | bytes 319520 | tf_op jit(solution)/shard_map/ppermute | solution.py:409
  143.3 5.6 collective-permute-done.18.a1
  148.9 10.5 %collective-permute-done.21.refs_1_ = bf16[384,768]{1,0:T(8,128)(2,1)S(1)} collective-permute-done((bf16[384,768]{1,0:T(8,128)(2,1)S(1)}, bf16[384,768]{1,0:T(8,128)(2,1)S(1)}, u32[]{:S(2)}, u32[]{:S(2)}) %collective-permute-start.21) | collective-permute-done | bytes 589856 | tf_op jit(solution)/shard_map/ppermute | solution.py:409
  159.6 4.7 shard_map.329
  168.9 9.1 %collective-permute-done.23.far_ref = bf16[208,768]{1,0:T(8,128)(2,1)S(1)} collective-permute-done((bf16[208,768]{1,0:T(8,128)(2,1)S(1)}, bf16[208,768]{1,0:T(8,128)(2,1)S(1)}, u32[]{:S(2)}, u32[]{:S(2)}) %collective-permute-start.23) | collective-permute-done | bytes 319520 | tf_op jit(solution)/shard_map/ppermute | solution.py:409
  179.6 8.2 %collective-permute-done.24.p1 = bf16[208,768]{1,0:T(8,128)(2,1)S(1)} collective-permute-done((bf16[208,768]{1,0:T(8,128)(2,1)S(1)}, bf16[208,768]{1,0:T(8,128)(2,1)S(1)}, u32[]{:S(2)}, u32[]{:S(2)}) %collective-permute-start.24) | collective-permute-done | bytes 319520 | tf_op jit(solution)/shard_map/ppermute | solution.py:409
  192.2 20.7 %all-to-all-start = ((bf16[8,112,768]{2,1,0:T(8,128)(2,1)}), bf16[8,112,768]{2,1,0:T(8,128)(2,1)}, u32[]{:S(2)}, u32[]{:S(2)}) async-start(bf16[8,112,768]{2,1,0:T(8,128)(2,1)} %pad_maximum_fusion.1), calls=%async_computation | async-start | bytes 2752512 | tf_op jit(solution)/shard_map/all_to_all | solution.py:946
  218.8 12.2 %collective-permute-done.27.rest_1_ = bf16[192,1536]{1,0:T(8,128)(2,1)S(1)} collective-permute-done((bf16[192,1536]{1,0:T(8,128)(2,1)S(1)}, bf16[192,1536]{1,0:T(8,128)(2,1)S(1)}, u32[]{:S(2)}, u32[]{:S(2)}) %collective-permute-start.27) | collective-permute-done | bytes 589856 | tf_op jit(solution)/shard_map/ppermute | solution.py:409
  231.8 11.8 %collective-permute-done.28.rest_2_ = bf16[192,1536]{1,0:T(8,128)(2,1)S(1)} collective-permute-done((bf16[192,1536]{1,0:T(8,128)(2,1)S(1)}, bf16[192,1536]{1,0:T(8,128)(2,1)S(1)}, u32[]{:S(2)}, u32[]{:S(2)}) %collective-permute-start.28) | collective-permute-done | bytes 589856 | tf_op jit(solution)/shard_map/ppermute | solution.py:409
  244.4 11.8 %collective-permute-done.29.rest_3_ = bf16[192,1536]{1,0:T(8,128)(2,1)S(1)} collective-permute-done((bf16[192,1536]{1,0:T(8,128)(2,1)S(1)}, bf16[192,1536]{1,0:T(8,128)(2,1)S(1)}, u32[]{:S(2)}, u32[]{:S(2)}) %collective-permute-start.29) | collective-permute-done | bytes 589856 | tf_op jit(solution)/shard_map/ppermute | solution.py:409
  257.1 10.7 %collective-permute-done.30.rest_4_ = bf16[192,1536]{1,0:T(8,128)(2,1)S(1)} collective-permute-done((bf16[192,1536]{1,0:T(8,128)(2,1)S(1)}, bf16[192,1536]{1,0:T(8,128)(2,1)S(1)}, u32[]{:S(2)}, u32[]{:S(2)}) %collective-permute-start.30) | collective-permute-done | bytes 589856 | tf_op jit(solution)/shard_map/ppermute | solution.py:409
  274.4 16.6 %shard_map.334 = (f32[448,768]{1,0:T(8,128)}, bf16[448,768]{1,0:T(8,128)(2,1)S(1)}, f32[448,768]{1,0:T(8,128)}, bf16[448,768]{1,0:T(8,128)(2,1)S(1)}, bf16[768,7...) custom-call(s32[1]{0:T(128)} %bitcast.26.number, ...), custom_call_target="tpu_custom_call" | custom-call | flops 1000 | bytes 1000 | tf_op jit(solution)/shard_map/pallas_call | solution.py:419
  301.9 6.1 %collective-permute-done.35.up0 = bf16[384,768]{1,0:T(8,128)(2,1)S(1)} collective-permute-done((bf16[384,768]{1,0:T(8,128)(2,1)S(1)}, bf16[384,768]{1,0:T(8,128)(2,1)S(1)}, u32[]{:S(2)}, u32[]{:S(2)}) %collective-permute-start.35) | collective-permute-done | bytes 589856 | tf_op jit(solution)/shard_map/ppermute | solution.py:409
  308.8 5.7 all-to-all-start.2
  316.6 14.4 %collective-permute-done.36.up1 = bf16[384,768]{1,0:T(8,128)(2,1)S(1)} collective-permute-done((bf16[384,768]{1,0:T(8,128)(2,1)}, bf16[384,768]{1,0:T(8,128)(2,1)S(1)}, u32[]{:S(2)}, u32[]{:S(2)}) %collective-permute-start.36) | collective-permute-done | bytes 589856 | tf_op jit(solution)/shard_map/ppermute | solution.py:409
  331.9 9.8 %collective-permute-done.37.down0 = bf16[384,768]{1,0:T(8,128)(2,1)S(1)} collective-permute-done((bf16[384,768]{1,0:T(8,128)(2,1)}, bf16[384,768]{1,0:T(8,128)(2,1)S(1)}, u32[]{:S(2)}, u32[]{:S(2)}) %collective-permute-start.37) | collective-permute-done | bytes 589856 | tf_op jit(solution)/shard_map/ppermute | solution.py:409
  342.5 4.5 all-to-all-done.2.both_ref
  347.0 2.9 shard_map.336
  352.9 9.0 %collective-permute-done.39.far_ref = bf16[208,768]{1,0:T(8,128)(2,1)S(1)} collective-permute-done((bf16[208,768]{1,0:T(8,128)(2,1)S(1)}, bf16[208,768]{1,0:T(8,128)(2,1)S(1)}, u32[]{:S(2)}, u32[]{:S(2)}) %collective-permute-start.39) | collective-permute-done | bytes 319520 | tf_op jit(solution)/shard_map/ppermute | solution.py:409
  363.8 8.2 %collective-permute-done.40.g1 = bf16[208,768]{1,0:T(8,128)(2,1)S(1)} collective-permute-done((bf16[208,768]{1,0:T(8,128)(2,1)S(1)}, bf16[208,768]{1,0:T(8,128)(2,1)S(1)}, u32[]{:S(2)}, u32[]{:S(2)}) %collective-permute-start.40) | collective-permute-done | bytes 319520 | tf_op jit(solution)/shard_map/ppermute | solution.py:409
  373.7 9.9 %shard_map.339 = (bf16[384,768]{1,0:T(8,128)(2,1)S(1)}, bf16[384,768]{1,0:T(8,128)(2,1)S(1)}, f32[416,768]{1,0:T(8,128)S(1)}, bf16[416,768]{1,0:T(8,128)(2,1)S(1)}) custom-call(bf16[208,768]{1,0:T(8,128)(2,1)S(1)} %get-tuple-element.230.g0, bf16[208,768]{1,0:T(8,128)(2,1)S(1)} %collective-permute-done.40.g1, ...), custom_call_target="tpu_custom_call" | custom-call | flops 8000000000 | bytes 1000 | tf_op jit(solution)/shard_map/pallas_call | solution.py:419
  383.7 4.1 collective-permute-done.45.down1
  393.0 4.6 all-to-all-start.3
  398.2 9.3 %collective-permute-done.47.far_ref = bf16[208,768]{1,0:T(8,128)(2,1)S(1)} collective-permute-done((bf16[208,768]{1,0:T(8,128)(2,1)}, bf16[208,768]{1,0:T(8,128)(2,1)S(1)}, u32[]{:S(2)}, u32[]{:S(2)}) %collective-permute-start.47) | collective-permute-done | bytes 319520 | tf_op jit(solution)/shard_map/ppermute | solution.py:409
  412.5 8.3 %collective-permute-done.48.g1 = bf16[208,768]{1,0:T(8,128)(2,1)S(1)} collective-permute-done((bf16[208,768]{1,0:T(8,128)(2,1)S(1)}, bf16[208,768]{1,0:T(8,128)(2,1)S(1)}, u32[]{:S(2)}, u32[]{:S(2)}) %collective-permute-start.48) | collective-permute-done | bytes 319520 | tf_op jit(solution)/shard_map/ppermute | solution.py:409
  425.1 4.7 shard_map.344
  430.9 14.4 %collective-permute-done.43.got = bf16[384,768]{1,0:T(8,128)(2,1)S(1)} collective-permute-done((bf16[384,768]{1,0:T(8,128)(2,1)S(1)}, bf16[384,768]{1,0:T(8,128)(2,1)S(1)}, u32[]{:S(2)}, u32[]{:S(2)}) %collective-permute-start.43) | collective-permute-done | bytes 589856 | tf_op jit(solution)/shard_map/ppermute | solution.py:409
  445.3 2.8 shard_map.340
  450.5 7.9 %collective-permute-done.52.far_ref = bf16[208,768]{1,0:T(8,128)(2,1)S(1)} collective-permute-done((bf16[208,768]{1,0:T(8,128)(2,1)S(1)}, bf16[208,768]{1,0:T(8,128)(2,1)S(1)}, u32[]{:S(2)}, u32[]{:S(2)}) %collective-permute-start.52) | collective-permute-done | bytes 319520 | tf_op jit(solution)/shard_map/ppermute | solution.py:409
  459.6 8.5 %collective-permute-done.53.g1 = bf16[208,768]{1,0:T(8,128)(2,1)S(1)} collective-permute-done((bf16[208,768]{1,0:T(8,128)(2,1)S(1)}, bf16[208,768]{1,0:T(8,128)(2,1)S(1)}, u32[]{:S(2)}, u32[]{:S(2)}) %collective-permute-start.53) | collective-permute-done | bytes 319520 | tf_op jit(solution)/shard_map/ppermute | solution.py:409
  469.0 5.2 collective-permute-start.58
  478.2 10.3 %shard_map.348 = (bf16[384,768]{1,0:T(8,128)(2,1)S(1)}, bf16[384,768]{1,0:T(8,128)(2,1)S(1)}, f32[416,768]{1,0:T(8,128)S(1)}, bf16[416,768]{1,0:T(8,128)(2,1)S(1)}) custom-call(bf16[208,768]{1,0:T(8,128)(2,1)S(1)} %get-tuple-element.261.g0, bf16[208,768]{1,0:T(8,128)(2,1)S(1)} %collective-permute-done.53.g1, ...), custom_call_target="tpu_custom_call" | custom-call | flops 8000000000 | bytes 1000 | tf_op jit(solution)/shard_map/pallas_call | solution.py:419
  498.6 3.8 collective-permute-start.65
  504.9 3.3 collective-permute-done.63.got
  512.2 13.9 %collective-permute-done.66.r2 = bf16[96,1536]{1,0:T(8,128)(2,1)S(1)} collective-permute-done((bf16[96,1536]{1,0:T(8,128)(2,1)}, bf16[96,1536]{1,0:T(8,128)(2,1)S(1)}, u32[]{:S(2)}, u32[]{:S(2)}) %collective-permute-start.66) | collective-permute-done | bytes 294944 | tf_op jit(solution)/shard_map/ppermute | solution.py:409
  546.7 5.5 collective-permute-start.70
  554.6 4.3 convert_bitcast_fusion
  560.7 6.1 %collective-permute-done.71.r2 = bf16[128,768]{1,0:T(8,128)(2,1)S(1)} collective-permute-done((bf16[128,768]{1,0:T(8,128)(2,1)S(1)}, bf16[128,768]{1,0:T(8,128)(2,1)S(1)}, u32[]{:S(2)}, u32[]{:S(2)}) %collective-permute-start.71) | collective-permute-done | bytes 196640 | tf_op jit(solution)/shard_map/ppermute | solution.py:409
  (555 shorter events, 173.6 us)
Async XLA Ops:
  7.3 71.2 %all-gather.2.cloned.1.call-start = ((), (), s32[]{:S(2)}) async-start(), calls=%async_computation.4 | async-start | bytes 2211840 | tf_op jit(solution)/shard_map/all_gather | solution.py:890
  13.5 10.2 %collective-permute-start = (bf16[96,896]{1,0:T(8,128)(2,1)S(1)}, bf16[96,896]{1,0:T(8,128)(2,1)S(1)}, u32[]{:S(2)}, u32[]{:S(2)}) collective-permute-start(bf16[96,896]{1,0:T(8,128)(2,1)S(1)} %shard_map.314.refs_0_), channel_id=1, source_target_pairs={{0,8},{1,9},{2,10},{3,11},{4,12},{5,13},{6,14},{7,15},{8,0},{9,1},... | collective-permute-start | bytes 516104 | tf_op jit(solution)/shard_map/ppermute | solution.py:409
  16.6 20.6 %collective-permute-start.1 = (bf16[96,896]{1,0:T(8,128)(2,1)S(1)}, bf16[96,896]{1,0:T(8,128)(2,1)S(1)}, u32[]{:S(2)}, u32[]{:S(2)}) collective-permute-start(bf16[96,896]{1,0:T(8,128)(2,1)S(1)} %shard_map.314.refs_0_), channel_id=1, source_target_pairs={{0,16},{1,17},{2,18},{3,19},{4,20},{5,21},{6,22},{7,23},{8,24},{9,... | collective-permute-start | bytes 516104 | tf_op jit(solution)/shard_map/ppermute | solution.py:409
  19.2 18.0 %collective-permute-start.2 = (bf16[96,896]{1,0:T(8,128)(2,1)S(1)}, bf16[96,896]{1,0:T(8,128)(2,1)S(1)}, u32[]{:S(2)}, u32[]{:S(2)}) collective-permute-start(bf16[96,896]{1,0:T(8,128)(2,1)S(1)} %shard_map.314.refs_0_), channel_id=1, source_target_pairs={{0,24},{1,25},{2,26},{3,27},{4,28},{5,29},{6,30},{7,31},{8,16},{9,... | collective-permute-start | bytes 516104 | tf_op jit(solution)/shard_map/ppermute | solution.py:409
  37.2 14.6 %collective-permute-start.3 = (bf16[384,896]{1,0:T(8,128)(2,1)S(1)}, bf16[384,896]{1,0:T(8,128)(2,1)S(1)}, u32[]{:S(2)}, u32[]{:S(2)}) collective-permute-start(bf16[384,896]{1,0:T(8,128)(2,1)S(1)} %shard_map.315.refs_0_), channel_id=1, source_target_pairs={{0,4},{1,5},{2,6},{3,7},{4,0},{5,1},{6,2},{7,3},{8,12},{9,13},{10,... | collective-permute-start | bytes 2064392 | tf_op jit(solution)/shard_map/ppermute | solution.py:409
  68.7 9.8 %collective-permute-start.8 = (bf16[208,768]{1,0:T(8,128)(2,1)S(1)}, bf16[208,768]{1,0:T(8,128)(2,1)S(1)}, u32[]{:S(2)}, u32[]{:S(2)}) collective-permute-start(bf16[208,768]{1,0:T(8,128)(2,1)S(1)} %get-tuple-element.177), channel_id=1, source_target_pairs={{0,2},{1,3},{2,0},{3,1},{4,6},{5,7},{6,4},{7,5},{8,10},{9,11},{10,... | collective-permute-start | bytes 958472 | tf_op jit(solution)/shard_map/ppermute | solution.py:409
  82.7 38.4 %collective-permute-start.15 = (bf16[384,1536]{1,0:T(8,128)(2,1)S(1)}, bf16[384,1536]{1,0:T(8,128)(2,1)}, u32[]{:S(2)}, u32[]{:S(2)}) collective-permute-start(bf16[384,1536]{1,0:T(8,128)(2,1)S(1)} %get-tuple-element.188.refs_0_), channel_id=1, source_target_pairs={{0,4},{1,5},{2,6},{3,7},{4,0},{5,1},{6,2},{7,3},{8,12},{9,13},{10,... | collective-permute-start | bytes 3538952 | tf_op jit(solution)/shard_map/ppermute | solution.py:409
  91.9 100.3 %all-to-all-start.1 = ((bf16[8,96,1536]{2,1,0:T(8,128)(2,1)}), bf16[8,96,1536]{2,1,0:T(8,128)(2,1)}, u32[]{:S(2)}, u32[]{:S(2)}) async-start(bf16[8,96,1536]{2,1,0:T(8,128)(2,1)} %pad_maximum_fusion), calls=%async_computation.1 | async-start | bytes 4718592 | tf_op jit(solution)/shard_map/all_to_all | solution.py:1013
  110.7 10.4 %collective-permute-start.10 = (bf16[208,768]{1,0:T(8,128)(2,1)S(1)}, bf16[208,768]{1,0:T(8,128)(2,1)S(1)}, u32[]{:S(2)}, u32[]{:S(2)}) collective-permute-start(bf16[208,768]{1,0:T(8,128)(2,1)S(1)} %get-tuple-element.183.b0), channel_id=1, source_target_pairs={{0,1},{1,0},{2,3},{3,2},{4,5},{5,4},{6,7},{7,6},{8,9},{9,8},{10,11... | collective-permute-start | bytes 958472 | tf_op jit(solution)/shard_map/ppermute | solution.py:409
  111.3 9.8 %collective-permute-start.11 = (bf16[208,768]{1,0:T(8,128)(2,1)S(1)}, bf16[208,768]{1,0:T(8,128)(2,1)S(1)}, u32[]{:S(2)}, u32[]{:S(2)}) collective-permute-start(bf16[208,768]{1,0:T(8,128)(2,1)S(1)} %collective-permute-done.9.b1), channel_id=1, source_target_pairs={{0,1},{1,0},{2,3},{3,2},{4,5},{5,4},{6,7},{7,6},{8,9},{9,8},{10,11... | collective-permute-start | bytes 958472 | tf_op jit(solution)/shard_map/ppermute | solution.py:409
  130.0 9.6 %collective-permute-start.17 = (bf16[208,768]{1,0:T(8,128)(2,1)S(1)}, bf16[208,768]{1,0:T(8,128)(2,1)S(1)}, u32[]{:S(2)}, u32[]{:S(2)}) collective-permute-start(bf16[208,768]{1,0:T(8,128)(2,1)S(1)} %get-tuple-element.192), channel_id=1, source_target_pairs={{0,2},{1,3},{2,0},{3,1},{4,6},{5,7},{6,4},{7,5},{8,10},{9,11},{10,... | collective-permute-start | bytes 958472 | tf_op jit(solution)/shard_map/ppermute | solution.py:409
  141.6 17.9 %collective-permute-start.21 = (bf16[384,768]{1,0:T(8,128)(2,1)S(1)}, bf16[384,768]{1,0:T(8,128)(2,1)S(1)}, u32[]{:S(2)}, u32[]{:S(2)}) collective-permute-start(bf16[384,768]{1,0:T(8,128)(2,1)S(1)} %copy-done.68), channel_id=1, source_target_pairs={{0,4},{1,5},{2,6},{3,7},{4,0},{5,1},{6,2},{7,3},{8,12},{9,13},{10,... | collective-permute-start | bytes 1769480 | tf_op jit(solution)/shard_map/ppermute | solution.py:409
  143.3 16.2 %collective-permute-start.19 = (bf16[208,768]{1,0:T(8,128)(2,1)S(1)}, bf16[208,768]{1,0:T(8,128)(2,1)S(1)}, u32[]{:S(2)}, u32[]{:S(2)}) collective-permute-start(bf16[208,768]{1,0:T(8,128)(2,1)S(1)} %get-tuple-element.194.a0), channel_id=1, source_target_pairs={{0,1},{1,0},{2,3},{3,2},{4,5},{5,4},{6,7},{7,6},{8,9},{9,8},{10,11... | collective-permute-start | bytes 958472 | tf_op jit(solution)/shard_map/ppermute | solution.py:409
  148.9 10.7 %collective-permute-start.20 = (bf16[208,768]{1,0:T(8,128)(2,1)S(1)}, bf16[208,768]{1,0:T(8,128)(2,1)S(1)}, u32[]{:S(2)}, u32[]{:S(2)}) collective-permute-start(bf16[208,768]{1,0:T(8,128)(2,1)S(1)} %collective-permute-done.18.a1), channel_id=1, source_target_pairs={{0,1},{1,0},{2,3},{3,2},{4,5},{5,4},{6,7},{7,6},{8,9},{9,8},{10,11... | collective-permute-start | bytes 958472 | tf_op jit(solution)/shard_map/ppermute | solution.py:409
  168.3 9.6 %collective-permute-start.23 = (bf16[208,768]{1,0:T(8,128)(2,1)S(1)}, bf16[208,768]{1,0:T(8,128)(2,1)S(1)}, u32[]{:S(2)}, u32[]{:S(2)}) collective-permute-start(bf16[208,768]{1,0:T(8,128)(2,1)S(1)} %get-tuple-element.200), channel_id=1, source_target_pairs={{0,2},{1,3},{2,0},{3,1},{4,6},{5,7},{6,4},{7,5},{8,10},{9,11},{10,... | collective-permute-start | bytes 958472 | tf_op jit(solution)/shard_map/ppermute | solution.py:409
  192.2 76.4 %all-to-all-start = ((bf16[8,112,768]{2,1,0:T(8,128)(2,1)}), bf16[8,112,768]{2,1,0:T(8,128)(2,1)}, u32[]{:S(2)}, u32[]{:S(2)}) async-start(bf16[8,112,768]{2,1,0:T(8,128)(2,1)} %pad_maximum_fusion.1), calls=%async_computation | async-start | bytes 2752512 | tf_op jit(solution)/shard_map/all_to_all | solution.py:946
  214.7 16.3 %collective-permute-start.27 = (bf16[192,1536]{1,0:T(8,128)(2,1)S(1)}, bf16[192,1536]{1,0:T(8,128)(2,1)S(1)}, u32[]{:S(2)}, u32[]{:S(2)}) collective-permute-start(bf16[192,1536]{1,0:T(8,128)(2,1)S(1)} %get-tuple-element.355), channel_id=1, source_target_pairs={{0,2},{1,3},{2,0},{3,1},{4,6},{5,7},{6,4},{7,5},{8,10},{9,11},{10,... | collective-permute-start | bytes 1769480 | tf_op jit(solution)/shard_map/ppermute | solution.py:409
  215.3 28.3 %collective-permute-start.28 = (bf16[192,1536]{1,0:T(8,128)(2,1)S(1)}, bf16[192,1536]{1,0:T(8,128)(2,1)S(1)}, u32[]{:S(2)}, u32[]{:S(2)}) collective-permute-start(bf16[192,1536]{1,0:T(8,128)(2,1)S(1)} %get-tuple-element.354), channel_id=1, source_target_pairs={{0,2},{1,3},{2,0},{3,1},{4,6},{5,7},{6,4},{7,5},{8,10},{9,11},{10,... | collective-permute-start | bytes 1769480 | tf_op jit(solution)/shard_map/ppermute | solution.py:409
  216.8 39.5 %collective-permute-start.29 = (bf16[192,1536]{1,0:T(8,128)(2,1)S(1)}, bf16[192,1536]{1,0:T(8,128)(2,1)S(1)}, u32[]{:S(2)}, u32[]{:S(2)}) collective-permute-start(bf16[192,1536]{1,0:T(8,128)(2,1)S(1)} %get-tuple-element.353), channel_id=1, source_target_pairs={{0,2},{1,3},{2,0},{3,1},{4,6},{5,7},{6,4},{7,5},{8,10},{9,11},{10,... | collective-permute-start | bytes 1769480 | tf_op jit(solution)/shard_map/ppermute | solution.py:409
  217.3 50.5 %collective-permute-start.30 = (bf16[192,1536]{1,0:T(8,128)(2,1)S(1)}, bf16[192,1536]{1,0:T(8,128)(2,1)S(1)}, u32[]{:S(2)}, u32[]{:S(2)}) collective-permute-start(bf16[192,1536]{1,0:T(8,128)(2,1)S(1)} %get-tuple-element.352), channel_id=1, source_target_pairs={{0,2},{1,3},{2,0},{3,1},{4,6},{5,7},{6,4},{7,5},{8,10},{9,11},{10,... | collective-permute-start | bytes 1769480 | tf_op jit(solution)/shard_map/ppermute | solution.py:409
  292.6 15.4 %collective-permute-start.35 = (bf16[384,768]{1,0:T(8,128)(2,1)S(1)}, bf16[384,768]{1,0:T(8,128)(2,1)S(1)}, u32[]{:S(2)}, u32[]{:S(2)}) collective-permute-start(bf16[384,768]{1,0:T(8,128)(2,1)S(1)} %get-tuple-element.215), channel_id=1, source_target_pairs={{0,2},{1,3},{2,0},{3,1},{4,6},{5,7},{6,4},{7,5},{8,10},{9,11},{10,... | collective-permute-start | bytes 1769480 | tf_op jit(solution)/shard_map/ppermute | solution.py:409
  308.8 38.1 %all-to-all-start.2 = ((bf16[8,112,768]{2,1,0:T(8,128)(2,1)}), bf16[8,112,768]{2,1,0:T(8,128)(2,1)}, u32[]{:S(2)}, u32[]{:S(2)}) async-start(bf16[8,112,768]{2,1,0:T(8,128)(2,1)} %copy-done.19), calls=%async_computation.2 | async-start | bytes 2752512 | tf_op jit(solution)/shard_map/all_to_all | solution.py:946
  314.6 16.5 %collective-permute-start.36 = (bf16[384,768]{1,0:T(8,128)(2,1)}, bf16[384,768]{1,0:T(8,128)(2,1)S(1)}, u32[]{:S(2)}, u32[]{:S(2)}) collective-permute-start(bf16[384,768]{1,0:T(8,128)(2,1)} %copy-done.149), channel_id=1, source_target_pairs={{0,2},{1,3},{2,0},{3,1},{4,6},{5,7},{6,4},{7,5},{8,10},{9,11},{10,... | collective-permute-start | bytes 1769480 | tf_op jit(solution)/shard_map/ppermute | solution.py:409
  315.1 26.6 %collective-permute-start.37 = (bf16[384,768]{1,0:T(8,128)(2,1)}, bf16[384,768]{1,0:T(8,128)(2,1)S(1)}, u32[]{:S(2)}, u32[]{:S(2)}) collective-permute-start(bf16[384,768]{1,0:T(8,128)(2,1)} %copy-done.148), channel_id=1, source_target_pairs={{0,2},{1,3},{2,0},{3,1},{4,6},{5,7},{6,4},{7,5},{8,10},{9,11},{10,... | collective-permute-start | bytes 1769480 | tf_op jit(solution)/shard_map/ppermute | solution.py:409
  352.3 9.6 %collective-permute-start.39 = (bf16[208,768]{1,0:T(8,128)(2,1)S(1)}, bf16[208,768]{1,0:T(8,128)(2,1)S(1)}, u32[]{:S(2)}, u32[]{:S(2)}) collective-permute-start(bf16[208,768]{1,0:T(8,128)(2,1)S(1)} %get-tuple-element.229), channel_id=1, source_target_pairs={{0,2},{1,3},{2,0},{3,1},{4,6},{5,7},{6,4},{7,5},{8,10},{9,11},{10,... | collective-permute-start | bytes 958472 | tf_op jit(solution)/shard_map/ppermute | solution.py:409
  372.0 15.7 %collective-permute-start.45 = (bf16[384,768]{1,0:T(8,128)(2,1)S(1)}, bf16[384,768]{1,0:T(8,128)(2,1)S(1)}, u32[]{:S(2)}, u32[]{:S(2)}) collective-permute-start(bf16[384,768]{1,0:T(8,128)(2,1)S(1)} %copy-done.144), channel_id=1, source_target_pairs={{0,2},{1,3},{2,0},{3,1},{4,6},{5,7},{6,4},{7,5},{8,10},{9,11},{10,... | collective-permute-start | bytes 1769480 | tf_op jit(solution)/shard_map/ppermute | solution.py:409
  393.0 99.2 %all-to-all-start.3 = ((bf16[8,96,1536]{2,1,0:T(8,128)(2,1)}), bf16[8,96,1536]{2,1,0:T(8,128)(2,1)}, u32[]{:S(2)}, u32[]{:S(2)}) async-start(bf16[8,96,1536]{2,1,0:T(8,128)(2,1)} %bitcast.64), calls=%async_computation.3 | async-start | bytes 4718592 | tf_op jit(solution)/shard_map/all_to_all | solution.py:1108
  397.6 9.9 %collective-permute-start.47 = (bf16[208,768]{1,0:T(8,128)(2,1)}, bf16[208,768]{1,0:T(8,128)(2,1)S(1)}, u32[]{:S(2)}, u32[]{:S(2)}) collective-permute-start(bf16[208,768]{1,0:T(8,128)(2,1)} %copy-done.154), channel_id=1, source_target_pairs={{0,2},{1,3},{2,0},{3,1},{4,6},{5,7},{6,4},{7,5},{8,10},{9,11},{10,... | collective-permute-start | bytes 958472 | tf_op jit(solution)/shard_map/ppermute | solution.py:409
  412.5 9.6 %collective-permute-start.49 = (bf16[208,768]{1,0:T(8,128)(2,1)S(1)}, bf16[208,768]{1,0:T(8,128)(2,1)S(1)}, u32[]{:S(2)}, u32[]{:S(2)}) collective-permute-start(bf16[208,768]{1,0:T(8,128)(2,1)S(1)} %get-tuple-element.248.g0), channel_id=1, source_target_pairs={{0,1},{1,0},{2,3},{3,2},{4,5},{5,4},{6,7},{7,6},{8,9},{9,8},{10,11... | collective-permute-start | bytes 958472 | tf_op jit(solution)/shard_map/ppermute | solution.py:409
  420.8 24.5 %collective-permute-start.43 = (bf16[384,768]{1,0:T(8,128)(2,1)S(1)}, bf16[384,768]{1,0:T(8,128)(2,1)S(1)}, u32[]{:S(2)}, u32[]{:S(2)}) collective-permute-start(bf16[384,768]{1,0:T(8,128)(2,1)S(1)} %copy-done.146), channel_id=1, source_target_pairs={{0,4},{1,5},{2,6},{3,7},{4,0},{5,1},{6,2},{7,3},{8,12},{9,13},{10,... | collective-permute-start | bytes 1769480 | tf_op jit(solution)/shard_map/ppermute | solution.py:409
  430.8 17.5 %collective-permute-start.51 = (bf16[416,768]{1,0:T(8,128)(2,1)S(1)}, bf16[416,768]{1,0:T(8,128)(2,1)S(1)}, u32[]{:S(2)}, u32[]{:S(2)}) collective-permute-start(bf16[416,768]{1,0:T(8,128)(2,1)S(1)} %get-tuple-element.252), channel_id=1, source_target_pairs={{0,1},{1,0},{2,3},{3,2},{4,5},{5,4},{6,7},{7,6},{8,9},{9,8},{10,11... | collective-permute-start | bytes 1916936 | tf_op jit(solution)/shard_map/ppermute | solution.py:409
  448.3 28.8 %collective-permute-start.57 = (bf16[384,1536]{1,0:T(8,128)(2,1)S(1)}, bf16[384,1536]{1,0:T(8,128)(2,1)S(1)}, u32[]{:S(2)}, u32[]{:S(2)}) collective-permute-start(bf16[384,1536]{1,0:T(8,128)(2,1)S(1)} %get-tuple-element.260), channel_id=1, source_target_pairs={{0,4},{1,5},{2,6},{3,7},{4,0},{5,1},{6,2},{7,3},{8,12},{9,13},{10,... | collective-permute-start | bytes 3538952 | tf_op jit(solution)/shard_map/ppermute | solution.py:409
  448.5 9.9 %collective-permute-start.52 = (bf16[208,768]{1,0:T(8,128)(2,1)S(1)}, bf16[208,768]{1,0:T(8,128)(2,1)S(1)}, u32[]{:S(2)}, u32[]{:S(2)}) collective-permute-start(bf16[208,768]{1,0:T(8,128)(2,1)S(1)} %get-tuple-element.254), channel_id=1, source_target_pairs={{0,2},{1,3},{2,0},{3,1},{4,6},{5,7},{6,4},{7,5},{8,10},{9,11},{10,... | collective-permute-start | bytes 958472 | tf_op jit(solution)/shard_map/ppermute | solution.py:409
  459.0 9.1 %collective-permute-start.53 = (bf16[208,768]{1,0:T(8,128)(2,1)S(1)}, bf16[208,768]{1,0:T(8,128)(2,1)S(1)}, u32[]{:S(2)}, u32[]{:S(2)}) collective-permute-start(bf16[208,768]{1,0:T(8,128)(2,1)S(1)} %get-tuple-element.261.g0), channel_id=1, source_target_pairs={{0,2},{1,3},{2,0},{3,1},{4,6},{5,7},{6,4},{7,5},{8,10},{9,11},{10,... | collective-permute-start | bytes 958472 | tf_op jit(solution)/shard_map/ppermute | solution.py:409
  459.6 14.6 %collective-permute-start.54 = (bf16[208,768]{1,0:T(8,128)(2,1)S(1)}, bf16[208,768]{1,0:T(8,128)(2,1)S(1)}, u32[]{:S(2)}, u32[]{:S(2)}) collective-permute-start(bf16[208,768]{1,0:T(8,128)(2,1)S(1)} %get-tuple-element.261.g0), channel_id=1, source_target_pairs={{0,1},{1,0},{2,3},{3,2},{4,5},{5,4},{6,7},{7,6},{8,9},{9,8},{10,11... | collective-permute-start | bytes 958472 | tf_op jit(solution)/shard_map/ppermute | solution.py:409
  469.0 21.2 %collective-permute-start.58 = (bf16[96,768]{1,0:T(8,128)(2,1)S(1)}, bf16[96,768]{1,0:T(8,128)(2,1)S(1)}, u32[]{:S(2)}, u32[]{:S(2)}) collective-permute-start(bf16[96,768]{1,0:T(8,128)(2,1)S(1)} %get-tuple-element.273), channel_id=1, source_target_pairs={{0,8},{1,9},{2,10},{3,11},{4,12},{5,13},{6,14},{7,15},{8,0},{9,1},... | collective-permute-start | bytes 442376 | tf_op jit(solution)/shard_map/ppermute | solution.py:409
  474.2 16.7 %collective-permute-start.59 = (bf16[96,768]{1,0:T(8,128)(2,1)S(1)}, bf16[96,768]{1,0:T(8,128)(2,1)S(1)}, u32[]{:S(2)}, u32[]{:S(2)}) collective-permute-start(bf16[96,768]{1,0:T(8,128)(2,1)S(1)} %get-tuple-element.274), channel_id=1, source_target_pairs={{0,16},{1,17},{2,18},{3,19},{4,20},{5,21},{6,22},{7,23},{8,24},{9,... | collective-permute-start | bytes 442376 | tf_op jit(solution)/shard_map/ppermute | solution.py:409
  474.2 17.4 %collective-permute-start.60 = (bf16[96,768]{1,0:T(8,128)(2,1)S(1)}, bf16[96,768]{1,0:T(8,128)(2,1)S(1)}, u32[]{:S(2)}, u32[]{:S(2)}) collective-permute-start(bf16[96,768]{1,0:T(8,128)(2,1)S(1)} %get-tuple-element.275), channel_id=1, source_target_pairs={{0,24},{1,25},{2,26},{3,27},{4,28},{5,29},{6,30},{7,31},{8,16},{9,... | collective-permute-start | bytes 442376 | tf_op jit(solution)/shard_map/ppermute | solution.py:409
  476.5 15.7 %collective-permute-start.56 = (bf16[208,768]{1,0:T(8,128)(2,1)S(1)}, bf16[208,768]{1,0:T(8,128)(2,1)S(1)}, u32[]{:S(2)}, u32[]{:S(2)}) collective-permute-start(bf16[208,768]{1,0:T(8,128)(2,1)S(1)} %get-tuple-element.257), channel_id=1, source_target_pairs={{0,2},{1,3},{2,0},{3,1},{4,6},{5,7},{6,4},{7,5},{8,10},{9,11},{10,... | collective-permute-start | bytes 958472 | tf_op jit(solution)/shard_map/ppermute | solution.py:409
  492.3 16.0 %collective-permute-start.63 = (bf16[384,768]{1,0:T(8,128)(2,1)}, bf16[384,768]{1,0:T(8,128)(2,1)S(1)}, u32[]{:S(2)}, u32[]{:S(2)}) collective-permute-start(bf16[384,768]{1,0:T(8,128)(2,1)} %copy-done.147), channel_id=1, source_target_pairs={{0,4},{1,5},{2,6},{3,7},{4,0},{5,1},{6,2},{7,3},{8,12},{9,13},{10,... | collective-permute-start | bytes 1769480 | tf_op jit(solution)/shard_map/ppermute | solution.py:409
  494.7 13.6 %collective-permute-start.62 = (bf16[208,768]{1,0:T(8,128)(2,1)S(1)}, bf16[208,768]{1,0:T(8,128)(2,1)S(1)}, u32[]{:S(2)}, u32[]{:S(2)}) collective-permute-start(bf16[208,768]{1,0:T(8,128)(2,1)S(1)} %get-tuple-element.282), channel_id=1, source_target_pairs={{0,2},{1,3},{2,0},{3,1},{4,6},{5,7},{6,4},{7,5},{8,10},{9,11},{10,... | collective-permute-start | bytes 958472 | tf_op jit(solution)/shard_map/ppermute | solution.py:409
  498.6 13.6 %collective-permute-start.65 = (bf16[96,1536]{1,0:T(8,128)(2,1)}, bf16[96,1536]{1,0:T(8,128)(2,1)S(1)}, u32[]{:S(2)}, u32[]{:S(2)}) collective-permute-start(bf16[96,1536]{1,0:T(8,128)(2,1)} %get-tuple-element.293), channel_id=1, source_target_pairs={{0,8},{1,9},{2,10},{3,11},{4,12},{5,13},{6,14},{7,15},{8,0},{9,1},... | collective-permute-start | bytes 884744 | tf_op jit(solution)/shard_map/ppermute | solution.py:409
  502.5 23.6 %collective-permute-start.66 = (bf16[96,1536]{1,0:T(8,128)(2,1)}, bf16[96,1536]{1,0:T(8,128)(2,1)S(1)}, u32[]{:S(2)}, u32[]{:S(2)}) collective-permute-start(bf16[96,1536]{1,0:T(8,128)(2,1)} %get-tuple-element.294), channel_id=1, source_target_pairs={{0,16},{1,17},{2,18},{3,19},{4,20},{5,21},{6,22},{7,23},{8,24},{9,... | collective-permute-start | bytes 884744 | tf_op jit(solution)/shard_map/ppermute | solution.py:409
  502.5 23.6 %collective-permute-start.67 = (bf16[96,1536]{1,0:T(8,128)(2,1)}, bf16[96,1536]{1,0:T(8,128)(2,1)S(1)}, u32[]{:S(2)}, u32[]{:S(2)}) collective-permute-start(bf16[96,1536]{1,0:T(8,128)(2,1)} %get-tuple-element.295), channel_id=1, source_target_pairs={{0,24},{1,25},{2,26},{3,27},{4,28},{5,29},{6,30},{7,31},{8,16},{9,... | collective-permute-start | bytes 884744 | tf_op jit(solution)/shard_map/ppermute | solution.py:409
  530.5 14.2 %collective-permute-start.69 = (f32[4,16,96]{2,1,0:T(8,128)S(1)}, f32[4,16,96]{2,1,0:T(8,128)S(1)}, u32[]{:S(2)}, u32[]{:S(2)}) collective-permute-start(f32[4,16,96]{2,1,0:T(8,128)S(1)} %slice.95), channel_id=1, source_target_pairs={{0,4},{1,5},{2,6},{3,7},{4,0},{5,1},{6,2},{7,3},{8,12},{9,13},{10,... | collective-permute-start | bytes 73736 | tf_op jit(solution)/shard_map/ppermute | solution.py:409
  546.7 14.0 %collective-permute-start.70 = (bf16[128,768]{1,0:T(8,128)(2,1)S(1)}, bf16[128,768]{1,0:T(8,128)(2,1)S(1)}, u32[]{:S(2)}, u32[]{:S(2)}) collective-permute-start(bf16[128,768]{1,0:T(8,128)(2,1)S(1)} %get-tuple-element.299), channel_id=1, source_target_pairs={{0,8},{1,9},{2,10},{3,11},{4,12},{5,13},{6,14},{7,15},{8,0},{9,1},... | collective-permute-start | bytes 589832 | tf_op jit(solution)/shard_map/ppermute | solution.py:409
  552.2 14.6 %collective-permute-start.71 = (bf16[128,768]{1,0:T(8,128)(2,1)S(1)}, bf16[128,768]{1,0:T(8,128)(2,1)S(1)}, u32[]{:S(2)}, u32[]{:S(2)}) collective-permute-start(bf16[128,768]{1,0:T(8,128)(2,1)S(1)} %get-tuple-element.300), channel_id=1, source_target_pairs={{0,16},{1,17},{2,18},{3,19},{4,20},{5,21},{6,22},{7,23},{8,24},{9,... | collective-permute-start | bytes 589832 | tf_op jit(solution)/shard_map/ppermute | solution.py:409
  552.2 14.6 %collective-permute-start.72 = (bf16[128,768]{1,0:T(8,128)(2,1)S(1)}, bf16[128,768]{1,0:T(8,128)(2,1)S(1)}, u32[]{:S(2)}, u32[]{:S(2)}) collective-permute-start(bf16[128,768]{1,0:T(8,128)(2,1)S(1)} %get-tuple-element.301), channel_id=1, source_target_pairs={{0,24},{1,25},{2,26},{3,27},{4,28},{5,29},{6,30},{7,31},{8,16},{9,... | collective-permute-start | bytes 589832 | tf_op jit(solution)/shard_map/ppermute | solution.py:409
  (201 other events, 1535.8 us)
Sparse Core Ops, SparseCore 0:
  12.3 50.9 all-gather.1

commit v5 on v4

--- a/solution.py
+++ b/solution.py
@@ -756,13 +756,11 @@
         refs[-1][i * rows : (i + 1) * rows] = ref[...]
 
 
-def order_kernel(places, in_ref, first_ref, second_ref):
-    rows = first_ref.shape[0] // 4
-    cut = first_ref.shape[1]
+def order_kernel(places, in_ref, out_ref):
+    rows = out_ref.shape[0] // 4
     for i in range(4):
         at = pl.multiple_of(places[i] * rows, rows)
-        first_ref[i * rows : (i + 1) * rows] = in_ref[pl.ds(at, rows), :cut]
-        second_ref[i * rows : (i + 1) * rows] = in_ref[pl.ds(at, rows), cut:]
+        out_ref[i * rows : (i + 1) * rows] = in_ref[pl.ds(at, rows), :]
 
 
 def sum_two(near, got, keep, s1, s2, s3):
@@ -1001,14 +999,14 @@
     near, far = over_group(own, sib)
     one, normed = join(start, near, hold(far, raw_late), gains[1])
     normed_mlp = spread(normed)
-    z_mlp, z_late = run(
+    z_late = run(
         order_kernel,
-        [((4 * width, 2 * ff_cols), BF), ((4 * width, 4 * head_cols), BF)],
+        [(raw_late.shape, BF)],
         (jnp.stack([z_index ^ k for k in range(4)]).astype(jnp.int32), hold(raw_late, one)),
         features,
         scalars=1,
-    )
-    x_mlp = swap(z_mlp, x=1)
+    )[0]
+    x_late = swap(z_late, x=1)
     e_pack = hold(e_pack, normed_mlp[1])
     e_own = lax.all_to_all(e_pack, "dp", split_axis=0, concat_axis=0, tiled=True)
     e_own = e_own.reshape(features, wide)
@@ -1016,25 +1014,23 @@
     far = [swap(e_own[i * 2 * width : (i + 1) * 2 * width], y=1) for i in range(4)]
     e_far = far
     grad_sent = to_experts(dispatch_kernel, spread(hold(grad_low, normed)))
-    full_mlp = stacked([z_mlp, x_mlp])
-    x_late = swap(hold(z_late, full_mlp), x=1)
+    full_late = stacked([z_late, x_late])
     ats = (0, ff_cols)
     act, slope, own, sib = run(
         functools.partial(mlp_kernel, ats),
         [((4 * ROWS, ff_cols), BF)] * 2 + pair_out,
-        (*hold(normed_mlp, grad_sent), full_mlp),
+        (*hold(normed_mlp, grad_sent), full_late),
         0,
         scratch=[group_scratch],
     )
     near, far = over_group(own, sib)
     two, normed = join(one, near, far, gains[2])
     normed_two = spread(normed)
-    full_late = stacked([z_late, x_late])
-    mixed_two, att_two, own, sib, peak_two = attend(normed_two, full_late, 0)
+    mixed_two, att_two, own, sib, peak_two = attend(normed_two, full_late, 2 * ff_cols)
     near, far = over_group(own, sib)
     three, normed = join(two, near, far, gains[3])
     tokens_sent = to_experts(token_kernel, spread(normed), peak_one, peak_two)
-    both = exchange(jnp.concatenate([grad_sent, tokens_sent], axis=1))
+    both = exchange(hold(jnp.concatenate([grad_sent, tokens_sent], axis=1), e_far[0]))
     grad_slots, tokens, peaks = run(
         collect_kernel,
         [((slot_rows, features), BF)] * 2 + [((2, 128), F32)],
@@ -1095,14 +1091,14 @@
     low = spread(low)
     down_got.append(swap(hold(e_packs[5], low[1]), y=1))
     *second, own, sib = attend_back(
-        low, normed_two, mixed_two, att_two, full_late, 0
+        low, normed_two, mixed_two, att_two, full_late, 2 * ff_cols
     )
     second = scatter_start(second)
     near, far = over_group(own, hold(sib, down_got[1]))
     e_sum = run(
         add_pack_kernel,
         [((features, wide), BF)],
-        (e_packs[0], *up_got, e_packs[3], *hold(down_got, near)),
+        (e_packs[0], *up_got, e_packs[3], *hold(down_got, second[1], far)),
         0,
     )[0].reshape(experts, width, wide)
     e_back = lax.all_to_all(e_sum, "dp", split_axis=0, concat_axis=0, tiled=True)
@@ -1113,14 +1109,14 @@
     *mlp, own, sib = run(
         functools.partial(mlp_back_kernel, ats),
         pack_shapes(2 * ff_cols),
-        (*low, *normed_mlp, act, slope, full_mlp),
+        (*low, *normed_mlp, act, slope, full_late),
         0,
         scratch=[group_scratch, pltpu.VMEM((4 * ROWS, ff_cols), BF)],
     )
     mlp = scatter_start(mlp)
     near, send = run(pair_add_kernel, [row, row_low], (own, swap(sib, core=1)), ROWS)
     far = swap(send, y=1)
-    mixed_own, mixed_sib = combine(1, hold(both, second[1]))
+    mixed_own, mixed_sib = combine(1, hold(both, sib))
     second = scatter_late(scatter_middle(hold(second, mixed_own)))
     mixed_own, mixed_send = run(
         pair_add_kernel, [row, row_low], (mixed_own, swap(mixed_sib, core=1)), ROWS
@@ -1142,13 +1138,25 @@
     first = scatter_start(first)
     near, far = over_group(own, hold(sib, mixed_far, second, e_back))
     grad_zero, _, gain_one = norm_back(start, grad_one, near, hold(far, first), gains[0])
+    block_output = run(
+        finish_kernel,
+        [((L, features), F32)],
+        (live_here, three, mixed_own, mixed_far, perm),
+        6 * ROWS * features**2,
+        scalars=1,
+    )[0]
+    up_g = e_back[:, :, :ff_cols].astype(F32)
+    down_g = jnp.swapaxes(e_back[:, :, ff_cols:], 1, 2).astype(F32)
+    clips = (clip_columns(first_qkv, roots[0], HD), clip_columns(second_qkv, roots[1], HD))
     gains_sum = run(
         small_kernel,
         [((8, 16, width), F32)],
         (gain_one, gain_two, gain_three, gain_four, grad_router),
         0,
     )[0]
-    gains_sum = hold(gains_sum + swap(gains_sum, core=1), mlp)
+    gains_sum = hold(
+        gains_sum + swap(gains_sum, core=1), mlp, block_output, up_g, down_g, clips
+    )
     gains_sum = gains_sum + swap(gains_sum, y=1)
     gains_sum = gains_sum[:4] + swap(gains_sum[4:], x=1)
     near_first, got_first = first
@@ -1160,15 +1168,6 @@
         0,
     )
     first = scatter_late(first)
-    block_output = run(
-        finish_kernel,
-        [((L, features), F32)],
-        (live_here, three, mixed_own, mixed_far, perm),
-        6 * ROWS * features**2,
-        scalars=1,
-    )[0]
-    up_g = e_back[:, :, :ff_cols].astype(F32)
-    down_g = jnp.swapaxes(e_back[:, :, ff_cols:], 1, 2).astype(F32)
     input_grad = run(
         leave_kernel,
         [((L, features), F32)],
@@ -1201,8 +1200,7 @@
         tail[4 : 4 + experts].T,
         up_g,
         down_g,
-        clip_columns(first_qkv, roots[0], HD),
-        clip_columns(second_qkv, roots[1], HD),
+        *clips,
         roots,
     )
 

time: 585 us -> 569 us (0.973)
  starting transfers between devices: 109 us -> 101 us
    unnamed x352 -> x296, local copies, waits for them, and re-layouts: 65.9 us -> 60.3 us
    ppermute x73 -> x72, starting transfers between devices: 61.4 us -> 58.1 us  [swap(): return lax.ppermute(values, AXES, pairs)]
    ppermute x73 -> x72, waiting for transfers between devices: 277 us -> 276 us  [swap(): return lax.ppermute(values, AXES, pairs)]
    pallas_call x47 -> x46, Pallas kernels: 84.9 us -> 85.7 us  [run(): pl.pallas_call(kernel, out_shape=shapes, in_specs=[SM] * scalars + [VM] *...]
  transfers between devices with their start and end apart: 78 -> 77, of which waited for: 49 -> 47; matrix products, arithmetic and copies ran while one was open for 3% -> 4% of each run, Pallas kernels for 10% -> 11%
where the time goes in v5:
time: 569 us; the launch traced here: 561 us
  waiting for transfers between devices  281 us (49%)
  starting transfers between devices  101 us (18%)
  Pallas kernels  85.7 us (15%)
  local copies, waits for them, and re-layouts  67.9 us (12%)
  between operations  16.5 us (3%)
  other arithmetic  8.64 us (2%)
    ppermute x72, waiting for transfers between devices, swap(): return lax.ppermute(values, AXES, pairs)  276 us
    pallas_call x46, Pallas kernels, run(): pl.pallas_call(kernel, out_shape=shapes, in_specs=[SM] * scalars + [VM] *...  85.7 us
    unnamed x296, local copies, waits for them, and re-layouts  60.3 us
    ppermute x72, starting transfers between devices, swap(): return lax.ppermute(values, AXES, pairs)  58.1 us
    all_to_all x2, starting transfers between devices, exchange(): return lax.all_to_all(both, 'dp', split_axis=0, concat_axis=0, tiled=True)  21.9 us
    all_to_all x1, starting transfers between devices, fast_local(): lax.all_to_all(e_pack, 'dp', split_axis=0, concat_axis=0, tiled=True)  16 us
  transfers between devices with their start and end apart: 77, of which 47 were waited for; matrix products, arithmetic and copies ran while one was open for 4% of the time, Pallas kernels for 11%

profile of v5, /device:TPU:0, one launch (start us, length us, event | category | flops | bytes accessed | tf_op | source)
XLA Modules:
  0.0 561.3 jit_solution(18155978913544481984)
XLA Ops:
  13.5 3.1 collective-permute-start
  16.6 2.6 collective-permute-start.1
  19.2 4.5 collective-permute-done.refs_1_
  23.7 13.5 %collective-permute-done.1.refs_2_ = bf16[96,896]{1,0:T(8,128)(2,1)S(1)} collective-permute-done((bf16[96,896]{1,0:T(8,128)(2,1)S(1)}, bf16[96,896]{1,0:T(8,128)(2,1)S(1)}, u32[]{:S(2)}, u32[]{:S(2)}) %collective-permute-start.1) | collective-permute-done | bytes 172064 | tf_op jit(solution)/shard_map/ppermute | solution.py:409
  44.5 4.7 collective-permute-done.4.refs_1_
  58.3 4.7 shard_map.318
  68.5 8.2 %collective-permute-done.8.far_ref = bf16[208,768]{1,0:T(8,128)(2,1)S(1)} collective-permute-done((bf16[208,768]{1,0:T(8,128)(2,1)S(1)}, bf16[208,768]{1,0:T(8,128)(2,1)S(1)}, u32[]{:S(2)}, u32[]{:S(2)}) %collective-permute-start.8) | collective-permute-done | bytes 319520 | tf_op jit(solution)/shard_map/ppermute | solution.py:409
  84.2 2.7 collective-permute-done.9.b1
  86.9 16.0 %all-to-all-start = ((bf16[8,96,1536]{2,1,0:T(8,128)(2,1)}), bf16[8,96,1536]{2,1,0:T(8,128)(2,1)}, u32[]{:S(2)}, u32[]{:S(2)}) async-start(bf16[8,96,1536]{2,1,0:T(8,128)(2,1)} %pad_maximum_fusion), calls=%async_computation | async-start | bytes 4718592 | tf_op jit(solution)/shard_map/all_to_all | solution.py:1011
  105.4 5.7 %collective-permute-done.12.p1 = bf16[208,768]{1,0:T(8,128)(2,1)} collective-permute-done((bf16[208,768]{1,0:T(8,128)(2,1)}, bf16[208,768]{1,0:T(8,128)(2,1)}, u32[]{:S(2)}, u32[]{:S(2)}) %collective-permute-start.12) | collective-permute-done | bytes 319520 | tf_op jit(solution)/shard_map/ppermute | solution.py:409
  117.3 25.0 %collective-permute-done.15.refs_1_ = bf16[384,2304]{1,0:T(8,128)(2,1)} collective-permute-done((bf16[384,2304]{1,0:T(8,128)(2,1)S(1)}, bf16[384,2304]{1,0:T(8,128)(2,1)}, u32[]{:S(2)}, u32[]{:S(2)}) %collective-permute-start.15) | collective-permute-done | bytes 1769504 | tf_op jit(solution)/shard_map/ppermute | solution.py:409
  144.0 4.0 shard_map.325
  151.9 9.1 %collective-permute-done.17.far_ref = bf16[208,768]{1,0:T(8,128)(2,1)S(1)} collective-permute-done((bf16[208,768]{1,0:T(8,128)(2,1)S(1)}, bf16[208,768]{1,0:T(8,128)(2,1)S(1)}, u32[]{:S(2)}, u32[]{:S(2)}) %collective-permute-start.17) | collective-permute-done | bytes 319520 | tf_op jit(solution)/shard_map/ppermute | solution.py:409
  161.9 8.2 %collective-permute-done.18.a1 = bf16[208,768]{1,0:T(8,128)(2,1)S(1)} collective-permute-done((bf16[208,768]{1,0:T(8,128)(2,1)S(1)}, bf16[208,768]{1,0:T(8,128)(2,1)S(1)}, u32[]{:S(2)}, u32[]{:S(2)}) %collective-permute-start.18) | collective-permute-done | bytes 319520 | tf_op jit(solution)/shard_map/ppermute | solution.py:409
  171.7 4.6 shard_map.328
  179.3 9.1 %collective-permute-done.22.far_ref = bf16[208,768]{1,0:T(8,128)(2,1)S(1)} collective-permute-done((bf16[208,768]{1,0:T(8,128)(2,1)S(1)}, bf16[208,768]{1,0:T(8,128)(2,1)S(1)}, u32[]{:S(2)}, u32[]{:S(2)}) %collective-permute-start.22) | collective-permute-done | bytes 319520 | tf_op jit(solution)/shard_map/ppermute | solution.py:409
  190.0 2.8 fusion.22
  194.4 5.6 collective-permute-done.23.p1
  204.4 6.5 %collective-permute-done.26.rest_1_ = bf16[192,1536]{1,0:T(8,128)(2,1)S(1)} collective-permute-done((bf16[192,1536]{1,0:T(8,128)(2,1)S(1)}, bf16[192,1536]{1,0:T(8,128)(2,1)S(1)}, u32[]{:S(2)}, u32[]{:S(2)}) %collective-permute-start.26) | collective-permute-done | bytes 589856 | tf_op jit(solution)/shard_map/ppermute | solution.py:409
  211.7 16.2 %all-to-all-start.1 = ((bf16[8,112,768]{2,1,0:T(8,128)(2,1)}), bf16[8,112,768]{2,1,0:T(8,128)(2,1)S(1)}, u32[]{:S(2)}, u32[]{:S(2)}) async-start(bf16[8,112,768]{2,1,0:T(8,128)(2,1)} %pad_maximum_fusion.1), calls=%async_computation.1 | async-start | bytes 2752512 | tf_op jit(solution)/shard_map/all_to_all | solution.py:944
  230.5 13.9 %collective-permute-done.27.rest_2_ = bf16[192,1536]{1,0:T(8,128)(2,1)S(1)} collective-permute-done((bf16[192,1536]{1,0:T(8,128)(2,1)}, bf16[192,1536]{1,0:T(8,128)(2,1)S(1)}, u32[]{:S(2)}, u32[]{:S(2)}) %collective-permute-start.27) | collective-permute-done | bytes 589856 | tf_op jit(solution)/shard_map/ppermute | solution.py:409
  245.2 11.8 %collective-permute-done.28.rest_3_ = bf16[192,1536]{1,0:T(8,128)(2,1)S(1)} collective-permute-done((bf16[192,1536]{1,0:T(8,128)(2,1)}, bf16[192,1536]{1,0:T(8,128)(2,1)S(1)}, u32[]{:S(2)}, u32[]{:S(2)}) %collective-permute-start.28) | collective-permute-done | bytes 589856 | tf_op jit(solution)/shard_map/ppermute | solution.py:409
  257.9 8.9 %collective-permute-done.29.rest_4_ = bf16[192,1536]{1,0:T(8,128)(2,1)S(1)} collective-permute-done((bf16[192,1536]{1,0:T(8,128)(2,1)}, bf16[192,1536]{1,0:T(8,128)(2,1)S(1)}, u32[]{:S(2)}, u32[]{:S(2)}) %collective-permute-start.29) | collective-permute-done | bytes 589856 | tf_op jit(solution)/shard_map/ppermute | solution.py:409
  272.0 16.6 %shard_map.333 = (f32[448,768]{1,0:T(8,128)}, bf16[448,768]{1,0:T(8,128)(2,1)S(1)}, f32[448,768]{1,0:T(8,128)}, bf16[448,768]{1,0:T(8,128)(2,1)S(1)}, bf16[768,7...) custom-call(s32[1]{0:T(128)} %bitcast.26.number, ...), custom_call_target="tpu_custom_call" | custom-call | flops 1000 | bytes 1000 | tf_op jit(solution)/shard_map/pallas_call | solution.py:419
  299.5 6.1 %collective-permute-done.34.up0 = bf16[384,768]{1,0:T(8,128)(2,1)S(1)} collective-permute-done((bf16[384,768]{1,0:T(8,128)(2,1)S(1)}, bf16[384,768]{1,0:T(8,128)(2,1)S(1)}, u32[]{:S(2)}, u32[]{:S(2)}) %collective-permute-start.34) | collective-permute-done | bytes 589856 | tf_op jit(solution)/shard_map/ppermute | solution.py:409
  306.5 5.7 %all-to-all-start.2 = ((bf16[8,112,768]{2,1,0:T(8,128)(2,1)}), bf16[8,112,768]{2,1,0:T(8,128)(2,1)S(1)}, u32[]{:S(2)}, u32[]{:S(2)}) async-start(bf16[8,112,768]{2,1,0:T(8,128)(2,1)} %copy-done.21), calls=%async_computation.2 | async-start | bytes 2752512 | tf_op jit(solution)/shard_map/all_to_all | solution.py:944
  314.2 14.4 %collective-permute-done.35.up1 = bf16[384,768]{1,0:T(8,128)(2,1)S(1)} collective-permute-done((bf16[384,768]{1,0:T(8,128)(2,1)}, bf16[384,768]{1,0:T(8,128)(2,1)S(1)}, u32[]{:S(2)}, u32[]{:S(2)}) %collective-permute-start.35) | collective-permute-done | bytes 589856 | tf_op jit(solution)/shard_map/ppermute | solution.py:409
  329.5 9.8 %collective-permute-done.36.down0 = bf16[384,768]{1,0:T(8,128)(2,1)S(1)} collective-permute-done((bf16[384,768]{1,0:T(8,128)(2,1)}, bf16[384,768]{1,0:T(8,128)(2,1)S(1)}, u32[]{:S(2)}, u32[]{:S(2)}) %collective-permute-start.36) | collective-permute-done | bytes 589856 | tf_op jit(solution)/shard_map/ppermute | solution.py:409
  340.1 4.4 all-to-all-done.2.both_ref
  348.9 9.1 %collective-permute-done.38.far_ref = bf16[208,768]{1,0:T(8,128)(2,1)S(1)} collective-permute-done((bf16[208,768]{1,0:T(8,128)(2,1)S(1)}, bf16[208,768]{1,0:T(8,128)(2,1)S(1)}, u32[]{:S(2)}, u32[]{:S(2)}) %collective-permute-start.38) | collective-permute-done | bytes 319520 | tf_op jit(solution)/shard_map/ppermute | solution.py:409
  359.8 8.2 %collective-permute-done.39.g1 = bf16[208,768]{1,0:T(8,128)(2,1)S(1)} collective-permute-done((bf16[208,768]{1,0:T(8,128)(2,1)S(1)}, bf16[208,768]{1,0:T(8,128)(2,1)S(1)}, u32[]{:S(2)}, u32[]{:S(2)}) %collective-permute-start.39) | collective-permute-done | bytes 319520 | tf_op jit(solution)/shard_map/ppermute | solution.py:409
  370.8 9.9 %shard_map.338 = (bf16[384,768]{1,0:T(8,128)(2,1)S(1)}, bf16[384,768]{1,0:T(8,128)(2,1)S(1)}, f32[416,768]{1,0:T(8,128)S(1)}, bf16[416,768]{1,0:T(8,128)(2,1)S(1)}) custom-call(bf16[208,768]{1,0:T(8,128)(2,1)S(1)} %get-tuple-element.227.g0, bf16[208,768]{1,0:T(8,128)(2,1)S(1)} %collective-permute-done.39.g1, ...), custom_call_target="tpu_custom_call" | custom-call | flops 8000000000 | bytes 1000 | tf_op jit(solution)/shard_map/pallas_call | solution.py:419
  381.5 2.6 collective-permute-done.42.down1
  387.6 12.2 %collective-permute-done.56.got = bf16[384,768]{1,0:T(8,128)(2,1)S(1)} collective-permute-done((bf16[384,768]{1,0:T(8,128)(2,1)S(1)}, bf16[384,768]{1,0:T(8,128)(2,1)S(1)}, u32[]{:S(2)}, u32[]{:S(2)}) %collective-permute-start.56) | collective-permute-done | bytes 589856 | tf_op jit(solution)/shard_map/ppermute | solution.py:409
  402.1 4.6 all-to-all-start.3
  412.0 8.7 %collective-permute-done.45.g1 = bf16[208,768]{1,0:T(8,128)(2,1)S(1)} collective-permute-done((bf16[208,768]{1,0:T(8,128)(2,1)S(1)}, bf16[208,768]{1,0:T(8,128)(2,1)S(1)}, u32[]{:S(2)}, u32[]{:S(2)}) %collective-permute-start.45) | collective-permute-done | bytes 319520 | tf_op jit(solution)/shard_map/ppermute | solution.py:409
  425.6 5.7 %shard_map.341 = (bf16[384,1536]{1,0:T(8,128)(2,1)S(1)}, bf16[384,1536]{1,0:T(8,128)(2,1)S(1)}, f32[416,768]{1,0:T(8,128)S(1)}, bf16[416,768]{1,0:T(8,128)(2,1)S(1)}) custom-call(bf16[208,768]{1,0:T(8,128)(2,1)S(1)} %get-tuple-element.237.g0, bf16[208,768]{1,0:T(8,128)(2,1)S(1)} %collective-permute-done.45.g1, ...), custom_call_target="tpu_custom_call" | custom-call | flops 1000 | bytes 1000 | tf_op jit(solution)/shard_map/pallas_call | solution.py:419
  436.0 8.6 %collective-permute-done.50.far_ref = bf16[208,768]{1,0:T(8,128)(2,1)S(1)} collective-permute-done((bf16[208,768]{1,0:T(8,128)(2,1)S(1)}, bf16[208,768]{1,0:T(8,128)(2,1)S(1)}, u32[]{:S(2)}, u32[]{:S(2)}) %collective-permute-start.50) | collective-permute-done | bytes 319520 | tf_op jit(solution)/shard_map/ppermute | solution.py:409
  445.7 8.0 %collective-permute-done.51.g1 = bf16[208,768]{1,0:T(8,128)(2,1)S(1)} collective-permute-done((bf16[208,768]{1,0:T(8,128)(2,1)S(1)}, bf16[208,768]{1,0:T(8,128)(2,1)S(1)}, u32[]{:S(2)}, u32[]{:S(2)}) %collective-permute-start.51) | collective-permute-done | bytes 319520 | tf_op jit(solution)/shard_map/ppermute | solution.py:409
  458.4 9.2 %collective-permute-done.55.got = bf16[384,1536]{1,0:T(8,128)(2,1)S(1)} collective-permute-done((bf16[384,1536]{1,0:T(8,128)(2,1)S(1)}, bf16[384,1536]{1,0:T(8,128)(2,1)S(1)}, u32[]{:S(2)}, u32[]{:S(2)}) %collective-permute-start.55) | collective-permute-done | bytes 1179680 | tf_op jit(solution)/shard_map/ppermute | solution.py:409
  471.7 10.1 %shard_map.347 = (bf16[384,768]{1,0:T(8,128)(2,1)S(1)}, bf16[384,768]{1,0:T(8,128)(2,1)S(1)}, f32[416,768]{1,0:T(8,128)S(1)}, bf16[416,768]{1,0:T(8,128)(2,1)S(1)}) custom-call(bf16[208,768]{1,0:T(8,128)(2,1)S(1)} %get-tuple-element.256.g0, bf16[208,768]{1,0:T(8,128)(2,1)S(1)} %collective-permute-done.51.g1, ...), custom_call_target="tpu_custom_call" | custom-call | flops 8000000000 | bytes 1000 | tf_op jit(solution)/shard_map/pallas_call | solution.py:419
  493.5 2.6 collective-permute-start.64
  500.7 2.6 collective-permute-done.62.got
  504.7 4.3 convert_bitcast_fusion
  509.1 10.4 %collective-permute-done.65.r2 = bf16[96,1536]{1,0:T(8,128)(2,1)S(1)} collective-permute-done((bf16[96,1536]{1,0:T(8,128)(2,1)S(1)}, bf16[96,1536]{1,0:T(8,128)(2,1)S(1)}, u32[]{:S(2)}, u32[]{:S(2)}) %collective-permute-start.65) | collective-permute-done | bytes 294944 | tf_op jit(solution)/shard_map/ppermute | solution.py:409
  520.1 3.8 collective-permute-done.67
  524.1 3.8 collective-permute-done.68
  529.8 5.4 collective-permute-start.69
  (496 shorter events, 166.4 us)
Async XLA Ops:
  7.3 69.5 %all-gather.2.cloned.1.call-start = ((), (), s32[]{:S(2)}) async-start(), calls=%async_computation.4 | async-start | bytes 2211840 | tf_op jit(solution)/shard_map/all_gather | solution.py:888
  13.5 10.2 %collective-permute-start = (bf16[96,896]{1,0:T(8,128)(2,1)S(1)}, bf16[96,896]{1,0:T(8,128)(2,1)S(1)}, u32[]{:S(2)}, u32[]{:S(2)}) collective-permute-start(bf16[96,896]{1,0:T(8,128)(2,1)S(1)} %shard_map.314.refs_0_), channel_id=1, source_target_pairs={{0,8},{1,9},{2,10},{3,11},{4,12},{5,13},{6,14},{7,15},{8,0},{9,1},... | collective-permute-start | bytes 516104 | tf_op jit(solution)/shard_map/ppermute | solution.py:409
  16.6 20.5 %collective-permute-start.1 = (bf16[96,896]{1,0:T(8,128)(2,1)S(1)}, bf16[96,896]{1,0:T(8,128)(2,1)S(1)}, u32[]{:S(2)}, u32[]{:S(2)}) collective-permute-start(bf16[96,896]{1,0:T(8,128)(2,1)S(1)} %shard_map.314.refs_0_), channel_id=1, source_target_pairs={{0,16},{1,17},{2,18},{3,19},{4,20},{5,21},{6,22},{7,23},{8,24},{9,... | collective-permute-start | bytes 516104 | tf_op jit(solution)/shard_map/ppermute | solution.py:409
  19.2 18.0 %collective-permute-start.2 = (bf16[96,896]{1,0:T(8,128)(2,1)S(1)}, bf16[96,896]{1,0:T(8,128)(2,1)S(1)}, u32[]{:S(2)}, u32[]{:S(2)}) collective-permute-start(bf16[96,896]{1,0:T(8,128)(2,1)S(1)} %shard_map.314.refs_0_), channel_id=1, source_target_pairs={{0,24},{1,25},{2,26},{3,27},{4,28},{5,29},{6,30},{7,31},{8,16},{9,... | collective-permute-start | bytes 516104 | tf_op jit(solution)/shard_map/ppermute | solution.py:409
  37.2 13.8 %collective-permute-start.3 = (bf16[384,896]{1,0:T(8,128)(2,1)S(1)}, bf16[384,896]{1,0:T(8,128)(2,1)S(1)}, u32[]{:S(2)}, u32[]{:S(2)}) collective-permute-start(bf16[384,896]{1,0:T(8,128)(2,1)S(1)} %shard_map.315.refs_0_), channel_id=1, source_target_pairs={{0,4},{1,5},{2,6},{3,7},{4,0},{5,1},{6,2},{7,3},{8,12},{9,13},{10,... | collective-permute-start | bytes 2064392 | tf_op jit(solution)/shard_map/ppermute | solution.py:409
  67.0 9.8 %collective-permute-start.8 = (bf16[208,768]{1,0:T(8,128)(2,1)S(1)}, bf16[208,768]{1,0:T(8,128)(2,1)S(1)}, u32[]{:S(2)}, u32[]{:S(2)}) collective-permute-start(bf16[208,768]{1,0:T(8,128)(2,1)S(1)} %get-tuple-element.175), channel_id=1, source_target_pairs={{0,2},{1,3},{2,0},{3,1},{4,6},{5,7},{6,4},{7,5},{8,10},{9,11},{10,... | collective-permute-start | bytes 958472 | tf_op jit(solution)/shard_map/ppermute | solution.py:409
  77.9 9.0 %collective-permute-start.9 = (bf16[208,768]{1,0:T(8,128)(2,1)S(1)}, bf16[208,768]{1,0:T(8,128)(2,1)}, u32[]{:S(2)}, u32[]{:S(2)}) collective-permute-start(bf16[208,768]{1,0:T(8,128)(2,1)S(1)} %get-tuple-element.181.b0), channel_id=1, source_target_pairs={{0,2},{1,3},{2,0},{3,1},{4,6},{5,7},{6,4},{7,5},{8,10},{9,11},{10,... | collective-permute-start | bytes 958472 | tf_op jit(solution)/shard_map/ppermute | solution.py:409
  81.6 60.7 %collective-permute-start.15 = (bf16[384,2304]{1,0:T(8,128)(2,1)S(1)}, bf16[384,2304]{1,0:T(8,128)(2,1)}, u32[]{:S(2)}, u32[]{:S(2)}) collective-permute-start(bf16[384,2304]{1,0:T(8,128)(2,1)S(1)} %shard_map.323.refs_0_), channel_id=1, source_target_pairs={{0,4},{1,5},{2,6},{3,7},{4,0},{5,1},{6,2},{7,3},{8,12},{9,13},{10,... | collective-permute-start | bytes 5308424 | tf_op jit(solution)/shard_map/ppermute | solution.py:409
  86.9 103.1 %all-to-all-start = ((bf16[8,96,1536]{2,1,0:T(8,128)(2,1)}), bf16[8,96,1536]{2,1,0:T(8,128)(2,1)}, u32[]{:S(2)}, u32[]{:S(2)}) async-start(bf16[8,96,1536]{2,1,0:T(8,128)(2,1)} %pad_maximum_fusion), calls=%async_computation | async-start | bytes 4718592 | tf_op jit(solution)/shard_map/all_to_all | solution.py:1011
  104.8 12.4 %collective-permute-start.10 = (bf16[208,768]{1,0:T(8,128)(2,1)S(1)}, bf16[208,768]{1,0:T(8,128)(2,1)S(1)}, u32[]{:S(2)}, u32[]{:S(2)}) collective-permute-start(bf16[208,768]{1,0:T(8,128)(2,1)S(1)} %get-tuple-element.181.b0), channel_id=1, source_target_pairs={{0,1},{1,0},{2,3},{3,2},{4,5},{5,4},{6,7},{7,6},{8,9},{9,8},{10,11... | collective-permute-start | bytes 958472 | tf_op jit(solution)/shard_map/ppermute | solution.py:409
  105.3 11.9 %collective-permute-start.11 = (bf16[208,768]{1,0:T(8,128)(2,1)}, bf16[208,768]{1,0:T(8,128)(2,1)S(1)}, u32[]{:S(2)}, u32[]{:S(2)}) collective-permute-start(bf16[208,768]{1,0:T(8,128)(2,1)} %collective-permute-done.9.b1), channel_id=1, source_target_pairs={{0,1},{1,0},{2,3},{3,2},{4,5},{5,4},{6,7},{7,6},{8,9},{9,8},{10,11... | collective-permute-start | bytes 958472 | tf_op jit(solution)/shard_map/ppermute | solution.py:409
  151.3 9.6 %collective-permute-start.17 = (bf16[208,768]{1,0:T(8,128)(2,1)S(1)}, bf16[208,768]{1,0:T(8,128)(2,1)S(1)}, u32[]{:S(2)}, u32[]{:S(2)}) collective-permute-start(bf16[208,768]{1,0:T(8,128)(2,1)S(1)} %get-tuple-element.189), channel_id=1, source_target_pairs={{0,2},{1,3},{2,0},{3,1},{4,6},{5,7},{6,4},{7,5},{8,10},{9,11},{10,... | collective-permute-start | bytes 958472 | tf_op jit(solution)/shard_map/ppermute | solution.py:409
  161.3 8.8 %collective-permute-start.18 = (bf16[208,768]{1,0:T(8,128)(2,1)S(1)}, bf16[208,768]{1,0:T(8,128)(2,1)S(1)}, u32[]{:S(2)}, u32[]{:S(2)}) collective-permute-start(bf16[208,768]{1,0:T(8,128)(2,1)S(1)} %get-tuple-element.191.a0), channel_id=1, source_target_pairs={{0,2},{1,3},{2,0},{3,1},{4,6},{5,7},{6,4},{7,5},{8,10},{9,11},{10,... | collective-permute-start | bytes 958472 | tf_op jit(solution)/shard_map/ppermute | solution.py:409
  178.7 9.6 %collective-permute-start.22 = (bf16[208,768]{1,0:T(8,128)(2,1)S(1)}, bf16[208,768]{1,0:T(8,128)(2,1)S(1)}, u32[]{:S(2)}, u32[]{:S(2)}) collective-permute-start(bf16[208,768]{1,0:T(8,128)(2,1)S(1)} %get-tuple-element.195), channel_id=1, source_target_pairs={{0,2},{1,3},{2,0},{3,1},{4,6},{5,7},{6,4},{7,5},{8,10},{9,11},{10,... | collective-permute-start | bytes 958472 | tf_op jit(solution)/shard_map/ppermute | solution.py:409
  189.5 10.5 %collective-permute-start.23 = (bf16[208,768]{1,0:T(8,128)(2,1)S(1)}, bf16[208,768]{1,0:T(8,128)(2,1)S(1)}, u32[]{:S(2)}, u32[]{:S(2)}) collective-permute-start(bf16[208,768]{1,0:T(8,128)(2,1)S(1)} %get-tuple-element.197.p0), channel_id=1, source_target_pairs={{0,2},{1,3},{2,0},{3,1},{4,6},{5,7},{6,4},{7,5},{8,10},{9,11},{10,... | collective-permute-start | bytes 958472 | tf_op jit(solution)/shard_map/ppermute | solution.py:409
  192.8 18.1 %collective-permute-start.26 = (bf16[192,1536]{1,0:T(8,128)(2,1)S(1)}, bf16[192,1536]{1,0:T(8,128)(2,1)S(1)}, u32[]{:S(2)}, u32[]{:S(2)}) collective-permute-start(bf16[192,1536]{1,0:T(8,128)(2,1)S(1)} %get-tuple-element.351), channel_id=1, source_target_pairs={{0,2},{1,3},{2,0},{3,1},{4,6},{5,7},{6,4},{7,5},{8,10},{9,11},{10,... | collective-permute-start | bytes 1769480 | tf_op jit(solution)/shard_map/ppermute | solution.py:409
  211.7 55.9 %all-to-all-start.1 = ((bf16[8,112,768]{2,1,0:T(8,128)(2,1)}), bf16[8,112,768]{2,1,0:T(8,128)(2,1)S(1)}, u32[]{:S(2)}, u32[]{:S(2)}) async-start(bf16[8,112,768]{2,1,0:T(8,128)(2,1)} %pad_maximum_fusion.1), calls=%async_computation.1 | async-start | bytes 2752512 | tf_op jit(solution)/shard_map/all_to_all | solution.py:944
  227.9 16.5 %collective-permute-start.27 = (bf16[192,1536]{1,0:T(8,128)(2,1)}, bf16[192,1536]{1,0:T(8,128)(2,1)S(1)}, u32[]{:S(2)}, u32[]{:S(2)}) collective-permute-start(bf16[192,1536]{1,0:T(8,128)(2,1)} %get-tuple-element.350), channel_id=1, source_target_pairs={{0,2},{1,3},{2,0},{3,1},{4,6},{5,7},{6,4},{7,5},{8,10},{9,11},{10,... | collective-permute-start | bytes 1769480 | tf_op jit(solution)/shard_map/ppermute | solution.py:409
  228.5 28.6 %collective-permute-start.28 = (bf16[192,1536]{1,0:T(8,128)(2,1)}, bf16[192,1536]{1,0:T(8,128)(2,1)S(1)}, u32[]{:S(2)}, u32[]{:S(2)}) collective-permute-start(bf16[192,1536]{1,0:T(8,128)(2,1)} %get-tuple-element.349), channel_id=1, source_target_pairs={{0,2},{1,3},{2,0},{3,1},{4,6},{5,7},{6,4},{7,5},{8,10},{9,11},{10,... | collective-permute-start | bytes 1769480 | tf_op jit(solution)/shard_map/ppermute | solution.py:409
  230.0 36.8 %collective-permute-start.29 = (bf16[192,1536]{1,0:T(8,128)(2,1)}, bf16[192,1536]{1,0:T(8,128)(2,1)S(1)}, u32[]{:S(2)}, u32[]{:S(2)}) collective-permute-start(bf16[192,1536]{1,0:T(8,128)(2,1)} %get-tuple-element.348), channel_id=1, source_target_pairs={{0,2},{1,3},{2,0},{3,1},{4,6},{5,7},{6,4},{7,5},{8,10},{9,11},{10,... | collective-permute-start | bytes 1769480 | tf_op jit(solution)/shard_map/ppermute | solution.py:409
  290.2 15.4 %collective-permute-start.34 = (bf16[384,768]{1,0:T(8,128)(2,1)S(1)}, bf16[384,768]{1,0:T(8,128)(2,1)S(1)}, u32[]{:S(2)}, u32[]{:S(2)}) collective-permute-start(bf16[384,768]{1,0:T(8,128)(2,1)S(1)} %get-tuple-element.211), channel_id=1, source_target_pairs={{0,2},{1,3},{2,0},{3,1},{4,6},{5,7},{6,4},{7,5},{8,10},{9,11},{10,... | collective-permute-start | bytes 1769480 | tf_op jit(solution)/shard_map/ppermute | solution.py:409
  306.5 38.0 %all-to-all-start.2 = ((bf16[8,112,768]{2,1,0:T(8,128)(2,1)}), bf16[8,112,768]{2,1,0:T(8,128)(2,1)S(1)}, u32[]{:S(2)}, u32[]{:S(2)}) async-start(bf16[8,112,768]{2,1,0:T(8,128)(2,1)} %copy-done.21), calls=%async_computation.2 | async-start | bytes 2752512 | tf_op jit(solution)/shard_map/all_to_all | solution.py:944
  312.2 16.5 %collective-permute-start.35 = (bf16[384,768]{1,0:T(8,128)(2,1)}, bf16[384,768]{1,0:T(8,128)(2,1)S(1)}, u32[]{:S(2)}, u32[]{:S(2)}) collective-permute-start(bf16[384,768]{1,0:T(8,128)(2,1)} %copy-done.123), channel_id=1, source_target_pairs={{0,2},{1,3},{2,0},{3,1},{4,6},{5,7},{6,4},{7,5},{8,10},{9,11},{10,... | collective-permute-start | bytes 1769480 | tf_op jit(solution)/shard_map/ppermute | solution.py:409
  312.7 26.6 %collective-permute-start.36 = (bf16[384,768]{1,0:T(8,128)(2,1)}, bf16[384,768]{1,0:T(8,128)(2,1)S(1)}, u32[]{:S(2)}, u32[]{:S(2)}) collective-permute-start(bf16[384,768]{1,0:T(8,128)(2,1)} %copy-done.122), channel_id=1, source_target_pairs={{0,2},{1,3},{2,0},{3,1},{4,6},{5,7},{6,4},{7,5},{8,10},{9,11},{10,... | collective-permute-start | bytes 1769480 | tf_op jit(solution)/shard_map/ppermute | solution.py:409
  348.3 9.6 %collective-permute-start.38 = (bf16[208,768]{1,0:T(8,128)(2,1)S(1)}, bf16[208,768]{1,0:T(8,128)(2,1)S(1)}, u32[]{:S(2)}, u32[]{:S(2)}) collective-permute-start(bf16[208,768]{1,0:T(8,128)(2,1)S(1)} %get-tuple-element.225), channel_id=1, source_target_pairs={{0,2},{1,3},{2,0},{3,1},{4,6},{5,7},{6,4},{7,5},{8,10},{9,11},{10,... | collective-permute-start | bytes 958472 | tf_op jit(solution)/shard_map/ppermute | solution.py:409
  359.3 8.7 %collective-permute-start.39 = (bf16[208,768]{1,0:T(8,128)(2,1)S(1)}, bf16[208,768]{1,0:T(8,128)(2,1)S(1)}, u32[]{:S(2)}, u32[]{:S(2)}) collective-permute-start(bf16[208,768]{1,0:T(8,128)(2,1)S(1)} %get-tuple-element.227.g0), channel_id=1, source_target_pairs={{0,2},{1,3},{2,0},{3,1},{4,6},{5,7},{6,4},{7,5},{8,10},{9,11},{10,... | collective-permute-start | bytes 958472 | tf_op jit(solution)/shard_map/ppermute | solution.py:409
  359.8 8.8 %collective-permute-start.40 = (bf16[208,768]{1,0:T(8,128)(2,1)S(1)}, bf16[208,768]{1,0:T(8,128)(2,1)S(1)}, u32[]{:S(2)}, u32[]{:S(2)}) collective-permute-start(bf16[208,768]{1,0:T(8,128)(2,1)S(1)} %get-tuple-element.227.g0), channel_id=1, source_target_pairs={{0,1},{1,0},{2,3},{3,2},{4,5},{5,4},{6,7},{7,6},{8,9},{9,8},{10,11... | collective-permute-start | bytes 958472 | tf_op jit(solution)/shard_map/ppermute | solution.py:409
  368.1 16.0 %collective-permute-start.42 = (bf16[384,768]{1,0:T(8,128)(2,1)}, bf16[384,768]{1,0:T(8,128)(2,1)S(1)}, u32[]{:S(2)}, u32[]{:S(2)}) collective-permute-start(bf16[384,768]{1,0:T(8,128)(2,1)} %copy-done.120), channel_id=1, source_target_pairs={{0,2},{1,3},{2,0},{3,1},{4,6},{5,7},{6,4},{7,5},{8,10},{9,11},{10,... | collective-permute-start | bytes 1769480 | tf_op jit(solution)/shard_map/ppermute | solution.py:409
  384.0 15.7 %collective-permute-start.56 = (bf16[384,768]{1,0:T(8,128)(2,1)S(1)}, bf16[384,768]{1,0:T(8,128)(2,1)S(1)}, u32[]{:S(2)}, u32[]{:S(2)}) collective-permute-start(bf16[384,768]{1,0:T(8,128)(2,1)S(1)} %get-tuple-element.265), channel_id=1, source_target_pairs={{0,4},{1,5},{2,6},{3,7},{4,0},{5,1},{6,2},{7,3},{8,12},{9,13},{10,... | collective-permute-start | bytes 1769480 | tf_op jit(solution)/shard_map/ppermute | solution.py:409
  387.1 12.7 %collective-permute-start.44 = (bf16[208,768]{1,0:T(8,128)(2,1)S(1)}, bf16[208,768]{1,0:T(8,128)(2,1)S(1)}, u32[]{:S(2)}, u32[]{:S(2)}) collective-permute-start(bf16[208,768]{1,0:T(8,128)(2,1)S(1)} %get-tuple-element.236), channel_id=1, source_target_pairs={{0,2},{1,3},{2,0},{3,1},{4,6},{5,7},{6,4},{7,5},{8,10},{9,11},{10,... | collective-permute-start | bytes 958472 | tf_op jit(solution)/shard_map/ppermute | solution.py:409
  402.1 84.2 %all-to-all-start.3 = ((bf16[8,96,1536]{2,1,0:T(8,128)(2,1)}), bf16[8,96,1536]{2,1,0:T(8,128)(2,1)}, u32[]{:S(2)}, u32[]{:S(2)}) async-start(bf16[8,96,1536]{2,1,0:T(8,128)(2,1)} %bitcast.64), calls=%async_computation.3 | async-start | bytes 4718592 | tf_op jit(solution)/shard_map/all_to_all | solution.py:1104
  411.5 9.2 %collective-permute-start.45 = (bf16[208,768]{1,0:T(8,128)(2,1)S(1)}, bf16[208,768]{1,0:T(8,128)(2,1)S(1)}, u32[]{:S(2)}, u32[]{:S(2)}) collective-permute-start(bf16[208,768]{1,0:T(8,128)(2,1)S(1)} %get-tuple-element.237.g0), channel_id=1, source_target_pairs={{0,2},{1,3},{2,0},{3,1},{4,6},{5,7},{6,4},{7,5},{8,10},{9,11},{10,... | collective-permute-start | bytes 958472 | tf_op jit(solution)/shard_map/ppermute | solution.py:409
  433.5 34.1 %collective-permute-start.55 = (bf16[384,1536]{1,0:T(8,128)(2,1)S(1)}, bf16[384,1536]{1,0:T(8,128)(2,1)S(1)}, u32[]{:S(2)}, u32[]{:S(2)}) collective-permute-start(bf16[384,1536]{1,0:T(8,128)(2,1)S(1)} %get-tuple-element.255), channel_id=1, source_target_pairs={{0,4},{1,5},{2,6},{3,7},{4,0},{5,1},{6,2},{7,3},{8,12},{9,13},{10,... | collective-permute-start | bytes 3538952 | tf_op jit(solution)/shard_map/ppermute | solution.py:409
  435.2 9.4 %collective-permute-start.50 = (bf16[208,768]{1,0:T(8,128)(2,1)S(1)}, bf16[208,768]{1,0:T(8,128)(2,1)S(1)}, u32[]{:S(2)}, u32[]{:S(2)}) collective-permute-start(bf16[208,768]{1,0:T(8,128)(2,1)S(1)} %get-tuple-element.249), channel_id=1, source_target_pairs={{0,2},{1,3},{2,0},{3,1},{4,6},{5,7},{6,4},{7,5},{8,10},{9,11},{10,... | collective-permute-start | bytes 958472 | tf_op jit(solution)/shard_map/ppermute | solution.py:409
  445.7 25.4 %collective-permute-start.52 = (bf16[208,768]{1,0:T(8,128)(2,1)S(1)}, bf16[208,768]{1,0:T(8,128)(2,1)S(1)}, u32[]{:S(2)}, u32[]{:S(2)}) collective-permute-start(bf16[208,768]{1,0:T(8,128)(2,1)S(1)} %get-tuple-element.256.g0), channel_id=1, source_target_pairs={{0,1},{1,0},{2,3},{3,2},{4,5},{5,4},{6,7},{7,6},{8,9},{9,8},{10,11... | collective-permute-start | bytes 958472 | tf_op jit(solution)/shard_map/ppermute | solution.py:409
  453.7 17.4 %collective-permute-start.53 = (bf16[208,768]{1,0:T(8,128)(2,1)S(1)}, bf16[208,768]{1,0:T(8,128)(2,1)S(1)}, u32[]{:S(2)}, u32[]{:S(2)}) collective-permute-start(bf16[208,768]{1,0:T(8,128)(2,1)S(1)} %collective-permute-done.51.g1), channel_id=1, source_target_pairs={{0,1},{1,0},{2,3},{3,2},{4,5},{5,4},{6,7},{7,6},{8,9},{9,8},{10,11... | collective-permute-start | bytes 958472 | tf_op jit(solution)/shard_map/ppermute | solution.py:409
  454.6 29.8 %collective-permute-start.57 = (bf16[96,768]{1,0:T(8,128)(2,1)S(1)}, bf16[96,768]{1,0:T(8,128)(2,1)S(1)}, u32[]{:S(2)}, u32[]{:S(2)}) collective-permute-start(bf16[96,768]{1,0:T(8,128)(2,1)S(1)} %get-tuple-element.269), channel_id=1, source_target_pairs={{0,8},{1,9},{2,10},{3,11},{4,12},{5,13},{6,14},{7,15},{8,0},{9,1},... | collective-permute-start | bytes 442376 | tf_op jit(solution)/shard_map/ppermute | solution.py:409
  456.1 28.9 %collective-permute-start.58 = (bf16[96,768]{1,0:T(8,128)(2,1)S(1)}, bf16[96,768]{1,0:T(8,128)(2,1)S(1)}, u32[]{:S(2)}, u32[]{:S(2)}) collective-permute-start(bf16[96,768]{1,0:T(8,128)(2,1)S(1)} %get-tuple-element.270), channel_id=1, source_target_pairs={{0,16},{1,17},{2,18},{3,19},{4,20},{5,21},{6,22},{7,23},{8,24},{9,... | collective-permute-start | bytes 442376 | tf_op jit(solution)/shard_map/ppermute | solution.py:409
  468.6 17.1 %collective-permute-start.59 = (bf16[96,768]{1,0:T(8,128)(2,1)S(1)}, bf16[96,768]{1,0:T(8,128)(2,1)S(1)}, u32[]{:S(2)}, u32[]{:S(2)}) collective-permute-start(bf16[96,768]{1,0:T(8,128)(2,1)S(1)} %get-tuple-element.271), channel_id=1, source_target_pairs={{0,24},{1,25},{2,26},{3,27},{4,28},{5,29},{6,30},{7,31},{8,16},{9,... | collective-permute-start | bytes 442376 | tf_op jit(solution)/shard_map/ppermute | solution.py:409
  471.1 15.2 %collective-permute-start.54 = (bf16[208,768]{1,0:T(8,128)(2,1)S(1)}, bf16[208,768]{1,0:T(8,128)(2,1)S(1)}, u32[]{:S(2)}, u32[]{:S(2)}) collective-permute-start(bf16[208,768]{1,0:T(8,128)(2,1)S(1)} %get-tuple-element.252), channel_id=1, source_target_pairs={{0,2},{1,3},{2,0},{3,1},{4,6},{5,7},{6,4},{7,5},{8,10},{9,11},{10,... | collective-permute-start | bytes 958472 | tf_op jit(solution)/shard_map/ppermute | solution.py:409
  486.4 16.9 %collective-permute-start.62 = (bf16[384,768]{1,0:T(8,128)(2,1)}, bf16[384,768]{1,0:T(8,128)(2,1)}, u32[]{:S(2)}, u32[]{:S(2)}) collective-permute-start(bf16[384,768]{1,0:T(8,128)(2,1)} %copy-done.121), channel_id=1, source_target_pairs={{0,4},{1,5},{2,6},{3,7},{4,0},{5,1},{6,2},{7,3},{8,12},{9,13},{10,... | collective-permute-start | bytes 1769480 | tf_op jit(solution)/shard_map/ppermute | solution.py:409
  490.7 12.6 %collective-permute-start.61 = (bf16[208,768]{1,0:T(8,128)(2,1)S(1)}, bf16[208,768]{1,0:T(8,128)(2,1)S(1)}, u32[]{:S(2)}, u32[]{:S(2)}) collective-permute-start(bf16[208,768]{1,0:T(8,128)(2,1)S(1)} %get-tuple-element.278), channel_id=1, source_target_pairs={{0,2},{1,3},{2,0},{3,1},{4,6},{5,7},{6,4},{7,5},{8,10},{9,11},{10,... | collective-permute-start | bytes 958472 | tf_op jit(solution)/shard_map/ppermute | solution.py:409
  493.5 15.6 %collective-permute-start.64 = (bf16[96,1536]{1,0:T(8,128)(2,1)S(1)}, bf16[96,1536]{1,0:T(8,128)(2,1)S(1)}, u32[]{:S(2)}, u32[]{:S(2)}) collective-permute-start(bf16[96,1536]{1,0:T(8,128)(2,1)S(1)} %get-tuple-element.289), channel_id=1, source_target_pairs={{0,8},{1,9},{2,10},{3,11},{4,12},{5,13},{6,14},{7,15},{8,0},{9,1},... | collective-permute-start | bytes 884744 | tf_op jit(solution)/shard_map/ppermute | solution.py:409
  496.1 23.5 %collective-permute-start.65 = (bf16[96,1536]{1,0:T(8,128)(2,1)S(1)}, bf16[96,1536]{1,0:T(8,128)(2,1)S(1)}, u32[]{:S(2)}, u32[]{:S(2)}) collective-permute-start(bf16[96,1536]{1,0:T(8,128)(2,1)S(1)} %get-tuple-element.290), channel_id=1, source_target_pairs={{0,16},{1,17},{2,18},{3,19},{4,20},{5,21},{6,22},{7,23},{8,24},{9,... | collective-permute-start | bytes 884744 | tf_op jit(solution)/shard_map/ppermute | solution.py:409
  497.5 22.0 %collective-permute-start.66 = (bf16[96,1536]{1,0:T(8,128)(2,1)S(1)}, bf16[96,1536]{1,0:T(8,128)(2,1)S(1)}, u32[]{:S(2)}, u32[]{:S(2)}) collective-permute-start(bf16[96,1536]{1,0:T(8,128)(2,1)S(1)} %get-tuple-element.291), channel_id=1, source_target_pairs={{0,24},{1,25},{2,26},{3,27},{4,28},{5,29},{6,30},{7,31},{8,16},{9,... | collective-permute-start | bytes 884744 | tf_op jit(solution)/shard_map/ppermute | solution.py:409
  529.8 18.8 %collective-permute-start.69 = (bf16[128,768]{1,0:T(8,128)(2,1)}, bf16[128,768]{1,0:T(8,128)(2,1)S(1)}, u32[]{:S(2)}, u32[]{:S(2)}) collective-permute-start(bf16[128,768]{1,0:T(8,128)(2,1)} %get-tuple-element.296), channel_id=1, source_target_pairs={{0,8},{1,9},{2,10},{3,11},{4,12},{5,13},{6,14},{7,15},{8,0},{9,1},... | collective-permute-start | bytes 589832 | tf_op jit(solution)/shard_map/ppermute | solution.py:409
  535.3 14.7 %collective-permute-start.70 = (bf16[128,768]{1,0:T(8,128)(2,1)}, bf16[128,768]{1,0:T(8,128)(2,1)}, u32[]{:S(2)}, u32[]{:S(2)}) collective-permute-start(bf16[128,768]{1,0:T(8,128)(2,1)} %get-tuple-element.297), channel_id=1, source_target_pairs={{0,16},{1,17},{2,18},{3,19},{4,20},{5,21},{6,22},{7,23},{8,24},{9,... | collective-permute-start | bytes 589832 | tf_op jit(solution)/shard_map/ppermute | solution.py:409
  536.7 13.3 %collective-permute-start.71 = (bf16[128,768]{1,0:T(8,128)(2,1)}, bf16[128,768]{1,0:T(8,128)(2,1)}, u32[]{:S(2)}, u32[]{:S(2)}) collective-permute-start(bf16[128,768]{1,0:T(8,128)(2,1)} %get-tuple-element.298), channel_id=1, source_target_pairs={{0,24},{1,25},{2,26},{3,27},{4,28},{5,29},{6,30},{7,31},{8,16},{9,... | collective-permute-start | bytes 589832 | tf_op jit(solution)/shard_map/ppermute | solution.py:409
  (172 other events, 1454.7 us)
Sparse Core Ops, SparseCore 0:
  12.3 50.9 all-gather.1

commit v6 on v5

--- a/solution.py
+++ b/solution.py
@@ -656,15 +656,16 @@
 def expert_kernel(
     number, t0, t1, g0, g1, router, *rest
 ):
-    own, far = rest[0], rest[1:5]
-    res_own, res_sib, grad_own, grad_sib = rest[5:9]
-    up_parts, down_parts = rest[9:12], rest[12:15]
-    act_ref, hid_ref, gout_ref, pair, whole = rest[15:]
+    own, far = rest[0], rest[1:3]
+    res_own, res_sib, grad_own, grad_sib = rest[3:7]
+    up_parts, down_parts = rest[7:10], rest[10:13]
+    act_ref, hid_ref, gout_ref, pair, whole = rest[13:]
     size = t0.shape[0]
     half, wide = own.shape[0] // 2, act_ref.shape[2]
     whole[0] = own[...]
-    for i, part in enumerate(far):
-        whole[1, i * half // 2 : (i + 1) * half // 2] = part[...]
+    cut = far[0].shape[0]
+    whole[1, :cut] = far[0][...]
+    whole[1, cut:] = far[1][...]
     for i, (t, g, res, grad) in enumerate(
         ((t1, g1, res_sib, grad_sib), (t0, g0, res_own, grad_own))
     ):
@@ -1007,13 +1008,12 @@
         scalars=1,
     )[0]
     x_late = swap(z_late, x=1)
-    e_pack = hold(e_pack, normed_mlp[1])
+    grad_sent = to_experts(dispatch_kernel, spread(hold(grad_low, normed)))
+    e_pack = hold(e_pack, grad_sent, normed_mlp[3])
     e_own = lax.all_to_all(e_pack, "dp", split_axis=0, concat_axis=0, tiled=True)
     e_own = e_own.reshape(features, wide)
     e_own = hold(e_own, normed_mlp[1])
-    far = [swap(e_own[i * 2 * width : (i + 1) * 2 * width], y=1) for i in range(4)]
-    e_far = far
-    grad_sent = to_experts(dispatch_kernel, spread(hold(grad_low, normed)))
+    e_far = [swap(e_own[: 2 * width], y=1), swap(e_own[2 * width :], y=1)]
     full_late = stacked([z_late, x_late])
     ats = (0, ff_cols)
     act, slope, own, sib = run(

time: 569 us -> 571 us (level)
  starting transfers between devices: 101 us -> 120 us
  waiting for transfers between devices: 281 us -> 267 us
    ppermute x72 -> x70, waiting for transfers between devices: 276 us -> 263 us  [swap(): return lax.ppermute(values, AXES, pairs)]
    ppermute x72 -> x70, starting transfers between devices: 58.1 us -> 68.9 us  [swap(): return lax.ppermute(values, AXES, pairs)]
    all_to_all x2, starting transfers between devices: 21.9 us -> 30.1 us  [exchange(): return lax.all_to_all(both, 'dp', split_axis=0, concat_axis=0, tiled=True)]
    unnamed x296 -> x292, local copies, waits for them, and re-layouts: 60.3 us -> 57.2 us
  transfers between devices with their start and end apart: 77 -> 75, of which waited for: 47 -> 44; matrix products, arithmetic and copies ran while one was open for 4% -> 3% of each run, Pallas kernels for 11% -> 11%
where the time goes in v6:
time: 571 us; the launch traced here: 562 us
  waiting for transfers between devices  267 us (47%)
  starting transfers between devices  120 us (21%)
  Pallas kernels  84.6 us (15%)
  local copies, waits for them, and re-layouts  64.7 us (11%)
  between operations  16.6 us (3%)
  other arithmetic  8.64 us (2%)
    ppermute x70, waiting for transfers between devices, swap(): return lax.ppermute(values, AXES, pairs)  263 us
    pallas_call x46, Pallas kernels, run(): pl.pallas_call(kernel, out_shape=shapes, in_specs=[SM] * scalars + [VM] *...  84.6 us
    ppermute x70, starting transfers between devices, swap(): return lax.ppermute(values, AXES, pairs)  68.9 us
    unnamed x292, local copies, waits for them, and re-layouts  57.2 us
    all_to_all x2, starting transfers between devices, exchange(): return lax.all_to_all(both, 'dp', split_axis=0, concat_axis=0, tiled=True)  30.1 us
    all_to_all x1, starting transfers between devices, fast_local(): lax.all_to_all(e_pack, 'dp', split_axis=0, concat_axis=0, tiled=True)  16 us
  transfers between devices with their start and end apart: 75, of which 44 were waited for; matrix products, arithmetic and copies ran while one was open for 3% of the time, Pallas kernels for 11%

profile of v6, /device:TPU:0, one launch (start us, length us, event | category | flops | bytes accessed | tf_op | source)
XLA Modules:
  0.0 562.1 jit_solution(17112136151909556153)
XLA Ops:
  13.5 3.1 collective-permute-start
  16.6 2.6 collective-permute-start.1
  19.2 4.5 collective-permute-done.refs_1_
  23.7 13.5 %collective-permute-done.1.refs_2_ = bf16[96,896]{1,0:T(8,128)(2,1)S(1)} collective-permute-done((bf16[96,896]{1,0:T(8,128)(2,1)S(1)}, bf16[96,896]{1,0:T(8,128)(2,1)S(1)}, u32[]{:S(2)}, u32[]{:S(2)}) %collective-permute-start.1) | collective-permute-done | bytes 172064 | tf_op jit(solution)/shard_map/ppermute | solution.py:409
  45.3 4.8 collective-permute-done.4.refs_1_
  59.0 4.7 shard_map.318
  69.5 8.0 %collective-permute-done.8.far_ref = bf16[208,768]{1,0:T(8,128)(2,1)S(1)} collective-permute-done((bf16[208,768]{1,0:T(8,128)(2,1)S(1)}, bf16[208,768]{1,0:T(8,128)(2,1)S(1)}, u32[]{:S(2)}, u32[]{:S(2)}) %collective-permute-start.8) | collective-permute-done | bytes 319520 | tf_op jit(solution)/shard_map/ppermute | solution.py:409
  83.6 10.8 %collective-permute-done.12.p1 = bf16[208,768]{1,0:T(8,128)(2,1)S(1)} collective-permute-done((bf16[208,768]{1,0:T(8,128)(2,1)}, bf16[208,768]{1,0:T(8,128)(2,1)S(1)}, u32[]{:S(2)}, u32[]{:S(2)}) %collective-permute-start.12) | collective-permute-done | bytes 319520 | tf_op jit(solution)/shard_map/ppermute | solution.py:409
  96.6 2.5 shard_map.322
  100.7 16.0 %all-to-all-start = ((bf16[8,96,1536]{2,1,0:T(8,128)(2,1)}), bf16[8,96,1536]{2,1,0:T(8,128)(2,1)}, u32[]{:S(2)}, u32[]{:S(2)}) async-start(bf16[8,96,1536]{2,1,0:T(8,128)(2,1)} %pad_maximum_fusion), calls=%async_computation | async-start | bytes 4718592 | tf_op jit(solution)/shard_map/all_to_all | solution.py:1013
  118.4 16.8 %collective-permute-done.15.refs_1_ = bf16[384,2304]{1,0:T(8,128)(2,1)} collective-permute-done((bf16[384,2304]{1,0:T(8,128)(2,1)S(1)}, bf16[384,2304]{1,0:T(8,128)(2,1)}, u32[]{:S(2)}, u32[]{:S(2)}) %collective-permute-start.15) | collective-permute-done | bytes 1769504 | tf_op jit(solution)/shard_map/ppermute | solution.py:409
  136.9 2.8 shard_map.325
  144.5 8.1 %collective-permute-done.17.far_ref = bf16[208,768]{1,0:T(8,128)(2,1)S(1)} collective-permute-done((bf16[208,768]{1,0:T(8,128)(2,1)S(1)}, bf16[208,768]{1,0:T(8,128)(2,1)S(1)}, u32[]{:S(2)}, u32[]{:S(2)}) %collective-permute-start.17) | collective-permute-done | bytes 319520 | tf_op jit(solution)/shard_map/ppermute | solution.py:409
  154.5 7.3 %collective-permute-done.18.a1 = bf16[208,768]{1,0:T(8,128)(2,1)S(1)} collective-permute-done((bf16[208,768]{1,0:T(8,128)(2,1)S(1)}, bf16[208,768]{1,0:T(8,128)(2,1)S(1)}, u32[]{:S(2)}, u32[]{:S(2)}) %collective-permute-start.18) | collective-permute-done | bytes 319520 | tf_op jit(solution)/shard_map/ppermute | solution.py:409
  163.5 4.6 shard_map.328
  172.0 8.1 %collective-permute-done.22.far_ref = bf16[208,768]{1,0:T(8,128)(2,1)S(1)} collective-permute-done((bf16[208,768]{1,0:T(8,128)(2,1)S(1)}, bf16[208,768]{1,0:T(8,128)(2,1)S(1)}, u32[]{:S(2)}, u32[]{:S(2)}) %collective-permute-start.22) | collective-permute-done | bytes 319520 | tf_op jit(solution)/shard_map/ppermute | solution.py:409
  184.4 7.3 %collective-permute-done.23.p1 = bf16[208,768]{1,0:T(8,128)(2,1)S(1)} collective-permute-done((bf16[208,768]{1,0:T(8,128)(2,1)S(1)}, bf16[208,768]{1,0:T(8,128)(2,1)S(1)}, u32[]{:S(2)}, u32[]{:S(2)}) %collective-permute-start.23) | collective-permute-done | bytes 319520 | tf_op jit(solution)/shard_map/ppermute | solution.py:409
  196.1 6.5 %collective-permute-done.26.rest_1_ = bf16[192,1536]{1,0:T(8,128)(2,1)S(1)} collective-permute-done((bf16[192,1536]{1,0:T(8,128)(2,1)S(1)}, bf16[192,1536]{1,0:T(8,128)(2,1)S(1)}, u32[]{:S(2)}, u32[]{:S(2)}) %collective-permute-start.26) | collective-permute-done | bytes 589856 | tf_op jit(solution)/shard_map/ppermute | solution.py:409
  203.4 24.4 %all-to-all-start.1 = ((bf16[8,112,768]{2,1,0:T(8,128)(2,1)}), bf16[8,112,768]{2,1,0:T(8,128)(2,1)S(1)}, u32[]{:S(2)}, u32[]{:S(2)}) async-start(bf16[8,112,768]{2,1,0:T(8,128)(2,1)} %pad_maximum_fusion.1), calls=%async_computation.1 | async-start | bytes 2752512 | tf_op jit(solution)/shard_map/all_to_all | solution.py:945
  231.0 37.2 %collective-permute-done.27.rest_2_ = bf16[576,1536]{1,0:T(8,128)(2,1)} collective-permute-done((bf16[576,1536]{1,0:T(8,128)(2,1)S(1)}, bf16[576,1536]{1,0:T(8,128)(2,1)}, u32[]{:S(2)}, u32[]{:S(2)}) %collective-permute-start.27) | collective-permute-done | bytes 1769504 | tf_op jit(solution)/shard_map/ppermute | solution.py:409
  271.5 16.9 %shard_map.333 = (f32[448,768]{1,0:T(8,128)}, bf16[448,768]{1,0:T(8,128)(2,1)S(1)}, f32[448,768]{1,0:T(8,128)}, bf16[448,768]{1,0:T(8,128)(2,1)S(1)}, bf16[768,7...) custom-call(s32[1]{0:T(128)} %bitcast.26.number, ...), custom_call_target="tpu_custom_call" | custom-call | flops 1000 | bytes 1000 | tf_op jit(solution)/shard_map/pallas_call | solution.py:419
  300.3 6.1 %collective-permute-done.32.up0 = bf16[384,768]{1,0:T(8,128)(2,1)S(1)} collective-permute-done((bf16[384,768]{1,0:T(8,128)(2,1)S(1)}, bf16[384,768]{1,0:T(8,128)(2,1)S(1)}, u32[]{:S(2)}, u32[]{:S(2)}) %collective-permute-start.32) | collective-permute-done | bytes 589856 | tf_op jit(solution)/shard_map/ppermute | solution.py:409
  307.3 5.7 %all-to-all-start.2 = ((bf16[8,112,768]{2,1,0:T(8,128)(2,1)}), bf16[8,112,768]{2,1,0:T(8,128)(2,1)S(1)}, u32[]{:S(2)}, u32[]{:S(2)}) async-start(bf16[8,112,768]{2,1,0:T(8,128)(2,1)} %copy-done.21), calls=%async_computation.2 | async-start | bytes 2752512 | tf_op jit(solution)/shard_map/all_to_all | solution.py:945
  315.0 14.4 %collective-permute-done.33.up1 = bf16[384,768]{1,0:T(8,128)(2,1)S(1)} collective-permute-done((bf16[384,768]{1,0:T(8,128)(2,1)}, bf16[384,768]{1,0:T(8,128)(2,1)S(1)}, u32[]{:S(2)}, u32[]{:S(2)}) %collective-permute-start.33) | collective-permute-done | bytes 589856 | tf_op jit(solution)/shard_map/ppermute | solution.py:409
  330.3 9.8 %collective-permute-done.34.down0 = bf16[384,768]{1,0:T(8,128)(2,1)S(1)} collective-permute-done((bf16[384,768]{1,0:T(8,128)(2,1)}, bf16[384,768]{1,0:T(8,128)(2,1)S(1)}, u32[]{:S(2)}, u32[]{:S(2)}) %collective-permute-start.34) | collective-permute-done | bytes 589856 | tf_op jit(solution)/shard_map/ppermute | solution.py:409
  340.9 4.4 all-to-all-done.2.both_ref
  350.7 8.0 %collective-permute-done.36.far_ref = bf16[208,768]{1,0:T(8,128)(2,1)S(1)} collective-permute-done((bf16[208,768]{1,0:T(8,128)(2,1)S(1)}, bf16[208,768]{1,0:T(8,128)(2,1)S(1)}, u32[]{:S(2)}, u32[]{:S(2)}) %collective-permute-start.36) | collective-permute-done | bytes 319520 | tf_op jit(solution)/shard_map/ppermute | solution.py:409
  361.7 7.2 %collective-permute-done.37.g1 = bf16[208,768]{1,0:T(8,128)(2,1)S(1)} collective-permute-done((bf16[208,768]{1,0:T(8,128)(2,1)S(1)}, bf16[208,768]{1,0:T(8,128)(2,1)S(1)}, u32[]{:S(2)}, u32[]{:S(2)}) %collective-permute-start.37) | collective-permute-done | bytes 319520 | tf_op jit(solution)/shard_map/ppermute | solution.py:409
  371.6 9.9 %shard_map.338 = (bf16[384,768]{1,0:T(8,128)(2,1)S(1)}, bf16[384,768]{1,0:T(8,128)(2,1)S(1)}, f32[416,768]{1,0:T(8,128)S(1)}, bf16[416,768]{1,0:T(8,128)(2,1)S(1)}) custom-call(bf16[208,768]{1,0:T(8,128)(2,1)S(1)} %get-tuple-element.227.g0, bf16[208,768]{1,0:T(8,128)(2,1)S(1)} %collective-permute-done.37.g1, ...), custom_call_target="tpu_custom_call" | custom-call | flops 8000000000 | bytes 1000 | tf_op jit(solution)/shard_map/pallas_call | solution.py:419
  382.3 2.6 collective-permute-done.40.down1
  389.5 11.1 %collective-permute-done.54.got = bf16[384,768]{1,0:T(8,128)(2,1)S(1)} collective-permute-done((bf16[384,768]{1,0:T(8,128)(2,1)S(1)}, bf16[384,768]{1,0:T(8,128)(2,1)S(1)}, u32[]{:S(2)}, u32[]{:S(2)}) %collective-permute-start.54) | collective-permute-done | bytes 589856 | tf_op jit(solution)/shard_map/ppermute | solution.py:409
  402.9 4.6 all-to-all-start.3
  413.9 7.6 %collective-permute-done.43.g1 = bf16[208,768]{1,0:T(8,128)(2,1)S(1)} collective-permute-done((bf16[208,768]{1,0:T(8,128)(2,1)S(1)}, bf16[208,768]{1,0:T(8,128)(2,1)S(1)}, u32[]{:S(2)}, u32[]{:S(2)}) %collective-permute-start.43) | collective-permute-done | bytes 319520 | tf_op jit(solution)/shard_map/ppermute | solution.py:409
  426.5 4.7 shard_map.341
  436.9 7.6 %collective-permute-done.48.far_ref = bf16[208,768]{1,0:T(8,128)(2,1)S(1)} collective-permute-done((bf16[208,768]{1,0:T(8,128)(2,1)S(1)}, bf16[208,768]{1,0:T(8,128)(2,1)S(1)}, u32[]{:S(2)}, u32[]{:S(2)}) %collective-permute-start.48) | collective-permute-done | bytes 319520 | tf_op jit(solution)/shard_map/ppermute | solution.py:409
  446.6 7.0 %collective-permute-done.49.g1 = bf16[208,768]{1,0:T(8,128)(2,1)S(1)} collective-permute-done((bf16[208,768]{1,0:T(8,128)(2,1)S(1)}, bf16[208,768]{1,0:T(8,128)(2,1)S(1)}, u32[]{:S(2)}, u32[]{:S(2)}) %collective-permute-start.49) | collective-permute-done | bytes 319520 | tf_op jit(solution)/shard_map/ppermute | solution.py:409
  455.9 2.3 collective-permute-start.56
  458.2 9.5 %collective-permute-done.53.got = bf16[384,1536]{1,0:T(8,128)(2,1)S(1)} collective-permute-done((bf16[384,1536]{1,0:T(8,128)(2,1)S(1)}, bf16[384,1536]{1,0:T(8,128)(2,1)S(1)}, u32[]{:S(2)}, u32[]{:S(2)}) %collective-permute-start.53) | collective-permute-done | bytes 1179680 | tf_op jit(solution)/shard_map/ppermute | solution.py:409
  468.7 2.3 collective-permute-start.57
  472.6 10.2 %shard_map.347 = (bf16[384,768]{1,0:T(8,128)(2,1)S(1)}, bf16[384,768]{1,0:T(8,128)(2,1)S(1)}, f32[416,768]{1,0:T(8,128)S(1)}, bf16[416,768]{1,0:T(8,128)(2,1)S(1)}) custom-call(bf16[208,768]{1,0:T(8,128)(2,1)S(1)} %get-tuple-element.256.g0, bf16[208,768]{1,0:T(8,128)(2,1)S(1)} %collective-permute-done.49.g1, ...), custom_call_target="tpu_custom_call" | custom-call | flops 8000000000 | bytes 1000 | tf_op jit(solution)/shard_map/pallas_call | solution.py:419
  487.3 2.5 collective-permute-start.60
  493.3 3.5 collective-permute-start.62
  501.5 2.7 collective-permute-done.60.got
  505.6 4.3 convert_bitcast_fusion
  510.0 10.3 %collective-permute-done.63.r2 = bf16[96,1536]{1,0:T(8,128)(2,1)S(1)} collective-permute-done((bf16[96,1536]{1,0:T(8,128)(2,1)S(1)}, bf16[96,1536]{1,0:T(8,128)(2,1)S(1)}, u32[]{:S(2)}, u32[]{:S(2)}) %collective-permute-start.63) | collective-permute-done | bytes 294944 | tf_op jit(solution)/shard_map/ppermute | solution.py:409
  521.9 2.7 collective-permute-done.65
  524.8 3.8 collective-permute-done.66
  530.6 5.4 collective-permute-start.67
  (489 shorter events, 164.9 us)
Async XLA Ops:
  7.3 70.2 %all-gather.2.cloned.1.call-start = ((), (), s32[]{:S(2)}) async-start(), calls=%async_computation.4 | async-start | bytes 2211840 | tf_op jit(solution)/shard_map/all_gather | solution.py:889
  13.5 10.2 %collective-permute-start = (bf16[96,896]{1,0:T(8,128)(2,1)S(1)}, bf16[96,896]{1,0:T(8,128)(2,1)S(1)}, u32[]{:S(2)}, u32[]{:S(2)}) collective-permute-start(bf16[96,896]{1,0:T(8,128)(2,1)S(1)} %shard_map.314.refs_0_), channel_id=1, source_target_pairs={{0,8},{1,9},{2,10},{3,11},{4,12},{5,13},{6,14},{7,15},{8,0},{9,1},... | collective-permute-start | bytes 516104 | tf_op jit(solution)/shard_map/ppermute | solution.py:409
  16.6 20.5 %collective-permute-start.1 = (bf16[96,896]{1,0:T(8,128)(2,1)S(1)}, bf16[96,896]{1,0:T(8,128)(2,1)S(1)}, u32[]{:S(2)}, u32[]{:S(2)}) collective-permute-start(bf16[96,896]{1,0:T(8,128)(2,1)S(1)} %shard_map.314.refs_0_), channel_id=1, source_target_pairs={{0,16},{1,17},{2,18},{3,19},{4,20},{5,21},{6,22},{7,23},{8,24},{9,... | collective-permute-start | bytes 516104 | tf_op jit(solution)/shard_map/ppermute | solution.py:409
  19.2 18.0 %collective-permute-start.2 = (bf16[96,896]{1,0:T(8,128)(2,1)S(1)}, bf16[96,896]{1,0:T(8,128)(2,1)S(1)}, u32[]{:S(2)}, u32[]{:S(2)}) collective-permute-start(bf16[96,896]{1,0:T(8,128)(2,1)S(1)} %shard_map.314.refs_0_), channel_id=1, source_target_pairs={{0,24},{1,25},{2,26},{3,27},{4,28},{5,29},{6,30},{7,31},{8,16},{9,... | collective-permute-start | bytes 516104 | tf_op jit(solution)/shard_map/ppermute | solution.py:409
  37.2 14.6 %collective-permute-start.3 = (bf16[384,896]{1,0:T(8,128)(2,1)S(1)}, bf16[384,896]{1,0:T(8,128)(2,1)S(1)}, u32[]{:S(2)}, u32[]{:S(2)}) collective-permute-start(bf16[384,896]{1,0:T(8,128)(2,1)S(1)} %shard_map.315.refs_0_), channel_id=1, source_target_pairs={{0,4},{1,5},{2,6},{3,7},{4,0},{5,1},{6,2},{7,3},{8,12},{9,13},{10,... | collective-permute-start | bytes 2064392 | tf_op jit(solution)/shard_map/ppermute | solution.py:409
  67.7 9.8 %collective-permute-start.8 = (bf16[208,768]{1,0:T(8,128)(2,1)S(1)}, bf16[208,768]{1,0:T(8,128)(2,1)S(1)}, u32[]{:S(2)}, u32[]{:S(2)}) collective-permute-start(bf16[208,768]{1,0:T(8,128)(2,1)S(1)} %get-tuple-element.175), channel_id=1, source_target_pairs={{0,2},{1,3},{2,0},{3,1},{4,6},{5,7},{6,4},{7,5},{8,10},{9,11},{10,... | collective-permute-start | bytes 958472 | tf_op jit(solution)/shard_map/ppermute | solution.py:409
  78.6 15.8 %collective-permute-start.9 = (bf16[208,768]{1,0:T(8,128)(2,1)S(1)}, bf16[208,768]{1,0:T(8,128)(2,1)S(1)}, u32[]{:S(2)}, u32[]{:S(2)}) collective-permute-start(bf16[208,768]{1,0:T(8,128)(2,1)S(1)} %get-tuple-element.181.b0), channel_id=1, source_target_pairs={{0,2},{1,3},{2,0},{3,1},{4,6},{5,7},{6,4},{7,5},{8,10},{9,11},{10,... | collective-permute-start | bytes 958472 | tf_op jit(solution)/shard_map/ppermute | solution.py:409
  80.1 14.3 %collective-permute-start.12 = (bf16[208,768]{1,0:T(8,128)(2,1)}, bf16[208,768]{1,0:T(8,128)(2,1)S(1)}, u32[]{:S(2)}, u32[]{:S(2)}) collective-permute-start(bf16[208,768]{1,0:T(8,128)(2,1)} %get-tuple-element.180.p0), channel_id=1, source_target_pairs={{0,2},{1,3},{2,0},{3,1},{4,6},{5,7},{6,4},{7,5},{8,10},{9,11},{10,... | collective-permute-start | bytes 958472 | tf_op jit(solution)/shard_map/ppermute | solution.py:409
  80.8 15.8 %collective-permute-start.13 = (bf16[208,768]{1,0:T(8,128)(2,1)}, bf16[208,768]{1,0:T(8,128)(2,1)S(1)}, u32[]{:S(2)}, u32[]{:S(2)}) collective-permute-start(bf16[208,768]{1,0:T(8,128)(2,1)} %get-tuple-element.180.p0), channel_id=1, source_target_pairs={{0,1},{1,0},{2,3},{3,2},{4,5},{5,4},{6,7},{7,6},{8,9},{9,8},{10,11... | collective-permute-start | bytes 958472 | tf_op jit(solution)/shard_map/ppermute | solution.py:409
  83.0 52.2 %collective-permute-start.15 = (bf16[384,2304]{1,0:T(8,128)(2,1)S(1)}, bf16[384,2304]{1,0:T(8,128)(2,1)}, u32[]{:S(2)}, u32[]{:S(2)}) collective-permute-start(bf16[384,2304]{1,0:T(8,128)(2,1)S(1)} %shard_map.323.refs_0_), channel_id=1, source_target_pairs={{0,4},{1,5},{2,6},{3,7},{4,0},{5,1},{6,2},{7,3},{8,12},{9,13},{10,... | collective-permute-start | bytes 5308424 | tf_op jit(solution)/shard_map/ppermute | solution.py:409
  100.7 82.0 %all-to-all-start = ((bf16[8,96,1536]{2,1,0:T(8,128)(2,1)}), bf16[8,96,1536]{2,1,0:T(8,128)(2,1)}, u32[]{:S(2)}, u32[]{:S(2)}) async-start(bf16[8,96,1536]{2,1,0:T(8,128)(2,1)} %pad_maximum_fusion), calls=%async_computation | async-start | bytes 4718592 | tf_op jit(solution)/shard_map/all_to_all | solution.py:1013
  143.0 9.6 %collective-permute-start.17 = (bf16[208,768]{1,0:T(8,128)(2,1)S(1)}, bf16[208,768]{1,0:T(8,128)(2,1)S(1)}, u32[]{:S(2)}, u32[]{:S(2)}) collective-permute-start(bf16[208,768]{1,0:T(8,128)(2,1)S(1)} %get-tuple-element.189), channel_id=1, source_target_pairs={{0,2},{1,3},{2,0},{3,1},{4,6},{5,7},{6,4},{7,5},{8,10},{9,11},{10,... | collective-permute-start | bytes 958472 | tf_op jit(solution)/shard_map/ppermute | solution.py:409
  152.9 8.9 %collective-permute-start.18 = (bf16[208,768]{1,0:T(8,128)(2,1)S(1)}, bf16[208,768]{1,0:T(8,128)(2,1)S(1)}, u32[]{:S(2)}, u32[]{:S(2)}) collective-permute-start(bf16[208,768]{1,0:T(8,128)(2,1)S(1)} %get-tuple-element.191.a0), channel_id=1, source_target_pairs={{0,2},{1,3},{2,0},{3,1},{4,6},{5,7},{6,4},{7,5},{8,10},{9,11},{10,... | collective-permute-start | bytes 958472 | tf_op jit(solution)/shard_map/ppermute | solution.py:409
  170.4 9.6 %collective-permute-start.22 = (bf16[208,768]{1,0:T(8,128)(2,1)S(1)}, bf16[208,768]{1,0:T(8,128)(2,1)S(1)}, u32[]{:S(2)}, u32[]{:S(2)}) collective-permute-start(bf16[208,768]{1,0:T(8,128)(2,1)S(1)} %get-tuple-element.195), channel_id=1, source_target_pairs={{0,2},{1,3},{2,0},{3,1},{4,6},{5,7},{6,4},{7,5},{8,10},{9,11},{10,... | collective-permute-start | bytes 958472 | tf_op jit(solution)/shard_map/ppermute | solution.py:409
  181.2 10.5 %collective-permute-start.23 = (bf16[208,768]{1,0:T(8,128)(2,1)S(1)}, bf16[208,768]{1,0:T(8,128)(2,1)S(1)}, u32[]{:S(2)}, u32[]{:S(2)}) collective-permute-start(bf16[208,768]{1,0:T(8,128)(2,1)S(1)} %get-tuple-element.197.p0), channel_id=1, source_target_pairs={{0,2},{1,3},{2,0},{3,1},{4,6},{5,7},{6,4},{7,5},{8,10},{9,11},{10,... | collective-permute-start | bytes 958472 | tf_op jit(solution)/shard_map/ppermute | solution.py:409
  183.8 18.8 %collective-permute-start.26 = (bf16[192,1536]{1,0:T(8,128)(2,1)S(1)}, bf16[192,1536]{1,0:T(8,128)(2,1)S(1)}, u32[]{:S(2)}, u32[]{:S(2)}) collective-permute-start(bf16[192,1536]{1,0:T(8,128)(2,1)S(1)} %slice.65), channel_id=1, source_target_pairs={{0,2},{1,3},{2,0},{3,1},{4,6},{5,7},{6,4},{7,5},{8,10},{9,11},{10,... | collective-permute-start | bytes 1769480 | tf_op jit(solution)/shard_map/ppermute | solution.py:409
  203.4 64.8 %all-to-all-start.1 = ((bf16[8,112,768]{2,1,0:T(8,128)(2,1)}), bf16[8,112,768]{2,1,0:T(8,128)(2,1)S(1)}, u32[]{:S(2)}, u32[]{:S(2)}) async-start(bf16[8,112,768]{2,1,0:T(8,128)(2,1)} %pad_maximum_fusion.1), calls=%async_computation.1 | async-start | bytes 2752512 | tf_op jit(solution)/shard_map/all_to_all | solution.py:945
  229.4 38.8 %collective-permute-start.27 = (bf16[576,1536]{1,0:T(8,128)(2,1)S(1)}, bf16[576,1536]{1,0:T(8,128)(2,1)}, u32[]{:S(2)}, u32[]{:S(2)}) collective-permute-start(bf16[576,1536]{1,0:T(8,128)(2,1)S(1)} %slice.66), channel_id=1, source_target_pairs={{0,2},{1,3},{2,0},{3,1},{4,6},{5,7},{6,4},{7,5},{8,10},{9,11},{10,... | collective-permute-start | bytes 5308424 | tf_op jit(solution)/shard_map/ppermute | solution.py:409
  291.1 15.4 %collective-permute-start.32 = (bf16[384,768]{1,0:T(8,128)(2,1)S(1)}, bf16[384,768]{1,0:T(8,128)(2,1)S(1)}, u32[]{:S(2)}, u32[]{:S(2)}) collective-permute-start(bf16[384,768]{1,0:T(8,128)(2,1)S(1)} %get-tuple-element.211), channel_id=1, source_target_pairs={{0,2},{1,3},{2,0},{3,1},{4,6},{5,7},{6,4},{7,5},{8,10},{9,11},{10,... | collective-permute-start | bytes 1769480 | tf_op jit(solution)/shard_map/ppermute | solution.py:409
  307.3 38.0 %all-to-all-start.2 = ((bf16[8,112,768]{2,1,0:T(8,128)(2,1)}), bf16[8,112,768]{2,1,0:T(8,128)(2,1)S(1)}, u32[]{:S(2)}, u32[]{:S(2)}) async-start(bf16[8,112,768]{2,1,0:T(8,128)(2,1)} %copy-done.21), calls=%async_computation.2 | async-start | bytes 2752512 | tf_op jit(solution)/shard_map/all_to_all | solution.py:945
  313.0 16.5 %collective-permute-start.33 = (bf16[384,768]{1,0:T(8,128)(2,1)}, bf16[384,768]{1,0:T(8,128)(2,1)S(1)}, u32[]{:S(2)}, u32[]{:S(2)}) collective-permute-start(bf16[384,768]{1,0:T(8,128)(2,1)} %copy-done.120), channel_id=1, source_target_pairs={{0,2},{1,3},{2,0},{3,1},{4,6},{5,7},{6,4},{7,5},{8,10},{9,11},{10,... | collective-permute-start | bytes 1769480 | tf_op jit(solution)/shard_map/ppermute | solution.py:409
  314.5 25.6 %collective-permute-start.34 = (bf16[384,768]{1,0:T(8,128)(2,1)}, bf16[384,768]{1,0:T(8,128)(2,1)S(1)}, u32[]{:S(2)}, u32[]{:S(2)}) collective-permute-start(bf16[384,768]{1,0:T(8,128)(2,1)} %copy-done.119), channel_id=1, source_target_pairs={{0,2},{1,3},{2,0},{3,1},{4,6},{5,7},{6,4},{7,5},{8,10},{9,11},{10,... | collective-permute-start | bytes 1769480 | tf_op jit(solution)/shard_map/ppermute | solution.py:409
  349.1 9.6 %collective-permute-start.36 = (bf16[208,768]{1,0:T(8,128)(2,1)S(1)}, bf16[208,768]{1,0:T(8,128)(2,1)S(1)}, u32[]{:S(2)}, u32[]{:S(2)}) collective-permute-start(bf16[208,768]{1,0:T(8,128)(2,1)S(1)} %get-tuple-element.225), channel_id=1, source_target_pairs={{0,2},{1,3},{2,0},{3,1},{4,6},{5,7},{6,4},{7,5},{8,10},{9,11},{10,... | collective-permute-start | bytes 958472 | tf_op jit(solution)/shard_map/ppermute | solution.py:409
  360.2 8.7 %collective-permute-start.37 = (bf16[208,768]{1,0:T(8,128)(2,1)S(1)}, bf16[208,768]{1,0:T(8,128)(2,1)S(1)}, u32[]{:S(2)}, u32[]{:S(2)}) collective-permute-start(bf16[208,768]{1,0:T(8,128)(2,1)S(1)} %get-tuple-element.227.g0), channel_id=1, source_target_pairs={{0,2},{1,3},{2,0},{3,1},{4,6},{5,7},{6,4},{7,5},{8,10},{9,11},{10,... | collective-permute-start | bytes 958472 | tf_op jit(solution)/shard_map/ppermute | solution.py:409
  361.7 8.8 %collective-permute-start.38 = (bf16[208,768]{1,0:T(8,128)(2,1)S(1)}, bf16[208,768]{1,0:T(8,128)(2,1)S(1)}, u32[]{:S(2)}, u32[]{:S(2)}) collective-permute-start(bf16[208,768]{1,0:T(8,128)(2,1)S(1)} %get-tuple-element.227.g0), channel_id=1, source_target_pairs={{0,1},{1,0},{2,3},{3,2},{4,5},{5,4},{6,7},{7,6},{8,9},{9,8},{10,11... | collective-permute-start | bytes 958472 | tf_op jit(solution)/shard_map/ppermute | solution.py:409
  368.9 16.0 %collective-permute-start.40 = (bf16[384,768]{1,0:T(8,128)(2,1)}, bf16[384,768]{1,0:T(8,128)(2,1)S(1)}, u32[]{:S(2)}, u32[]{:S(2)}) collective-permute-start(bf16[384,768]{1,0:T(8,128)(2,1)} %copy-done.117), channel_id=1, source_target_pairs={{0,2},{1,3},{2,0},{3,1},{4,6},{5,7},{6,4},{7,5},{8,10},{9,11},{10,... | collective-permute-start | bytes 1769480 | tf_op jit(solution)/shard_map/ppermute | solution.py:409
  384.9 15.7 %collective-permute-start.54 = (bf16[384,768]{1,0:T(8,128)(2,1)S(1)}, bf16[384,768]{1,0:T(8,128)(2,1)S(1)}, u32[]{:S(2)}, u32[]{:S(2)}) collective-permute-start(bf16[384,768]{1,0:T(8,128)(2,1)S(1)} %get-tuple-element.265), channel_id=1, source_target_pairs={{0,4},{1,5},{2,6},{3,7},{4,0},{5,1},{6,2},{7,3},{8,12},{9,13},{10,... | collective-permute-start | bytes 1769480 | tf_op jit(solution)/shard_map/ppermute | solution.py:409
  387.9 12.7 %collective-permute-start.42 = (bf16[208,768]{1,0:T(8,128)(2,1)S(1)}, bf16[208,768]{1,0:T(8,128)(2,1)S(1)}, u32[]{:S(2)}, u32[]{:S(2)}) collective-permute-start(bf16[208,768]{1,0:T(8,128)(2,1)S(1)} %get-tuple-element.236), channel_id=1, source_target_pairs={{0,2},{1,3},{2,0},{3,1},{4,6},{5,7},{6,4},{7,5},{8,10},{9,11},{10,... | collective-permute-start | bytes 958472 | tf_op jit(solution)/shard_map/ppermute | solution.py:409
  402.9 84.3 %all-to-all-start.3 = ((bf16[8,96,1536]{2,1,0:T(8,128)(2,1)}), bf16[8,96,1536]{2,1,0:T(8,128)(2,1)}, u32[]{:S(2)}, u32[]{:S(2)}) async-start(bf16[8,96,1536]{2,1,0:T(8,128)(2,1)} %bitcast.64), calls=%async_computation.3 | async-start | bytes 4718592 | tf_op jit(solution)/shard_map/all_to_all | solution.py:1104
  412.3 9.2 %collective-permute-start.43 = (bf16[208,768]{1,0:T(8,128)(2,1)S(1)}, bf16[208,768]{1,0:T(8,128)(2,1)S(1)}, u32[]{:S(2)}, u32[]{:S(2)}) collective-permute-start(bf16[208,768]{1,0:T(8,128)(2,1)S(1)} %get-tuple-element.237.g0), channel_id=1, source_target_pairs={{0,2},{1,3},{2,0},{3,1},{4,6},{5,7},{6,4},{7,5},{8,10},{9,11},{10,... | collective-permute-start | bytes 958472 | tf_op jit(solution)/shard_map/ppermute | solution.py:409
  413.9 7.6 %collective-permute-start.44 = (bf16[208,768]{1,0:T(8,128)(2,1)S(1)}, bf16[208,768]{1,0:T(8,128)(2,1)S(1)}, u32[]{:S(2)}, u32[]{:S(2)}) collective-permute-start(bf16[208,768]{1,0:T(8,128)(2,1)S(1)} %get-tuple-element.237.g0), channel_id=1, source_target_pairs={{0,1},{1,0},{2,3},{3,2},{4,5},{5,4},{6,7},{7,6},{8,9},{9,8},{10,11... | collective-permute-start | bytes 958472 | tf_op jit(solution)/shard_map/ppermute | solution.py:409
  433.3 34.3 %collective-permute-start.53 = (bf16[384,1536]{1,0:T(8,128)(2,1)S(1)}, bf16[384,1536]{1,0:T(8,128)(2,1)S(1)}, u32[]{:S(2)}, u32[]{:S(2)}) collective-permute-start(bf16[384,1536]{1,0:T(8,128)(2,1)S(1)} %get-tuple-element.255), channel_id=1, source_target_pairs={{0,4},{1,5},{2,6},{3,7},{4,0},{5,1},{6,2},{7,3},{8,12},{9,13},{10,... | collective-permute-start | bytes 3538952 | tf_op jit(solution)/shard_map/ppermute | solution.py:409
  435.1 9.4 %collective-permute-start.48 = (bf16[208,768]{1,0:T(8,128)(2,1)S(1)}, bf16[208,768]{1,0:T(8,128)(2,1)S(1)}, u32[]{:S(2)}, u32[]{:S(2)}) collective-permute-start(bf16[208,768]{1,0:T(8,128)(2,1)S(1)} %get-tuple-element.249), channel_id=1, source_target_pairs={{0,2},{1,3},{2,0},{3,1},{4,6},{5,7},{6,4},{7,5},{8,10},{9,11},{10,... | collective-permute-start | bytes 958472 | tf_op jit(solution)/shard_map/ppermute | solution.py:409
  445.0 8.6 %collective-permute-start.49 = (bf16[208,768]{1,0:T(8,128)(2,1)S(1)}, bf16[208,768]{1,0:T(8,128)(2,1)S(1)}, u32[]{:S(2)}, u32[]{:S(2)}) collective-permute-start(bf16[208,768]{1,0:T(8,128)(2,1)S(1)} %get-tuple-element.256.g0), channel_id=1, source_target_pairs={{0,2},{1,3},{2,0},{3,1},{4,6},{5,7},{6,4},{7,5},{8,10},{9,11},{10,... | collective-permute-start | bytes 958472 | tf_op jit(solution)/shard_map/ppermute | solution.py:409
  446.6 24.4 %collective-permute-start.50 = (bf16[208,768]{1,0:T(8,128)(2,1)S(1)}, bf16[208,768]{1,0:T(8,128)(2,1)S(1)}, u32[]{:S(2)}, u32[]{:S(2)}) collective-permute-start(bf16[208,768]{1,0:T(8,128)(2,1)S(1)} %get-tuple-element.256.g0), channel_id=1, source_target_pairs={{0,1},{1,0},{2,3},{3,2},{4,5},{5,4},{6,7},{7,6},{8,9},{9,8},{10,11... | collective-permute-start | bytes 958472 | tf_op jit(solution)/shard_map/ppermute | solution.py:409
  453.6 17.4 %collective-permute-start.51 = (bf16[208,768]{1,0:T(8,128)(2,1)S(1)}, bf16[208,768]{1,0:T(8,128)(2,1)S(1)}, u32[]{:S(2)}, u32[]{:S(2)}) collective-permute-start(bf16[208,768]{1,0:T(8,128)(2,1)S(1)} %collective-permute-done.49.g1), channel_id=1, source_target_pairs={{0,1},{1,0},{2,3},{3,2},{4,5},{5,4},{6,7},{7,6},{8,9},{9,8},{10,11... | collective-permute-start | bytes 958472 | tf_op jit(solution)/shard_map/ppermute | solution.py:409
  454.5 30.7 %collective-permute-start.55 = (bf16[96,768]{1,0:T(8,128)(2,1)S(1)}, bf16[96,768]{1,0:T(8,128)(2,1)S(1)}, u32[]{:S(2)}, u32[]{:S(2)}) collective-permute-start(bf16[96,768]{1,0:T(8,128)(2,1)S(1)} %get-tuple-element.269), channel_id=1, source_target_pairs={{0,8},{1,9},{2,10},{3,11},{4,12},{5,13},{6,14},{7,15},{8,0},{9,1},... | collective-permute-start | bytes 442376 | tf_op jit(solution)/shard_map/ppermute | solution.py:409
  455.9 29.9 %collective-permute-start.56 = (bf16[96,768]{1,0:T(8,128)(2,1)S(1)}, bf16[96,768]{1,0:T(8,128)(2,1)S(1)}, u32[]{:S(2)}, u32[]{:S(2)}) collective-permute-start(bf16[96,768]{1,0:T(8,128)(2,1)S(1)} %get-tuple-element.270), channel_id=1, source_target_pairs={{0,16},{1,17},{2,18},{3,19},{4,20},{5,21},{6,22},{7,23},{8,24},{9,... | collective-permute-start | bytes 442376 | tf_op jit(solution)/shard_map/ppermute | solution.py:409
  468.7 17.9 %collective-permute-start.57 = (bf16[96,768]{1,0:T(8,128)(2,1)S(1)}, bf16[96,768]{1,0:T(8,128)(2,1)S(1)}, u32[]{:S(2)}, u32[]{:S(2)}) collective-permute-start(bf16[96,768]{1,0:T(8,128)(2,1)S(1)} %get-tuple-element.271), channel_id=1, source_target_pairs={{0,24},{1,25},{2,26},{3,27},{4,28},{5,29},{6,30},{7,31},{8,16},{9,... | collective-permute-start | bytes 442376 | tf_op jit(solution)/shard_map/ppermute | solution.py:409
  471.0 16.2 %collective-permute-start.52 = (bf16[208,768]{1,0:T(8,128)(2,1)S(1)}, bf16[208,768]{1,0:T(8,128)(2,1)S(1)}, u32[]{:S(2)}, u32[]{:S(2)}) collective-permute-start(bf16[208,768]{1,0:T(8,128)(2,1)S(1)} %get-tuple-element.252), channel_id=1, source_target_pairs={{0,2},{1,3},{2,0},{3,1},{4,6},{5,7},{6,4},{7,5},{8,10},{9,11},{10,... | collective-permute-start | bytes 958472 | tf_op jit(solution)/shard_map/ppermute | solution.py:409
  487.3 16.9 %collective-permute-start.60 = (bf16[384,768]{1,0:T(8,128)(2,1)}, bf16[384,768]{1,0:T(8,128)(2,1)}, u32[]{:S(2)}, u32[]{:S(2)}) collective-permute-start(bf16[384,768]{1,0:T(8,128)(2,1)} %copy-done.118), channel_id=1, source_target_pairs={{0,4},{1,5},{2,6},{3,7},{4,0},{5,1},{6,2},{7,3},{8,12},{9,13},{10,... | collective-permute-start | bytes 1769480 | tf_op jit(solution)/shard_map/ppermute | solution.py:409
  491.5 12.6 %collective-permute-start.59 = (bf16[208,768]{1,0:T(8,128)(2,1)S(1)}, bf16[208,768]{1,0:T(8,128)(2,1)S(1)}, u32[]{:S(2)}, u32[]{:S(2)}) collective-permute-start(bf16[208,768]{1,0:T(8,128)(2,1)S(1)} %get-tuple-element.278), channel_id=1, source_target_pairs={{0,2},{1,3},{2,0},{3,1},{4,6},{5,7},{6,4},{7,5},{8,10},{9,11},{10,... | collective-permute-start | bytes 958472 | tf_op jit(solution)/shard_map/ppermute | solution.py:409
  493.3 16.7 %collective-permute-start.62 = (bf16[96,1536]{1,0:T(8,128)(2,1)S(1)}, bf16[96,1536]{1,0:T(8,128)(2,1)S(1)}, u32[]{:S(2)}, u32[]{:S(2)}) collective-permute-start(bf16[96,1536]{1,0:T(8,128)(2,1)S(1)} %get-tuple-element.289), channel_id=1, source_target_pairs={{0,8},{1,9},{2,10},{3,11},{4,12},{5,13},{6,14},{7,15},{8,0},{9,1},... | collective-permute-start | bytes 884744 | tf_op jit(solution)/shard_map/ppermute | solution.py:409
  496.8 23.5 %collective-permute-start.63 = (bf16[96,1536]{1,0:T(8,128)(2,1)S(1)}, bf16[96,1536]{1,0:T(8,128)(2,1)S(1)}, u32[]{:S(2)}, u32[]{:S(2)}) collective-permute-start(bf16[96,1536]{1,0:T(8,128)(2,1)S(1)} %get-tuple-element.290), channel_id=1, source_target_pairs={{0,16},{1,17},{2,18},{3,19},{4,20},{5,21},{6,22},{7,23},{8,24},{9,... | collective-permute-start | bytes 884744 | tf_op jit(solution)/shard_map/ppermute | solution.py:409
  498.3 22.0 %collective-permute-start.64 = (bf16[96,1536]{1,0:T(8,128)(2,1)S(1)}, bf16[96,1536]{1,0:T(8,128)(2,1)S(1)}, u32[]{:S(2)}, u32[]{:S(2)}) collective-permute-start(bf16[96,1536]{1,0:T(8,128)(2,1)S(1)} %get-tuple-element.291), channel_id=1, source_target_pairs={{0,24},{1,25},{2,26},{3,27},{4,28},{5,29},{6,30},{7,31},{8,16},{9,... | collective-permute-start | bytes 884744 | tf_op jit(solution)/shard_map/ppermute | solution.py:409
  530.6 18.8 %collective-permute-start.67 = (bf16[128,768]{1,0:T(8,128)(2,1)}, bf16[128,768]{1,0:T(8,128)(2,1)S(1)}, u32[]{:S(2)}, u32[]{:S(2)}) collective-permute-start(bf16[128,768]{1,0:T(8,128)(2,1)} %get-tuple-element.296), channel_id=1, source_target_pairs={{0,8},{1,9},{2,10},{3,11},{4,12},{5,13},{6,14},{7,15},{8,0},{9,1},... | collective-permute-start | bytes 589832 | tf_op jit(solution)/shard_map/ppermute | solution.py:409
  536.0 14.7 %collective-permute-start.68 = (bf16[128,768]{1,0:T(8,128)(2,1)}, bf16[128,768]{1,0:T(8,128)(2,1)}, u32[]{:S(2)}, u32[]{:S(2)}) collective-permute-start(bf16[128,768]{1,0:T(8,128)(2,1)} %get-tuple-element.297), channel_id=1, source_target_pairs={{0,16},{1,17},{2,18},{3,19},{4,20},{5,21},{6,22},{7,23},{8,24},{9,... | collective-permute-start | bytes 589832 | tf_op jit(solution)/shard_map/ppermute | solution.py:409
  537.4 13.3 %collective-permute-start.69 = (bf16[128,768]{1,0:T(8,128)(2,1)}, bf16[128,768]{1,0:T(8,128)(2,1)}, u32[]{:S(2)}, u32[]{:S(2)}) collective-permute-start(bf16[128,768]{1,0:T(8,128)(2,1)} %get-tuple-element.298), channel_id=1, source_target_pairs={{0,24},{1,25},{2,26},{3,27},{4,28},{5,29},{6,30},{7,31},{8,16},{9,... | collective-permute-start | bytes 589832 | tf_op jit(solution)/shard_map/ppermute | solution.py:409
  (168 other events, 1419.9 us)
Sparse Core Ops, SparseCore 0:
  12.3 50.9 all-gather.1

commit v7 on v5

--- a/solution.py
+++ b/solution.py
@@ -658,8 +658,8 @@
 ):
     own, far = rest[0], rest[1:5]
     res_own, res_sib, grad_own, grad_sib = rest[5:9]
-    up_parts, down_parts = rest[9:12], rest[12:15]
-    act_ref, hid_ref, gout_ref, pair, whole = rest[15:]
+    up_parts, down_parts = rest[9:13], rest[13:16]
+    act_ref, hid_ref, gout_ref, pair, whole = rest[16:]
     size = t0.shape[0]
     half, wide = own.shape[0] // 2, act_ref.shape[2]
     whole[0] = own[...]
@@ -692,8 +692,10 @@
     for parts, left, right in ((up_parts, pair, hid_ref), (down_parts, gout_ref, act_ref)):
         parts[0][...] = dot(left[...], right[0], 0, 0).astype(BF)
         far = dot(left[...], right[1], 0, 0).astype(BF)
-        parts[1][...] = far[:half]
-        parts[2][...] = far[half:]
+        at = 0
+        for part in parts[1:]:
+            part[...] = far[at : at + part.shape[0]]
+            at += part.shape[0]
 
 
 def answer_kernel(
@@ -733,13 +735,15 @@
     out_ref[...] = total[: out_ref.shape[0]]
 
 
-def add_pack_kernel(up_own, up0, up1, down_own, down0, down1, out):
-    half, wide = up0.shape
-    for c, (own, parts) in enumerate(((up_own, (up0, up1)), (down_own, (down0, down1)))):
-        for s, part in enumerate(parts):
-            span = slice(s * half, (s + 1) * half)
+def add_pack_kernel(up_own, up0, up1, up2, down_own, down0, down1, out):
+    wide = up_own.shape[1]
+    for c, (own, parts) in enumerate(((up_own, (up0, up1, up2)), (down_own, (down0, down1)))):
+        at = 0
+        for part in parts:
+            span = slice(at, at + part.shape[0])
             total = own[span].astype(F32) + part[...].astype(F32)
             out[span, c * wide : (c + 1) * wide] = total.astype(BF)
+            at += part.shape[0]
 
 
 def pack_kernel(*refs):
@@ -1044,7 +1048,13 @@
     slot_out = [((slot_rows, features), F32), ((slot_rows, features), BF)]
     res_own, res_sib, eg_own, eg_sib, *e_packs = run(
         expert_kernel,
-        slot_out + slot_out + ([((features, ff_cols), BF)] + half_shape) * 2,
+        slot_out
+        + slot_out
+        + [((features, ff_cols), BF)]
+        + [((2 * width, ff_cols), BF)] * 2
+        + half_shape[:1]
+        + [((features, ff_cols), BF)]
+        + half_shape,
         (number, tokens, far_tokens, grad_slots, far_slots, router)
         + (e_own, *e_far),
         8 * 2 * slot_rows * features * 2 * ff_cols,
@@ -1071,7 +1081,8 @@
     e_packs = hold(e_packs, both)
     both = exchange(both)
     up_got.append(swap(e_packs[2], y=1))
-    down_got = [swap(e_packs[4], y=1)]
+    up_got.append(swap(e_packs[3], y=1))
+    down_got = [swap(e_packs[5], y=1)]
     both = hold(both, up_got, down_got)
 
     def combine(which, both):
@@ -1089,7 +1100,7 @@
         three, grad_four, back_own, back_far, gains[3]
     )
     low = spread(low)
-    down_got.append(swap(hold(e_packs[5], low[1]), y=1))
+    down_got.append(swap(hold(e_packs[6], low[1]), y=1))
     *second, own, sib = attend_back(
         low, normed_two, mixed_two, att_two, full_late, 2 * ff_cols
     )
@@ -1098,7 +1109,7 @@
     e_sum = run(
         add_pack_kernel,
         [((features, wide), BF)],
-        (e_packs[0], *up_got, e_packs[3], *hold(down_got, second[1], far)),
+        (e_packs[0], *up_got, e_packs[4], *hold(down_got, second[1], far)),
         0,
     )[0].reshape(experts, width, wide)
     e_back = lax.all_to_all(e_sum, "dp", split_axis=0, concat_axis=0, tiled=True)

time: 569 us -> 569 us (level)
    ppermute x72 -> x73, starting transfers between devices: 58.1 us -> 59.4 us  [swap(): return lax.ppermute(values, AXES, pairs)]
    unnamed x296 -> x302, local copies, waits for them, and re-layouts: 60.3 us -> 60.9 us
    ppermute x72 -> x73, waiting for transfers between devices: 276 us -> 277 us  [swap(): return lax.ppermute(values, AXES, pairs)]
  transfers between devices with their start and end apart: 77 -> 78, of which waited for: 47 -> 44; matrix products, arithmetic and copies ran while one was open for 4% -> 4% of each run, Pallas kernels for 11% -> 11%
where the time goes in v7:
time: 569 us; the launch traced here: 561 us
  waiting for transfers between devices  277 us (49%)
  starting transfers between devices  103 us (18%)
  Pallas kernels  85.7 us (15%)
  local copies, waits for them, and re-layouts  68.5 us (12%)
  between operations  16.6 us (3%)
  other arithmetic  8.64 us (2%)
    ppermute x73, waiting for transfers between devices, swap(): return lax.ppermute(values, AXES, pairs)  277 us
    pallas_call x46, Pallas kernels, run(): pl.pallas_call(kernel, out_shape=shapes, in_specs=[SM] * scalars + [VM] *...  85.7 us
    unnamed x302, local copies, waits for them, and re-layouts  60.9 us
    ppermute x73, starting transfers between devices, swap(): return lax.ppermute(values, AXES, pairs)  59.4 us
    all_to_all x2, starting transfers between devices, exchange(): return lax.all_to_all(both, 'dp', split_axis=0, concat_axis=0, tiled=True)  21.9 us
    all_to_all x1, starting transfers between devices, fast_local(): lax.all_to_all(e_pack, 'dp', split_axis=0, concat_axis=0, tiled=True)  16 us
  transfers between devices with their start and end apart: 78, of which 44 were waited for; matrix products, arithmetic and copies ran while one was open for 4% of the time, Pallas kernels for 11%

profile of v7, /device:TPU:0, one launch (start us, length us, event | category | flops | bytes accessed | tf_op | source)
XLA Modules:
  0.0 560.6 jit_solution(17036467305910241760)
XLA Ops:
  13.5 3.1 collective-permute-start
  16.6 2.6 collective-permute-start.1
  19.2 4.5 collective-permute-done.refs_1_
  23.7 13.5 %collective-permute-done.1.refs_2_ = bf16[96,896]{1,0:T(8,128)(2,1)S(1)} collective-permute-done((bf16[96,896]{1,0:T(8,128)(2,1)S(1)}, bf16[96,896]{1,0:T(8,128)(2,1)S(1)}, u32[]{:S(2)}, u32[]{:S(2)}) %collective-permute-start.1) | collective-permute-done | bytes 172064 | tf_op jit(solution)/shard_map/ppermute | solution.py:409
  44.5 4.7 collective-permute-done.4.refs_1_
  58.3 4.7 shard_map.318
  68.6 8.2 %collective-permute-done.8.far_ref = bf16[208,768]{1,0:T(8,128)(2,1)S(1)} collective-permute-done((bf16[208,768]{1,0:T(8,128)(2,1)S(1)}, bf16[208,768]{1,0:T(8,128)(2,1)S(1)}, u32[]{:S(2)}, u32[]{:S(2)}) %collective-permute-start.8) | collective-permute-done | bytes 319520 | tf_op jit(solution)/shard_map/ppermute | solution.py:409
  84.2 2.7 collective-permute-done.9.b1
  86.9 16.0 %all-to-all-start = ((bf16[8,96,1536]{2,1,0:T(8,128)(2,1)}), bf16[8,96,1536]{2,1,0:T(8,128)(2,1)}, u32[]{:S(2)}, u32[]{:S(2)}) async-start(bf16[8,96,1536]{2,1,0:T(8,128)(2,1)} %pad_maximum_fusion), calls=%async_computation | async-start | bytes 4718592 | tf_op jit(solution)/shard_map/all_to_all | solution.py:1015
  105.4 5.7 %collective-permute-done.12.p1 = bf16[208,768]{1,0:T(8,128)(2,1)} collective-permute-done((bf16[208,768]{1,0:T(8,128)(2,1)}, bf16[208,768]{1,0:T(8,128)(2,1)}, u32[]{:S(2)}, u32[]{:S(2)}) %collective-permute-start.12) | collective-permute-done | bytes 319520 | tf_op jit(solution)/shard_map/ppermute | solution.py:409
  113.9 2.5 shard_map.322
  117.3 25.0 %collective-permute-done.15.refs_1_ = bf16[384,2304]{1,0:T(8,128)(2,1)} collective-permute-done((bf16[384,2304]{1,0:T(8,128)(2,1)S(1)}, bf16[384,2304]{1,0:T(8,128)(2,1)}, u32[]{:S(2)}, u32[]{:S(2)}) %collective-permute-start.15) | collective-permute-done | bytes 1769504 | tf_op jit(solution)/shard_map/ppermute | solution.py:409
  144.1 4.0 shard_map.325
  151.9 9.1 %collective-permute-done.17.far_ref = bf16[208,768]{1,0:T(8,128)(2,1)S(1)} collective-permute-done((bf16[208,768]{1,0:T(8,128)(2,1)S(1)}, bf16[208,768]{1,0:T(8,128)(2,1)S(1)}, u32[]{:S(2)}, u32[]{:S(2)}) %collective-permute-start.17) | collective-permute-done | bytes 319520 | tf_op jit(solution)/shard_map/ppermute | solution.py:409
  161.9 8.2 %collective-permute-done.18.a1 = bf16[208,768]{1,0:T(8,128)(2,1)S(1)} collective-permute-done((bf16[208,768]{1,0:T(8,128)(2,1)S(1)}, bf16[208,768]{1,0:T(8,128)(2,1)S(1)}, u32[]{:S(2)}, u32[]{:S(2)}) %collective-permute-start.18) | collective-permute-done | bytes 319520 | tf_op jit(solution)/shard_map/ppermute | solution.py:409
  171.8 4.6 shard_map.328
  179.3 9.1 %collective-permute-done.22.far_ref = bf16[208,768]{1,0:T(8,128)(2,1)S(1)} collective-permute-done((bf16[208,768]{1,0:T(8,128)(2,1)S(1)}, bf16[208,768]{1,0:T(8,128)(2,1)S(1)}, u32[]{:S(2)}, u32[]{:S(2)}) %collective-permute-start.22) | collective-permute-done | bytes 319520 | tf_op jit(solution)/shard_map/ppermute | solution.py:409
  190.0 2.8 fusion.22
  194.4 5.6 collective-permute-done.23.p1
  204.4 6.5 %collective-permute-done.26.rest_1_ = bf16[192,1536]{1,0:T(8,128)(2,1)S(1)} collective-permute-done((bf16[192,1536]{1,0:T(8,128)(2,1)S(1)}, bf16[192,1536]{1,0:T(8,128)(2,1)S(1)}, u32[]{:S(2)}, u32[]{:S(2)}) %collective-permute-start.26) | collective-permute-done | bytes 589856 | tf_op jit(solution)/shard_map/ppermute | solution.py:409
  211.7 16.2 %all-to-all-start.1 = ((bf16[8,112,768]{2,1,0:T(8,128)(2,1)}), bf16[8,112,768]{2,1,0:T(8,128)(2,1)S(1)}, u32[]{:S(2)}, u32[]{:S(2)}) async-start(bf16[8,112,768]{2,1,0:T(8,128)(2,1)} %pad_maximum_fusion.1), calls=%async_computation.1 | async-start | bytes 2752512 | tf_op jit(solution)/shard_map/all_to_all | solution.py:948
  230.5 13.9 %collective-permute-done.27.rest_2_ = bf16[192,1536]{1,0:T(8,128)(2,1)S(1)} collective-permute-done((bf16[192,1536]{1,0:T(8,128)(2,1)}, bf16[192,1536]{1,0:T(8,128)(2,1)S(1)}, u32[]{:S(2)}, u32[]{:S(2)}) %collective-permute-start.27) | collective-permute-done | bytes 589856 | tf_op jit(solution)/shard_map/ppermute | solution.py:409
  245.3 11.8 %collective-permute-done.28.rest_3_ = bf16[192,1536]{1,0:T(8,128)(2,1)S(1)} collective-permute-done((bf16[192,1536]{1,0:T(8,128)(2,1)}, bf16[192,1536]{1,0:T(8,128)(2,1)S(1)}, u32[]{:S(2)}, u32[]{:S(2)}) %collective-permute-start.28) | collective-permute-done | bytes 589856 | tf_op jit(solution)/shard_map/ppermute | solution.py:409
  257.9 8.9 %collective-permute-done.29.rest_4_ = bf16[192,1536]{1,0:T(8,128)(2,1)S(1)} collective-permute-done((bf16[192,1536]{1,0:T(8,128)(2,1)}, bf16[192,1536]{1,0:T(8,128)(2,1)S(1)}, u32[]{:S(2)}, u32[]{:S(2)}) %collective-permute-start.29) | collective-permute-done | bytes 589856 | tf_op jit(solution)/shard_map/ppermute | solution.py:409
  272.0 16.6 %shard_map.333 = (f32[448,768]{1,0:T(8,128)}, bf16[448,768]{1,0:T(8,128)(2,1)S(1)}, f32[448,768]{1,0:T(8,128)}, bf16[448,768]{1,0:T(8,128)(2,1)S(1)}, bf16[768,7...) custom-call(s32[1]{0:T(128)} %bitcast.26.number, ...), custom_call_target="tpu_custom_call" | custom-call | flops 1000 | bytes 1000 | tf_op jit(solution)/shard_map/pallas_call | solution.py:419
  300.3 5.7 %all-to-all-start.2 = ((bf16[8,112,768]{2,1,0:T(8,128)(2,1)}), bf16[8,112,768]{2,1,0:T(8,128)(2,1)S(1)}, u32[]{:S(2)}, u32[]{:S(2)}) async-start(bf16[8,112,768]{2,1,0:T(8,128)(2,1)} %copy-done.19), calls=%async_computation.2 | async-start | bytes 2752512 | tf_op jit(solution)/shard_map/all_to_all | solution.py:948
  308.6 31.7 %collective-permute-done.35.up1 = bf16[192,768]{1,0:T(8,128)(2,1)S(1)} collective-permute-done((bf16[192,768]{1,0:T(8,128)(2,1)}, bf16[192,768]{1,0:T(8,128)(2,1)S(1)}, u32[]{:S(2)}, u32[]{:S(2)}) %collective-permute-start.35) | collective-permute-done | bytes 294944 | tf_op jit(solution)/shard_map/ppermute | solution.py:409
  347.1 9.1 %collective-permute-done.39.far_ref = bf16[208,768]{1,0:T(8,128)(2,1)S(1)} collective-permute-done((bf16[208,768]{1,0:T(8,128)(2,1)S(1)}, bf16[208,768]{1,0:T(8,128)(2,1)S(1)}, u32[]{:S(2)}, u32[]{:S(2)}) %collective-permute-start.39) | collective-permute-done | bytes 319520 | tf_op jit(solution)/shard_map/ppermute | solution.py:409
  358.0 8.2 %collective-permute-done.40.g1 = bf16[208,768]{1,0:T(8,128)(2,1)S(1)} collective-permute-done((bf16[208,768]{1,0:T(8,128)(2,1)S(1)}, bf16[208,768]{1,0:T(8,128)(2,1)S(1)}, u32[]{:S(2)}, u32[]{:S(2)}) %collective-permute-start.40) | collective-permute-done | bytes 319520 | tf_op jit(solution)/shard_map/ppermute | solution.py:409
  368.9 9.9 %shard_map.338 = (bf16[384,768]{1,0:T(8,128)(2,1)S(1)}, bf16[384,768]{1,0:T(8,128)(2,1)S(1)}, f32[416,768]{1,0:T(8,128)S(1)}, bf16[416,768]{1,0:T(8,128)(2,1)S(1)}) custom-call(bf16[208,768]{1,0:T(8,128)(2,1)S(1)} %get-tuple-element.231.g0, bf16[208,768]{1,0:T(8,128)(2,1)S(1)} %collective-permute-done.40.g1, ...), custom_call_target="tpu_custom_call" | custom-call | flops 8000000000 | bytes 1000 | tf_op jit(solution)/shard_map/pallas_call | solution.py:419
  379.7 2.5 collective-permute-done.43.down1
  385.8 12.2 %collective-permute-done.57.got = bf16[384,768]{1,0:T(8,128)(2,1)S(1)} collective-permute-done((bf16[384,768]{1,0:T(8,128)(2,1)S(1)}, bf16[384,768]{1,0:T(8,128)(2,1)S(1)}, u32[]{:S(2)}, u32[]{:S(2)}) %collective-permute-start.57) | collective-permute-done | bytes 589856 | tf_op jit(solution)/shard_map/ppermute | solution.py:409
  400.3 5.9 %all-to-all-start.3 = ((bf16[8,96,1536]{2,1,0:T(8,128)(2,1)}), bf16[8,96,1536]{2,1,0:T(8,128)(2,1)}, u32[]{:S(2)}, u32[]{:S(2)}) async-start(bf16[8,96,1536]{2,1,0:T(8,128)(2,1)} %bitcast.64), calls=%async_computation.3 | async-start | bytes 4718592 | tf_op jit(solution)/shard_map/all_to_all | solution.py:1115
  411.5 8.4 %collective-permute-done.46.g1 = bf16[208,768]{1,0:T(8,128)(2,1)S(1)} collective-permute-done((bf16[208,768]{1,0:T(8,128)(2,1)S(1)}, bf16[208,768]{1,0:T(8,128)(2,1)S(1)}, u32[]{:S(2)}, u32[]{:S(2)}) %collective-permute-start.46) | collective-permute-done | bytes 319520 | tf_op jit(solution)/shard_map/ppermute | solution.py:409
  424.8 5.7 %shard_map.341 = (bf16[384,1536]{1,0:T(8,128)(2,1)S(1)}, bf16[384,1536]{1,0:T(8,128)(2,1)S(1)}, f32[416,768]{1,0:T(8,128)S(1)}, bf16[416,768]{1,0:T(8,128)(2,1)S(1)}) custom-call(bf16[208,768]{1,0:T(8,128)(2,1)S(1)} %get-tuple-element.241.g0, bf16[208,768]{1,0:T(8,128)(2,1)S(1)} %collective-permute-done.46.g1, ...), custom_call_target="tpu_custom_call" | custom-call | flops 1000 | bytes 1000 | tf_op jit(solution)/shard_map/pallas_call | solution.py:419
  435.4 8.6 %collective-permute-done.51.far_ref = bf16[208,768]{1,0:T(8,128)(2,1)S(1)} collective-permute-done((bf16[208,768]{1,0:T(8,128)(2,1)S(1)}, bf16[208,768]{1,0:T(8,128)(2,1)S(1)}, u32[]{:S(2)}, u32[]{:S(2)}) %collective-permute-start.51) | collective-permute-done | bytes 319520 | tf_op jit(solution)/shard_map/ppermute | solution.py:409
  445.1 8.0 %collective-permute-done.52.g1 = bf16[208,768]{1,0:T(8,128)(2,1)S(1)} collective-permute-done((bf16[208,768]{1,0:T(8,128)(2,1)S(1)}, bf16[208,768]{1,0:T(8,128)(2,1)S(1)}, u32[]{:S(2)}, u32[]{:S(2)}) %collective-permute-start.52) | collective-permute-done | bytes 319520 | tf_op jit(solution)/shard_map/ppermute | solution.py:409
  457.7 9.0 %collective-permute-done.56.got = bf16[384,1536]{1,0:T(8,128)(2,1)S(1)} collective-permute-done((bf16[384,1536]{1,0:T(8,128)(2,1)S(1)}, bf16[384,1536]{1,0:T(8,128)(2,1)S(1)}, u32[]{:S(2)}, u32[]{:S(2)}) %collective-permute-start.56) | collective-permute-done | bytes 1179680 | tf_op jit(solution)/shard_map/ppermute | solution.py:409
  467.7 2.8 collective-permute-start.60
  471.1 10.1 %shard_map.347 = (bf16[384,768]{1,0:T(8,128)(2,1)S(1)}, bf16[384,768]{1,0:T(8,128)(2,1)S(1)}, f32[416,768]{1,0:T(8,128)S(1)}, bf16[416,768]{1,0:T(8,128)(2,1)S(1)}) custom-call(bf16[208,768]{1,0:T(8,128)(2,1)S(1)} %get-tuple-element.260.g0, bf16[208,768]{1,0:T(8,128)(2,1)S(1)} %collective-permute-done.52.g1, ...), custom_call_target="tpu_custom_call" | custom-call | flops 8000000000 | bytes 1000 | tf_op jit(solution)/shard_map/pallas_call | solution.py:419
  485.8 2.5 collective-permute-start.63
  492.9 2.5 collective-permute-start.65
  500.1 2.6 collective-permute-done.63.got
  504.1 4.3 convert_bitcast_fusion
  508.5 10.4 %collective-permute-done.66.r2 = bf16[96,1536]{1,0:T(8,128)(2,1)S(1)} collective-permute-done((bf16[96,1536]{1,0:T(8,128)(2,1)S(1)}, bf16[96,1536]{1,0:T(8,128)(2,1)S(1)}, u32[]{:S(2)}, u32[]{:S(2)}) %collective-permute-start.66) | collective-permute-done | bytes 294944 | tf_op jit(solution)/shard_map/ppermute | solution.py:409
  519.5 3.8 collective-permute-done.68
  523.4 3.8 collective-permute-done.69
  529.2 5.4 collective-permute-start.70
  (504 shorter events, 160.1 us)
Async XLA Ops:
  7.3 69.5 %all-gather.2.cloned.1.call-start = ((), (), s32[]{:S(2)}) async-start(), calls=%async_computation.4 | async-start | bytes 2211840 | tf_op jit(solution)/shard_map/all_gather | solution.py:892
  13.5 10.2 %collective-permute-start = (bf16[96,896]{1,0:T(8,128)(2,1)S(1)}, bf16[96,896]{1,0:T(8,128)(2,1)S(1)}, u32[]{:S(2)}, u32[]{:S(2)}) collective-permute-start(bf16[96,896]{1,0:T(8,128)(2,1)S(1)} %shard_map.314.refs_0_), channel_id=1, source_target_pairs={{0,8},{1,9},{2,10},{3,11},{4,12},{5,13},{6,14},{7,15},{8,0},{9,1},... | collective-permute-start | bytes 516104 | tf_op jit(solution)/shard_map/ppermute | solution.py:409
  16.6 20.5 %collective-permute-start.1 = (bf16[96,896]{1,0:T(8,128)(2,1)S(1)}, bf16[96,896]{1,0:T(8,128)(2,1)S(1)}, u32[]{:S(2)}, u32[]{:S(2)}) collective-permute-start(bf16[96,896]{1,0:T(8,128)(2,1)S(1)} %shard_map.314.refs_0_), channel_id=1, source_target_pairs={{0,16},{1,17},{2,18},{3,19},{4,20},{5,21},{6,22},{7,23},{8,24},{9,... | collective-permute-start | bytes 516104 | tf_op jit(solution)/shard_map/ppermute | solution.py:409
  19.2 18.0 %collective-permute-start.2 = (bf16[96,896]{1,0:T(8,128)(2,1)S(1)}, bf16[96,896]{1,0:T(8,128)(2,1)S(1)}, u32[]{:S(2)}, u32[]{:S(2)}) collective-permute-start(bf16[96,896]{1,0:T(8,128)(2,1)S(1)} %shard_map.314.refs_0_), channel_id=1, source_target_pairs={{0,24},{1,25},{2,26},{3,27},{4,28},{5,29},{6,30},{7,31},{8,16},{9,... | collective-permute-start | bytes 516104 | tf_op jit(solution)/shard_map/ppermute | solution.py:409
  37.2 13.8 %collective-permute-start.3 = (bf16[384,896]{1,0:T(8,128)(2,1)S(1)}, bf16[384,896]{1,0:T(8,128)(2,1)S(1)}, u32[]{:S(2)}, u32[]{:S(2)}) collective-permute-start(bf16[384,896]{1,0:T(8,128)(2,1)S(1)} %shard_map.315.refs_0_), channel_id=1, source_target_pairs={{0,4},{1,5},{2,6},{3,7},{4,0},{5,1},{6,2},{7,3},{8,12},{9,13},{10,... | collective-permute-start | bytes 2064392 | tf_op jit(solution)/shard_map/ppermute | solution.py:409
  67.0 9.8 %collective-permute-start.8 = (bf16[208,768]{1,0:T(8,128)(2,1)S(1)}, bf16[208,768]{1,0:T(8,128)(2,1)S(1)}, u32[]{:S(2)}, u32[]{:S(2)}) collective-permute-start(bf16[208,768]{1,0:T(8,128)(2,1)S(1)} %get-tuple-element.177), channel_id=1, source_target_pairs={{0,2},{1,3},{2,0},{3,1},{4,6},{5,7},{6,4},{7,5},{8,10},{9,11},{10,... | collective-permute-start | bytes 958472 | tf_op jit(solution)/shard_map/ppermute | solution.py:409
  77.9 9.0 %collective-permute-start.9 = (bf16[208,768]{1,0:T(8,128)(2,1)S(1)}, bf16[208,768]{1,0:T(8,128)(2,1)}, u32[]{:S(2)}, u32[]{:S(2)}) collective-permute-start(bf16[208,768]{1,0:T(8,128)(2,1)S(1)} %get-tuple-element.183.b0), channel_id=1, source_target_pairs={{0,2},{1,3},{2,0},{3,1},{4,6},{5,7},{6,4},{7,5},{8,10},{9,11},{10,... | collective-permute-start | bytes 958472 | tf_op jit(solution)/shard_map/ppermute | solution.py:409
  81.6 60.7 %collective-permute-start.15 = (bf16[384,2304]{1,0:T(8,128)(2,1)S(1)}, bf16[384,2304]{1,0:T(8,128)(2,1)}, u32[]{:S(2)}, u32[]{:S(2)}) collective-permute-start(bf16[384,2304]{1,0:T(8,128)(2,1)S(1)} %shard_map.323.refs_0_), channel_id=1, source_target_pairs={{0,4},{1,5},{2,6},{3,7},{4,0},{5,1},{6,2},{7,3},{8,12},{9,13},{10,... | collective-permute-start | bytes 5308424 | tf_op jit(solution)/shard_map/ppermute | solution.py:409
  86.9 103.1 %all-to-all-start = ((bf16[8,96,1536]{2,1,0:T(8,128)(2,1)}), bf16[8,96,1536]{2,1,0:T(8,128)(2,1)}, u32[]{:S(2)}, u32[]{:S(2)}) async-start(bf16[8,96,1536]{2,1,0:T(8,128)(2,1)} %pad_maximum_fusion), calls=%async_computation | async-start | bytes 4718592 | tf_op jit(solution)/shard_map/all_to_all | solution.py:1015
  104.8 12.4 %collective-permute-start.10 = (bf16[208,768]{1,0:T(8,128)(2,1)S(1)}, bf16[208,768]{1,0:T(8,128)(2,1)S(1)}, u32[]{:S(2)}, u32[]{:S(2)}) collective-permute-start(bf16[208,768]{1,0:T(8,128)(2,1)S(1)} %get-tuple-element.183.b0), channel_id=1, source_target_pairs={{0,1},{1,0},{2,3},{3,2},{4,5},{5,4},{6,7},{7,6},{8,9},{9,8},{10,11... | collective-permute-start | bytes 958472 | tf_op jit(solution)/shard_map/ppermute | solution.py:409
  105.3 11.9 %collective-permute-start.11 = (bf16[208,768]{1,0:T(8,128)(2,1)}, bf16[208,768]{1,0:T(8,128)(2,1)S(1)}, u32[]{:S(2)}, u32[]{:S(2)}) collective-permute-start(bf16[208,768]{1,0:T(8,128)(2,1)} %collective-permute-done.9.b1), channel_id=1, source_target_pairs={{0,1},{1,0},{2,3},{3,2},{4,5},{5,4},{6,7},{7,6},{8,9},{9,8},{10,11... | collective-permute-start | bytes 958472 | tf_op jit(solution)/shard_map/ppermute | solution.py:409
  151.4 9.6 %collective-permute-start.17 = (bf16[208,768]{1,0:T(8,128)(2,1)S(1)}, bf16[208,768]{1,0:T(8,128)(2,1)S(1)}, u32[]{:S(2)}, u32[]{:S(2)}) collective-permute-start(bf16[208,768]{1,0:T(8,128)(2,1)S(1)} %get-tuple-element.191), channel_id=1, source_target_pairs={{0,2},{1,3},{2,0},{3,1},{4,6},{5,7},{6,4},{7,5},{8,10},{9,11},{10,... | collective-permute-start | bytes 958472 | tf_op jit(solution)/shard_map/ppermute | solution.py:409
  161.3 8.8 %collective-permute-start.18 = (bf16[208,768]{1,0:T(8,128)(2,1)S(1)}, bf16[208,768]{1,0:T(8,128)(2,1)S(1)}, u32[]{:S(2)}, u32[]{:S(2)}) collective-permute-start(bf16[208,768]{1,0:T(8,128)(2,1)S(1)} %get-tuple-element.193.a0), channel_id=1, source_target_pairs={{0,2},{1,3},{2,0},{3,1},{4,6},{5,7},{6,4},{7,5},{8,10},{9,11},{10,... | collective-permute-start | bytes 958472 | tf_op jit(solution)/shard_map/ppermute | solution.py:409
  178.7 9.6 %collective-permute-start.22 = (bf16[208,768]{1,0:T(8,128)(2,1)S(1)}, bf16[208,768]{1,0:T(8,128)(2,1)S(1)}, u32[]{:S(2)}, u32[]{:S(2)}) collective-permute-start(bf16[208,768]{1,0:T(8,128)(2,1)S(1)} %get-tuple-element.197), channel_id=1, source_target_pairs={{0,2},{1,3},{2,0},{3,1},{4,6},{5,7},{6,4},{7,5},{8,10},{9,11},{10,... | collective-permute-start | bytes 958472 | tf_op jit(solution)/shard_map/ppermute | solution.py:409
  189.5 10.5 %collective-permute-start.23 = (bf16[208,768]{1,0:T(8,128)(2,1)S(1)}, bf16[208,768]{1,0:T(8,128)(2,1)S(1)}, u32[]{:S(2)}, u32[]{:S(2)}) collective-permute-start(bf16[208,768]{1,0:T(8,128)(2,1)S(1)} %get-tuple-element.199.p0), channel_id=1, source_target_pairs={{0,2},{1,3},{2,0},{3,1},{4,6},{5,7},{6,4},{7,5},{8,10},{9,11},{10,... | collective-permute-start | bytes 958472 | tf_op jit(solution)/shard_map/ppermute | solution.py:409
  192.9 18.0 %collective-permute-start.26 = (bf16[192,1536]{1,0:T(8,128)(2,1)S(1)}, bf16[192,1536]{1,0:T(8,128)(2,1)S(1)}, u32[]{:S(2)}, u32[]{:S(2)}) collective-permute-start(bf16[192,1536]{1,0:T(8,128)(2,1)S(1)} %get-tuple-element.355), channel_id=1, source_target_pairs={{0,2},{1,3},{2,0},{3,1},{4,6},{5,7},{6,4},{7,5},{8,10},{9,11},{10,... | collective-permute-start | bytes 1769480 | tf_op jit(solution)/shard_map/ppermute | solution.py:409
  211.7 55.9 %all-to-all-start.1 = ((bf16[8,112,768]{2,1,0:T(8,128)(2,1)}), bf16[8,112,768]{2,1,0:T(8,128)(2,1)S(1)}, u32[]{:S(2)}, u32[]{:S(2)}) async-start(bf16[8,112,768]{2,1,0:T(8,128)(2,1)} %pad_maximum_fusion.1), calls=%async_computation.1 | async-start | bytes 2752512 | tf_op jit(solution)/shard_map/all_to_all | solution.py:948
  227.9 16.5 %collective-permute-start.27 = (bf16[192,1536]{1,0:T(8,128)(2,1)}, bf16[192,1536]{1,0:T(8,128)(2,1)S(1)}, u32[]{:S(2)}, u32[]{:S(2)}) collective-permute-start(bf16[192,1536]{1,0:T(8,128)(2,1)} %get-tuple-element.354), channel_id=1, source_target_pairs={{0,2},{1,3},{2,0},{3,1},{4,6},{5,7},{6,4},{7,5},{8,10},{9,11},{10,... | collective-permute-start | bytes 1769480 | tf_op jit(solution)/shard_map/ppermute | solution.py:409
  228.5 28.6 %collective-permute-start.28 = (bf16[192,1536]{1,0:T(8,128)(2,1)}, bf16[192,1536]{1,0:T(8,128)(2,1)S(1)}, u32[]{:S(2)}, u32[]{:S(2)}) collective-permute-start(bf16[192,1536]{1,0:T(8,128)(2,1)} %get-tuple-element.353), channel_id=1, source_target_pairs={{0,2},{1,3},{2,0},{3,1},{4,6},{5,7},{6,4},{7,5},{8,10},{9,11},{10,... | collective-permute-start | bytes 1769480 | tf_op jit(solution)/shard_map/ppermute | solution.py:409
  230.0 36.8 %collective-permute-start.29 = (bf16[192,1536]{1,0:T(8,128)(2,1)}, bf16[192,1536]{1,0:T(8,128)(2,1)S(1)}, u32[]{:S(2)}, u32[]{:S(2)}) collective-permute-start(bf16[192,1536]{1,0:T(8,128)(2,1)} %get-tuple-element.352), channel_id=1, source_target_pairs={{0,2},{1,3},{2,0},{3,1},{4,6},{5,7},{6,4},{7,5},{8,10},{9,11},{10,... | collective-permute-start | bytes 1769480 | tf_op jit(solution)/shard_map/ppermute | solution.py:409
  290.3 9.3 %collective-permute-start.34 = (bf16[192,768]{1,0:T(8,128)(2,1)S(1)}, bf16[192,768]{1,0:T(8,128)(2,1)S(1)}, u32[]{:S(2)}, u32[]{:S(2)}) collective-permute-start(bf16[192,768]{1,0:T(8,128)(2,1)S(1)} %get-tuple-element.213), channel_id=1, source_target_pairs={{0,2},{1,3},{2,0},{3,1},{4,6},{5,7},{6,4},{7,5},{8,10},{9,11},{10,... | collective-permute-start | bytes 884744 | tf_op jit(solution)/shard_map/ppermute | solution.py:409
  300.3 42.4 %all-to-all-start.2 = ((bf16[8,112,768]{2,1,0:T(8,128)(2,1)}), bf16[8,112,768]{2,1,0:T(8,128)(2,1)S(1)}, u32[]{:S(2)}, u32[]{:S(2)}) async-start(bf16[8,112,768]{2,1,0:T(8,128)(2,1)} %copy-done.19), calls=%async_computation.2 | async-start | bytes 2752512 | tf_op jit(solution)/shard_map/all_to_all | solution.py:948
  306.0 35.0 %collective-permute-start.36 = (bf16[384,768]{1,0:T(8,128)(2,1)}, bf16[384,768]{1,0:T(8,128)(2,1)S(1)}, u32[]{:S(2)}, u32[]{:S(2)}) collective-permute-start(bf16[384,768]{1,0:T(8,128)(2,1)} %copy-done.125), channel_id=1, source_target_pairs={{0,2},{1,3},{2,0},{3,1},{4,6},{5,7},{6,4},{7,5},{8,10},{9,11},{10,... | collective-permute-start | bytes 1769480 | tf_op jit(solution)/shard_map/ppermute | solution.py:409
  306.5 35.3 %collective-permute-start.37 = (bf16[384,768]{1,0:T(8,128)(2,1)}, bf16[384,768]{1,0:T(8,128)(2,1)S(1)}, u32[]{:S(2)}, u32[]{:S(2)}) collective-permute-start(bf16[384,768]{1,0:T(8,128)(2,1)} %copy-done.124), channel_id=1, source_target_pairs={{0,2},{1,3},{2,0},{3,1},{4,6},{5,7},{6,4},{7,5},{8,10},{9,11},{10,... | collective-permute-start | bytes 1769480 | tf_op jit(solution)/shard_map/ppermute | solution.py:409
  308.1 32.2 %collective-permute-start.35 = (bf16[192,768]{1,0:T(8,128)(2,1)}, bf16[192,768]{1,0:T(8,128)(2,1)S(1)}, u32[]{:S(2)}, u32[]{:S(2)}) collective-permute-start(bf16[192,768]{1,0:T(8,128)(2,1)} %copy-done.130), channel_id=1, source_target_pairs={{0,2},{1,3},{2,0},{3,1},{4,6},{5,7},{6,4},{7,5},{8,10},{9,11},{10,... | collective-permute-start | bytes 884744 | tf_op jit(solution)/shard_map/ppermute | solution.py:409
  346.5 9.6 %collective-permute-start.39 = (bf16[208,768]{1,0:T(8,128)(2,1)S(1)}, bf16[208,768]{1,0:T(8,128)(2,1)S(1)}, u32[]{:S(2)}, u32[]{:S(2)}) collective-permute-start(bf16[208,768]{1,0:T(8,128)(2,1)S(1)} %get-tuple-element.229), channel_id=1, source_target_pairs={{0,2},{1,3},{2,0},{3,1},{4,6},{5,7},{6,4},{7,5},{8,10},{9,11},{10,... | collective-permute-start | bytes 958472 | tf_op jit(solution)/shard_map/ppermute | solution.py:409
  358.0 8.8 %collective-permute-start.41 = (bf16[208,768]{1,0:T(8,128)(2,1)S(1)}, bf16[208,768]{1,0:T(8,128)(2,1)S(1)}, u32[]{:S(2)}, u32[]{:S(2)}) collective-permute-start(bf16[208,768]{1,0:T(8,128)(2,1)S(1)} %get-tuple-element.231.g0), channel_id=1, source_target_pairs={{0,1},{1,0},{2,3},{3,2},{4,5},{5,4},{6,7},{7,6},{8,9},{9,8},{10,11... | collective-permute-start | bytes 958472 | tf_op jit(solution)/shard_map/ppermute | solution.py:409
  366.3 16.0 %collective-permute-start.43 = (bf16[384,768]{1,0:T(8,128)(2,1)}, bf16[384,768]{1,0:T(8,128)(2,1)S(1)}, u32[]{:S(2)}, u32[]{:S(2)}) collective-permute-start(bf16[384,768]{1,0:T(8,128)(2,1)} %copy-done.122), channel_id=1, source_target_pairs={{0,2},{1,3},{2,0},{3,1},{4,6},{5,7},{6,4},{7,5},{8,10},{9,11},{10,... | collective-permute-start | bytes 1769480 | tf_op jit(solution)/shard_map/ppermute | solution.py:409
  382.2 15.7 %collective-permute-start.57 = (bf16[384,768]{1,0:T(8,128)(2,1)S(1)}, bf16[384,768]{1,0:T(8,128)(2,1)S(1)}, u32[]{:S(2)}, u32[]{:S(2)}) collective-permute-start(bf16[384,768]{1,0:T(8,128)(2,1)S(1)} %get-tuple-element.269), channel_id=1, source_target_pairs={{0,4},{1,5},{2,6},{3,7},{4,0},{5,1},{6,2},{7,3},{8,12},{9,13},{10,... | collective-permute-start | bytes 1769480 | tf_op jit(solution)/shard_map/ppermute | solution.py:409
  385.3 12.7 %collective-permute-start.45 = (bf16[208,768]{1,0:T(8,128)(2,1)S(1)}, bf16[208,768]{1,0:T(8,128)(2,1)S(1)}, u32[]{:S(2)}, u32[]{:S(2)}) collective-permute-start(bf16[208,768]{1,0:T(8,128)(2,1)S(1)} %get-tuple-element.240), channel_id=1, source_target_pairs={{0,2},{1,3},{2,0},{3,1},{4,6},{5,7},{6,4},{7,5},{8,10},{9,11},{10,... | collective-permute-start | bytes 958472 | tf_op jit(solution)/shard_map/ppermute | solution.py:409
  400.3 85.4 %all-to-all-start.3 = ((bf16[8,96,1536]{2,1,0:T(8,128)(2,1)}), bf16[8,96,1536]{2,1,0:T(8,128)(2,1)}, u32[]{:S(2)}, u32[]{:S(2)}) async-start(bf16[8,96,1536]{2,1,0:T(8,128)(2,1)} %bitcast.64), calls=%async_computation.3 | async-start | bytes 4718592 | tf_op jit(solution)/shard_map/all_to_all | solution.py:1115
  410.9 9.0 %collective-permute-start.46 = (bf16[208,768]{1,0:T(8,128)(2,1)S(1)}, bf16[208,768]{1,0:T(8,128)(2,1)S(1)}, u32[]{:S(2)}, u32[]{:S(2)}) collective-permute-start(bf16[208,768]{1,0:T(8,128)(2,1)S(1)} %get-tuple-element.241.g0), channel_id=1, source_target_pairs={{0,2},{1,3},{2,0},{3,1},{4,6},{5,7},{6,4},{7,5},{8,10},{9,11},{10,... | collective-permute-start | bytes 958472 | tf_op jit(solution)/shard_map/ppermute | solution.py:409
  432.7 34.0 %collective-permute-start.56 = (bf16[384,1536]{1,0:T(8,128)(2,1)S(1)}, bf16[384,1536]{1,0:T(8,128)(2,1)S(1)}, u32[]{:S(2)}, u32[]{:S(2)}) collective-permute-start(bf16[384,1536]{1,0:T(8,128)(2,1)S(1)} %get-tuple-element.259), channel_id=1, source_target_pairs={{0,4},{1,5},{2,6},{3,7},{4,0},{5,1},{6,2},{7,3},{8,12},{9,13},{10,... | collective-permute-start | bytes 3538952 | tf_op jit(solution)/shard_map/ppermute | solution.py:409
  434.6 9.4 %collective-permute-start.51 = (bf16[208,768]{1,0:T(8,128)(2,1)S(1)}, bf16[208,768]{1,0:T(8,128)(2,1)S(1)}, u32[]{:S(2)}, u32[]{:S(2)}) collective-permute-start(bf16[208,768]{1,0:T(8,128)(2,1)S(1)} %get-tuple-element.253), channel_id=1, source_target_pairs={{0,2},{1,3},{2,0},{3,1},{4,6},{5,7},{6,4},{7,5},{8,10},{9,11},{10,... | collective-permute-start | bytes 958472 | tf_op jit(solution)/shard_map/ppermute | solution.py:409
  445.1 25.5 %collective-permute-start.53 = (bf16[208,768]{1,0:T(8,128)(2,1)S(1)}, bf16[208,768]{1,0:T(8,128)(2,1)S(1)}, u32[]{:S(2)}, u32[]{:S(2)}) collective-permute-start(bf16[208,768]{1,0:T(8,128)(2,1)S(1)} %get-tuple-element.260.g0), channel_id=1, source_target_pairs={{0,1},{1,0},{2,3},{3,2},{4,5},{5,4},{6,7},{7,6},{8,9},{9,8},{10,11... | collective-permute-start | bytes 958472 | tf_op jit(solution)/shard_map/ppermute | solution.py:409
  453.1 17.4 %collective-permute-start.54 = (bf16[208,768]{1,0:T(8,128)(2,1)S(1)}, bf16[208,768]{1,0:T(8,128)(2,1)S(1)}, u32[]{:S(2)}, u32[]{:S(2)}) collective-permute-start(bf16[208,768]{1,0:T(8,128)(2,1)S(1)} %collective-permute-done.52.g1), channel_id=1, source_target_pairs={{0,1},{1,0},{2,3},{3,2},{4,5},{5,4},{6,7},{7,6},{8,9},{9,8},{10,11... | collective-permute-start | bytes 958472 | tf_op jit(solution)/shard_map/ppermute | solution.py:409
  454.0 29.8 %collective-permute-start.58 = (bf16[96,768]{1,0:T(8,128)(2,1)S(1)}, bf16[96,768]{1,0:T(8,128)(2,1)S(1)}, u32[]{:S(2)}, u32[]{:S(2)}) collective-permute-start(bf16[96,768]{1,0:T(8,128)(2,1)S(1)} %get-tuple-element.273), channel_id=1, source_target_pairs={{0,8},{1,9},{2,10},{3,11},{4,12},{5,13},{6,14},{7,15},{8,0},{9,1},... | collective-permute-start | bytes 442376 | tf_op jit(solution)/shard_map/ppermute | solution.py:409
  455.4 29.0 %collective-permute-start.59 = (bf16[96,768]{1,0:T(8,128)(2,1)S(1)}, bf16[96,768]{1,0:T(8,128)(2,1)S(1)}, u32[]{:S(2)}, u32[]{:S(2)}) collective-permute-start(bf16[96,768]{1,0:T(8,128)(2,1)S(1)} %get-tuple-element.274), channel_id=1, source_target_pairs={{0,16},{1,17},{2,18},{3,19},{4,20},{5,21},{6,22},{7,23},{8,24},{9,... | collective-permute-start | bytes 442376 | tf_op jit(solution)/shard_map/ppermute | solution.py:409
  467.7 17.3 %collective-permute-start.60 = (bf16[96,768]{1,0:T(8,128)(2,1)S(1)}, bf16[96,768]{1,0:T(8,128)(2,1)S(1)}, u32[]{:S(2)}, u32[]{:S(2)}) collective-permute-start(bf16[96,768]{1,0:T(8,128)(2,1)S(1)} %get-tuple-element.275), channel_id=1, source_target_pairs={{0,24},{1,25},{2,26},{3,27},{4,28},{5,29},{6,30},{7,31},{8,16},{9,... | collective-permute-start | bytes 442376 | tf_op jit(solution)/shard_map/ppermute | solution.py:409
  470.5 15.2 %collective-permute-start.55 = (bf16[208,768]{1,0:T(8,128)(2,1)S(1)}, bf16[208,768]{1,0:T(8,128)(2,1)S(1)}, u32[]{:S(2)}, u32[]{:S(2)}) collective-permute-start(bf16[208,768]{1,0:T(8,128)(2,1)S(1)} %get-tuple-element.256), channel_id=1, source_target_pairs={{0,2},{1,3},{2,0},{3,1},{4,6},{5,7},{6,4},{7,5},{8,10},{9,11},{10,... | collective-permute-start | bytes 958472 | tf_op jit(solution)/shard_map/ppermute | solution.py:409
  485.8 16.9 %collective-permute-start.63 = (bf16[384,768]{1,0:T(8,128)(2,1)}, bf16[384,768]{1,0:T(8,128)(2,1)}, u32[]{:S(2)}, u32[]{:S(2)}) collective-permute-start(bf16[384,768]{1,0:T(8,128)(2,1)} %copy-done.123), channel_id=1, source_target_pairs={{0,4},{1,5},{2,6},{3,7},{4,0},{5,1},{6,2},{7,3},{8,12},{9,13},{10,... | collective-permute-start | bytes 1769480 | tf_op jit(solution)/shard_map/ppermute | solution.py:409
  490.0 12.6 %collective-permute-start.62 = (bf16[208,768]{1,0:T(8,128)(2,1)S(1)}, bf16[208,768]{1,0:T(8,128)(2,1)S(1)}, u32[]{:S(2)}, u32[]{:S(2)}) collective-permute-start(bf16[208,768]{1,0:T(8,128)(2,1)S(1)} %get-tuple-element.282), channel_id=1, source_target_pairs={{0,2},{1,3},{2,0},{3,1},{4,6},{5,7},{6,4},{7,5},{8,10},{9,11},{10,... | collective-permute-start | bytes 958472 | tf_op jit(solution)/shard_map/ppermute | solution.py:409
  492.9 15.6 %collective-permute-start.65 = (bf16[96,1536]{1,0:T(8,128)(2,1)S(1)}, bf16[96,1536]{1,0:T(8,128)(2,1)S(1)}, u32[]{:S(2)}, u32[]{:S(2)}) collective-permute-start(bf16[96,1536]{1,0:T(8,128)(2,1)S(1)} %get-tuple-element.293), channel_id=1, source_target_pairs={{0,8},{1,9},{2,10},{3,11},{4,12},{5,13},{6,14},{7,15},{8,0},{9,1},... | collective-permute-start | bytes 884744 | tf_op jit(solution)/shard_map/ppermute | solution.py:409
  495.4 23.5 %collective-permute-start.66 = (bf16[96,1536]{1,0:T(8,128)(2,1)S(1)}, bf16[96,1536]{1,0:T(8,128)(2,1)S(1)}, u32[]{:S(2)}, u32[]{:S(2)}) collective-permute-start(bf16[96,1536]{1,0:T(8,128)(2,1)S(1)} %get-tuple-element.294), channel_id=1, source_target_pairs={{0,16},{1,17},{2,18},{3,19},{4,20},{5,21},{6,22},{7,23},{8,24},{9,... | collective-permute-start | bytes 884744 | tf_op jit(solution)/shard_map/ppermute | solution.py:409
  496.9 22.0 %collective-permute-start.67 = (bf16[96,1536]{1,0:T(8,128)(2,1)S(1)}, bf16[96,1536]{1,0:T(8,128)(2,1)S(1)}, u32[]{:S(2)}, u32[]{:S(2)}) collective-permute-start(bf16[96,1536]{1,0:T(8,128)(2,1)S(1)} %get-tuple-element.295), channel_id=1, source_target_pairs={{0,24},{1,25},{2,26},{3,27},{4,28},{5,29},{6,30},{7,31},{8,16},{9,... | collective-permute-start | bytes 884744 | tf_op jit(solution)/shard_map/ppermute | solution.py:409
  529.2 18.8 %collective-permute-start.70 = (bf16[128,768]{1,0:T(8,128)(2,1)}, bf16[128,768]{1,0:T(8,128)(2,1)S(1)}, u32[]{:S(2)}, u32[]{:S(2)}) collective-permute-start(bf16[128,768]{1,0:T(8,128)(2,1)} %get-tuple-element.300), channel_id=1, source_target_pairs={{0,8},{1,9},{2,10},{3,11},{4,12},{5,13},{6,14},{7,15},{8,0},{9,1},... | collective-permute-start | bytes 589832 | tf_op jit(solution)/shard_map/ppermute | solution.py:409
  534.6 14.7 %collective-permute-start.71 = (bf16[128,768]{1,0:T(8,128)(2,1)}, bf16[128,768]{1,0:T(8,128)(2,1)}, u32[]{:S(2)}, u32[]{:S(2)}) collective-permute-start(bf16[128,768]{1,0:T(8,128)(2,1)} %get-tuple-element.301), channel_id=1, source_target_pairs={{0,16},{1,17},{2,18},{3,19},{4,20},{5,21},{6,22},{7,23},{8,24},{9,... | collective-permute-start | bytes 589832 | tf_op jit(solution)/shard_map/ppermute | solution.py:409
  536.0 13.3 %collective-permute-start.72 = (bf16[128,768]{1,0:T(8,128)(2,1)}, bf16[128,768]{1,0:T(8,128)(2,1)}, u32[]{:S(2)}, u32[]{:S(2)}) collective-permute-start(bf16[128,768]{1,0:T(8,128)(2,1)} %get-tuple-element.302), channel_id=1, source_target_pairs={{0,24},{1,25},{2,26},{3,27},{4,28},{5,29},{6,30},{7,31},{8,16},{9,... | collective-permute-start | bytes 589832 | tf_op jit(solution)/shard_map/ppermute | solution.py:409
  (176 other events, 1500.6 us)
Sparse Core Ops, SparseCore 0:
  12.3 50.9 all-gather.1

commit v8 on v7

--- a/solution.py
+++ b/solution.py
@@ -656,15 +656,14 @@
 def expert_kernel(
     number, t0, t1, g0, g1, router, *rest
 ):
-    own, far = rest[0], rest[1:5]
-    res_own, res_sib, grad_own, grad_sib = rest[5:9]
-    up_parts, down_parts = rest[9:13], rest[13:16]
-    act_ref, hid_ref, gout_ref, pair, whole = rest[16:]
+    own, far = rest[0], rest[1]
+    res_own, res_sib, grad_own, grad_sib = rest[2:6]
+    up_parts, down_parts = rest[6:10], rest[10:13]
+    act_ref, hid_ref, gout_ref, pair, whole = rest[13:]
     size = t0.shape[0]
     half, wide = own.shape[0] // 2, act_ref.shape[2]
     whole[0] = own[...]
-    for i, part in enumerate(far):
-        whole[1, i * half // 2 : (i + 1) * half // 2] = part[...]
+    whole[1] = far[...]
     for i, (t, g, res, grad) in enumerate(
         ((t1, g1, res_sib, grad_sib), (t0, g0, res_own, grad_own))
     ):
@@ -1011,13 +1010,10 @@
         scalars=1,
     )[0]
     x_late = swap(z_late, x=1)
-    e_pack = hold(e_pack, normed_mlp[1])
+    grad_sent = to_experts(dispatch_kernel, spread(hold(grad_low, normed)))
+    e_pack = hold(e_pack, grad_sent, normed_mlp[3])
     e_own = lax.all_to_all(e_pack, "dp", split_axis=0, concat_axis=0, tiled=True)
     e_own = e_own.reshape(features, wide)
-    e_own = hold(e_own, normed_mlp[1])
-    far = [swap(e_own[i * 2 * width : (i + 1) * 2 * width], y=1) for i in range(4)]
-    e_far = far
-    grad_sent = to_experts(dispatch_kernel, spread(hold(grad_low, normed)))
     full_late = stacked([z_late, x_late])
     ats = (0, ff_cols)
     act, slope, own, sib = run(
@@ -1033,8 +1029,10 @@
     mixed_two, att_two, own, sib, peak_two = attend(normed_two, full_late, 2 * ff_cols)
     near, far = over_group(own, sib)
     three, normed = join(two, near, far, gains[3])
-    tokens_sent = to_experts(token_kernel, spread(normed), peak_one, peak_two)
-    both = exchange(hold(jnp.concatenate([grad_sent, tokens_sent], axis=1), e_far[0]))
+    group_four = spread(normed)
+    e_far = [swap(hold(e_own, group_four[1]), y=1)]
+    tokens_sent = to_experts(token_kernel, group_four, peak_one, peak_two)
+    both = exchange(jnp.concatenate([grad_sent, tokens_sent], axis=1))
     grad_slots, tokens, peaks = run(
         collect_kernel,
         [((slot_rows, features), BF)] * 2 + [((2, 128), F32)],

time: 569 us -> 566 us (level)
  starting transfers between devices: 103 us -> 126 us
  waiting for transfers between devices: 277 us -> 256 us
  local copies, waits for them, and re-layouts: 68.5 us -> 60.4 us
    ppermute x73 -> x70, waiting for transfers between devices: 277 us -> 256 us  [swap(): return lax.ppermute(values, AXES, pairs)]
    all_to_all x2, starting transfers between devices: 21.9 us -> 33.2 us  [exchange(): return lax.all_to_all(both, 'dp', split_axis=0, concat_axis=0, tiled=True)]
    ppermute x73 -> x70, starting transfers between devices: 59.4 us -> 69.9 us  [swap(): return lax.ppermute(values, AXES, pairs)]
    unnamed x302 -> x282, local copies, waits for them, and re-layouts: 60.9 us -> 55.7 us
  transfers between devices with their start and end apart: 78 -> 75, of which waited for: 44 -> 41; matrix products, arithmetic and copies ran while one was open for 4% -> 3% of each run, Pallas kernels for 11% -> 11%
where the time goes in v8:
time: 566 us; the launch traced here: 557 us
  waiting for transfers between devices  256 us (45%)
  starting transfers between devices  126 us (22%)
  Pallas kernels  87.2 us (15%)
  local copies, waits for them, and re-layouts  60.4 us (11%)
  between operations  16.5 us (3%)
  other arithmetic  10.3 us (2%)
    ppermute x70, waiting for transfers between devices, swap(): return lax.ppermute(values, AXES, pairs)  256 us
    pallas_call x46, Pallas kernels, run(): pl.pallas_call(kernel, out_shape=shapes, in_specs=[SM] * scalars + [VM] *...  87.2 us
    ppermute x70, starting transfers between devices, swap(): return lax.ppermute(values, AXES, pairs)  69.9 us
    unnamed x282, local copies, waits for them, and re-layouts  55.7 us
    all_to_all x2, starting transfers between devices, exchange(): return lax.all_to_all(both, 'dp', split_axis=0, concat_axis=0, tiled=True)  33.2 us
    all_to_all x1, starting transfers between devices, fast_local(): lax.all_to_all(e_pack, 'dp', split_axis=0, concat_axis=0, tiled=True)  16.9 us
  transfers between devices with their start and end apart: 75, of which 41 were waited for; matrix products, arithmetic and copies ran while one was open for 3% of the time, Pallas kernels for 11%

profile of v8, /device:TPU:0, one launch (start us, length us, event | category | flops | bytes accessed | tf_op | source)
XLA Modules:
  0.0 557.3 jit_solution(30328317717462652)
XLA Ops:
  13.5 3.1 collective-permute-start
  16.6 2.6 collective-permute-start.1
  19.2 4.5 collective-permute-done.refs_1_
  23.7 13.5 %collective-permute-done.1.refs_2_ = bf16[96,896]{1,0:T(8,128)(2,1)S(1)} collective-permute-done((bf16[96,896]{1,0:T(8,128)(2,1)S(1)}, bf16[96,896]{1,0:T(8,128)(2,1)S(1)}, u32[]{:S(2)}, u32[]{:S(2)}) %collective-permute-start.1) | collective-permute-done | bytes 172064 | tf_op jit(solution)/shard_map/ppermute | solution.py:409
  45.2 4.8 collective-permute-done.4.refs_1_
  59.0 4.7 shard_map.318
  69.3 8.1 %collective-permute-done.8.far_ref = bf16[208,768]{1,0:T(8,128)(2,1)S(1)} collective-permute-done((bf16[208,768]{1,0:T(8,128)(2,1)S(1)}, bf16[208,768]{1,0:T(8,128)(2,1)S(1)}, u32[]{:S(2)}, u32[]{:S(2)}) %collective-permute-start.8) | collective-permute-done | bytes 319520 | tf_op jit(solution)/shard_map/ppermute | solution.py:409
  83.7 8.4 %collective-permute-done.12.p1 = bf16[208,768]{1,0:T(8,128)(2,1)} collective-permute-done((bf16[208,768]{1,0:T(8,128)(2,1)}, bf16[208,768]{1,0:T(8,128)(2,1)}, u32[]{:S(2)}, u32[]{:S(2)}) %collective-permute-start.12) | collective-permute-done | bytes 319520 | tf_op jit(solution)/shard_map/ppermute | solution.py:409
  92.1 5.0 collective-permute-done.9.b1
  97.2 3.2 pad_maximum_fusion
  100.4 2.6 shard_map.322
  104.6 16.9 %all-to-all-start.1 = ((bf16[8,96,1536]{2,1,0:T(8,128)(2,1)}), bf16[8,96,1536]{2,1,0:T(8,128)(2,1)}, u32[]{:S(2)}, u32[]{:S(2)}) async-start(bf16[8,96,1536]{2,1,0:T(8,128)(2,1)} %pad_maximum_fusion), calls=%async_computation.1 | async-start | bytes 4718592 | tf_op jit(solution)/shard_map/all_to_all | solution.py:1015
  125.1 4.0 shard_map.325
  133.9 8.2 %collective-permute-done.17.far_ref = bf16[208,768]{1,0:T(8,128)(2,1)S(1)} collective-permute-done((bf16[208,768]{1,0:T(8,128)(2,1)S(1)}, bf16[208,768]{1,0:T(8,128)(2,1)S(1)}, u32[]{:S(2)}, u32[]{:S(2)}) %collective-permute-start.17) | collective-permute-done | bytes 319520 | tf_op jit(solution)/shard_map/ppermute | solution.py:409
  143.9 7.4 %collective-permute-done.18.a1 = bf16[208,768]{1,0:T(8,128)(2,1)S(1)} collective-permute-done((bf16[208,768]{1,0:T(8,128)(2,1)S(1)}, bf16[208,768]{1,0:T(8,128)(2,1)S(1)}, u32[]{:S(2)}, u32[]{:S(2)}) %collective-permute-start.18) | collective-permute-done | bytes 319520 | tf_op jit(solution)/shard_map/ppermute | solution.py:409
  153.0 4.7 shard_map.328
  161.6 8.1 %collective-permute-done.22.far_ref = bf16[208,768]{1,0:T(8,128)(2,1)S(1)} collective-permute-done((bf16[208,768]{1,0:T(8,128)(2,1)S(1)}, bf16[208,768]{1,0:T(8,128)(2,1)S(1)}, u32[]{:S(2)}, u32[]{:S(2)}) %collective-permute-start.22) | collective-permute-done | bytes 319520 | tf_op jit(solution)/shard_map/ppermute | solution.py:409
  172.3 7.2 %collective-permute-done.23.p1 = bf16[208,768]{1,0:T(8,128)(2,1)S(1)} collective-permute-done((bf16[208,768]{1,0:T(8,128)(2,1)S(1)}, bf16[208,768]{1,0:T(8,128)(2,1)S(1)}, u32[]{:S(2)}, u32[]{:S(2)}) %collective-permute-start.23) | collective-permute-done | bytes 319520 | tf_op jit(solution)/shard_map/ppermute | solution.py:409
  183.9 27.5 %all-to-all-start = ((bf16[8,112,768]{2,1,0:T(8,128)(2,1)}), bf16[8,112,768]{2,1,0:T(8,128)(2,1)S(1)}, u32[]{:S(2)}, u32[]{:S(2)}) async-start(bf16[8,112,768]{2,1,0:T(8,128)(2,1)} %pad_maximum_fusion.1), calls=%async_computation | async-start | bytes 2752512 | tf_op jit(solution)/shard_map/all_to_all | solution.py:947
  213.0 51.8 %collective-permute-done.26.rest_1_ = bf16[768,1536]{1,0:T(8,128)(2,1)} collective-permute-done((bf16[768,1536]{1,0:T(8,128)(2,1)}, bf16[768,1536]{1,0:T(8,128)(2,1)}, u32[]{:S(2)}, u32[]{:S(2)}) %collective-permute-start.26) | collective-permute-done | bytes 2359328 | tf_op jit(solution)/shard_map/ppermute | solution.py:409
  268.1 17.1 %shard_map.333 = (f32[448,768]{1,0:T(8,128)S(1)}, bf16[448,768]{1,0:T(8,128)(2,1)S(1)}, f32[448,768]{1,0:T(8,128)}, bf16[448,768]{1,0:T(8,128)(2,1)S(1)}, bf16[7...) custom-call(s32[1]{0:T(128)} %bitcast.26.number, ...), custom_call_target="tpu_custom_call" | custom-call | flops 1000 | bytes 1000 | tf_op jit(solution)/shard_map/pallas_call | solution.py:419
  291.9 2.2 shard_map.334
  297.7 5.7 %all-to-all-start.2 = ((bf16[8,112,768]{2,1,0:T(8,128)(2,1)}), bf16[8,112,768]{2,1,0:T(8,128)(2,1)S(1)}, u32[]{:S(2)}, u32[]{:S(2)}) async-start(bf16[8,112,768]{2,1,0:T(8,128)(2,1)} %copy-done.19), calls=%async_computation.2 | async-start | bytes 2752512 | tf_op jit(solution)/shard_map/all_to_all | solution.py:947
  307.0 29.9 %collective-permute-done.32.up1 = bf16[192,768]{1,0:T(8,128)(2,1)S(1)} collective-permute-done((bf16[192,768]{1,0:T(8,128)(2,1)}, bf16[192,768]{1,0:T(8,128)(2,1)S(1)}, u32[]{:S(2)}, u32[]{:S(2)}) %collective-permute-start.32) | collective-permute-done | bytes 294944 | tf_op jit(solution)/shard_map/ppermute | solution.py:409
  340.9 2.1 collective-permute-done.35.far_ref
  344.7 8.0 %collective-permute-done.36.far_ref = bf16[208,768]{1,0:T(8,128)(2,1)S(1)} collective-permute-done((bf16[208,768]{1,0:T(8,128)(2,1)S(1)}, bf16[208,768]{1,0:T(8,128)(2,1)S(1)}, u32[]{:S(2)}, u32[]{:S(2)}) %collective-permute-start.36) | collective-permute-done | bytes 319520 | tf_op jit(solution)/shard_map/ppermute | solution.py:409
  355.7 7.2 %collective-permute-done.37.g1 = bf16[208,768]{1,0:T(8,128)(2,1)S(1)} collective-permute-done((bf16[208,768]{1,0:T(8,128)(2,1)S(1)}, bf16[208,768]{1,0:T(8,128)(2,1)S(1)}, u32[]{:S(2)}, u32[]{:S(2)}) %collective-permute-start.37) | collective-permute-done | bytes 319520 | tf_op jit(solution)/shard_map/ppermute | solution.py:409
  365.6 9.9 %shard_map.338 = (bf16[384,768]{1,0:T(8,128)(2,1)S(1)}, bf16[384,768]{1,0:T(8,128)(2,1)S(1)}, f32[416,768]{1,0:T(8,128)S(1)}, bf16[416,768]{1,0:T(8,128)(2,1)S(1)}) custom-call(bf16[208,768]{1,0:T(8,128)(2,1)S(1)} %get-tuple-element.229.g0, bf16[208,768]{1,0:T(8,128)(2,1)S(1)} %collective-permute-done.37.g1, ...), custom_call_target="tpu_custom_call" | custom-call | flops 8000000000 | bytes 1000 | tf_op jit(solution)/shard_map/pallas_call | solution.py:419
  376.3 2.5 collective-permute-done.40.down1
  383.4 11.1 %collective-permute-done.54.got = bf16[384,768]{1,0:T(8,128)(2,1)S(1)} collective-permute-done((bf16[384,768]{1,0:T(8,128)(2,1)S(1)}, bf16[384,768]{1,0:T(8,128)(2,1)S(1)}, u32[]{:S(2)}, u32[]{:S(2)}) %collective-permute-start.54) | collective-permute-done | bytes 589856 | tf_op jit(solution)/shard_map/ppermute | solution.py:409
  396.9 5.9 %all-to-all-start.3 = ((bf16[8,96,1536]{2,1,0:T(8,128)(2,1)}), bf16[8,96,1536]{2,1,0:T(8,128)(2,1)}, u32[]{:S(2)}, u32[]{:S(2)}) async-start(bf16[8,96,1536]{2,1,0:T(8,128)(2,1)} %bitcast.64), calls=%async_computation.3 | async-start | bytes 4718592 | tf_op jit(solution)/shard_map/all_to_all | solution.py:1113
  409.2 7.4 %collective-permute-done.43.g1 = bf16[208,768]{1,0:T(8,128)(2,1)S(1)} collective-permute-done((bf16[208,768]{1,0:T(8,128)(2,1)S(1)}, bf16[208,768]{1,0:T(8,128)(2,1)S(1)}, u32[]{:S(2)}, u32[]{:S(2)}) %collective-permute-start.43) | collective-permute-done | bytes 319520 | tf_op jit(solution)/shard_map/ppermute | solution.py:409
  418.1 2.0 copy-done.2
  421.4 5.7 %shard_map.341 = (bf16[384,1536]{1,0:T(8,128)(2,1)S(1)}, bf16[384,1536]{1,0:T(8,128)(2,1)S(1)}, f32[416,768]{1,0:T(8,128)S(1)}, bf16[416,768]{1,0:T(8,128)(2,1)S(1)}) custom-call(bf16[208,768]{1,0:T(8,128)(2,1)S(1)} %get-tuple-element.239.g0, bf16[208,768]{1,0:T(8,128)(2,1)S(1)} %collective-permute-done.43.g1, ...), custom_call_target="tpu_custom_call" | custom-call | flops 1000 | bytes 1000 | tf_op jit(solution)/shard_map/pallas_call | solution.py:419
  433.0 7.6 %collective-permute-done.48.far_ref = bf16[208,768]{1,0:T(8,128)(2,1)S(1)} collective-permute-done((bf16[208,768]{1,0:T(8,128)(2,1)S(1)}, bf16[208,768]{1,0:T(8,128)(2,1)S(1)}, u32[]{:S(2)}, u32[]{:S(2)}) %collective-permute-start.48) | collective-permute-done | bytes 319520 | tf_op jit(solution)/shard_map/ppermute | solution.py:409
  442.7 7.0 %collective-permute-done.49.g1 = bf16[208,768]{1,0:T(8,128)(2,1)S(1)} collective-permute-done((bf16[208,768]{1,0:T(8,128)(2,1)S(1)}, bf16[208,768]{1,0:T(8,128)(2,1)S(1)}, u32[]{:S(2)}, u32[]{:S(2)}) %collective-permute-start.49) | collective-permute-done | bytes 319520 | tf_op jit(solution)/shard_map/ppermute | solution.py:409
  452.0 2.3 collective-permute-start.56
  454.3 9.0 %collective-permute-done.53.got = bf16[384,1536]{1,0:T(8,128)(2,1)S(1)} collective-permute-done((bf16[384,1536]{1,0:T(8,128)(2,1)S(1)}, bf16[384,1536]{1,0:T(8,128)(2,1)S(1)}, u32[]{:S(2)}, u32[]{:S(2)}) %collective-permute-start.53) | collective-permute-done | bytes 1179680 | tf_op jit(solution)/shard_map/ppermute | solution.py:409
  464.3 2.8 collective-permute-start.57
  468.7 10.1 %shard_map.347 = (bf16[384,768]{1,0:T(8,128)(2,1)S(1)}, bf16[384,768]{1,0:T(8,128)(2,1)S(1)}, f32[416,768]{1,0:T(8,128)S(1)}, bf16[416,768]{1,0:T(8,128)(2,1)S(1)}) custom-call(bf16[208,768]{1,0:T(8,128)(2,1)S(1)} %get-tuple-element.258.g0, bf16[208,768]{1,0:T(8,128)(2,1)S(1)} %collective-permute-done.49.g1, ...), custom_call_target="tpu_custom_call" | custom-call | flops 8000000000 | bytes 1000 | tf_op jit(solution)/shard_map/pallas_call | solution.py:419
  483.5 2.5 collective-permute-start.60
  489.5 2.5 collective-permute-start.62
  496.7 3.6 collective-permute-done.60.got
  501.8 4.3 convert_bitcast_fusion
  506.2 9.3 %collective-permute-done.63.r2 = bf16[96,1536]{1,0:T(8,128)(2,1)S(1)} collective-permute-done((bf16[96,1536]{1,0:T(8,128)(2,1)S(1)}, bf16[96,1536]{1,0:T(8,128)(2,1)S(1)}, u32[]{:S(2)}, u32[]{:S(2)}) %collective-permute-start.63) | collective-permute-done | bytes 294944 | tf_op jit(solution)/shard_map/ppermute | solution.py:409
  517.1 2.7 collective-permute-done.65
  520.0 3.8 collective-permute-done.66
  525.8 5.4 collective-permute-start.67
  (477 shorter events, 154.7 us)
Async XLA Ops:
  7.3 70.2 %all-gather.2.cloned.1.call-start = ((), (), s32[]{:S(2)}) async-start(), calls=%async_computation.4 | async-start | bytes 2211840 | tf_op jit(solution)/shard_map/all_gather | solution.py:891
  13.5 10.2 %collective-permute-start = (bf16[96,896]{1,0:T(8,128)(2,1)S(1)}, bf16[96,896]{1,0:T(8,128)(2,1)S(1)}, u32[]{:S(2)}, u32[]{:S(2)}) collective-permute-start(bf16[96,896]{1,0:T(8,128)(2,1)S(1)} %shard_map.314.refs_0_), channel_id=1, source_target_pairs={{0,8},{1,9},{2,10},{3,11},{4,12},{5,13},{6,14},{7,15},{8,0},{9,1},... | collective-permute-start | bytes 516104 | tf_op jit(solution)/shard_map/ppermute | solution.py:409
  16.6 20.5 %collective-permute-start.1 = (bf16[96,896]{1,0:T(8,128)(2,1)S(1)}, bf16[96,896]{1,0:T(8,128)(2,1)S(1)}, u32[]{:S(2)}, u32[]{:S(2)}) collective-permute-start(bf16[96,896]{1,0:T(8,128)(2,1)S(1)} %shard_map.314.refs_0_), channel_id=1, source_target_pairs={{0,16},{1,17},{2,18},{3,19},{4,20},{5,21},{6,22},{7,23},{8,24},{9,... | collective-permute-start | bytes 516104 | tf_op jit(solution)/shard_map/ppermute | solution.py:409
  19.2 18.0 %collective-permute-start.2 = (bf16[96,896]{1,0:T(8,128)(2,1)S(1)}, bf16[96,896]{1,0:T(8,128)(2,1)S(1)}, u32[]{:S(2)}, u32[]{:S(2)}) collective-permute-start(bf16[96,896]{1,0:T(8,128)(2,1)S(1)} %shard_map.314.refs_0_), channel_id=1, source_target_pairs={{0,24},{1,25},{2,26},{3,27},{4,28},{5,29},{6,30},{7,31},{8,16},{9,... | collective-permute-start | bytes 516104 | tf_op jit(solution)/shard_map/ppermute | solution.py:409
  37.2 14.5 %collective-permute-start.3 = (bf16[384,896]{1,0:T(8,128)(2,1)S(1)}, bf16[384,896]{1,0:T(8,128)(2,1)S(1)}, u32[]{:S(2)}, u32[]{:S(2)}) collective-permute-start(bf16[384,896]{1,0:T(8,128)(2,1)S(1)} %shard_map.315.refs_0_), channel_id=1, source_target_pairs={{0,4},{1,5},{2,6},{3,7},{4,0},{5,1},{6,2},{7,3},{8,12},{9,13},{10,... | collective-permute-start | bytes 2064392 | tf_op jit(solution)/shard_map/ppermute | solution.py:409
  67.7 9.8 %collective-permute-start.8 = (bf16[208,768]{1,0:T(8,128)(2,1)S(1)}, bf16[208,768]{1,0:T(8,128)(2,1)S(1)}, u32[]{:S(2)}, u32[]{:S(2)}) collective-permute-start(bf16[208,768]{1,0:T(8,128)(2,1)S(1)} %get-tuple-element.176), channel_id=1, source_target_pairs={{0,2},{1,3},{2,0},{3,1},{4,6},{5,7},{6,4},{7,5},{8,10},{9,11},{10,... | collective-permute-start | bytes 958472 | tf_op jit(solution)/shard_map/ppermute | solution.py:409
  80.7 42.5 %collective-permute-start.15 = (bf16[384,2304]{1,0:T(8,128)(2,1)S(1)}, bf16[384,2304]{1,0:T(8,128)(2,1)}, u32[]{:S(2)}, u32[]{:S(2)}) collective-permute-start(bf16[384,2304]{1,0:T(8,128)(2,1)S(1)} %shard_map.323.refs_0_), channel_id=1, source_target_pairs={{0,4},{1,5},{2,6},{3,7},{4,0},{5,1},{6,2},{7,3},{8,12},{9,13},{10,... | collective-permute-start | bytes 5308424 | tf_op jit(solution)/shard_map/ppermute | solution.py:409
  81.3 10.8 %collective-permute-start.12 = (bf16[208,768]{1,0:T(8,128)(2,1)}, bf16[208,768]{1,0:T(8,128)(2,1)}, u32[]{:S(2)}, u32[]{:S(2)}) collective-permute-start(bf16[208,768]{1,0:T(8,128)(2,1)} %get-tuple-element.181.p0), channel_id=1, source_target_pairs={{0,2},{1,3},{2,0},{3,1},{4,6},{5,7},{6,4},{7,5},{8,10},{9,11},{10,... | collective-permute-start | bytes 958472 | tf_op jit(solution)/shard_map/ppermute | solution.py:409
  82.8 14.3 %collective-permute-start.9 = (bf16[208,768]{1,0:T(8,128)(2,1)S(1)}, bf16[208,768]{1,0:T(8,128)(2,1)}, u32[]{:S(2)}, u32[]{:S(2)}) collective-permute-start(bf16[208,768]{1,0:T(8,128)(2,1)S(1)} %get-tuple-element.182.b0), channel_id=1, source_target_pairs={{0,2},{1,3},{2,0},{3,1},{4,6},{5,7},{6,4},{7,5},{8,10},{9,11},{10,... | collective-permute-start | bytes 958472 | tf_op jit(solution)/shard_map/ppermute | solution.py:409
  83.6 16.7 %collective-permute-start.13 = (bf16[208,768]{1,0:T(8,128)(2,1)}, bf16[208,768]{1,0:T(8,128)(2,1)S(1)}, u32[]{:S(2)}, u32[]{:S(2)}) collective-permute-start(bf16[208,768]{1,0:T(8,128)(2,1)} %get-tuple-element.181.p0), channel_id=1, source_target_pairs={{0,1},{1,0},{2,3},{3,2},{4,5},{5,4},{6,7},{7,6},{8,9},{9,8},{10,11... | collective-permute-start | bytes 958472 | tf_op jit(solution)/shard_map/ppermute | solution.py:409
  92.1 8.3 %collective-permute-start.14 = (bf16[208,768]{1,0:T(8,128)(2,1)}, bf16[208,768]{1,0:T(8,128)(2,1)S(1)}, u32[]{:S(2)}, u32[]{:S(2)}) collective-permute-start(bf16[208,768]{1,0:T(8,128)(2,1)} %collective-permute-done.12.p1), channel_id=1, source_target_pairs={{0,1},{1,0},{2,3},{3,2},{4,5},{5,4},{6,7},{7,6},{8,9},{9,8},{10,11... | collective-permute-start | bytes 958472 | tf_op jit(solution)/shard_map/ppermute | solution.py:409
  104.6 79.3 %all-to-all-start.1 = ((bf16[8,96,1536]{2,1,0:T(8,128)(2,1)}), bf16[8,96,1536]{2,1,0:T(8,128)(2,1)}, u32[]{:S(2)}, u32[]{:S(2)}) async-start(bf16[8,96,1536]{2,1,0:T(8,128)(2,1)} %pad_maximum_fusion), calls=%async_computation.1 | async-start | bytes 4718592 | tf_op jit(solution)/shard_map/all_to_all | solution.py:1015
  132.3 9.7 %collective-permute-start.17 = (bf16[208,768]{1,0:T(8,128)(2,1)S(1)}, bf16[208,768]{1,0:T(8,128)(2,1)S(1)}, u32[]{:S(2)}, u32[]{:S(2)}) collective-permute-start(bf16[208,768]{1,0:T(8,128)(2,1)S(1)} %get-tuple-element.190), channel_id=1, source_target_pairs={{0,2},{1,3},{2,0},{3,1},{4,6},{5,7},{6,4},{7,5},{8,10},{9,11},{10,... | collective-permute-start | bytes 958472 | tf_op jit(solution)/shard_map/ppermute | solution.py:409
  142.4 9.0 %collective-permute-start.18 = (bf16[208,768]{1,0:T(8,128)(2,1)S(1)}, bf16[208,768]{1,0:T(8,128)(2,1)S(1)}, u32[]{:S(2)}, u32[]{:S(2)}) collective-permute-start(bf16[208,768]{1,0:T(8,128)(2,1)S(1)} %get-tuple-element.192.a0), channel_id=1, source_target_pairs={{0,2},{1,3},{2,0},{3,1},{4,6},{5,7},{6,4},{7,5},{8,10},{9,11},{10,... | collective-permute-start | bytes 958472 | tf_op jit(solution)/shard_map/ppermute | solution.py:409
  160.0 9.6 %collective-permute-start.22 = (bf16[208,768]{1,0:T(8,128)(2,1)S(1)}, bf16[208,768]{1,0:T(8,128)(2,1)S(1)}, u32[]{:S(2)}, u32[]{:S(2)}) collective-permute-start(bf16[208,768]{1,0:T(8,128)(2,1)S(1)} %get-tuple-element.196), channel_id=1, source_target_pairs={{0,2},{1,3},{2,0},{3,1},{4,6},{5,7},{6,4},{7,5},{8,10},{9,11},{10,... | collective-permute-start | bytes 958472 | tf_op jit(solution)/shard_map/ppermute | solution.py:409
  170.8 8.7 %collective-permute-start.23 = (bf16[208,768]{1,0:T(8,128)(2,1)S(1)}, bf16[208,768]{1,0:T(8,128)(2,1)S(1)}, u32[]{:S(2)}, u32[]{:S(2)}) collective-permute-start(bf16[208,768]{1,0:T(8,128)(2,1)S(1)} %get-tuple-element.198.p0), channel_id=1, source_target_pairs={{0,2},{1,3},{2,0},{3,1},{4,6},{5,7},{6,4},{7,5},{8,10},{9,11},{10,... | collective-permute-start | bytes 958472 | tf_op jit(solution)/shard_map/ppermute | solution.py:409
  183.9 80.9 %all-to-all-start = ((bf16[8,112,768]{2,1,0:T(8,128)(2,1)}), bf16[8,112,768]{2,1,0:T(8,128)(2,1)S(1)}, u32[]{:S(2)}, u32[]{:S(2)}) async-start(bf16[8,112,768]{2,1,0:T(8,128)(2,1)} %pad_maximum_fusion.1), calls=%async_computation | async-start | bytes 2752512 | tf_op jit(solution)/shard_map/all_to_all | solution.py:947
  211.4 53.4 %collective-permute-start.26 = (bf16[768,1536]{1,0:T(8,128)(2,1)}, bf16[768,1536]{1,0:T(8,128)(2,1)}, u32[]{:S(2)}, u32[]{:S(2)}) collective-permute-start(bf16[768,1536]{1,0:T(8,128)(2,1)} %bitcast.29.rest_0_), channel_id=1, source_target_pairs={{0,2},{1,3},{2,0},{3,1},{4,6},{5,7},{6,4},{7,5},{8,10},{9,11},{10,... | collective-permute-start | bytes 7077896 | tf_op jit(solution)/shard_map/ppermute | solution.py:409
  288.0 9.0 %collective-permute-start.31 = (bf16[192,768]{1,0:T(8,128)(2,1)S(1)}, bf16[192,768]{1,0:T(8,128)(2,1)S(1)}, u32[]{:S(2)}, u32[]{:S(2)}) collective-permute-start(bf16[192,768]{1,0:T(8,128)(2,1)S(1)} %get-tuple-element.211), channel_id=1, source_target_pairs={{0,2},{1,3},{2,0},{3,1},{4,6},{5,7},{6,4},{7,5},{8,10},{9,11},{10,... | collective-permute-start | bytes 884744 | tf_op jit(solution)/shard_map/ppermute | solution.py:409
  297.7 41.6 %all-to-all-start.2 = ((bf16[8,112,768]{2,1,0:T(8,128)(2,1)}), bf16[8,112,768]{2,1,0:T(8,128)(2,1)S(1)}, u32[]{:S(2)}, u32[]{:S(2)}) async-start(bf16[8,112,768]{2,1,0:T(8,128)(2,1)} %copy-done.19), calls=%async_computation.2 | async-start | bytes 2752512 | tf_op jit(solution)/shard_map/all_to_all | solution.py:947
  303.4 34.2 %collective-permute-start.33 = (bf16[384,768]{1,0:T(8,128)(2,1)}, bf16[384,768]{1,0:T(8,128)(2,1)S(1)}, u32[]{:S(2)}, u32[]{:S(2)}) collective-permute-start(bf16[384,768]{1,0:T(8,128)(2,1)} %copy-done.116), channel_id=1, source_target_pairs={{0,2},{1,3},{2,0},{3,1},{4,6},{5,7},{6,4},{7,5},{8,10},{9,11},{10,... | collective-permute-start | bytes 1769480 | tf_op jit(solution)/shard_map/ppermute | solution.py:409
  305.0 33.5 %collective-permute-start.34 = (bf16[384,768]{1,0:T(8,128)(2,1)}, bf16[384,768]{1,0:T(8,128)(2,1)S(1)}, u32[]{:S(2)}, u32[]{:S(2)}) collective-permute-start(bf16[384,768]{1,0:T(8,128)(2,1)} %copy-done.115), channel_id=1, source_target_pairs={{0,2},{1,3},{2,0},{3,1},{4,6},{5,7},{6,4},{7,5},{8,10},{9,11},{10,... | collective-permute-start | bytes 1769480 | tf_op jit(solution)/shard_map/ppermute | solution.py:409
  305.5 31.4 %collective-permute-start.32 = (bf16[192,768]{1,0:T(8,128)(2,1)}, bf16[192,768]{1,0:T(8,128)(2,1)S(1)}, u32[]{:S(2)}, u32[]{:S(2)}) collective-permute-start(bf16[192,768]{1,0:T(8,128)(2,1)} %copy-done.121), channel_id=1, source_target_pairs={{0,2},{1,3},{2,0},{3,1},{4,6},{5,7},{6,4},{7,5},{8,10},{9,11},{10,... | collective-permute-start | bytes 884744 | tf_op jit(solution)/shard_map/ppermute | solution.py:409
  343.1 9.6 %collective-permute-start.36 = (bf16[208,768]{1,0:T(8,128)(2,1)S(1)}, bf16[208,768]{1,0:T(8,128)(2,1)S(1)}, u32[]{:S(2)}, u32[]{:S(2)}) collective-permute-start(bf16[208,768]{1,0:T(8,128)(2,1)S(1)} %get-tuple-element.227), channel_id=1, source_target_pairs={{0,2},{1,3},{2,0},{3,1},{4,6},{5,7},{6,4},{7,5},{8,10},{9,11},{10,... | collective-permute-start | bytes 958472 | tf_op jit(solution)/shard_map/ppermute | solution.py:409
  354.1 8.7 %collective-permute-start.37 = (bf16[208,768]{1,0:T(8,128)(2,1)S(1)}, bf16[208,768]{1,0:T(8,128)(2,1)S(1)}, u32[]{:S(2)}, u32[]{:S(2)}) collective-permute-start(bf16[208,768]{1,0:T(8,128)(2,1)S(1)} %get-tuple-element.229.g0), channel_id=1, source_target_pairs={{0,2},{1,3},{2,0},{3,1},{4,6},{5,7},{6,4},{7,5},{8,10},{9,11},{10,... | collective-permute-start | bytes 958472 | tf_op jit(solution)/shard_map/ppermute | solution.py:409
  355.7 8.8 %collective-permute-start.38 = (bf16[208,768]{1,0:T(8,128)(2,1)S(1)}, bf16[208,768]{1,0:T(8,128)(2,1)S(1)}, u32[]{:S(2)}, u32[]{:S(2)}) collective-permute-start(bf16[208,768]{1,0:T(8,128)(2,1)S(1)} %get-tuple-element.229.g0), channel_id=1, source_target_pairs={{0,1},{1,0},{2,3},{3,2},{4,5},{5,4},{6,7},{7,6},{8,9},{9,8},{10,11... | collective-permute-start | bytes 958472 | tf_op jit(solution)/shard_map/ppermute | solution.py:409
  362.9 16.0 %collective-permute-start.40 = (bf16[384,768]{1,0:T(8,128)(2,1)}, bf16[384,768]{1,0:T(8,128)(2,1)S(1)}, u32[]{:S(2)}, u32[]{:S(2)}) collective-permute-start(bf16[384,768]{1,0:T(8,128)(2,1)} %copy-done.113), channel_id=1, source_target_pairs={{0,2},{1,3},{2,0},{3,1},{4,6},{5,7},{6,4},{7,5},{8,10},{9,11},{10,... | collective-permute-start | bytes 1769480 | tf_op jit(solution)/shard_map/ppermute | solution.py:409
  378.8 15.7 %collective-permute-start.54 = (bf16[384,768]{1,0:T(8,128)(2,1)S(1)}, bf16[384,768]{1,0:T(8,128)(2,1)S(1)}, u32[]{:S(2)}, u32[]{:S(2)}) collective-permute-start(bf16[384,768]{1,0:T(8,128)(2,1)S(1)} %get-tuple-element.267), channel_id=1, source_target_pairs={{0,4},{1,5},{2,6},{3,7},{4,0},{5,1},{6,2},{7,3},{8,12},{9,13},{10,... | collective-permute-start | bytes 1769480 | tf_op jit(solution)/shard_map/ppermute | solution.py:409
  381.9 12.7 %collective-permute-start.42 = (bf16[208,768]{1,0:T(8,128)(2,1)S(1)}, bf16[208,768]{1,0:T(8,128)(2,1)S(1)}, u32[]{:S(2)}, u32[]{:S(2)}) collective-permute-start(bf16[208,768]{1,0:T(8,128)(2,1)S(1)} %get-tuple-element.238), channel_id=1, source_target_pairs={{0,2},{1,3},{2,0},{3,1},{4,6},{5,7},{6,4},{7,5},{8,10},{9,11},{10,... | collective-permute-start | bytes 958472 | tf_op jit(solution)/shard_map/ppermute | solution.py:409
  396.9 86.5 %all-to-all-start.3 = ((bf16[8,96,1536]{2,1,0:T(8,128)(2,1)}), bf16[8,96,1536]{2,1,0:T(8,128)(2,1)}, u32[]{:S(2)}, u32[]{:S(2)}) async-start(bf16[8,96,1536]{2,1,0:T(8,128)(2,1)} %bitcast.64), calls=%async_computation.3 | async-start | bytes 4718592 | tf_op jit(solution)/shard_map/all_to_all | solution.py:1113
  407.6 9.0 %collective-permute-start.43 = (bf16[208,768]{1,0:T(8,128)(2,1)S(1)}, bf16[208,768]{1,0:T(8,128)(2,1)S(1)}, u32[]{:S(2)}, u32[]{:S(2)}) collective-permute-start(bf16[208,768]{1,0:T(8,128)(2,1)S(1)} %get-tuple-element.239.g0), channel_id=1, source_target_pairs={{0,2},{1,3},{2,0},{3,1},{4,6},{5,7},{6,4},{7,5},{8,10},{9,11},{10,... | collective-permute-start | bytes 958472 | tf_op jit(solution)/shard_map/ppermute | solution.py:409
  429.3 34.0 %collective-permute-start.53 = (bf16[384,1536]{1,0:T(8,128)(2,1)S(1)}, bf16[384,1536]{1,0:T(8,128)(2,1)S(1)}, u32[]{:S(2)}, u32[]{:S(2)}) collective-permute-start(bf16[384,1536]{1,0:T(8,128)(2,1)S(1)} %get-tuple-element.257), channel_id=1, source_target_pairs={{0,4},{1,5},{2,6},{3,7},{4,0},{5,1},{6,2},{7,3},{8,12},{9,13},{10,... | collective-permute-start | bytes 3538952 | tf_op jit(solution)/shard_map/ppermute | solution.py:409
  431.2 9.4 %collective-permute-start.48 = (bf16[208,768]{1,0:T(8,128)(2,1)S(1)}, bf16[208,768]{1,0:T(8,128)(2,1)S(1)}, u32[]{:S(2)}, u32[]{:S(2)}) collective-permute-start(bf16[208,768]{1,0:T(8,128)(2,1)S(1)} %get-tuple-element.251), channel_id=1, source_target_pairs={{0,2},{1,3},{2,0},{3,1},{4,6},{5,7},{6,4},{7,5},{8,10},{9,11},{10,... | collective-permute-start | bytes 958472 | tf_op jit(solution)/shard_map/ppermute | solution.py:409
  441.1 8.6 %collective-permute-start.49 = (bf16[208,768]{1,0:T(8,128)(2,1)S(1)}, bf16[208,768]{1,0:T(8,128)(2,1)S(1)}, u32[]{:S(2)}, u32[]{:S(2)}) collective-permute-start(bf16[208,768]{1,0:T(8,128)(2,1)S(1)} %get-tuple-element.258.g0), channel_id=1, source_target_pairs={{0,2},{1,3},{2,0},{3,1},{4,6},{5,7},{6,4},{7,5},{8,10},{9,11},{10,... | collective-permute-start | bytes 958472 | tf_op jit(solution)/shard_map/ppermute | solution.py:409
  442.7 24.4 %collective-permute-start.50 = (bf16[208,768]{1,0:T(8,128)(2,1)S(1)}, bf16[208,768]{1,0:T(8,128)(2,1)S(1)}, u32[]{:S(2)}, u32[]{:S(2)}) collective-permute-start(bf16[208,768]{1,0:T(8,128)(2,1)S(1)} %get-tuple-element.258.g0), channel_id=1, source_target_pairs={{0,1},{1,0},{2,3},{3,2},{4,5},{5,4},{6,7},{7,6},{8,9},{9,8},{10,11... | collective-permute-start | bytes 958472 | tf_op jit(solution)/shard_map/ppermute | solution.py:409
  449.7 17.4 %collective-permute-start.51 = (bf16[208,768]{1,0:T(8,128)(2,1)S(1)}, bf16[208,768]{1,0:T(8,128)(2,1)S(1)}, u32[]{:S(2)}, u32[]{:S(2)}) collective-permute-start(bf16[208,768]{1,0:T(8,128)(2,1)S(1)} %collective-permute-done.49.g1), channel_id=1, source_target_pairs={{0,1},{1,0},{2,3},{3,2},{4,5},{5,4},{6,7},{7,6},{8,9},{9,8},{10,11... | collective-permute-start | bytes 958472 | tf_op jit(solution)/shard_map/ppermute | solution.py:409
  450.6 30.8 %collective-permute-start.55 = (bf16[96,768]{1,0:T(8,128)(2,1)S(1)}, bf16[96,768]{1,0:T(8,128)(2,1)S(1)}, u32[]{:S(2)}, u32[]{:S(2)}) collective-permute-start(bf16[96,768]{1,0:T(8,128)(2,1)S(1)} %get-tuple-element.271), channel_id=1, source_target_pairs={{0,8},{1,9},{2,10},{3,11},{4,12},{5,13},{6,14},{7,15},{8,0},{9,1},... | collective-permute-start | bytes 442376 | tf_op jit(solution)/shard_map/ppermute | solution.py:409
  452.0 30.0 %collective-permute-start.56 = (bf16[96,768]{1,0:T(8,128)(2,1)S(1)}, bf16[96,768]{1,0:T(8,128)(2,1)S(1)}, u32[]{:S(2)}, u32[]{:S(2)}) collective-permute-start(bf16[96,768]{1,0:T(8,128)(2,1)S(1)} %get-tuple-element.272), channel_id=1, source_target_pairs={{0,16},{1,17},{2,18},{3,19},{4,20},{5,21},{6,22},{7,23},{8,24},{9,... | collective-permute-start | bytes 442376 | tf_op jit(solution)/shard_map/ppermute | solution.py:409
  464.3 18.4 %collective-permute-start.57 = (bf16[96,768]{1,0:T(8,128)(2,1)S(1)}, bf16[96,768]{1,0:T(8,128)(2,1)S(1)}, u32[]{:S(2)}, u32[]{:S(2)}) collective-permute-start(bf16[96,768]{1,0:T(8,128)(2,1)S(1)} %get-tuple-element.273), channel_id=1, source_target_pairs={{0,24},{1,25},{2,26},{3,27},{4,28},{5,29},{6,30},{7,31},{8,16},{9,... | collective-permute-start | bytes 442376 | tf_op jit(solution)/shard_map/ppermute | solution.py:409
  467.1 16.2 %collective-permute-start.52 = (bf16[208,768]{1,0:T(8,128)(2,1)S(1)}, bf16[208,768]{1,0:T(8,128)(2,1)S(1)}, u32[]{:S(2)}, u32[]{:S(2)}) collective-permute-start(bf16[208,768]{1,0:T(8,128)(2,1)S(1)} %get-tuple-element.254), channel_id=1, source_target_pairs={{0,2},{1,3},{2,0},{3,1},{4,6},{5,7},{6,4},{7,5},{8,10},{9,11},{10,... | collective-permute-start | bytes 958472 | tf_op jit(solution)/shard_map/ppermute | solution.py:409
  483.5 16.9 %collective-permute-start.60 = (bf16[384,768]{1,0:T(8,128)(2,1)}, bf16[384,768]{1,0:T(8,128)(2,1)}, u32[]{:S(2)}, u32[]{:S(2)}) collective-permute-start(bf16[384,768]{1,0:T(8,128)(2,1)} %copy-done.114), channel_id=1, source_target_pairs={{0,4},{1,5},{2,6},{3,7},{4,0},{5,1},{6,2},{7,3},{8,12},{9,13},{10,... | collective-permute-start | bytes 1769480 | tf_op jit(solution)/shard_map/ppermute | solution.py:409
  487.7 12.6 %collective-permute-start.59 = (bf16[208,768]{1,0:T(8,128)(2,1)S(1)}, bf16[208,768]{1,0:T(8,128)(2,1)S(1)}, u32[]{:S(2)}, u32[]{:S(2)}) collective-permute-start(bf16[208,768]{1,0:T(8,128)(2,1)S(1)} %get-tuple-element.280), channel_id=1, source_target_pairs={{0,2},{1,3},{2,0},{3,1},{4,6},{5,7},{6,4},{7,5},{8,10},{9,11},{10,... | collective-permute-start | bytes 958472 | tf_op jit(solution)/shard_map/ppermute | solution.py:409
  489.5 16.6 %collective-permute-start.62 = (bf16[96,1536]{1,0:T(8,128)(2,1)S(1)}, bf16[96,1536]{1,0:T(8,128)(2,1)S(1)}, u32[]{:S(2)}, u32[]{:S(2)}) collective-permute-start(bf16[96,1536]{1,0:T(8,128)(2,1)S(1)} %get-tuple-element.291), channel_id=1, source_target_pairs={{0,8},{1,9},{2,10},{3,11},{4,12},{5,13},{6,14},{7,15},{8,0},{9,1},... | collective-permute-start | bytes 884744 | tf_op jit(solution)/shard_map/ppermute | solution.py:409
  492.0 23.5 %collective-permute-start.63 = (bf16[96,1536]{1,0:T(8,128)(2,1)S(1)}, bf16[96,1536]{1,0:T(8,128)(2,1)S(1)}, u32[]{:S(2)}, u32[]{:S(2)}) collective-permute-start(bf16[96,1536]{1,0:T(8,128)(2,1)S(1)} %get-tuple-element.292), channel_id=1, source_target_pairs={{0,16},{1,17},{2,18},{3,19},{4,20},{5,21},{6,22},{7,23},{8,24},{9,... | collective-permute-start | bytes 884744 | tf_op jit(solution)/shard_map/ppermute | solution.py:409
  493.5 22.0 %collective-permute-start.64 = (bf16[96,1536]{1,0:T(8,128)(2,1)S(1)}, bf16[96,1536]{1,0:T(8,128)(2,1)S(1)}, u32[]{:S(2)}, u32[]{:S(2)}) collective-permute-start(bf16[96,1536]{1,0:T(8,128)(2,1)S(1)} %get-tuple-element.293), channel_id=1, source_target_pairs={{0,24},{1,25},{2,26},{3,27},{4,28},{5,29},{6,30},{7,31},{8,16},{9,... | collective-permute-start | bytes 884744 | tf_op jit(solution)/shard_map/ppermute | solution.py:409
  525.8 18.8 %collective-permute-start.67 = (bf16[128,768]{1,0:T(8,128)(2,1)}, bf16[128,768]{1,0:T(8,128)(2,1)S(1)}, u32[]{:S(2)}, u32[]{:S(2)}) collective-permute-start(bf16[128,768]{1,0:T(8,128)(2,1)} %get-tuple-element.298), channel_id=1, source_target_pairs={{0,8},{1,9},{2,10},{3,11},{4,12},{5,13},{6,14},{7,15},{8,0},{9,1},... | collective-permute-start | bytes 589832 | tf_op jit(solution)/shard_map/ppermute | solution.py:409
  531.2 14.7 %collective-permute-start.68 = (bf16[128,768]{1,0:T(8,128)(2,1)}, bf16[128,768]{1,0:T(8,128)(2,1)}, u32[]{:S(2)}, u32[]{:S(2)}) collective-permute-start(bf16[128,768]{1,0:T(8,128)(2,1)} %get-tuple-element.299), channel_id=1, source_target_pairs={{0,16},{1,17},{2,18},{3,19},{4,20},{5,21},{6,22},{7,23},{8,24},{9,... | collective-permute-start | bytes 589832 | tf_op jit(solution)/shard_map/ppermute | solution.py:409
  532.6 13.3 %collective-permute-start.69 = (bf16[128,768]{1,0:T(8,128)(2,1)}, bf16[128,768]{1,0:T(8,128)(2,1)}, u32[]{:S(2)}, u32[]{:S(2)}) collective-permute-start(bf16[128,768]{1,0:T(8,128)(2,1)} %get-tuple-element.300), channel_id=1, source_target_pairs={{0,24},{1,25},{2,26},{3,27},{4,28},{5,29},{6,30},{7,31},{8,16},{9,... | collective-permute-start | bytes 589832 | tf_op jit(solution)/shard_map/ppermute | solution.py:409
  (163 other events, 1356.0 us)
Sparse Core Ops, SparseCore 0:
  12.3 50.9 all-gather.1

commit v9 on v8

--- a/solution.py
+++ b/solution.py
@@ -1011,7 +1011,7 @@
     )[0]
     x_late = swap(z_late, x=1)
     grad_sent = to_experts(dispatch_kernel, spread(hold(grad_low, normed)))
-    e_pack = hold(e_pack, grad_sent, normed_mlp[3])
+    e_pack = hold(e_pack, grad_sent, x_late, normed_mlp)
     e_own = lax.all_to_all(e_pack, "dp", split_axis=0, concat_axis=0, tiled=True)
     e_own = e_own.reshape(features, wide)
     full_late = stacked([z_late, x_late])

time: 566 us -> 559 us (0.988)
  starting transfers between devices: 126 us -> 104 us
  waiting for transfers between devices: 256 us -> 270 us
    all_to_all x2, waiting for transfers between devices: 0.01 us -> 31.1 us  [exchange(): return lax.all_to_all(both, 'dp', split_axis=0, concat_axis=0, tiled=True)]
    all_to_all x2, starting transfers between devices: 33.2 us -> 12.2 us  [exchange(): return lax.all_to_all(both, 'dp', split_axis=0, concat_axis=0, tiled=True)]
    ppermute x70, waiting for transfers between devices: 256 us -> 239 us  [swap(): return lax.ppermute(values, AXES, pairs)]
    unnamed x282 -> x284, local copies, waits for them, and re-layouts: 55.7 us -> 56.4 us
  transfers between devices with their start and end apart: 75 -> 75, of which waited for: 41 -> 42; matrix products, arithmetic and copies ran while one was open for 3% -> 3% of each run, Pallas kernels for 11% -> 11%
where the time goes in v9:
time: 559 us; the launch traced here: 550 us
  waiting for transfers between devices  270 us (48%)
  starting transfers between devices  104 us (19%)
  Pallas kernels  87.1 us (16%)
  local copies, waits for them, and re-layouts  61.1 us (11%)
  between operations  16.5 us (3%)
  other arithmetic  10.3 us (2%)
    ppermute x70, waiting for transfers between devices, swap(): return lax.ppermute(values, AXES, pairs)  239 us
    pallas_call x46, Pallas kernels, run(): pl.pallas_call(kernel, out_shape=shapes, in_specs=[SM] * scalars + [VM] *...  87.1 us
    ppermute x70, starting transfers between devices, swap(): return lax.ppermute(values, AXES, pairs)  69.8 us
    unnamed x284, local copies, waits for them, and re-layouts  56.4 us
    all_to_all x2, waiting for transfers between devices, exchange(): return lax.all_to_all(both, 'dp', split_axis=0, concat_axis=0, tiled=True)  31.1 us
    all_to_all x1, starting transfers between devices, fast_local(): lax.all_to_all(e_pack, 'dp', split_axis=0, concat_axis=0, tiled=True)  16 us
    all_to_all x2, starting transfers between devices, exchange(): return lax.all_to_all(both, 'dp', split_axis=0, concat_axis=0, tiled=True)  12.2 us
  transfers between devices with their start and end apart: 75, of which 42 were waited for; matrix products, arithmetic and copies ran while one was open for 3% of the time, Pallas kernels for 11%

profile of v9, /device:TPU:0, one launch (start us, length us, event | category | flops | bytes accessed | tf_op | source)
XLA Modules:
  0.0 549.7 jit_solution(5729584178820067368)
XLA Ops:
  13.5 3.1 collective-permute-start
  16.6 2.6 collective-permute-start.1
  19.2 4.5 collective-permute-done.refs_1_
  23.7 13.5 %collective-permute-done.1.refs_2_ = bf16[96,896]{1,0:T(8,128)(2,1)S(1)} collective-permute-done((bf16[96,896]{1,0:T(8,128)(2,1)S(1)}, bf16[96,896]{1,0:T(8,128)(2,1)S(1)}, u32[]{:S(2)}, u32[]{:S(2)}) %collective-permute-start.1) | collective-permute-done | bytes 172064 | tf_op jit(solution)/shard_map/ppermute | solution.py:409
  45.3 4.8 collective-permute-done.4.refs_1_
  59.0 4.7 shard_map.318
  69.3 8.1 %collective-permute-done.8.far_ref = bf16[208,768]{1,0:T(8,128)(2,1)S(1)} collective-permute-done((bf16[208,768]{1,0:T(8,128)(2,1)S(1)}, bf16[208,768]{1,0:T(8,128)(2,1)S(1)}, u32[]{:S(2)}, u32[]{:S(2)}) %collective-permute-start.8) | collective-permute-done | bytes 319520 | tf_op jit(solution)/shard_map/ppermute | solution.py:409
  84.2 7.9 %collective-permute-done.12.p1 = bf16[208,768]{1,0:T(8,128)(2,1)} collective-permute-done((bf16[208,768]{1,0:T(8,128)(2,1)}, bf16[208,768]{1,0:T(8,128)(2,1)}, u32[]{:S(2)}, u32[]{:S(2)}) %collective-permute-start.12) | collective-permute-done | bytes 319520 | tf_op jit(solution)/shard_map/ppermute | solution.py:409
  92.1 5.0 collective-permute-done.9.b1
  97.2 3.2 pad_maximum_fusion
  100.4 2.6 shard_map.322
  105.4 15.5 %collective-permute-done.15.refs_1_ = bf16[384,2304]{1,0:T(8,128)(2,1)} collective-permute-done((bf16[384,2304]{1,0:T(8,128)(2,1)S(1)}, bf16[384,2304]{1,0:T(8,128)(2,1)}, u32[]{:S(2)}, u32[]{:S(2)}) %collective-permute-start.15) | collective-permute-done | bytes 1769504 | tf_op jit(solution)/shard_map/ppermute | solution.py:409
  120.9 16.0 %all-to-all-start.1 = ((bf16[8,96,1536]{2,1,0:T(8,128)(2,1)}), bf16[8,96,1536]{2,1,0:T(8,128)(2,1)}, u32[]{:S(2)}, u32[]{:S(2)}) async-start(bf16[8,96,1536]{2,1,0:T(8,128)(2,1)} %pad_maximum_fusion), calls=%async_computation.1 | async-start | bytes 4718592 | tf_op jit(solution)/shard_map/all_to_all | solution.py:1015
  138.7 4.0 shard_map.325
  147.5 8.1 %collective-permute-done.17.far_ref = bf16[208,768]{1,0:T(8,128)(2,1)S(1)} collective-permute-done((bf16[208,768]{1,0:T(8,128)(2,1)S(1)}, bf16[208,768]{1,0:T(8,128)(2,1)S(1)}, u32[]{:S(2)}, u32[]{:S(2)}) %collective-permute-start.17) | collective-permute-done | bytes 319520 | tf_op jit(solution)/shard_map/ppermute | solution.py:409
  157.5 7.3 %collective-permute-done.18.a1 = bf16[208,768]{1,0:T(8,128)(2,1)S(1)} collective-permute-done((bf16[208,768]{1,0:T(8,128)(2,1)S(1)}, bf16[208,768]{1,0:T(8,128)(2,1)S(1)}, u32[]{:S(2)}, u32[]{:S(2)}) %collective-permute-start.18) | collective-permute-done | bytes 319520 | tf_op jit(solution)/shard_map/ppermute | solution.py:409
  166.4 4.6 shard_map.328
  175.0 8.1 %collective-permute-done.22.far_ref = bf16[208,768]{1,0:T(8,128)(2,1)S(1)} collective-permute-done((bf16[208,768]{1,0:T(8,128)(2,1)S(1)}, bf16[208,768]{1,0:T(8,128)(2,1)S(1)}, u32[]{:S(2)}, u32[]{:S(2)}) %collective-permute-start.22) | collective-permute-done | bytes 319520 | tf_op jit(solution)/shard_map/ppermute | solution.py:409
  185.7 7.2 %collective-permute-done.23.p1 = bf16[208,768]{1,0:T(8,128)(2,1)S(1)} collective-permute-done((bf16[208,768]{1,0:T(8,128)(2,1)S(1)}, bf16[208,768]{1,0:T(8,128)(2,1)S(1)}, u32[]{:S(2)}, u32[]{:S(2)}) %collective-permute-start.23) | collective-permute-done | bytes 319520 | tf_op jit(solution)/shard_map/ppermute | solution.py:409
  197.4 6.5 %all-to-all-start = ((bf16[8,112,768]{2,1,0:T(8,128)(2,1)}), bf16[8,112,768]{2,1,0:T(8,128)(2,1)S(1)}, u32[]{:S(2)}, u32[]{:S(2)}) async-start(bf16[8,112,768]{2,1,0:T(8,128)(2,1)} %pad_maximum_fusion.1), calls=%async_computation | async-start | bytes 2752512 | tf_op jit(solution)/shard_map/all_to_all | solution.py:947
  205.4 31.1 %all-to-all-done.both_ref = bf16[8,112,768]{2,1,0:T(8,128)(2,1)S(1)} async-done(((bf16[8,112,768]{2,1,0:T(8,128)(2,1)}), bf16[8,112,768]{2,1,0:T(8,128)(2,1)S(1)}, u32[]{:S(2)}, u32[]{:S(2)}) %all-to-all-start) | async-done | bytes 1376288 | tf_op jit(solution)/shard_map/all_to_all | solution.py:947
  236.6 20.7 %collective-permute-done.26.rest_1_ = bf16[768,1536]{1,0:T(8,128)(2,1)} collective-permute-done((bf16[768,1536]{1,0:T(8,128)(2,1)}, bf16[768,1536]{1,0:T(8,128)(2,1)}, u32[]{:S(2)}, u32[]{:S(2)}) %collective-permute-start.26) | collective-permute-done | bytes 2359328 | tf_op jit(solution)/shard_map/ppermute | solution.py:409
  260.5 17.1 %shard_map.333 = (f32[448,768]{1,0:T(8,128)S(1)}, bf16[448,768]{1,0:T(8,128)(2,1)S(1)}, f32[448,768]{1,0:T(8,128)}, bf16[448,768]{1,0:T(8,128)(2,1)S(1)}, bf16[7...) custom-call(s32[1]{0:T(128)} %bitcast.26.number, ...), custom_call_target="tpu_custom_call" | custom-call | flops 1000 | bytes 1000 | tf_op jit(solution)/shard_map/pallas_call | solution.py:419
  284.3 2.2 shard_map.334
  290.1 5.7 %all-to-all-start.2 = ((bf16[8,112,768]{2,1,0:T(8,128)(2,1)}), bf16[8,112,768]{2,1,0:T(8,128)(2,1)S(1)}, u32[]{:S(2)}, u32[]{:S(2)}) async-start(bf16[8,112,768]{2,1,0:T(8,128)(2,1)} %copy-done.19), calls=%async_computation.2 | async-start | bytes 2752512 | tf_op jit(solution)/shard_map/all_to_all | solution.py:947
  299.4 29.9 %collective-permute-done.32.up1 = bf16[192,768]{1,0:T(8,128)(2,1)S(1)} collective-permute-done((bf16[192,768]{1,0:T(8,128)(2,1)}, bf16[192,768]{1,0:T(8,128)(2,1)S(1)}, u32[]{:S(2)}, u32[]{:S(2)}) %collective-permute-start.32) | collective-permute-done | bytes 294944 | tf_op jit(solution)/shard_map/ppermute | solution.py:409
  337.1 8.1 %collective-permute-done.36.far_ref = bf16[208,768]{1,0:T(8,128)(2,1)S(1)} collective-permute-done((bf16[208,768]{1,0:T(8,128)(2,1)S(1)}, bf16[208,768]{1,0:T(8,128)(2,1)S(1)}, u32[]{:S(2)}, u32[]{:S(2)}) %collective-permute-start.36) | collective-permute-done | bytes 319520 | tf_op jit(solution)/shard_map/ppermute | solution.py:409
  348.1 7.2 %collective-permute-done.37.g1 = bf16[208,768]{1,0:T(8,128)(2,1)S(1)} collective-permute-done((bf16[208,768]{1,0:T(8,128)(2,1)S(1)}, bf16[208,768]{1,0:T(8,128)(2,1)S(1)}, u32[]{:S(2)}, u32[]{:S(2)}) %collective-permute-start.37) | collective-permute-done | bytes 319520 | tf_op jit(solution)/shard_map/ppermute | solution.py:409
  358.0 9.9 %shard_map.338 = (bf16[384,768]{1,0:T(8,128)(2,1)S(1)}, bf16[384,768]{1,0:T(8,128)(2,1)S(1)}, f32[416,768]{1,0:T(8,128)S(1)}, bf16[416,768]{1,0:T(8,128)(2,1)S(1)}) custom-call(bf16[208,768]{1,0:T(8,128)(2,1)S(1)} %get-tuple-element.229.g0, bf16[208,768]{1,0:T(8,128)(2,1)S(1)} %collective-permute-done.37.g1, ...), custom_call_target="tpu_custom_call" | custom-call | flops 8000000000 | bytes 1000 | tf_op jit(solution)/shard_map/pallas_call | solution.py:419
  368.7 2.5 collective-permute-done.40.down1
  375.8 11.2 %collective-permute-done.54.got = bf16[384,768]{1,0:T(8,128)(2,1)S(1)} collective-permute-done((bf16[384,768]{1,0:T(8,128)(2,1)S(1)}, bf16[384,768]{1,0:T(8,128)(2,1)S(1)}, u32[]{:S(2)}, u32[]{:S(2)}) %collective-permute-start.54) | collective-permute-done | bytes 589856 | tf_op jit(solution)/shard_map/ppermute | solution.py:409
  389.3 5.9 %all-to-all-start.3 = ((bf16[8,96,1536]{2,1,0:T(8,128)(2,1)}), bf16[8,96,1536]{2,1,0:T(8,128)(2,1)}, u32[]{:S(2)}, u32[]{:S(2)}) async-start(bf16[8,96,1536]{2,1,0:T(8,128)(2,1)} %bitcast.64), calls=%async_computation.3 | async-start | bytes 4718592 | tf_op jit(solution)/shard_map/all_to_all | solution.py:1113
  401.6 7.4 %collective-permute-done.43.g1 = bf16[208,768]{1,0:T(8,128)(2,1)S(1)} collective-permute-done((bf16[208,768]{1,0:T(8,128)(2,1)S(1)}, bf16[208,768]{1,0:T(8,128)(2,1)S(1)}, u32[]{:S(2)}, u32[]{:S(2)}) %collective-permute-start.43) | collective-permute-done | bytes 319520 | tf_op jit(solution)/shard_map/ppermute | solution.py:409
  413.9 5.7 %shard_map.341 = (bf16[384,1536]{1,0:T(8,128)(2,1)S(1)}, bf16[384,1536]{1,0:T(8,128)(2,1)S(1)}, f32[416,768]{1,0:T(8,128)S(1)}, bf16[416,768]{1,0:T(8,128)(2,1)S(1)}) custom-call(bf16[208,768]{1,0:T(8,128)(2,1)S(1)} %get-tuple-element.239.g0, bf16[208,768]{1,0:T(8,128)(2,1)S(1)} %collective-permute-done.43.g1, ...), custom_call_target="tpu_custom_call" | custom-call | flops 1000 | bytes 1000 | tf_op jit(solution)/shard_map/pallas_call | solution.py:419
  425.4 7.6 %collective-permute-done.48.far_ref = bf16[208,768]{1,0:T(8,128)(2,1)S(1)} collective-permute-done((bf16[208,768]{1,0:T(8,128)(2,1)S(1)}, bf16[208,768]{1,0:T(8,128)(2,1)S(1)}, u32[]{:S(2)}, u32[]{:S(2)}) %collective-permute-start.48) | collective-permute-done | bytes 319520 | tf_op jit(solution)/shard_map/ppermute | solution.py:409
  435.1 7.0 %collective-permute-done.49.g1 = bf16[208,768]{1,0:T(8,128)(2,1)S(1)} collective-permute-done((bf16[208,768]{1,0:T(8,128)(2,1)S(1)}, bf16[208,768]{1,0:T(8,128)(2,1)S(1)}, u32[]{:S(2)}, u32[]{:S(2)}) %collective-permute-start.49) | collective-permute-done | bytes 319520 | tf_op jit(solution)/shard_map/ppermute | solution.py:409
  444.4 2.3 collective-permute-start.56
  446.7 9.0 %collective-permute-done.53.got = bf16[384,1536]{1,0:T(8,128)(2,1)S(1)} collective-permute-done((bf16[384,1536]{1,0:T(8,128)(2,1)S(1)}, bf16[384,1536]{1,0:T(8,128)(2,1)S(1)}, u32[]{:S(2)}, u32[]{:S(2)}) %collective-permute-start.53) | collective-permute-done | bytes 1179680 | tf_op jit(solution)/shard_map/ppermute | solution.py:409
  456.7 2.8 collective-permute-start.57
  461.1 10.1 %shard_map.347 = (bf16[384,768]{1,0:T(8,128)(2,1)S(1)}, bf16[384,768]{1,0:T(8,128)(2,1)S(1)}, f32[416,768]{1,0:T(8,128)S(1)}, bf16[416,768]{1,0:T(8,128)(2,1)S(1)}) custom-call(bf16[208,768]{1,0:T(8,128)(2,1)S(1)} %get-tuple-element.258.g0, bf16[208,768]{1,0:T(8,128)(2,1)S(1)} %collective-permute-done.49.g1, ...), custom_call_target="tpu_custom_call" | custom-call | flops 8000000000 | bytes 1000 | tf_op jit(solution)/shard_map/pallas_call | solution.py:419
  475.9 2.5 collective-permute-start.60
  481.9 2.5 collective-permute-start.62
  489.1 3.6 collective-permute-done.60.got
  494.2 4.3 convert_bitcast_fusion
  498.6 9.3 %collective-permute-done.63.r2 = bf16[96,1536]{1,0:T(8,128)(2,1)S(1)} collective-permute-done((bf16[96,1536]{1,0:T(8,128)(2,1)S(1)}, bf16[96,1536]{1,0:T(8,128)(2,1)S(1)}, u32[]{:S(2)}, u32[]{:S(2)}) %collective-permute-start.63) | collective-permute-done | bytes 294944 | tf_op jit(solution)/shard_map/ppermute | solution.py:409
  509.5 2.7 collective-permute-done.65
  512.4 3.8 collective-permute-done.66
  518.2 5.4 collective-permute-start.67
  (479 shorter events, 158.2 us)
Async XLA Ops:
  7.3 70.2 %all-gather.2.cloned.1.call-start = ((), (), s32[]{:S(2)}) async-start(), calls=%async_computation.4 | async-start | bytes 2211840 | tf_op jit(solution)/shard_map/all_gather | solution.py:891
  13.5 10.2 %collective-permute-start = (bf16[96,896]{1,0:T(8,128)(2,1)S(1)}, bf16[96,896]{1,0:T(8,128)(2,1)S(1)}, u32[]{:S(2)}, u32[]{:S(2)}) collective-permute-start(bf16[96,896]{1,0:T(8,128)(2,1)S(1)} %shard_map.314.refs_0_), channel_id=1, source_target_pairs={{0,8},{1,9},{2,10},{3,11},{4,12},{5,13},{6,14},{7,15},{8,0},{9,1},... | collective-permute-start | bytes 516104 | tf_op jit(solution)/shard_map/ppermute | solution.py:409
  16.6 20.5 %collective-permute-start.1 = (bf16[96,896]{1,0:T(8,128)(2,1)S(1)}, bf16[96,896]{1,0:T(8,128)(2,1)S(1)}, u32[]{:S(2)}, u32[]{:S(2)}) collective-permute-start(bf16[96,896]{1,0:T(8,128)(2,1)S(1)} %shard_map.314.refs_0_), channel_id=1, source_target_pairs={{0,16},{1,17},{2,18},{3,19},{4,20},{5,21},{6,22},{7,23},{8,24},{9,... | collective-permute-start | bytes 516104 | tf_op jit(solution)/shard_map/ppermute | solution.py:409
  19.2 18.0 %collective-permute-start.2 = (bf16[96,896]{1,0:T(8,128)(2,1)S(1)}, bf16[96,896]{1,0:T(8,128)(2,1)S(1)}, u32[]{:S(2)}, u32[]{:S(2)}) collective-permute-start(bf16[96,896]{1,0:T(8,128)(2,1)S(1)} %shard_map.314.refs_0_), channel_id=1, source_target_pairs={{0,24},{1,25},{2,26},{3,27},{4,28},{5,29},{6,30},{7,31},{8,16},{9,... | collective-permute-start | bytes 516104 | tf_op jit(solution)/shard_map/ppermute | solution.py:409
  37.2 14.6 %collective-permute-start.3 = (bf16[384,896]{1,0:T(8,128)(2,1)S(1)}, bf16[384,896]{1,0:T(8,128)(2,1)S(1)}, u32[]{:S(2)}, u32[]{:S(2)}) collective-permute-start(bf16[384,896]{1,0:T(8,128)(2,1)S(1)} %shard_map.315.refs_0_), channel_id=1, source_target_pairs={{0,4},{1,5},{2,6},{3,7},{4,0},{5,1},{6,2},{7,3},{8,12},{9,13},{10,... | collective-permute-start | bytes 2064392 | tf_op jit(solution)/shard_map/ppermute | solution.py:409
  67.7 9.8 %collective-permute-start.8 = (bf16[208,768]{1,0:T(8,128)(2,1)S(1)}, bf16[208,768]{1,0:T(8,128)(2,1)S(1)}, u32[]{:S(2)}, u32[]{:S(2)}) collective-permute-start(bf16[208,768]{1,0:T(8,128)(2,1)S(1)} %get-tuple-element.176), channel_id=1, source_target_pairs={{0,2},{1,3},{2,0},{3,1},{4,6},{5,7},{6,4},{7,5},{8,10},{9,11},{10,... | collective-permute-start | bytes 958472 | tf_op jit(solution)/shard_map/ppermute | solution.py:409
  80.7 40.2 %collective-permute-start.15 = (bf16[384,2304]{1,0:T(8,128)(2,1)S(1)}, bf16[384,2304]{1,0:T(8,128)(2,1)}, u32[]{:S(2)}, u32[]{:S(2)}) collective-permute-start(bf16[384,2304]{1,0:T(8,128)(2,1)S(1)} %shard_map.323.refs_0_), channel_id=1, source_target_pairs={{0,4},{1,5},{2,6},{3,7},{4,0},{5,1},{6,2},{7,3},{8,12},{9,13},{10,... | collective-permute-start | bytes 5308424 | tf_op jit(solution)/shard_map/ppermute | solution.py:409
  81.3 10.8 %collective-permute-start.12 = (bf16[208,768]{1,0:T(8,128)(2,1)}, bf16[208,768]{1,0:T(8,128)(2,1)}, u32[]{:S(2)}, u32[]{:S(2)}) collective-permute-start(bf16[208,768]{1,0:T(8,128)(2,1)} %get-tuple-element.181.p0), channel_id=1, source_target_pairs={{0,2},{1,3},{2,0},{3,1},{4,6},{5,7},{6,4},{7,5},{8,10},{9,11},{10,... | collective-permute-start | bytes 958472 | tf_op jit(solution)/shard_map/ppermute | solution.py:409
  82.8 14.3 %collective-permute-start.9 = (bf16[208,768]{1,0:T(8,128)(2,1)S(1)}, bf16[208,768]{1,0:T(8,128)(2,1)}, u32[]{:S(2)}, u32[]{:S(2)}) collective-permute-start(bf16[208,768]{1,0:T(8,128)(2,1)S(1)} %get-tuple-element.182.b0), channel_id=1, source_target_pairs={{0,2},{1,3},{2,0},{3,1},{4,6},{5,7},{6,4},{7,5},{8,10},{9,11},{10,... | collective-permute-start | bytes 958472 | tf_op jit(solution)/shard_map/ppermute | solution.py:409
  83.6 16.7 %collective-permute-start.13 = (bf16[208,768]{1,0:T(8,128)(2,1)}, bf16[208,768]{1,0:T(8,128)(2,1)S(1)}, u32[]{:S(2)}, u32[]{:S(2)}) collective-permute-start(bf16[208,768]{1,0:T(8,128)(2,1)} %get-tuple-element.181.p0), channel_id=1, source_target_pairs={{0,1},{1,0},{2,3},{3,2},{4,5},{5,4},{6,7},{7,6},{8,9},{9,8},{10,11... | collective-permute-start | bytes 958472 | tf_op jit(solution)/shard_map/ppermute | solution.py:409
  83.7 20.2 %collective-permute-start.10 = (bf16[208,768]{1,0:T(8,128)(2,1)S(1)}, bf16[208,768]{1,0:T(8,128)(2,1)S(1)}, u32[]{:S(2)}, u32[]{:S(2)}) collective-permute-start(bf16[208,768]{1,0:T(8,128)(2,1)S(1)} %get-tuple-element.182.b0), channel_id=1, source_target_pairs={{0,1},{1,0},{2,3},{3,2},{4,5},{5,4},{6,7},{7,6},{8,9},{9,8},{10,11... | collective-permute-start | bytes 958472 | tf_op jit(solution)/shard_map/ppermute | solution.py:409
  120.9 76.5 %all-to-all-start.1 = ((bf16[8,96,1536]{2,1,0:T(8,128)(2,1)}), bf16[8,96,1536]{2,1,0:T(8,128)(2,1)}, u32[]{:S(2)}, u32[]{:S(2)}) async-start(bf16[8,96,1536]{2,1,0:T(8,128)(2,1)} %pad_maximum_fusion), calls=%async_computation.1 | async-start | bytes 4718592 | tf_op jit(solution)/shard_map/all_to_all | solution.py:1015
  145.9 9.6 %collective-permute-start.17 = (bf16[208,768]{1,0:T(8,128)(2,1)S(1)}, bf16[208,768]{1,0:T(8,128)(2,1)S(1)}, u32[]{:S(2)}, u32[]{:S(2)}) collective-permute-start(bf16[208,768]{1,0:T(8,128)(2,1)S(1)} %get-tuple-element.190), channel_id=1, source_target_pairs={{0,2},{1,3},{2,0},{3,1},{4,6},{5,7},{6,4},{7,5},{8,10},{9,11},{10,... | collective-permute-start | bytes 958472 | tf_op jit(solution)/shard_map/ppermute | solution.py:409
  155.9 8.9 %collective-permute-start.18 = (bf16[208,768]{1,0:T(8,128)(2,1)S(1)}, bf16[208,768]{1,0:T(8,128)(2,1)S(1)}, u32[]{:S(2)}, u32[]{:S(2)}) collective-permute-start(bf16[208,768]{1,0:T(8,128)(2,1)S(1)} %get-tuple-element.192.a0), channel_id=1, source_target_pairs={{0,2},{1,3},{2,0},{3,1},{4,6},{5,7},{6,4},{7,5},{8,10},{9,11},{10,... | collective-permute-start | bytes 958472 | tf_op jit(solution)/shard_map/ppermute | solution.py:409
  173.4 9.6 %collective-permute-start.22 = (bf16[208,768]{1,0:T(8,128)(2,1)S(1)}, bf16[208,768]{1,0:T(8,128)(2,1)S(1)}, u32[]{:S(2)}, u32[]{:S(2)}) collective-permute-start(bf16[208,768]{1,0:T(8,128)(2,1)S(1)} %get-tuple-element.196), channel_id=1, source_target_pairs={{0,2},{1,3},{2,0},{3,1},{4,6},{5,7},{6,4},{7,5},{8,10},{9,11},{10,... | collective-permute-start | bytes 958472 | tf_op jit(solution)/shard_map/ppermute | solution.py:409
  184.2 8.7 %collective-permute-start.23 = (bf16[208,768]{1,0:T(8,128)(2,1)S(1)}, bf16[208,768]{1,0:T(8,128)(2,1)S(1)}, u32[]{:S(2)}, u32[]{:S(2)}) collective-permute-start(bf16[208,768]{1,0:T(8,128)(2,1)S(1)} %get-tuple-element.198.p0), channel_id=1, source_target_pairs={{0,2},{1,3},{2,0},{3,1},{4,6},{5,7},{6,4},{7,5},{8,10},{9,11},{10,... | collective-permute-start | bytes 958472 | tf_op jit(solution)/shard_map/ppermute | solution.py:409
  197.4 39.2 %all-to-all-start = ((bf16[8,112,768]{2,1,0:T(8,128)(2,1)}), bf16[8,112,768]{2,1,0:T(8,128)(2,1)S(1)}, u32[]{:S(2)}, u32[]{:S(2)}) async-start(bf16[8,112,768]{2,1,0:T(8,128)(2,1)} %pad_maximum_fusion.1), calls=%async_computation | async-start | bytes 2752512 | tf_op jit(solution)/shard_map/all_to_all | solution.py:947
  203.8 53.4 %collective-permute-start.26 = (bf16[768,1536]{1,0:T(8,128)(2,1)}, bf16[768,1536]{1,0:T(8,128)(2,1)}, u32[]{:S(2)}, u32[]{:S(2)}) collective-permute-start(bf16[768,1536]{1,0:T(8,128)(2,1)} %bitcast.29.rest_0_), channel_id=1, source_target_pairs={{0,2},{1,3},{2,0},{3,1},{4,6},{5,7},{6,4},{7,5},{8,10},{9,11},{10,... | collective-permute-start | bytes 7077896 | tf_op jit(solution)/shard_map/ppermute | solution.py:409
  280.4 9.0 %collective-permute-start.31 = (bf16[192,768]{1,0:T(8,128)(2,1)S(1)}, bf16[192,768]{1,0:T(8,128)(2,1)S(1)}, u32[]{:S(2)}, u32[]{:S(2)}) collective-permute-start(bf16[192,768]{1,0:T(8,128)(2,1)S(1)} %get-tuple-element.211), channel_id=1, source_target_pairs={{0,2},{1,3},{2,0},{3,1},{4,6},{5,7},{6,4},{7,5},{8,10},{9,11},{10,... | collective-permute-start | bytes 884744 | tf_op jit(solution)/shard_map/ppermute | solution.py:409
  290.1 41.6 %all-to-all-start.2 = ((bf16[8,112,768]{2,1,0:T(8,128)(2,1)}), bf16[8,112,768]{2,1,0:T(8,128)(2,1)S(1)}, u32[]{:S(2)}, u32[]{:S(2)}) async-start(bf16[8,112,768]{2,1,0:T(8,128)(2,1)} %copy-done.19), calls=%async_computation.2 | async-start | bytes 2752512 | tf_op jit(solution)/shard_map/all_to_all | solution.py:947
  295.9 34.2 %collective-permute-start.33 = (bf16[384,768]{1,0:T(8,128)(2,1)}, bf16[384,768]{1,0:T(8,128)(2,1)S(1)}, u32[]{:S(2)}, u32[]{:S(2)}) collective-permute-start(bf16[384,768]{1,0:T(8,128)(2,1)} %copy-done.117), channel_id=1, source_target_pairs={{0,2},{1,3},{2,0},{3,1},{4,6},{5,7},{6,4},{7,5},{8,10},{9,11},{10,... | collective-permute-start | bytes 1769480 | tf_op jit(solution)/shard_map/ppermute | solution.py:409
  297.4 33.5 %collective-permute-start.34 = (bf16[384,768]{1,0:T(8,128)(2,1)}, bf16[384,768]{1,0:T(8,128)(2,1)S(1)}, u32[]{:S(2)}, u32[]{:S(2)}) collective-permute-start(bf16[384,768]{1,0:T(8,128)(2,1)} %copy-done.116), channel_id=1, source_target_pairs={{0,2},{1,3},{2,0},{3,1},{4,6},{5,7},{6,4},{7,5},{8,10},{9,11},{10,... | collective-permute-start | bytes 1769480 | tf_op jit(solution)/shard_map/ppermute | solution.py:409
  297.9 31.4 %collective-permute-start.32 = (bf16[192,768]{1,0:T(8,128)(2,1)}, bf16[192,768]{1,0:T(8,128)(2,1)S(1)}, u32[]{:S(2)}, u32[]{:S(2)}) collective-permute-start(bf16[192,768]{1,0:T(8,128)(2,1)} %copy-done.122), channel_id=1, source_target_pairs={{0,2},{1,3},{2,0},{3,1},{4,6},{5,7},{6,4},{7,5},{8,10},{9,11},{10,... | collective-permute-start | bytes 884744 | tf_op jit(solution)/shard_map/ppermute | solution.py:409
  335.5 9.6 %collective-permute-start.36 = (bf16[208,768]{1,0:T(8,128)(2,1)S(1)}, bf16[208,768]{1,0:T(8,128)(2,1)S(1)}, u32[]{:S(2)}, u32[]{:S(2)}) collective-permute-start(bf16[208,768]{1,0:T(8,128)(2,1)S(1)} %get-tuple-element.227), channel_id=1, source_target_pairs={{0,2},{1,3},{2,0},{3,1},{4,6},{5,7},{6,4},{7,5},{8,10},{9,11},{10,... | collective-permute-start | bytes 958472 | tf_op jit(solution)/shard_map/ppermute | solution.py:409
  346.5 8.7 %collective-permute-start.37 = (bf16[208,768]{1,0:T(8,128)(2,1)S(1)}, bf16[208,768]{1,0:T(8,128)(2,1)S(1)}, u32[]{:S(2)}, u32[]{:S(2)}) collective-permute-start(bf16[208,768]{1,0:T(8,128)(2,1)S(1)} %get-tuple-element.229.g0), channel_id=1, source_target_pairs={{0,2},{1,3},{2,0},{3,1},{4,6},{5,7},{6,4},{7,5},{8,10},{9,11},{10,... | collective-permute-start | bytes 958472 | tf_op jit(solution)/shard_map/ppermute | solution.py:409
  348.1 8.8 %collective-permute-start.38 = (bf16[208,768]{1,0:T(8,128)(2,1)S(1)}, bf16[208,768]{1,0:T(8,128)(2,1)S(1)}, u32[]{:S(2)}, u32[]{:S(2)}) collective-permute-start(bf16[208,768]{1,0:T(8,128)(2,1)S(1)} %get-tuple-element.229.g0), channel_id=1, source_target_pairs={{0,1},{1,0},{2,3},{3,2},{4,5},{5,4},{6,7},{7,6},{8,9},{9,8},{10,11... | collective-permute-start | bytes 958472 | tf_op jit(solution)/shard_map/ppermute | solution.py:409
  355.3 16.0 %collective-permute-start.40 = (bf16[384,768]{1,0:T(8,128)(2,1)}, bf16[384,768]{1,0:T(8,128)(2,1)S(1)}, u32[]{:S(2)}, u32[]{:S(2)}) collective-permute-start(bf16[384,768]{1,0:T(8,128)(2,1)} %copy-done.114), channel_id=1, source_target_pairs={{0,2},{1,3},{2,0},{3,1},{4,6},{5,7},{6,4},{7,5},{8,10},{9,11},{10,... | collective-permute-start | bytes 1769480 | tf_op jit(solution)/shard_map/ppermute | solution.py:409
  371.3 15.7 %collective-permute-start.54 = (bf16[384,768]{1,0:T(8,128)(2,1)S(1)}, bf16[384,768]{1,0:T(8,128)(2,1)S(1)}, u32[]{:S(2)}, u32[]{:S(2)}) collective-permute-start(bf16[384,768]{1,0:T(8,128)(2,1)S(1)} %get-tuple-element.267), channel_id=1, source_target_pairs={{0,4},{1,5},{2,6},{3,7},{4,0},{5,1},{6,2},{7,3},{8,12},{9,13},{10,... | collective-permute-start | bytes 1769480 | tf_op jit(solution)/shard_map/ppermute | solution.py:409
  374.3 12.7 %collective-permute-start.42 = (bf16[208,768]{1,0:T(8,128)(2,1)S(1)}, bf16[208,768]{1,0:T(8,128)(2,1)S(1)}, u32[]{:S(2)}, u32[]{:S(2)}) collective-permute-start(bf16[208,768]{1,0:T(8,128)(2,1)S(1)} %get-tuple-element.238), channel_id=1, source_target_pairs={{0,2},{1,3},{2,0},{3,1},{4,6},{5,7},{6,4},{7,5},{8,10},{9,11},{10,... | collective-permute-start | bytes 958472 | tf_op jit(solution)/shard_map/ppermute | solution.py:409
  389.3 86.5 %all-to-all-start.3 = ((bf16[8,96,1536]{2,1,0:T(8,128)(2,1)}), bf16[8,96,1536]{2,1,0:T(8,128)(2,1)}, u32[]{:S(2)}, u32[]{:S(2)}) async-start(bf16[8,96,1536]{2,1,0:T(8,128)(2,1)} %bitcast.64), calls=%async_computation.3 | async-start | bytes 4718592 | tf_op jit(solution)/shard_map/all_to_all | solution.py:1113
  400.0 9.0 %collective-permute-start.43 = (bf16[208,768]{1,0:T(8,128)(2,1)S(1)}, bf16[208,768]{1,0:T(8,128)(2,1)S(1)}, u32[]{:S(2)}, u32[]{:S(2)}) collective-permute-start(bf16[208,768]{1,0:T(8,128)(2,1)S(1)} %get-tuple-element.239.g0), channel_id=1, source_target_pairs={{0,2},{1,3},{2,0},{3,1},{4,6},{5,7},{6,4},{7,5},{8,10},{9,11},{10,... | collective-permute-start | bytes 958472 | tf_op jit(solution)/shard_map/ppermute | solution.py:409
  421.7 34.0 %collective-permute-start.53 = (bf16[384,1536]{1,0:T(8,128)(2,1)S(1)}, bf16[384,1536]{1,0:T(8,128)(2,1)S(1)}, u32[]{:S(2)}, u32[]{:S(2)}) collective-permute-start(bf16[384,1536]{1,0:T(8,128)(2,1)S(1)} %get-tuple-element.257), channel_id=1, source_target_pairs={{0,4},{1,5},{2,6},{3,7},{4,0},{5,1},{6,2},{7,3},{8,12},{9,13},{10,... | collective-permute-start | bytes 3538952 | tf_op jit(solution)/shard_map/ppermute | solution.py:409
  423.6 9.4 %collective-permute-start.48 = (bf16[208,768]{1,0:T(8,128)(2,1)S(1)}, bf16[208,768]{1,0:T(8,128)(2,1)S(1)}, u32[]{:S(2)}, u32[]{:S(2)}) collective-permute-start(bf16[208,768]{1,0:T(8,128)(2,1)S(1)} %get-tuple-element.251), channel_id=1, source_target_pairs={{0,2},{1,3},{2,0},{3,1},{4,6},{5,7},{6,4},{7,5},{8,10},{9,11},{10,... | collective-permute-start | bytes 958472 | tf_op jit(solution)/shard_map/ppermute | solution.py:409
  433.5 8.6 %collective-permute-start.49 = (bf16[208,768]{1,0:T(8,128)(2,1)S(1)}, bf16[208,768]{1,0:T(8,128)(2,1)S(1)}, u32[]{:S(2)}, u32[]{:S(2)}) collective-permute-start(bf16[208,768]{1,0:T(8,128)(2,1)S(1)} %get-tuple-element.258.g0), channel_id=1, source_target_pairs={{0,2},{1,3},{2,0},{3,1},{4,6},{5,7},{6,4},{7,5},{8,10},{9,11},{10,... | collective-permute-start | bytes 958472 | tf_op jit(solution)/shard_map/ppermute | solution.py:409
  435.1 24.5 %collective-permute-start.50 = (bf16[208,768]{1,0:T(8,128)(2,1)S(1)}, bf16[208,768]{1,0:T(8,128)(2,1)S(1)}, u32[]{:S(2)}, u32[]{:S(2)}) collective-permute-start(bf16[208,768]{1,0:T(8,128)(2,1)S(1)} %get-tuple-element.258.g0), channel_id=1, source_target_pairs={{0,1},{1,0},{2,3},{3,2},{4,5},{5,4},{6,7},{7,6},{8,9},{9,8},{10,11... | collective-permute-start | bytes 958472 | tf_op jit(solution)/shard_map/ppermute | solution.py:409
  442.1 17.5 %collective-permute-start.51 = (bf16[208,768]{1,0:T(8,128)(2,1)S(1)}, bf16[208,768]{1,0:T(8,128)(2,1)S(1)}, u32[]{:S(2)}, u32[]{:S(2)}) collective-permute-start(bf16[208,768]{1,0:T(8,128)(2,1)S(1)} %collective-permute-done.49.g1), channel_id=1, source_target_pairs={{0,1},{1,0},{2,3},{3,2},{4,5},{5,4},{6,7},{7,6},{8,9},{9,8},{10,11... | collective-permute-start | bytes 958472 | tf_op jit(solution)/shard_map/ppermute | solution.py:409
  443.0 30.8 %collective-permute-start.55 = (bf16[96,768]{1,0:T(8,128)(2,1)S(1)}, bf16[96,768]{1,0:T(8,128)(2,1)S(1)}, u32[]{:S(2)}, u32[]{:S(2)}) collective-permute-start(bf16[96,768]{1,0:T(8,128)(2,1)S(1)} %get-tuple-element.271), channel_id=1, source_target_pairs={{0,8},{1,9},{2,10},{3,11},{4,12},{5,13},{6,14},{7,15},{8,0},{9,1},... | collective-permute-start | bytes 442376 | tf_op jit(solution)/shard_map/ppermute | solution.py:409
  444.4 30.0 %collective-permute-start.56 = (bf16[96,768]{1,0:T(8,128)(2,1)S(1)}, bf16[96,768]{1,0:T(8,128)(2,1)S(1)}, u32[]{:S(2)}, u32[]{:S(2)}) collective-permute-start(bf16[96,768]{1,0:T(8,128)(2,1)S(1)} %get-tuple-element.272), channel_id=1, source_target_pairs={{0,16},{1,17},{2,18},{3,19},{4,20},{5,21},{6,22},{7,23},{8,24},{9,... | collective-permute-start | bytes 442376 | tf_op jit(solution)/shard_map/ppermute | solution.py:409
  456.7 18.4 %collective-permute-start.57 = (bf16[96,768]{1,0:T(8,128)(2,1)S(1)}, bf16[96,768]{1,0:T(8,128)(2,1)S(1)}, u32[]{:S(2)}, u32[]{:S(2)}) collective-permute-start(bf16[96,768]{1,0:T(8,128)(2,1)S(1)} %get-tuple-element.273), channel_id=1, source_target_pairs={{0,24},{1,25},{2,26},{3,27},{4,28},{5,29},{6,30},{7,31},{8,16},{9,... | collective-permute-start | bytes 442376 | tf_op jit(solution)/shard_map/ppermute | solution.py:409
  459.6 16.2 %collective-permute-start.52 = (bf16[208,768]{1,0:T(8,128)(2,1)S(1)}, bf16[208,768]{1,0:T(8,128)(2,1)S(1)}, u32[]{:S(2)}, u32[]{:S(2)}) collective-permute-start(bf16[208,768]{1,0:T(8,128)(2,1)S(1)} %get-tuple-element.254), channel_id=1, source_target_pairs={{0,2},{1,3},{2,0},{3,1},{4,6},{5,7},{6,4},{7,5},{8,10},{9,11},{10,... | collective-permute-start | bytes 958472 | tf_op jit(solution)/shard_map/ppermute | solution.py:409
  475.9 16.9 %collective-permute-start.60 = (bf16[384,768]{1,0:T(8,128)(2,1)}, bf16[384,768]{1,0:T(8,128)(2,1)}, u32[]{:S(2)}, u32[]{:S(2)}) collective-permute-start(bf16[384,768]{1,0:T(8,128)(2,1)} %copy-done.115), channel_id=1, source_target_pairs={{0,4},{1,5},{2,6},{3,7},{4,0},{5,1},{6,2},{7,3},{8,12},{9,13},{10,... | collective-permute-start | bytes 1769480 | tf_op jit(solution)/shard_map/ppermute | solution.py:409
  480.1 12.6 %collective-permute-start.59 = (bf16[208,768]{1,0:T(8,128)(2,1)S(1)}, bf16[208,768]{1,0:T(8,128)(2,1)S(1)}, u32[]{:S(2)}, u32[]{:S(2)}) collective-permute-start(bf16[208,768]{1,0:T(8,128)(2,1)S(1)} %get-tuple-element.280), channel_id=1, source_target_pairs={{0,2},{1,3},{2,0},{3,1},{4,6},{5,7},{6,4},{7,5},{8,10},{9,11},{10,... | collective-permute-start | bytes 958472 | tf_op jit(solution)/shard_map/ppermute | solution.py:409
  481.9 16.6 %collective-permute-start.62 = (bf16[96,1536]{1,0:T(8,128)(2,1)S(1)}, bf16[96,1536]{1,0:T(8,128)(2,1)S(1)}, u32[]{:S(2)}, u32[]{:S(2)}) collective-permute-start(bf16[96,1536]{1,0:T(8,128)(2,1)S(1)} %get-tuple-element.291), channel_id=1, source_target_pairs={{0,8},{1,9},{2,10},{3,11},{4,12},{5,13},{6,14},{7,15},{8,0},{9,1},... | collective-permute-start | bytes 884744 | tf_op jit(solution)/shard_map/ppermute | solution.py:409
  484.4 23.5 %collective-permute-start.63 = (bf16[96,1536]{1,0:T(8,128)(2,1)S(1)}, bf16[96,1536]{1,0:T(8,128)(2,1)S(1)}, u32[]{:S(2)}, u32[]{:S(2)}) collective-permute-start(bf16[96,1536]{1,0:T(8,128)(2,1)S(1)} %get-tuple-element.292), channel_id=1, source_target_pairs={{0,16},{1,17},{2,18},{3,19},{4,20},{5,21},{6,22},{7,23},{8,24},{9,... | collective-permute-start | bytes 884744 | tf_op jit(solution)/shard_map/ppermute | solution.py:409
  485.9 22.0 %collective-permute-start.64 = (bf16[96,1536]{1,0:T(8,128)(2,1)S(1)}, bf16[96,1536]{1,0:T(8,128)(2,1)S(1)}, u32[]{:S(2)}, u32[]{:S(2)}) collective-permute-start(bf16[96,1536]{1,0:T(8,128)(2,1)S(1)} %get-tuple-element.293), channel_id=1, source_target_pairs={{0,24},{1,25},{2,26},{3,27},{4,28},{5,29},{6,30},{7,31},{8,16},{9,... | collective-permute-start | bytes 884744 | tf_op jit(solution)/shard_map/ppermute | solution.py:409
  518.2 18.8 %collective-permute-start.67 = (bf16[128,768]{1,0:T(8,128)(2,1)}, bf16[128,768]{1,0:T(8,128)(2,1)S(1)}, u32[]{:S(2)}, u32[]{:S(2)}) collective-permute-start(bf16[128,768]{1,0:T(8,128)(2,1)} %get-tuple-element.298), channel_id=1, source_target_pairs={{0,8},{1,9},{2,10},{3,11},{4,12},{5,13},{6,14},{7,15},{8,0},{9,1},... | collective-permute-start | bytes 589832 | tf_op jit(solution)/shard_map/ppermute | solution.py:409
  523.6 14.7 %collective-permute-start.68 = (bf16[128,768]{1,0:T(8,128)(2,1)}, bf16[128,768]{1,0:T(8,128)(2,1)}, u32[]{:S(2)}, u32[]{:S(2)}) collective-permute-start(bf16[128,768]{1,0:T(8,128)(2,1)} %get-tuple-element.299), channel_id=1, source_target_pairs={{0,16},{1,17},{2,18},{3,19},{4,20},{5,21},{6,22},{7,23},{8,24},{9,... | collective-permute-start | bytes 589832 | tf_op jit(solution)/shard_map/ppermute | solution.py:409
  525.0 13.3 %collective-permute-start.69 = (bf16[128,768]{1,0:T(8,128)(2,1)}, bf16[128,768]{1,0:T(8,128)(2,1)}, u32[]{:S(2)}, u32[]{:S(2)}) collective-permute-start(bf16[128,768]{1,0:T(8,128)(2,1)} %get-tuple-element.300), channel_id=1, source_target_pairs={{0,24},{1,25},{2,26},{3,27},{4,28},{5,29},{6,30},{7,31},{8,16},{9,... | collective-permute-start | bytes 589832 | tf_op jit(solution)/shard_map/ppermute | solution.py:409
  (164 other events, 1382.2 us)
Sparse Core Ops, SparseCore 0:
  12.3 50.9 all-gather.1

commit v10 on v9

--- a/solution.py
+++ b/solution.py
@@ -1136,7 +1136,7 @@
     low = spread(low)
     mixed_far = swap(hold(mixed_send, low), y=1)
     *first, own, sib = attend_back(
-        hold(low, mlp),
+        low,
         normed_one,
         mixed_one,
         att_one,

time: 559 us -> 548 us (0.980)
  waiting for transfers between devices: 270 us -> 263 us
    ppermute x70, waiting for transfers between devices: 239 us -> 232 us  [swap(): return lax.ppermute(values, AXES, pairs)]
    unnamed x284 -> x280, local copies, waits for them, and re-layouts: 56.4 us -> 55.3 us
  transfers between devices with their start and end apart: 75 -> 75, of which waited for: 42 -> 43; matrix products, arithmetic and copies ran while one was open for 3% -> 3% of each run, Pallas kernels for 11% -> 12%
where the time goes in v10:
time: 548 us; the launch traced here: 539 us
  waiting for transfers between devices  263 us (48%)
  starting transfers between devices  98.9 us (18%)
  Pallas kernels  89.4 us (16%)
  local copies, waits for them, and re-layouts  60.1 us (11%)
  between operations  16.5 us (3%)
  other arithmetic  10.3 us (2%)
    ppermute x70, waiting for transfers between devices, swap(): return lax.ppermute(values, AXES, pairs)  232 us
    pallas_call x46, Pallas kernels, run(): pl.pallas_call(kernel, out_shape=shapes, in_specs=[SM] * scalars + [VM] *...  89.4 us
    ppermute x70, starting transfers between devices, swap(): return lax.ppermute(values, AXES, pairs)  64.8 us
    unnamed x280, local copies, waits for them, and re-layouts  55.3 us
    all_to_all x2, waiting for transfers between devices, exchange(): return lax.all_to_all(both, 'dp', split_axis=0, concat_axis=0, tiled=True)  31.1 us
    all_to_all x1, starting transfers between devices, fast_local(): lax.all_to_all(e_pack, 'dp', split_axis=0, concat_axis=0, tiled=True)  16 us
    all_to_all x2, starting transfers between devices, exchange(): return lax.all_to_all(both, 'dp', split_axis=0, concat_axis=0, tiled=True)  12.2 us
  transfers between devices with their start and end apart: 75, of which 43 were waited for; matrix products, arithmetic and copies ran while one was open for 3% of the time, Pallas kernels for 12%

profile of v10, /device:TPU:0, one launch (start us, length us, event | category | flops | bytes accessed | tf_op | source)
XLA Modules:
  0.0 538.8 jit_solution(1565645732131532773)
XLA Ops:
  13.5 3.1 collective-permute-start
  16.6 2.6 collective-permute-start.1
  19.2 4.5 collective-permute-done.refs_1_
  23.7 13.5 %collective-permute-done.1.refs_2_ = bf16[96,896]{1,0:T(8,128)(2,1)S(1)} collective-permute-done((bf16[96,896]{1,0:T(8,128)(2,1)S(1)}, bf16[96,896]{1,0:T(8,128)(2,1)S(1)}, u32[]{:S(2)}, u32[]{:S(2)}) %collective-permute-start.1) | collective-permute-done | bytes 172064 | tf_op jit(solution)/shard_map/ppermute | solution.py:409
  45.3 4.8 collective-permute-done.4.refs_1_
  59.0 4.7 shard_map.318
  69.3 8.1 %collective-permute-done.8.far_ref = bf16[208,768]{1,0:T(8,128)(2,1)S(1)} collective-permute-done((bf16[208,768]{1,0:T(8,128)(2,1)S(1)}, bf16[208,768]{1,0:T(8,128)(2,1)S(1)}, u32[]{:S(2)}, u32[]{:S(2)}) %collective-permute-start.8) | collective-permute-done | bytes 319520 | tf_op jit(solution)/shard_map/ppermute | solution.py:409
  84.2 7.9 %collective-permute-done.12.p1 = bf16[208,768]{1,0:T(8,128)(2,1)} collective-permute-done((bf16[208,768]{1,0:T(8,128)(2,1)}, bf16[208,768]{1,0:T(8,128)(2,1)}, u32[]{:S(2)}, u32[]{:S(2)}) %collective-permute-start.12) | collective-permute-done | bytes 319520 | tf_op jit(solution)/shard_map/ppermute | solution.py:409
  92.1 5.0 collective-permute-done.9.b1
  97.2 3.2 pad_maximum_fusion
  100.4 2.6 shard_map.322
  105.4 15.5 %collective-permute-done.15.refs_1_ = bf16[384,2304]{1,0:T(8,128)(2,1)} collective-permute-done((bf16[384,2304]{1,0:T(8,128)(2,1)S(1)}, bf16[384,2304]{1,0:T(8,128)(2,1)}, u32[]{:S(2)}, u32[]{:S(2)}) %collective-permute-start.15) | collective-permute-done | bytes 1769504 | tf_op jit(solution)/shard_map/ppermute | solution.py:409
  120.9 16.0 %all-to-all-start.1 = ((bf16[8,96,1536]{2,1,0:T(8,128)(2,1)}), bf16[8,96,1536]{2,1,0:T(8,128)(2,1)}, u32[]{:S(2)}, u32[]{:S(2)}) async-start(bf16[8,96,1536]{2,1,0:T(8,128)(2,1)} %pad_maximum_fusion), calls=%async_computation.1 | async-start | bytes 4718592 | tf_op jit(solution)/shard_map/all_to_all | solution.py:1015
  138.7 4.0 shard_map.325
  143.8 2.1 collective-permute-done.16.far_ref
  147.5 8.1 %collective-permute-done.17.far_ref = bf16[208,768]{1,0:T(8,128)(2,1)S(1)} collective-permute-done((bf16[208,768]{1,0:T(8,128)(2,1)S(1)}, bf16[208,768]{1,0:T(8,128)(2,1)S(1)}, u32[]{:S(2)}, u32[]{:S(2)}) %collective-permute-start.17) | collective-permute-done | bytes 319520 | tf_op jit(solution)/shard_map/ppermute | solution.py:409
  157.5 7.3 %collective-permute-done.18.a1 = bf16[208,768]{1,0:T(8,128)(2,1)S(1)} collective-permute-done((bf16[208,768]{1,0:T(8,128)(2,1)S(1)}, bf16[208,768]{1,0:T(8,128)(2,1)S(1)}, u32[]{:S(2)}, u32[]{:S(2)}) %collective-permute-start.18) | collective-permute-done | bytes 319520 | tf_op jit(solution)/shard_map/ppermute | solution.py:409
  166.4 4.6 shard_map.328
  175.0 8.1 %collective-permute-done.22.far_ref = bf16[208,768]{1,0:T(8,128)(2,1)S(1)} collective-permute-done((bf16[208,768]{1,0:T(8,128)(2,1)S(1)}, bf16[208,768]{1,0:T(8,128)(2,1)S(1)}, u32[]{:S(2)}, u32[]{:S(2)}) %collective-permute-start.22) | collective-permute-done | bytes 319520 | tf_op jit(solution)/shard_map/ppermute | solution.py:409
  185.7 7.2 %collective-permute-done.23.p1 = bf16[208,768]{1,0:T(8,128)(2,1)S(1)} collective-permute-done((bf16[208,768]{1,0:T(8,128)(2,1)S(1)}, bf16[208,768]{1,0:T(8,128)(2,1)S(1)}, u32[]{:S(2)}, u32[]{:S(2)}) %collective-permute-start.23) | collective-permute-done | bytes 319520 | tf_op jit(solution)/shard_map/ppermute | solution.py:409
  197.4 6.5 %all-to-all-start = ((bf16[8,112,768]{2,1,0:T(8,128)(2,1)}), bf16[8,112,768]{2,1,0:T(8,128)(2,1)S(1)}, u32[]{:S(2)}, u32[]{:S(2)}) async-start(bf16[8,112,768]{2,1,0:T(8,128)(2,1)} %pad_maximum_fusion.1), calls=%async_computation | async-start | bytes 2752512 | tf_op jit(solution)/shard_map/all_to_all | solution.py:947
  205.4 31.1 %all-to-all-done.both_ref = bf16[8,112,768]{2,1,0:T(8,128)(2,1)S(1)} async-done(((bf16[8,112,768]{2,1,0:T(8,128)(2,1)}), bf16[8,112,768]{2,1,0:T(8,128)(2,1)S(1)}, u32[]{:S(2)}, u32[]{:S(2)}) %all-to-all-start) | async-done | bytes 1376288 | tf_op jit(solution)/shard_map/all_to_all | solution.py:947
  236.6 20.7 %collective-permute-done.26.rest_1_ = bf16[768,1536]{1,0:T(8,128)(2,1)} collective-permute-done((bf16[768,1536]{1,0:T(8,128)(2,1)}, bf16[768,1536]{1,0:T(8,128)(2,1)}, u32[]{:S(2)}, u32[]{:S(2)}) %collective-permute-start.26) | collective-permute-done | bytes 2359328 | tf_op jit(solution)/shard_map/ppermute | solution.py:409
  260.5 17.1 %shard_map.333 = (f32[448,768]{1,0:T(8,128)S(1)}, bf16[448,768]{1,0:T(8,128)(2,1)S(1)}, f32[448,768]{1,0:T(8,128)}, bf16[448,768]{1,0:T(8,128)(2,1)S(1)}, bf16[7...) custom-call(s32[1]{0:T(128)} %bitcast.26.number, ...), custom_call_target="tpu_custom_call" | custom-call | flops 1000 | bytes 1000 | tf_op jit(solution)/shard_map/pallas_call | solution.py:419
  284.3 2.2 shard_map.334
  290.1 5.7 %all-to-all-start.2 = ((bf16[8,112,768]{2,1,0:T(8,128)(2,1)}), bf16[8,112,768]{2,1,0:T(8,128)(2,1)S(1)}, u32[]{:S(2)}, u32[]{:S(2)}) async-start(bf16[8,112,768]{2,1,0:T(8,128)(2,1)} %copy-done.19), calls=%async_computation.2 | async-start | bytes 2752512 | tf_op jit(solution)/shard_map/all_to_all | solution.py:947
  299.4 29.9 %collective-permute-done.32.up1 = bf16[192,768]{1,0:T(8,128)(2,1)S(1)} collective-permute-done((bf16[192,768]{1,0:T(8,128)(2,1)}, bf16[192,768]{1,0:T(8,128)(2,1)S(1)}, u32[]{:S(2)}, u32[]{:S(2)}) %collective-permute-start.32) | collective-permute-done | bytes 294944 | tf_op jit(solution)/shard_map/ppermute | solution.py:409
  333.3 2.1 collective-permute-done.35.far_ref
  337.1 8.1 %collective-permute-done.36.far_ref = bf16[208,768]{1,0:T(8,128)(2,1)S(1)} collective-permute-done((bf16[208,768]{1,0:T(8,128)(2,1)S(1)}, bf16[208,768]{1,0:T(8,128)(2,1)S(1)}, u32[]{:S(2)}, u32[]{:S(2)}) %collective-permute-start.36) | collective-permute-done | bytes 319520 | tf_op jit(solution)/shard_map/ppermute | solution.py:409
  348.1 7.2 %collective-permute-done.37.g1 = bf16[208,768]{1,0:T(8,128)(2,1)S(1)} collective-permute-done((bf16[208,768]{1,0:T(8,128)(2,1)S(1)}, bf16[208,768]{1,0:T(8,128)(2,1)S(1)}, u32[]{:S(2)}, u32[]{:S(2)}) %collective-permute-start.37) | collective-permute-done | bytes 319520 | tf_op jit(solution)/shard_map/ppermute | solution.py:409
  358.0 9.9 %shard_map.338 = (bf16[384,768]{1,0:T(8,128)(2,1)S(1)}, bf16[384,768]{1,0:T(8,128)(2,1)S(1)}, f32[416,768]{1,0:T(8,128)S(1)}, bf16[416,768]{1,0:T(8,128)(2,1)S(1)}) custom-call(bf16[208,768]{1,0:T(8,128)(2,1)S(1)} %get-tuple-element.225.g0, bf16[208,768]{1,0:T(8,128)(2,1)S(1)} %collective-permute-done.37.g1, ...), custom_call_target="tpu_custom_call" | custom-call | flops 8000000000 | bytes 1000 | tf_op jit(solution)/shard_map/pallas_call | solution.py:419
  368.7 2.5 collective-permute-done.40.down1
  375.8 11.2 %collective-permute-done.53.got = bf16[384,768]{1,0:T(8,128)(2,1)S(1)} collective-permute-done((bf16[384,768]{1,0:T(8,128)(2,1)S(1)}, bf16[384,768]{1,0:T(8,128)(2,1)S(1)}, u32[]{:S(2)}, u32[]{:S(2)}) %collective-permute-start.53) | collective-permute-done | bytes 589856 | tf_op jit(solution)/shard_map/ppermute | solution.py:409
  389.3 5.9 %all-to-all-start.3 = ((bf16[8,96,1536]{2,1,0:T(8,128)(2,1)}), bf16[8,96,1536]{2,1,0:T(8,128)(2,1)}, u32[]{:S(2)}, u32[]{:S(2)}) async-start(bf16[8,96,1536]{2,1,0:T(8,128)(2,1)} %bitcast.64), calls=%async_computation.3 | async-start | bytes 4718592 | tf_op jit(solution)/shard_map/all_to_all | solution.py:1113
  401.6 7.4 %collective-permute-done.43.g1 = bf16[208,768]{1,0:T(8,128)(2,1)S(1)} collective-permute-done((bf16[208,768]{1,0:T(8,128)(2,1)S(1)}, bf16[208,768]{1,0:T(8,128)(2,1)S(1)}, u32[]{:S(2)}, u32[]{:S(2)}) %collective-permute-start.43) | collective-permute-done | bytes 319520 | tf_op jit(solution)/shard_map/ppermute | solution.py:409
  410.6 2.0 copy-done.2
  413.9 6.7 %shard_map.341 = (bf16[384,1536]{1,0:T(8,128)(2,1)S(1)}, bf16[384,1536]{1,0:T(8,128)(2,1)}, f32[416,768]{1,0:T(8,128)S(1)}, bf16[416,768]{1,0:T(8,128)(2,1)S(1)}) custom-call(bf16[208,768]{1,0:T(8,128)(2,1)S(1)} %get-tuple-element.235.g0, bf16[208,768]{1,0:T(8,128)(2,1)S(1)} %collective-permute-done.43.g1, bf16[208,768]{1,0:T(8,128)(2,1)S(1)} %collective-permute-done.44.g2, ...), custom_call_target="tpu_custom_call" | custom-call | flops 1000 | bytes 1000 | tf_op jit(solution)/shard_map/pallas_call | solution.py:419
  424.6 7.8 %collective-permute-done.48.far_ref = bf16[208,768]{1,0:T(8,128)(2,1)S(1)} collective-permute-done((bf16[208,768]{1,0:T(8,128)(2,1)S(1)}, bf16[208,768]{1,0:T(8,128)(2,1)S(1)}, u32[]{:S(2)}, u32[]{:S(2)}) %collective-permute-start.48) | collective-permute-done | bytes 319520 | tf_op jit(solution)/shard_map/ppermute | solution.py:409
  434.6 7.3 %collective-permute-done.49.g1 = bf16[208,768]{1,0:T(8,128)(2,1)S(1)} collective-permute-done((bf16[208,768]{1,0:T(8,128)(2,1)S(1)}, bf16[208,768]{1,0:T(8,128)(2,1)S(1)}, u32[]{:S(2)}, u32[]{:S(2)}) %collective-permute-start.49) | collective-permute-done | bytes 319520 | tf_op jit(solution)/shard_map/ppermute | solution.py:409
  446.0 2.3 collective-permute-start.55
  450.4 10.1 %shard_map.347 = (bf16[384,768]{1,0:T(8,128)(2,1)S(1)}, bf16[384,768]{1,0:T(8,128)(2,1)S(1)}, f32[416,768]{1,0:T(8,128)S(1)}, bf16[416,768]{1,0:T(8,128)(2,1)S(1)}) custom-call(bf16[208,768]{1,0:T(8,128)(2,1)S(1)} %get-tuple-element.249.g0, bf16[208,768]{1,0:T(8,128)(2,1)S(1)} %collective-permute-done.49.g1, ...), custom_call_target="tpu_custom_call" | custom-call | flops 8000000000 | bytes 1000 | tf_op jit(solution)/shard_map/pallas_call | solution.py:419
  474.3 2.3 collective-permute-start.63
  478.8 4.5 collective-permute-done.59.got
  484.7 4.3 convert_bitcast_fusion
  489.1 8.7 %collective-permute-done.63.r2 = bf16[96,1536]{1,0:T(8,128)(2,1)S(1)} collective-permute-done((bf16[96,1536]{1,0:T(8,128)(2,1)S(1)}, bf16[96,1536]{1,0:T(8,128)(2,1)S(1)}, u32[]{:S(2)}, u32[]{:S(2)}) %collective-permute-start.63) | collective-permute-done | bytes 294944 | tf_op jit(solution)/shard_map/ppermute | solution.py:409
  499.4 2.7 collective-permute-done.65
  503.7 2.5 collective-permute-done.66
  508.1 4.9 collective-permute-start.67
  (475 shorter events, 156.0 us)
Async XLA Ops:
  7.3 70.2 %all-gather.2.cloned.1.call-start = ((), (), s32[]{:S(2)}) async-start(), calls=%async_computation.4 | async-start | bytes 2211840 | tf_op jit(solution)/shard_map/all_gather | solution.py:891
  13.5 10.2 %collective-permute-start = (bf16[96,896]{1,0:T(8,128)(2,1)S(1)}, bf16[96,896]{1,0:T(8,128)(2,1)S(1)}, u32[]{:S(2)}, u32[]{:S(2)}) collective-permute-start(bf16[96,896]{1,0:T(8,128)(2,1)S(1)} %shard_map.314.refs_0_), channel_id=1, source_target_pairs={{0,8},{1,9},{2,10},{3,11},{4,12},{5,13},{6,14},{7,15},{8,0},{9,1},... | collective-permute-start | bytes 516104 | tf_op jit(solution)/shard_map/ppermute | solution.py:409
  16.6 20.5 %collective-permute-start.1 = (bf16[96,896]{1,0:T(8,128)(2,1)S(1)}, bf16[96,896]{1,0:T(8,128)(2,1)S(1)}, u32[]{:S(2)}, u32[]{:S(2)}) collective-permute-start(bf16[96,896]{1,0:T(8,128)(2,1)S(1)} %shard_map.314.refs_0_), channel_id=1, source_target_pairs={{0,16},{1,17},{2,18},{3,19},{4,20},{5,21},{6,22},{7,23},{8,24},{9,... | collective-permute-start | bytes 516104 | tf_op jit(solution)/shard_map/ppermute | solution.py:409
  19.2 18.0 %collective-permute-start.2 = (bf16[96,896]{1,0:T(8,128)(2,1)S(1)}, bf16[96,896]{1,0:T(8,128)(2,1)S(1)}, u32[]{:S(2)}, u32[]{:S(2)}) collective-permute-start(bf16[96,896]{1,0:T(8,128)(2,1)S(1)} %shard_map.314.refs_0_), channel_id=1, source_target_pairs={{0,24},{1,25},{2,26},{3,27},{4,28},{5,29},{6,30},{7,31},{8,16},{9,... | collective-permute-start | bytes 516104 | tf_op jit(solution)/shard_map/ppermute | solution.py:409
  37.2 14.5 %collective-permute-start.3 = (bf16[384,896]{1,0:T(8,128)(2,1)S(1)}, bf16[384,896]{1,0:T(8,128)(2,1)S(1)}, u32[]{:S(2)}, u32[]{:S(2)}) collective-permute-start(bf16[384,896]{1,0:T(8,128)(2,1)S(1)} %shard_map.315.refs_0_), channel_id=1, source_target_pairs={{0,4},{1,5},{2,6},{3,7},{4,0},{5,1},{6,2},{7,3},{8,12},{9,13},{10,... | collective-permute-start | bytes 2064392 | tf_op jit(solution)/shard_map/ppermute | solution.py:409
  67.7 9.8 %collective-permute-start.8 = (bf16[208,768]{1,0:T(8,128)(2,1)S(1)}, bf16[208,768]{1,0:T(8,128)(2,1)S(1)}, u32[]{:S(2)}, u32[]{:S(2)}) collective-permute-start(bf16[208,768]{1,0:T(8,128)(2,1)S(1)} %get-tuple-element.172), channel_id=1, source_target_pairs={{0,2},{1,3},{2,0},{3,1},{4,6},{5,7},{6,4},{7,5},{8,10},{9,11},{10,... | collective-permute-start | bytes 958472 | tf_op jit(solution)/shard_map/ppermute | solution.py:409
  80.7 40.2 %collective-permute-start.15 = (bf16[384,2304]{1,0:T(8,128)(2,1)S(1)}, bf16[384,2304]{1,0:T(8,128)(2,1)}, u32[]{:S(2)}, u32[]{:S(2)}) collective-permute-start(bf16[384,2304]{1,0:T(8,128)(2,1)S(1)} %shard_map.323.refs_0_), channel_id=1, source_target_pairs={{0,4},{1,5},{2,6},{3,7},{4,0},{5,1},{6,2},{7,3},{8,12},{9,13},{10,... | collective-permute-start | bytes 5308424 | tf_op jit(solution)/shard_map/ppermute | solution.py:409
  81.3 10.8 %collective-permute-start.12 = (bf16[208,768]{1,0:T(8,128)(2,1)}, bf16[208,768]{1,0:T(8,128)(2,1)}, u32[]{:S(2)}, u32[]{:S(2)}) collective-permute-start(bf16[208,768]{1,0:T(8,128)(2,1)} %get-tuple-element.177.p0), channel_id=1, source_target_pairs={{0,2},{1,3},{2,0},{3,1},{4,6},{5,7},{6,4},{7,5},{8,10},{9,11},{10,... | collective-permute-start | bytes 958472 | tf_op jit(solution)/shard_map/ppermute | solution.py:409
  82.8 14.3 %collective-permute-start.9 = (bf16[208,768]{1,0:T(8,128)(2,1)S(1)}, bf16[208,768]{1,0:T(8,128)(2,1)}, u32[]{:S(2)}, u32[]{:S(2)}) collective-permute-start(bf16[208,768]{1,0:T(8,128)(2,1)S(1)} %get-tuple-element.178.b0), channel_id=1, source_target_pairs={{0,2},{1,3},{2,0},{3,1},{4,6},{5,7},{6,4},{7,5},{8,10},{9,11},{10,... | collective-permute-start | bytes 958472 | tf_op jit(solution)/shard_map/ppermute | solution.py:409
  83.6 16.7 %collective-permute-start.13 = (bf16[208,768]{1,0:T(8,128)(2,1)}, bf16[208,768]{1,0:T(8,128)(2,1)S(1)}, u32[]{:S(2)}, u32[]{:S(2)}) collective-permute-start(bf16[208,768]{1,0:T(8,128)(2,1)} %get-tuple-element.177.p0), channel_id=1, source_target_pairs={{0,1},{1,0},{2,3},{3,2},{4,5},{5,4},{6,7},{7,6},{8,9},{9,8},{10,11... | collective-permute-start | bytes 958472 | tf_op jit(solution)/shard_map/ppermute | solution.py:409
  83.7 20.2 %collective-permute-start.10 = (bf16[208,768]{1,0:T(8,128)(2,1)S(1)}, bf16[208,768]{1,0:T(8,128)(2,1)S(1)}, u32[]{:S(2)}, u32[]{:S(2)}) collective-permute-start(bf16[208,768]{1,0:T(8,128)(2,1)S(1)} %get-tuple-element.178.b0), channel_id=1, source_target_pairs={{0,1},{1,0},{2,3},{3,2},{4,5},{5,4},{6,7},{7,6},{8,9},{9,8},{10,11... | collective-permute-start | bytes 958472 | tf_op jit(solution)/shard_map/ppermute | solution.py:409
  92.1 8.3 %collective-permute-start.14 = (bf16[208,768]{1,0:T(8,128)(2,1)}, bf16[208,768]{1,0:T(8,128)(2,1)S(1)}, u32[]{:S(2)}, u32[]{:S(2)}) collective-permute-start(bf16[208,768]{1,0:T(8,128)(2,1)} %collective-permute-done.12.p1), channel_id=1, source_target_pairs={{0,1},{1,0},{2,3},{3,2},{4,5},{5,4},{6,7},{7,6},{8,9},{9,8},{10,11... | collective-permute-start | bytes 958472 | tf_op jit(solution)/shard_map/ppermute | solution.py:409
  120.9 76.5 %all-to-all-start.1 = ((bf16[8,96,1536]{2,1,0:T(8,128)(2,1)}), bf16[8,96,1536]{2,1,0:T(8,128)(2,1)}, u32[]{:S(2)}, u32[]{:S(2)}) async-start(bf16[8,96,1536]{2,1,0:T(8,128)(2,1)} %pad_maximum_fusion), calls=%async_computation.1 | async-start | bytes 4718592 | tf_op jit(solution)/shard_map/all_to_all | solution.py:1015
  145.9 9.6 %collective-permute-start.17 = (bf16[208,768]{1,0:T(8,128)(2,1)S(1)}, bf16[208,768]{1,0:T(8,128)(2,1)S(1)}, u32[]{:S(2)}, u32[]{:S(2)}) collective-permute-start(bf16[208,768]{1,0:T(8,128)(2,1)S(1)} %get-tuple-element.186), channel_id=1, source_target_pairs={{0,2},{1,3},{2,0},{3,1},{4,6},{5,7},{6,4},{7,5},{8,10},{9,11},{10,... | collective-permute-start | bytes 958472 | tf_op jit(solution)/shard_map/ppermute | solution.py:409
  155.9 8.9 %collective-permute-start.18 = (bf16[208,768]{1,0:T(8,128)(2,1)S(1)}, bf16[208,768]{1,0:T(8,128)(2,1)S(1)}, u32[]{:S(2)}, u32[]{:S(2)}) collective-permute-start(bf16[208,768]{1,0:T(8,128)(2,1)S(1)} %get-tuple-element.188.a0), channel_id=1, source_target_pairs={{0,2},{1,3},{2,0},{3,1},{4,6},{5,7},{6,4},{7,5},{8,10},{9,11},{10,... | collective-permute-start | bytes 958472 | tf_op jit(solution)/shard_map/ppermute | solution.py:409
  173.4 9.6 %collective-permute-start.22 = (bf16[208,768]{1,0:T(8,128)(2,1)S(1)}, bf16[208,768]{1,0:T(8,128)(2,1)S(1)}, u32[]{:S(2)}, u32[]{:S(2)}) collective-permute-start(bf16[208,768]{1,0:T(8,128)(2,1)S(1)} %get-tuple-element.192), channel_id=1, source_target_pairs={{0,2},{1,3},{2,0},{3,1},{4,6},{5,7},{6,4},{7,5},{8,10},{9,11},{10,... | collective-permute-start | bytes 958472 | tf_op jit(solution)/shard_map/ppermute | solution.py:409
  184.2 8.7 %collective-permute-start.23 = (bf16[208,768]{1,0:T(8,128)(2,1)S(1)}, bf16[208,768]{1,0:T(8,128)(2,1)S(1)}, u32[]{:S(2)}, u32[]{:S(2)}) collective-permute-start(bf16[208,768]{1,0:T(8,128)(2,1)S(1)} %get-tuple-element.194.p0), channel_id=1, source_target_pairs={{0,2},{1,3},{2,0},{3,1},{4,6},{5,7},{6,4},{7,5},{8,10},{9,11},{10,... | collective-permute-start | bytes 958472 | tf_op jit(solution)/shard_map/ppermute | solution.py:409
  197.4 39.2 %all-to-all-start = ((bf16[8,112,768]{2,1,0:T(8,128)(2,1)}), bf16[8,112,768]{2,1,0:T(8,128)(2,1)S(1)}, u32[]{:S(2)}, u32[]{:S(2)}) async-start(bf16[8,112,768]{2,1,0:T(8,128)(2,1)} %pad_maximum_fusion.1), calls=%async_computation | async-start | bytes 2752512 | tf_op jit(solution)/shard_map/all_to_all | solution.py:947
  203.9 53.4 %collective-permute-start.26 = (bf16[768,1536]{1,0:T(8,128)(2,1)}, bf16[768,1536]{1,0:T(8,128)(2,1)}, u32[]{:S(2)}, u32[]{:S(2)}) collective-permute-start(bf16[768,1536]{1,0:T(8,128)(2,1)} %bitcast.29.rest_0_), channel_id=1, source_target_pairs={{0,2},{1,3},{2,0},{3,1},{4,6},{5,7},{6,4},{7,5},{8,10},{9,11},{10,... | collective-permute-start | bytes 7077896 | tf_op jit(solution)/shard_map/ppermute | solution.py:409
  280.4 9.1 %collective-permute-start.31 = (bf16[192,768]{1,0:T(8,128)(2,1)S(1)}, bf16[192,768]{1,0:T(8,128)(2,1)S(1)}, u32[]{:S(2)}, u32[]{:S(2)}) collective-permute-start(bf16[192,768]{1,0:T(8,128)(2,1)S(1)} %get-tuple-element.207), channel_id=1, source_target_pairs={{0,2},{1,3},{2,0},{3,1},{4,6},{5,7},{6,4},{7,5},{8,10},{9,11},{10,... | collective-permute-start | bytes 884744 | tf_op jit(solution)/shard_map/ppermute | solution.py:409
  290.1 41.6 %all-to-all-start.2 = ((bf16[8,112,768]{2,1,0:T(8,128)(2,1)}), bf16[8,112,768]{2,1,0:T(8,128)(2,1)S(1)}, u32[]{:S(2)}, u32[]{:S(2)}) async-start(bf16[8,112,768]{2,1,0:T(8,128)(2,1)} %copy-done.19), calls=%async_computation.2 | async-start | bytes 2752512 | tf_op jit(solution)/shard_map/all_to_all | solution.py:947
  295.8 34.1 %collective-permute-start.33 = (bf16[384,768]{1,0:T(8,128)(2,1)}, bf16[384,768]{1,0:T(8,128)(2,1)S(1)}, u32[]{:S(2)}, u32[]{:S(2)}) collective-permute-start(bf16[384,768]{1,0:T(8,128)(2,1)} %copy-done.115), channel_id=1, source_target_pairs={{0,2},{1,3},{2,0},{3,1},{4,6},{5,7},{6,4},{7,5},{8,10},{9,11},{10,... | collective-permute-start | bytes 1769480 | tf_op jit(solution)/shard_map/ppermute | solution.py:409
  297.4 33.5 %collective-permute-start.34 = (bf16[384,768]{1,0:T(8,128)(2,1)}, bf16[384,768]{1,0:T(8,128)(2,1)S(1)}, u32[]{:S(2)}, u32[]{:S(2)}) collective-permute-start(bf16[384,768]{1,0:T(8,128)(2,1)} %copy-done.114), channel_id=1, source_target_pairs={{0,2},{1,3},{2,0},{3,1},{4,6},{5,7},{6,4},{7,5},{8,10},{9,11},{10,... | collective-permute-start | bytes 1769480 | tf_op jit(solution)/shard_map/ppermute | solution.py:409
  297.9 31.4 %collective-permute-start.32 = (bf16[192,768]{1,0:T(8,128)(2,1)}, bf16[192,768]{1,0:T(8,128)(2,1)S(1)}, u32[]{:S(2)}, u32[]{:S(2)}) collective-permute-start(bf16[192,768]{1,0:T(8,128)(2,1)} %copy-done.120), channel_id=1, source_target_pairs={{0,2},{1,3},{2,0},{3,1},{4,6},{5,7},{6,4},{7,5},{8,10},{9,11},{10,... | collective-permute-start | bytes 884744 | tf_op jit(solution)/shard_map/ppermute | solution.py:409
  335.5 9.6 %collective-permute-start.36 = (bf16[208,768]{1,0:T(8,128)(2,1)S(1)}, bf16[208,768]{1,0:T(8,128)(2,1)S(1)}, u32[]{:S(2)}, u32[]{:S(2)}) collective-permute-start(bf16[208,768]{1,0:T(8,128)(2,1)S(1)} %get-tuple-element.223), channel_id=1, source_target_pairs={{0,2},{1,3},{2,0},{3,1},{4,6},{5,7},{6,4},{7,5},{8,10},{9,11},{10,... | collective-permute-start | bytes 958472 | tf_op jit(solution)/shard_map/ppermute | solution.py:409
  346.5 8.7 %collective-permute-start.37 = (bf16[208,768]{1,0:T(8,128)(2,1)S(1)}, bf16[208,768]{1,0:T(8,128)(2,1)S(1)}, u32[]{:S(2)}, u32[]{:S(2)}) collective-permute-start(bf16[208,768]{1,0:T(8,128)(2,1)S(1)} %get-tuple-element.225.g0), channel_id=1, source_target_pairs={{0,2},{1,3},{2,0},{3,1},{4,6},{5,7},{6,4},{7,5},{8,10},{9,11},{10,... | collective-permute-start | bytes 958472 | tf_op jit(solution)/shard_map/ppermute | solution.py:409
  348.1 8.8 %collective-permute-start.38 = (bf16[208,768]{1,0:T(8,128)(2,1)S(1)}, bf16[208,768]{1,0:T(8,128)(2,1)S(1)}, u32[]{:S(2)}, u32[]{:S(2)}) collective-permute-start(bf16[208,768]{1,0:T(8,128)(2,1)S(1)} %get-tuple-element.225.g0), channel_id=1, source_target_pairs={{0,1},{1,0},{2,3},{3,2},{4,5},{5,4},{6,7},{7,6},{8,9},{9,8},{10,11... | collective-permute-start | bytes 958472 | tf_op jit(solution)/shard_map/ppermute | solution.py:409
  355.3 16.0 %collective-permute-start.40 = (bf16[384,768]{1,0:T(8,128)(2,1)}, bf16[384,768]{1,0:T(8,128)(2,1)S(1)}, u32[]{:S(2)}, u32[]{:S(2)}) collective-permute-start(bf16[384,768]{1,0:T(8,128)(2,1)} %copy-done.112), channel_id=1, source_target_pairs={{0,2},{1,3},{2,0},{3,1},{4,6},{5,7},{6,4},{7,5},{8,10},{9,11},{10,... | collective-permute-start | bytes 1769480 | tf_op jit(solution)/shard_map/ppermute | solution.py:409
  371.3 15.7 %collective-permute-start.53 = (bf16[384,768]{1,0:T(8,128)(2,1)S(1)}, bf16[384,768]{1,0:T(8,128)(2,1)S(1)}, u32[]{:S(2)}, u32[]{:S(2)}) collective-permute-start(bf16[384,768]{1,0:T(8,128)(2,1)S(1)} %get-tuple-element.257), channel_id=1, source_target_pairs={{0,4},{1,5},{2,6},{3,7},{4,0},{5,1},{6,2},{7,3},{8,12},{9,13},{10,... | collective-permute-start | bytes 1769480 | tf_op jit(solution)/shard_map/ppermute | solution.py:409
  374.3 12.7 %collective-permute-start.42 = (bf16[208,768]{1,0:T(8,128)(2,1)S(1)}, bf16[208,768]{1,0:T(8,128)(2,1)S(1)}, u32[]{:S(2)}, u32[]{:S(2)}) collective-permute-start(bf16[208,768]{1,0:T(8,128)(2,1)S(1)} %get-tuple-element.234), channel_id=1, source_target_pairs={{0,2},{1,3},{2,0},{3,1},{4,6},{5,7},{6,4},{7,5},{8,10},{9,11},{10,... | collective-permute-start | bytes 958472 | tf_op jit(solution)/shard_map/ppermute | solution.py:409
  389.3 75.7 %all-to-all-start.3 = ((bf16[8,96,1536]{2,1,0:T(8,128)(2,1)}), bf16[8,96,1536]{2,1,0:T(8,128)(2,1)}, u32[]{:S(2)}, u32[]{:S(2)}) async-start(bf16[8,96,1536]{2,1,0:T(8,128)(2,1)} %bitcast.64), calls=%async_computation.3 | async-start | bytes 4718592 | tf_op jit(solution)/shard_map/all_to_all | solution.py:1113
  400.0 9.0 %collective-permute-start.43 = (bf16[208,768]{1,0:T(8,128)(2,1)S(1)}, bf16[208,768]{1,0:T(8,128)(2,1)S(1)}, u32[]{:S(2)}, u32[]{:S(2)}) collective-permute-start(bf16[208,768]{1,0:T(8,128)(2,1)S(1)} %get-tuple-element.235.g0), channel_id=1, source_target_pairs={{0,2},{1,3},{2,0},{3,1},{4,6},{5,7},{6,4},{7,5},{8,10},{9,11},{10,... | collective-permute-start | bytes 958472 | tf_op jit(solution)/shard_map/ppermute | solution.py:409
  422.8 9.6 %collective-permute-start.48 = (bf16[208,768]{1,0:T(8,128)(2,1)S(1)}, bf16[208,768]{1,0:T(8,128)(2,1)S(1)}, u32[]{:S(2)}, u32[]{:S(2)}) collective-permute-start(bf16[208,768]{1,0:T(8,128)(2,1)S(1)} %get-tuple-element.247), channel_id=1, source_target_pairs={{0,2},{1,3},{2,0},{3,1},{4,6},{5,7},{6,4},{7,5},{8,10},{9,11},{10,... | collective-permute-start | bytes 958472 | tf_op jit(solution)/shard_map/ppermute | solution.py:409
  433.0 8.9 %collective-permute-start.49 = (bf16[208,768]{1,0:T(8,128)(2,1)S(1)}, bf16[208,768]{1,0:T(8,128)(2,1)S(1)}, u32[]{:S(2)}, u32[]{:S(2)}) collective-permute-start(bf16[208,768]{1,0:T(8,128)(2,1)S(1)} %get-tuple-element.249.g0), channel_id=1, source_target_pairs={{0,2},{1,3},{2,0},{3,1},{4,6},{5,7},{6,4},{7,5},{8,10},{9,11},{10,... | collective-permute-start | bytes 958472 | tf_op jit(solution)/shard_map/ppermute | solution.py:409
  434.6 13.7 %collective-permute-start.50 = (bf16[208,768]{1,0:T(8,128)(2,1)S(1)}, bf16[208,768]{1,0:T(8,128)(2,1)S(1)}, u32[]{:S(2)}, u32[]{:S(2)}) collective-permute-start(bf16[208,768]{1,0:T(8,128)(2,1)S(1)} %get-tuple-element.249.g0), channel_id=1, source_target_pairs={{0,1},{1,0},{2,3},{3,2},{4,5},{5,4},{6,7},{7,6},{8,9},{9,8},{10,11... | collective-permute-start | bytes 958472 | tf_op jit(solution)/shard_map/ppermute | solution.py:409
  441.9 29.1 %collective-permute-start.61 = (bf16[384,1536]{1,0:T(8,128)(2,1)}, bf16[384,1536]{1,0:T(8,128)(2,1)}, u32[]{:S(2)}, u32[]{:S(2)}) collective-permute-start(bf16[384,1536]{1,0:T(8,128)(2,1)} %get-tuple-element.281), channel_id=1, source_target_pairs={{0,4},{1,5},{2,6},{3,7},{4,0},{5,1},{6,2},{7,3},{8,12},{9,13},{10,... | collective-permute-start | bytes 3538952 | tf_op jit(solution)/shard_map/ppermute | solution.py:409
  444.4 18.6 %collective-permute-start.54 = (bf16[96,768]{1,0:T(8,128)(2,1)S(1)}, bf16[96,768]{1,0:T(8,128)(2,1)S(1)}, u32[]{:S(2)}, u32[]{:S(2)}) collective-permute-start(bf16[96,768]{1,0:T(8,128)(2,1)S(1)} %get-tuple-element.261), channel_id=1, source_target_pairs={{0,8},{1,9},{2,10},{3,11},{4,12},{5,13},{6,14},{7,15},{8,0},{9,1},... | collective-permute-start | bytes 442376 | tf_op jit(solution)/shard_map/ppermute | solution.py:409
  446.0 17.7 %collective-permute-start.55 = (bf16[96,768]{1,0:T(8,128)(2,1)S(1)}, bf16[96,768]{1,0:T(8,128)(2,1)S(1)}, u32[]{:S(2)}, u32[]{:S(2)}) collective-permute-start(bf16[96,768]{1,0:T(8,128)(2,1)S(1)} %get-tuple-element.262), channel_id=1, source_target_pairs={{0,16},{1,17},{2,18},{3,19},{4,20},{5,21},{6,22},{7,23},{8,24},{9,... | collective-permute-start | bytes 442376 | tf_op jit(solution)/shard_map/ppermute | solution.py:409
  448.2 16.1 %collective-permute-start.56 = (bf16[96,768]{1,0:T(8,128)(2,1)S(1)}, bf16[96,768]{1,0:T(8,128)(2,1)S(1)}, u32[]{:S(2)}, u32[]{:S(2)}) collective-permute-start(bf16[96,768]{1,0:T(8,128)(2,1)S(1)} %get-tuple-element.263), channel_id=1, source_target_pairs={{0,24},{1,25},{2,26},{3,27},{4,28},{5,29},{6,30},{7,31},{8,16},{9,... | collective-permute-start | bytes 442376 | tf_op jit(solution)/shard_map/ppermute | solution.py:409
  448.8 16.2 %collective-permute-start.52 = (bf16[208,768]{1,0:T(8,128)(2,1)S(1)}, bf16[208,768]{1,0:T(8,128)(2,1)S(1)}, u32[]{:S(2)}, u32[]{:S(2)}) collective-permute-start(bf16[208,768]{1,0:T(8,128)(2,1)S(1)} %get-tuple-element.250), channel_id=1, source_target_pairs={{0,2},{1,3},{2,0},{3,1},{4,6},{5,7},{6,4},{7,5},{8,10},{9,11},{10,... | collective-permute-start | bytes 958472 | tf_op jit(solution)/shard_map/ppermute | solution.py:409
  465.1 18.2 %collective-permute-start.59 = (bf16[384,768]{1,0:T(8,128)(2,1)}, bf16[384,768]{1,0:T(8,128)(2,1)}, u32[]{:S(2)}, u32[]{:S(2)}) collective-permute-start(bf16[384,768]{1,0:T(8,128)(2,1)} %copy-done.113), channel_id=1, source_target_pairs={{0,4},{1,5},{2,6},{3,7},{4,0},{5,1},{6,2},{7,3},{8,12},{9,13},{10,... | collective-permute-start | bytes 1769480 | tf_op jit(solution)/shard_map/ppermute | solution.py:409
  468.7 14.6 %collective-permute-start.58 = (bf16[208,768]{1,0:T(8,128)(2,1)S(1)}, bf16[208,768]{1,0:T(8,128)(2,1)S(1)}, u32[]{:S(2)}, u32[]{:S(2)}) collective-permute-start(bf16[208,768]{1,0:T(8,128)(2,1)S(1)} %get-tuple-element.270), channel_id=1, source_target_pairs={{0,2},{1,3},{2,0},{3,1},{4,6},{5,7},{6,4},{7,5},{8,10},{9,11},{10,... | collective-permute-start | bytes 958472 | tf_op jit(solution)/shard_map/ppermute | solution.py:409
  472.5 16.5 %collective-permute-start.62 = (bf16[96,1536]{1,0:T(8,128)(2,1)S(1)}, bf16[96,1536]{1,0:T(8,128)(2,1)S(1)}, u32[]{:S(2)}, u32[]{:S(2)}) collective-permute-start(bf16[96,1536]{1,0:T(8,128)(2,1)S(1)} %get-tuple-element.283), channel_id=1, source_target_pairs={{0,8},{1,9},{2,10},{3,11},{4,12},{5,13},{6,14},{7,15},{8,0},{9,1},... | collective-permute-start | bytes 884744 | tf_op jit(solution)/shard_map/ppermute | solution.py:409
  474.3 23.5 %collective-permute-start.63 = (bf16[96,1536]{1,0:T(8,128)(2,1)S(1)}, bf16[96,1536]{1,0:T(8,128)(2,1)S(1)}, u32[]{:S(2)}, u32[]{:S(2)}) collective-permute-start(bf16[96,1536]{1,0:T(8,128)(2,1)S(1)} %get-tuple-element.284), channel_id=1, source_target_pairs={{0,16},{1,17},{2,18},{3,19},{4,20},{5,21},{6,22},{7,23},{8,24},{9,... | collective-permute-start | bytes 884744 | tf_op jit(solution)/shard_map/ppermute | solution.py:409
  476.6 21.2 %collective-permute-start.64 = (bf16[96,1536]{1,0:T(8,128)(2,1)S(1)}, bf16[96,1536]{1,0:T(8,128)(2,1)S(1)}, u32[]{:S(2)}, u32[]{:S(2)}) collective-permute-start(bf16[96,1536]{1,0:T(8,128)(2,1)S(1)} %get-tuple-element.285), channel_id=1, source_target_pairs={{0,24},{1,25},{2,26},{3,27},{4,28},{5,29},{6,30},{7,31},{8,16},{9,... | collective-permute-start | bytes 884744 | tf_op jit(solution)/shard_map/ppermute | solution.py:409
  508.1 17.7 %collective-permute-start.67 = (bf16[128,768]{1,0:T(8,128)(2,1)}, bf16[128,768]{1,0:T(8,128)(2,1)S(1)}, u32[]{:S(2)}, u32[]{:S(2)}) collective-permute-start(bf16[128,768]{1,0:T(8,128)(2,1)} %get-tuple-element.290), channel_id=1, source_target_pairs={{0,8},{1,9},{2,10},{3,11},{4,12},{5,13},{6,14},{7,15},{8,0},{9,1},... | collective-permute-start | bytes 589832 | tf_op jit(solution)/shard_map/ppermute | solution.py:409
  513.0 14.4 %collective-permute-start.68 = (bf16[128,768]{1,0:T(8,128)(2,1)}, bf16[128,768]{1,0:T(8,128)(2,1)}, u32[]{:S(2)}, u32[]{:S(2)}) collective-permute-start(bf16[128,768]{1,0:T(8,128)(2,1)} %get-tuple-element.291), channel_id=1, source_target_pairs={{0,16},{1,17},{2,18},{3,19},{4,20},{5,21},{6,22},{7,23},{8,24},{9,... | collective-permute-start | bytes 589832 | tf_op jit(solution)/shard_map/ppermute | solution.py:409
  513.9 13.5 %collective-permute-start.69 = (bf16[128,768]{1,0:T(8,128)(2,1)}, bf16[128,768]{1,0:T(8,128)(2,1)}, u32[]{:S(2)}, u32[]{:S(2)}) collective-permute-start(bf16[128,768]{1,0:T(8,128)(2,1)} %get-tuple-element.292), channel_id=1, source_target_pairs={{0,24},{1,25},{2,26},{3,27},{4,28},{5,29},{6,30},{7,31},{8,16},{9,... | collective-permute-start | bytes 589832 | tf_op jit(solution)/shard_map/ppermute | solution.py:409
  (162 other events, 1303.3 us)
Sparse Core Ops, SparseCore 0:
  12.3 50.9 all-gather.1
